TPU v7x, 32 devices: a whole 2x2x4 slice. The times are simulated.
32 devices in a mesh: blk: 8 (over z, x), rep: 4 (over y, core).
Axes of the slice: x: 2, y: 2, z: 4, core: 2. Of those that a mesh axis runs over, the one named last changes fastest.
Arguments:
- signals: bfloat16 [8192, 2048], P('rep', 'blk'), may hold values from -6 to 6
- omega: float32 [8, 5, 256, 256], P('blk', None, 'rep'), may hold values from -1.2 to 3, as said below
- pattern: int32 [8, 5], P('blk'), may hold values from 0 to 7, as said below
Outputs:
- omega_next: float32 [8, 5, 256, 256], P('blk', None, 'rep')
Inputs may be any that keep to these rules, and one draw needn't show every extreme that they name: pattern[i, 0] = i. For two distinct whole numbers A and B from 1 to 3, the same in every row, pattern[i, 1] to pattern[i, 4] are i + A, i - A, i + B and i - B modulo 8 in some order, the same order in every row. Omega is symmetric: omega[i, k] is the transpose of omega[pattern[i, k], k2] where pattern[pattern[i, k], k2] = i. The diagonal entries of omega[i, 0] lie between 1 and 3.
All inputs are finite; a program needn't handle non-finite values.
Results may differ from a plain program's by a relative error of at most 0.0033.
Values may be sent and summed in bfloat16 or wider, within the bound.
No kernel may reach another device: no remote copies, remote signals or barrier semaphores. Data moves between devices by JAX's collectives and lax.ppermute only.
A program may use at most 128 MiB of HBM per device.

v0:
```python
import functools

import jax
import jax.numpy as jnp
from jax import lax
from jax.experimental import pallas as pl
from jax.experimental.pallas import tpu as pltpu
from jax.sharding import PartitionSpec as P

STEP_SIZE = 0.5
PENALTY = 0.1
LOW = 2
F32 = jnp.float32
BF16 = jnp.bfloat16

VMEM = pl.BlockSpec(memory_space=pltpu.VMEM)
ANY = pl.BlockSpec(memory_space=pl.ANY)
SMEM = pl.BlockSpec(memory_space=pltpu.SMEM)
SMALL = pltpu.CompilerParams(vmem_limit_bytes=8 * 2**20)


def stored_offsets(pattern_ref, team, teams):
    drawn = [lax.rem(pattern_ref[0, k] - team + teams, teams) for k in range(1, 5)]
    a = functools.reduce(jnp.minimum, drawn)
    b = functools.reduce(jnp.minimum, [jnp.where(d == a, teams, d) for d in drawn])
    offsets = [jnp.int32(0), a, b, teams - b, teams - a]
    slots = [jnp.int32(0)]
    for offset in offsets[1:]:
        slots.append(sum(jnp.where(d == offset, k + 1, 0) for k, d in enumerate(drawn)))
    return offsets, slots


def prepare_kernel(teams, place_ref, pattern_ref, omega_ref, out_ref):
    _, slots = stored_offsets(pattern_ref, place_ref[0], teams)
    for k in range(3):
        out_ref[k] = omega_ref[0, slots[k]].astype(BF16)


def product_kernel(teams, replicas, tile_rows, place_ref, pattern_ref, own_ref, other_ref, *rest):
    chips = replicas // 2
    planes = LOW * chips
    depth = teams // LOW
    weight_refs, rest = rest[: 2 * planes], rest[2 * planes :]
    outs, rest = rest[:planes], rest[planes:]
    data_ref, omega_ref, mixed_ref, flip_ref, left_ref, data_sems, omega_sems = rest
    team, replica = place_ref[0], place_ref[1]
    core, chip = lax.rem(replica, 2), lax.div(replica, 2)
    high, low = lax.div(team, LOW), lax.rem(team, LOW)
    offsets, _ = stored_offsets(pattern_ref, team, teams)
    times, width = data_ref.shape[1] // 2, data_ref.shape[2]

    copies = [
        pltpu.make_async_copy(source, data_ref.at[:, pl.ds(half * times, times)], data_sems.at[half])
        for half, source in enumerate([own_ref, other_ref])
    ]
    for half in range(2):
        for mx in range(LOW):
            for my in range(chips):
                plane = mx * chips + my
                row = (2 * (chip ^ my) + (core ^ half)) * tile_rows
                for mz in range(depth):
                    i = (high ^ mz) * LOW + (low ^ mx)
                    target = omega_ref.at[i, :, pl.ds(pl.multiple_of(row, tile_rows), tile_rows)]
                    copies.append(
                        pltpu.make_async_copy(
                            weight_refs[half * planes + plane].at[mz],
                            target,
                            omega_sems.at[(half * planes + plane) * depth + mz],
                        )
                    )
    for copy in copies:
        copy.start()
    for copy in copies:
        copy.wait()

    nn = (((1,), (0,)), ((), ()))
    nt = (((1,), (1,)), ((), ()))

    def mix(i, carry):
        total = None
        for k, offset in enumerate(offsets):
            c = lax.rem(i + offset, teams)
            if k < 3:
                term = lax.dot_general(data_ref[c], omega_ref[i, k], nt, preferred_element_type=F32)
            else:
                term = lax.dot_general(data_ref[c], omega_ref[c, 5 - k], nn, preferred_element_type=F32)
            total = term if total is None else total + term
        mixed = total.astype(BF16)
        mixed_ref[i] = mixed
        flip_ref[:, : 2 * times] = mixed.T
        flip_ref[:, 2 * times :] = data_ref[i].T
        for m in range(chips):
            row = (2 * (chip ^ m) + core) * tile_rows
            left_ref[i, m * tile_rows : (m + 1) * tile_rows] = flip_ref[
                pl.ds(pl.multiple_of(row, tile_rows), tile_rows)
            ]
        return carry

    unroll = teams <= 8
    lax.fori_loop(0, teams, mix, 0, unroll=unroll)
    for mx in range(LOW):

        def outer(z, carry):
            i = z * LOW + (low ^ mx)
            for k, offset in enumerate(offsets):
                c = lax.rem(i + offset, teams)
                right = jnp.concatenate([data_ref[c], mixed_ref[c]], axis=0)
                part = lax.dot_general(left_ref[i], right, nn, preferred_element_type=F32).astype(BF16)
                for m in range(chips):
                    outs[mx * chips + m][z, k] = part[m * tile_rows : (m + 1) * tile_rows]
            return carry

        lax.fori_loop(0, depth, outer, 0, unroll=unroll)


def add_kernel(teams, place_ref, *rest):
    count = teams // LOW
    parts, outs = rest[:-count], rest[-count:]
    z = lax.div(place_ref[0], LOW)
    for m in range(count):
        total = parts[0][z ^ m].astype(F32)
        for part in parts[1:]:
            total = total + part[z ^ m].astype(F32)
        outs[m][...] = total.astype(outs[m].dtype)


def update_kernel(teams, scale, place_ref, pattern_ref, omega_ref, *rest):
    parts, out_ref = rest[:-1], rest[-1]
    _, slots = stored_offsets(pattern_ref, place_ref[0], teams)
    rows, width = out_ref.shape[2:]
    first = place_ref[1] * rows
    row_ids = first + lax.broadcasted_iota(jnp.int32, (rows, width), 0)
    diagonal = row_ids == lax.broadcasted_iota(jnp.int32, (rows, width), 1)
    for k in range(5):
        total = parts[0][k].astype(F32)
        for part in parts[1:]:
            total = total + part[k].astype(F32)
        current = omega_ref[0, slots[k]]
        gradient = total * scale
        if k == 0:
            gradient = gradient - jnp.where(diagonal, 1.0 / current, 0.0)
        value = current - STEP_SIZE * gradient
        bound = STEP_SIZE * PENALTY
        shrunk = jnp.where(value > bound, value - bound, jnp.where(value < -bound, value + bound, 0.0))
        if k == 0:
            shrunk = jnp.where(diagonal, value, shrunk)
        out_ref[0, slots[k]] = shrunk


def per_device(teams, replicas, signals, omega, pattern):
    chips = replicas // 2
    slots, tile_rows, width = omega.shape[1:]
    times = signals.shape[0] // teams
    place = jnp.stack([lax.axis_index("blk"), lax.axis_index("rep")]).astype(jnp.int32)

    def swap(array, blk_mask, rep_mask):
        route = [
            (b * replicas + r, (b ^ blk_mask) * replicas + (r ^ rep_mask))
            for b in range(teams)
            for r in range(replicas)
        ]
        return lax.ppermute(array, ("blk", "rep"), route)

    planes = LOW * chips
    count = teams // LOW
    upper = pl.pallas_call(
        functools.partial(prepare_kernel, teams),
        out_shape=jax.ShapeDtypeStruct((3, tile_rows, width), BF16),
        in_specs=[SMEM, SMEM, VMEM],
        out_specs=VMEM,
        compiler_params=SMALL,
        name="prepare",
    )(place, pattern, omega)

    line = jnp.stack([upper] + [swap(upper, m * LOW, 0) for m in range(1, count)])
    line, signals = lax.optimization_barrier((line, signals))
    weights = [
        swap(line, mx, 2 * my) if mx + my else line for mx in range(LOW) for my in range(chips)
    ]
    own = lax.all_to_all(signals.reshape(teams, times, width), "blk", 0, 0)
    other = swap(own, 0, 1)
    weights += [swap(array, 0, 1) for array in weights]

    partial = pl.pallas_call(
        functools.partial(product_kernel, teams, replicas, tile_rows),
        out_shape=[jax.ShapeDtypeStruct((count, slots, tile_rows, width), BF16)] * planes,
        in_specs=[SMEM, SMEM] + [ANY] * (2 + 2 * planes),
        out_specs=[VMEM] * planes,
        scratch_shapes=[
            pltpu.VMEM((teams, 2 * times, width), BF16),
            pltpu.VMEM((teams, 3, width, width), BF16),
            pltpu.VMEM((teams, 2 * times, width), BF16),
            pltpu.VMEM((width, 4 * times), BF16),
            pltpu.VMEM((teams, chips * tile_rows, 4 * times), BF16),
            pltpu.SemaphoreType.DMA((2,)),
            pltpu.SemaphoreType.DMA((2 * planes * count,)),
        ],
        compiler_params=pltpu.CompilerParams(vmem_limit_bytes=(16 if teams <= 8 else 48) * 2**20),
        name="products",
    )(place, pattern, own, other, *weights)
    received = [
        swap(partial[mx * chips + my], mx, 2 * my) if mx + my else partial[0]
        for mx in range(LOW)
        for my in range(chips)
    ]

    summed = pl.pallas_call(
        functools.partial(add_kernel, teams),
        out_shape=[
            jax.ShapeDtypeStruct((slots, tile_rows, width), BF16 if m else F32) for m in range(count)
        ],
        in_specs=[SMEM] + [VMEM] * planes,
        out_specs=[VMEM] * count,
        compiler_params=pltpu.CompilerParams(vmem_limit_bytes=(8 if teams <= 8 else 48) * 2**20),
        name="plane_sum",
    )(place, *received)
    arrived = [swap(summed[m], m * LOW, 0) if m else summed[0] for m in range(count)]

    scale = 1.0 / (2.0 * signals.shape[0] * replicas)
    return pl.pallas_call(
        functools.partial(update_kernel, teams, scale),
        out_shape=jax.ShapeDtypeStruct(omega.shape, F32),
        in_specs=[SMEM, SMEM, VMEM] + [VMEM] * count,
        out_specs=VMEM,
        compiler_params=pltpu.CompilerParams(vmem_limit_bytes=(8 if teams <= 8 else 48) * 2**20),
        name="update",
    )(place, pattern, omega, *arrived)


def solution(mesh):
    return jax.shard_map(
        functools.partial(per_device, mesh.shape["blk"], mesh.shape["rep"]),
        mesh=mesh,
        in_specs=(P("rep", "blk"), P("blk", None, "rep", None), P("blk", None)),
        out_specs=P("blk", None, "rep", None),
        check_vma=False,
    )
```

profile of v0, /device:TPU:0, one launch (start us, length us, event | category | flops | bytes accessed | tf_op | source)
XLA Modules:
  0.0 126.6 jit_solution(856990187335668168)
XLA Ops:
  0.0 0.1 pad_add_fusion.place_ref
  0.1 0.6 copy-done.2
  0.7 0.0 copy-start
  0.7 1.0 copy-done
  1.6 0.0 copy-start.3
  1.6 0.6 prepare.1
  2.2 5.1 %collective-permute-start.2 = (bf16[3,64,256]{2,1,0:T(8,128)(2,1)S(1)}, bf16[3,64,256]{2,1,0:T(8,128)(2,1)S(1)}, u32[]{:S(2)}, u32[]{:S(2)}) collective-permute-start(bf16[3,64,256]{2,1,0:T(8,128)(2,1)S(1)} %prepare.1), channel_id=1, source_target_pairs={{0,24},{1,25},{2,26},{3,27},{4,28},{5,29},{6,30},{7,31},{8,16},{9,... | collective-permute-start | bytes 294920 | tf_op jit(solution)/shard_map/ppermute | solution.py:162
  7.3 0.0 collective-permute-start.1
  7.3 0.6 collective-permute-start
  8.0 3.1 %collective-permute-done.2 = bf16[3,64,256]{2,1,0:T(8,128)(2,1)S(1)} collective-permute-done((bf16[3,64,256]{2,1,0:T(8,128)(2,1)S(1)}, bf16[3,64,256]{2,1,0:T(8,128)(2,1)S(1)}, u32[]{:S(2)}, u32[]{:S(2)}) %collective-permute-start.2) | collective-permute-done | bytes 98336 | tf_op jit(solution)/shard_map/ppermute | solution.py:162
  11.0 4.6 %collective-permute-done.1 = bf16[3,64,256]{2,1,0:T(8,128)(2,1)S(1)} collective-permute-done((bf16[3,64,256]{2,1,0:T(8,128)(2,1)S(1)}, bf16[3,64,256]{2,1,0:T(8,128)(2,1)S(1)}, u32[]{:S(2)}, u32[]{:S(2)}) %collective-permute-start.1) | collective-permute-done | bytes 98336 | tf_op jit(solution)/shard_map/ppermute | solution.py:162
  15.6 0.0 collective-permute-done
  15.6 0.1 pad_maximum_fusion.rest_0_
  15.7 0.0 copy-done.3
  15.7 29.2 %all_to_all.5.own_ref = bf16[8,256,256]{2,1,0:T(8,128)(2,1)S(1)} all-to-all(bf16[8,256,256]{2,1,0:T(8,128)(2,1)S(1)} %bitcast.8), channel_id=1, replica_groups=mesh['blk'=8,'rep'=4] {'blk'}, dimensions={0} | all-to-all | bytes 2097152 | tf_op jit(solution)/shard_map/all_to_all | solution.py:180
  44.9 0.0 collective-permute-start.3
  44.9 2.4 %collective-permute-start.6 = (bf16[4,3,64,256]{3,2,1,0:T(8,128)(2,1)S(1)}, bf16[4,3,64,256]{3,2,1,0:T(8,128)(2,1)S(1)}, u32[]{:S(2)}, u32[]{:S(2)}) collective-permute-start(bf16[4,3,64,256]{3,2,1,0:T(8,128)(2,1)S(1)} %pad_maximum_fusion.rest_0_), channel_id=1, source_target_pairs={{0,6},{1,7},{2,4},{3,5},{4,2},{5,3},{6,0},{7,1},{8,14},{9,15},{10,... | collective-permute-start | bytes 1179656 | tf_op jit(solution)/shard_map/ppermute | solution.py:162
  47.3 0.6 collective-permute-start.5
  47.9 0.5 collective-permute-start.4
  48.4 0.0 collective-permute-start.7
  48.4 9.4 %collective-permute-done.6.rest_3_ = bf16[4,3,64,256]{3,2,1,0:T(8,128)(2,1)S(1)} collective-permute-done((bf16[4,3,64,256]{3,2,1,0:T(8,128)(2,1)S(1)}, bf16[4,3,64,256]{3,2,1,0:T(8,128)(2,1)S(1)}, u32[]{:S(2)}, u32[]{:S(2)}) %collective-permute-start.6) | collective-permute-done | bytes 393248 | tf_op jit(solution)/shard_map/ppermute | solution.py:162
  57.7 0.0 collective-permute-start.10
  57.7 8.1 %collective-permute-done.5.rest_2_ = bf16[4,3,64,256]{3,2,1,0:T(8,128)(2,1)S(1)} collective-permute-done((bf16[4,3,64,256]{3,2,1,0:T(8,128)(2,1)S(1)}, bf16[4,3,64,256]{3,2,1,0:T(8,128)(2,1)S(1)}, u32[]{:S(2)}, u32[]{:S(2)}) %collective-permute-start.5) | collective-permute-done | bytes 393248 | tf_op jit(solution)/shard_map/ppermute | solution.py:162
  65.8 0.0 collective-permute-start.9
  65.8 0.0 collective-permute-done.4.rest_1_
  65.8 0.5 collective-permute-start.8
  66.4 0.0 collective-permute-done.7.rest_4_
  66.4 0.0 collective-permute-done.10.rest_7_
  66.4 1.2 collective-permute-done.9.rest_6_
  67.6 0.6 collective-permute-done.8.rest_5_
  68.1 0.0 collective-permute-done.3.other_ref
  68.1 8.8 %products.1 = (bf16[4,5,64,256]{3,2,1,0:T(8,128)(2,1)S(1)}, bf16[4,5,64,256]{3,2,1,0:T(8,128)(2,1)S(1)}, bf16[4,5,64,256]{3,2,1,0:T(8,128)(2,1)S(1)}, bf16[4,5,64,256]{3,2,1,0:T(8,128)(2,1)S(1)}) custom-call(s32[2]{0:T(128)S(1)} %pad_add_fusion.place_ref, s32[1,5]{1,0:T(1,128)S(1)} %copy-done.2, bf16[8,256,256]{2,1,0:T(8,128)(2,1)S(1)} %all_to_all.5.own_ref, ...), custom_call_target="tpu_custom_call" | custom-call | tf_op jit(solution)/shard_map/products/pallas_call | solution.py:184
  77.0 0.9 collective-permute-start.11
  77.9 1.4 %collective-permute-start.12 = (bf16[4,5,64,256]{3,2,1,0:T(8,128)(2,1)S(1)}, bf16[4,5,64,256]{3,2,1,0:T(8,128)(2,1)S(1)}, u32[]{:S(2)}, u32[]{:S(2)}) collective-permute-start(bf16[4,5,64,256]{3,2,1,0:T(8,128)(2,1)S(1)} %get-tuple-element.19), channel_id=1, source_target_pairs={{0,4},{1,5},{2,6},{3,7},{4,0},{5,1},{6,2},{7,3},{8,12},{9,13},{10,... | collective-permute-start | bytes 1966088 | tf_op jit(solution)/shard_map/ppermute | solution.py:162
  79.3 1.2 collective-permute-start.13
  80.5 13.3 %collective-permute-done.11.rest_1_ = bf16[4,5,64,256]{3,2,1,0:T(8,128)(2,1)S(1)} collective-permute-done((bf16[4,5,64,256]{3,2,1,0:T(8,128)(2,1)S(1)}, bf16[4,5,64,256]{3,2,1,0:T(8,128)(2,1)S(1)}, u32[]{:S(2)}, u32[]{:S(2)}) %collective-permute-start.11) | collective-permute-done | bytes 655392 | tf_op jit(solution)/shard_map/ppermute | solution.py:162
  93.8 1.7 %collective-permute-done.12.rest_2_ = bf16[4,5,64,256]{3,2,1,0:T(8,128)(2,1)S(1)} collective-permute-done((bf16[4,5,64,256]{3,2,1,0:T(8,128)(2,1)S(1)}, bf16[4,5,64,256]{3,2,1,0:T(8,128)(2,1)S(1)}, u32[]{:S(2)}, u32[]{:S(2)}) %collective-permute-start.12) | collective-permute-done | bytes 655392 | tf_op jit(solution)/shard_map/ppermute | solution.py:162
  95.5 13.5 %collective-permute-done.13.rest_3_ = bf16[4,5,64,256]{3,2,1,0:T(8,128)(2,1)S(1)} collective-permute-done((bf16[4,5,64,256]{3,2,1,0:T(8,128)(2,1)S(1)}, bf16[4,5,64,256]{3,2,1,0:T(8,128)(2,1)S(1)}, u32[]{:S(2)}, u32[]{:S(2)}) %collective-permute-start.13) | collective-permute-done | bytes 655392 | tf_op jit(solution)/shard_map/ppermute | solution.py:162
  109.1 0.0 copy-start.1
  109.1 0.9 plane_sum.1
  109.9 1.1 collective-permute-start.14
  111.1 0.6 collective-permute-start.15
  111.6 2.7 %collective-permute-start.16 = (bf16[5,64,256]{2,1,0:T(8,128)(2,1)S(1)}, bf16[5,64,256]{2,1,0:T(8,128)(2,1)S(1)}, u32[]{:S(2)}, u32[]{:S(2)}) collective-permute-start(bf16[5,64,256]{2,1,0:T(8,128)(2,1)S(1)} %get-tuple-element.24), channel_id=1, source_target_pairs={{0,24},{1,25},{2,26},{3,27},{4,28},{5,29},{6,30},{7,31},{8,16},{9,... | collective-permute-start | bytes 491528 | tf_op jit(solution)/shard_map/ppermute | solution.py:162
  114.4 3.2 %collective-permute-done.14.rest_1_ = bf16[5,64,256]{2,1,0:T(8,128)(2,1)S(1)} collective-permute-done((bf16[5,64,256]{2,1,0:T(8,128)(2,1)S(1)}, bf16[5,64,256]{2,1,0:T(8,128)(2,1)S(1)}, u32[]{:S(2)}, u32[]{:S(2)}) %collective-permute-start.14) | collective-permute-done | bytes 163872 | tf_op jit(solution)/shard_map/ppermute | solution.py:162
  117.6 7.5 %collective-permute-done.15.rest_2_ = bf16[5,64,256]{2,1,0:T(8,128)(2,1)S(1)} collective-permute-done((bf16[5,64,256]{2,1,0:T(8,128)(2,1)S(1)}, bf16[5,64,256]{2,1,0:T(8,128)(2,1)S(1)}, u32[]{:S(2)}, u32[]{:S(2)}) %collective-permute-start.15) | collective-permute-done | bytes 163872 | tf_op jit(solution)/shard_map/ppermute | solution.py:162
  125.1 0.0 collective-permute-done.16.rest_3_
  125.1 0.0 copy-done.1
  125.1 1.5 %update.1 = f32[1,5,64,256]{3,2,1,0:T(8,128)} custom-call(s32[2]{0:T(128)S(1)} %pad_add_fusion.place_ref, s32[1,5]{1,0:T(1,128)S(1)} %copy-done.2, f32[1,5,64,256]{3,2,1,0:T(8,128)S(1)} %copy-done.1, f32[5,64,256]{2,1,0:T(8,128)S(1)} %get-tuple-element.21.rest_0_, bf16[5,64,256]{2,1,0:T(8,128)(2,1)S(1)} %collective-permute-done.14.rest_1_, ...), custom_call_target="tpu_custom_call" | custom-call | tf_op jit(solution)/shard_map/update/pallas_call | solution.py:220
  (1 shorter events, 0.0 us)
Async XLA Ops:
  0.0 0.7 copy-start.2
  0.7 1.0 copy-start
  1.6 14.0 %copy-start.3 = (bf16[2048,256]{1,0:T(8,128)(2,1)S(1)}, bf16[2048,256]{1,0:T(8,128)(2,1)}, u32[]{:S(2)}) copy-start(bf16[2048,256]{1,0:T(8,128)(2,1)} %param.3) | copy-start | bytes 3145732
  2.2 8.8 %collective-permute-start.2 = (bf16[3,64,256]{2,1,0:T(8,128)(2,1)S(1)}, bf16[3,64,256]{2,1,0:T(8,128)(2,1)S(1)}, u32[]{:S(2)}, u32[]{:S(2)}) collective-permute-start(bf16[3,64,256]{2,1,0:T(8,128)(2,1)S(1)} %prepare.1), channel_id=1, source_target_pairs={{0,24},{1,25},{2,26},{3,27},{4,28},{5,29},{6,30},{7,31},{8,16},{9,... | collective-permute-start | bytes 294920 | tf_op jit(solution)/shard_map/ppermute | solution.py:162
  7.3 8.3 %collective-permute-start.1 = (bf16[3,64,256]{2,1,0:T(8,128)(2,1)S(1)}, bf16[3,64,256]{2,1,0:T(8,128)(2,1)S(1)}, u32[]{:S(2)}, u32[]{:S(2)}) collective-permute-start(bf16[3,64,256]{2,1,0:T(8,128)(2,1)S(1)} %prepare.1), channel_id=1, source_target_pairs={{0,16},{1,17},{2,18},{3,19},{4,20},{5,21},{6,22},{7,23},{8,24},{9,... | collective-permute-start | bytes 294920 | tf_op jit(solution)/shard_map/ppermute | solution.py:162
  7.3 8.3 %collective-permute-start = (bf16[3,64,256]{2,1,0:T(8,128)(2,1)S(1)}, bf16[3,64,256]{2,1,0:T(8,128)(2,1)S(1)}, u32[]{:S(2)}, u32[]{:S(2)}) collective-permute-start(bf16[3,64,256]{2,1,0:T(8,128)(2,1)S(1)} %prepare.1), channel_id=1, source_target_pairs={{0,8},{1,9},{2,10},{3,11},{4,12},{5,13},{6,14},{7,15},{8,0},{9,1},... | collective-permute-start | bytes 294920 | tf_op jit(solution)/shard_map/ppermute | solution.py:162
  44.9 23.2 %collective-permute-start.3 = (bf16[8,256,256]{2,1,0:T(8,128)(2,1)S(1)}, bf16[8,256,256]{2,1,0:T(8,128)(2,1)S(1)}, u32[]{:S(2)}, u32[]{:S(2)}) collective-permute-start(bf16[8,256,256]{2,1,0:T(8,128)(2,1)S(1)} %all_to_all.5.own_ref), channel_id=1, source_target_pairs={{0,1},{1,0},{2,3},{3,2},{4,5},{5,4},{6,7},{7,6},{8,9},{9,8},{10,11... | collective-permute-start | bytes 3145736 | tf_op jit(solution)/shard_map/ppermute | solution.py:162
  44.9 12.9 %collective-permute-start.6 = (bf16[4,3,64,256]{3,2,1,0:T(8,128)(2,1)S(1)}, bf16[4,3,64,256]{3,2,1,0:T(8,128)(2,1)S(1)}, u32[]{:S(2)}, u32[]{:S(2)}) collective-permute-start(bf16[4,3,64,256]{3,2,1,0:T(8,128)(2,1)S(1)} %pad_maximum_fusion.rest_0_), channel_id=1, source_target_pairs={{0,6},{1,7},{2,4},{3,5},{4,2},{5,3},{6,0},{7,1},{8,14},{9,15},{10,... | collective-permute-start | bytes 1179656 | tf_op jit(solution)/shard_map/ppermute | solution.py:162
  47.3 18.6 %collective-permute-start.5 = (bf16[4,3,64,256]{3,2,1,0:T(8,128)(2,1)S(1)}, bf16[4,3,64,256]{3,2,1,0:T(8,128)(2,1)S(1)}, u32[]{:S(2)}, u32[]{:S(2)}) collective-permute-start(bf16[4,3,64,256]{3,2,1,0:T(8,128)(2,1)S(1)} %pad_maximum_fusion.rest_0_), channel_id=1, source_target_pairs={{0,4},{1,5},{2,6},{3,7},{4,0},{5,1},{6,2},{7,3},{8,12},{9,13},{10,... | collective-permute-start | bytes 1179656 | tf_op jit(solution)/shard_map/ppermute | solution.py:162
  47.9 18.0 %collective-permute-start.4 = (bf16[4,3,64,256]{3,2,1,0:T(8,128)(2,1)S(1)}, bf16[4,3,64,256]{3,2,1,0:T(8,128)(2,1)S(1)}, u32[]{:S(2)}, u32[]{:S(2)}) collective-permute-start(bf16[4,3,64,256]{3,2,1,0:T(8,128)(2,1)S(1)} %pad_maximum_fusion.rest_0_), channel_id=1, source_target_pairs={{0,2},{1,3},{2,0},{3,1},{4,6},{5,7},{6,4},{7,5},{8,10},{9,11},{10,... | collective-permute-start | bytes 1179656 | tf_op jit(solution)/shard_map/ppermute | solution.py:162
  48.4 18.0 %collective-permute-start.7 = (bf16[4,3,64,256]{3,2,1,0:T(8,128)(2,1)S(1)}, bf16[4,3,64,256]{3,2,1,0:T(8,128)(2,1)S(1)}, u32[]{:S(2)}, u32[]{:S(2)}) collective-permute-start(bf16[4,3,64,256]{3,2,1,0:T(8,128)(2,1)S(1)} %pad_maximum_fusion.rest_0_), channel_id=1, source_target_pairs={{0,1},{1,0},{2,3},{3,2},{4,5},{5,4},{6,7},{7,6},{8,9},{9,8},{10,11... | collective-permute-start | bytes 1179656 | tf_op jit(solution)/shard_map/ppermute | solution.py:162
  57.7 8.6 %collective-permute-start.10 = (bf16[4,3,64,256]{3,2,1,0:T(8,128)(2,1)S(1)}, bf16[4,3,64,256]{3,2,1,0:T(8,128)(2,1)S(1)}, u32[]{:S(2)}, u32[]{:S(2)}) collective-permute-start(bf16[4,3,64,256]{3,2,1,0:T(8,128)(2,1)S(1)} %collective-permute-done.6.rest_3_), channel_id=1, source_target_pairs={{0,1},{1,0},{2,3},{3,2},{4,5},{5,4},{6,7},{7,6},{8,9},{9,8},{10,11... | collective-permute-start | bytes 1179656 | tf_op jit(solution)/shard_map/ppermute | solution.py:162
  65.8 1.7 %collective-permute-start.9 = (bf16[4,3,64,256]{3,2,1,0:T(8,128)(2,1)S(1)}, bf16[4,3,64,256]{3,2,1,0:T(8,128)(2,1)S(1)}, u32[]{:S(2)}, u32[]{:S(2)}) collective-permute-start(bf16[4,3,64,256]{3,2,1,0:T(8,128)(2,1)S(1)} %collective-permute-done.5.rest_2_), channel_id=1, source_target_pairs={{0,1},{1,0},{2,3},{3,2},{4,5},{5,4},{6,7},{7,6},{8,9},{9,8},{10,11... | collective-permute-start | bytes 1179656 | tf_op jit(solution)/shard_map/ppermute | solution.py:162
  65.8 2.3 %collective-permute-start.8 = (bf16[4,3,64,256]{3,2,1,0:T(8,128)(2,1)S(1)}, bf16[4,3,64,256]{3,2,1,0:T(8,128)(2,1)S(1)}, u32[]{:S(2)}, u32[]{:S(2)}) collective-permute-start(bf16[4,3,64,256]{3,2,1,0:T(8,128)(2,1)S(1)} %collective-permute-done.4.rest_1_), channel_id=1, source_target_pairs={{0,1},{1,0},{2,3},{3,2},{4,5},{5,4},{6,7},{7,6},{8,9},{9,8},{10,11... | collective-permute-start | bytes 1179656 | tf_op jit(solution)/shard_map/ppermute | solution.py:162
  77.0 16.8 %collective-permute-start.11 = (bf16[4,5,64,256]{3,2,1,0:T(8,128)(2,1)S(1)}, bf16[4,5,64,256]{3,2,1,0:T(8,128)(2,1)S(1)}, u32[]{:S(2)}, u32[]{:S(2)}) collective-permute-start(bf16[4,5,64,256]{3,2,1,0:T(8,128)(2,1)S(1)} %get-tuple-element.18), channel_id=1, source_target_pairs={{0,2},{1,3},{2,0},{3,1},{4,6},{5,7},{6,4},{7,5},{8,10},{9,11},{10,... | collective-permute-start | bytes 1966088 | tf_op jit(solution)/shard_map/ppermute | solution.py:162
  77.9 17.6 %collective-permute-start.12 = (bf16[4,5,64,256]{3,2,1,0:T(8,128)(2,1)S(1)}, bf16[4,5,64,256]{3,2,1,0:T(8,128)(2,1)S(1)}, u32[]{:S(2)}, u32[]{:S(2)}) collective-permute-start(bf16[4,5,64,256]{3,2,1,0:T(8,128)(2,1)S(1)} %get-tuple-element.19), channel_id=1, source_target_pairs={{0,4},{1,5},{2,6},{3,7},{4,0},{5,1},{6,2},{7,3},{8,12},{9,13},{10,... | collective-permute-start | bytes 1966088 | tf_op jit(solution)/shard_map/ppermute | solution.py:162
  79.3 29.7 %collective-permute-start.13 = (bf16[4,5,64,256]{3,2,1,0:T(8,128)(2,1)S(1)}, bf16[4,5,64,256]{3,2,1,0:T(8,128)(2,1)S(1)}, u32[]{:S(2)}, u32[]{:S(2)}) collective-permute-start(bf16[4,5,64,256]{3,2,1,0:T(8,128)(2,1)S(1)} %get-tuple-element.20), channel_id=1, source_target_pairs={{0,6},{1,7},{2,4},{3,5},{4,2},{5,3},{6,0},{7,1},{8,14},{9,15},{10,... | collective-permute-start | bytes 1966088 | tf_op jit(solution)/shard_map/ppermute | solution.py:162
  109.1 16.1 %copy-start.1 = (f32[1,5,64,256]{3,2,1,0:T(8,128)S(1)}, f32[1,5,64,256]{3,2,1,0:T(8,128)}, u32[]{:S(2)}) copy-start(f32[1,5,64,256]{3,2,1,0:T(8,128)} %omega_ref.3) | copy-start | bytes 983044
  109.9 7.7 %collective-permute-start.14 = (bf16[5,64,256]{2,1,0:T(8,128)(2,1)S(1)}, bf16[5,64,256]{2,1,0:T(8,128)(2,1)S(1)}, u32[]{:S(2)}, u32[]{:S(2)}) collective-permute-start(bf16[5,64,256]{2,1,0:T(8,128)(2,1)S(1)} %get-tuple-element.22), channel_id=1, source_target_pairs={{0,8},{1,9},{2,10},{3,11},{4,12},{5,13},{6,14},{7,15},{8,0},{9,1},... | collective-permute-start | bytes 491528 | tf_op jit(solution)/shard_map/ppermute | solution.py:162
  111.1 14.1 %collective-permute-start.15 = (bf16[5,64,256]{2,1,0:T(8,128)(2,1)S(1)}, bf16[5,64,256]{2,1,0:T(8,128)(2,1)S(1)}, u32[]{:S(2)}, u32[]{:S(2)}) collective-permute-start(bf16[5,64,256]{2,1,0:T(8,128)(2,1)S(1)} %get-tuple-element.23), channel_id=1, source_target_pairs={{0,16},{1,17},{2,18},{3,19},{4,20},{5,21},{6,22},{7,23},{8,24},{9,... | collective-permute-start | bytes 491528 | tf_op jit(solution)/shard_map/ppermute | solution.py:162
  111.6 13.5 %collective-permute-start.16 = (bf16[5,64,256]{2,1,0:T(8,128)(2,1)S(1)}, bf16[5,64,256]{2,1,0:T(8,128)(2,1)S(1)}, u32[]{:S(2)}, u32[]{:S(2)}) collective-permute-start(bf16[5,64,256]{2,1,0:T(8,128)(2,1)S(1)} %get-tuple-element.24), channel_id=1, source_target_pairs={{0,24},{1,25},{2,26},{3,27},{4,28},{5,29},{6,30},{7,31},{8,16},{9,... | collective-permute-start | bytes 491528 | tf_op jit(solution)/shard_map/ppermute | solution.py:162
where the time goes:
time: 127 us
  waiting for transfers between devices  66.1 us (52%)
  blocking collectives  29.2 us (23%)
  starting transfers between devices  17.8 us (14%)
  Pallas kernels  11.8 us (9%)
  local copies, waits for them, and re-layouts  1.56 us (1%)
    ppermute x17, waiting for transfers between devices, swap(): return lax.ppermute(array, ('blk', 'rep'), route)  66.1 us
    all_to_all x1, blocking collectives, per_device(): own = lax.all_to_all(signals.reshape(teams, times, width), 'blk', 0, 0)  29.2 us
    ppermute x17, starting transfers between devices, swap(): return lax.ppermute(array, ('blk', 'rep'), route)  17.8 us
    pallas_call x1, Pallas kernels, per_device(): pl.pallas_call(functools.partial(product_kernel, teams, replicas, tile_ro...  8.85 us
  transfers between devices with their start and end apart: 17, of which 11 were waited for; matrix products, arithmetic and copies ran while one was open for 0% of the time, Pallas kernels for 0%

commit v1 on v0

--- a/solution.py
+++ b/solution.py
@@ -36,7 +36,7 @@
         out_ref[k] = omega_ref[0, slots[k]].astype(BF16)
 
 
-def product_kernel(teams, replicas, tile_rows, place_ref, pattern_ref, own_ref, other_ref, *rest):
+def product_kernel(teams, replicas, tile_rows, place_ref, pattern_ref, own_ref, low_ref, high_ref, *rest):
     chips = replicas // 2
     planes = LOW * chips
     depth = teams // LOW
@@ -49,10 +49,10 @@
     offsets, _ = stored_offsets(pattern_ref, team, teams)
     times, width = data_ref.shape[1] // 2, data_ref.shape[2]
 
-    copies = [
-        pltpu.make_async_copy(source, data_ref.at[:, pl.ds(half * times, times)], data_sems.at[half])
-        for half, source in enumerate([own_ref, other_ref])
-    ]
+    copies = []
+    for n, (source, first, half) in enumerate([(own_ref, 0, 0), (low_ref, 0, 1), (high_ref, teams // 2, 1)]):
+        target = data_ref.at[pl.ds(first, source.shape[0]), pl.ds(half * times, times)]
+        copies.append(pltpu.make_async_copy(source, target, data_sems.at[n]))
     for half in range(2):
         for mx in range(LOW):
             for my in range(chips):
@@ -178,13 +178,13 @@
         swap(line, mx, 2 * my) if mx + my else line for mx in range(LOW) for my in range(chips)
     ]
     own = lax.all_to_all(signals.reshape(teams, times, width), "blk", 0, 0)
-    other = swap(own, 0, 1)
+    other = [swap(part, 0, 1) for part in jnp.split(own, 2)]
     weights += [swap(array, 0, 1) for array in weights]
 
     partial = pl.pallas_call(
         functools.partial(product_kernel, teams, replicas, tile_rows),
         out_shape=[jax.ShapeDtypeStruct((count, slots, tile_rows, width), BF16)] * planes,
-        in_specs=[SMEM, SMEM] + [ANY] * (2 + 2 * planes),
+        in_specs=[SMEM, SMEM] + [ANY] * (3 + 2 * planes),
         out_specs=[VMEM] * planes,
         scratch_shapes=[
             pltpu.VMEM((teams, 2 * times, width), BF16),
@@ -192,12 +192,12 @@
             pltpu.VMEM((teams, 2 * times, width), BF16),
             pltpu.VMEM((width, 4 * times), BF16),
             pltpu.VMEM((teams, chips * tile_rows, 4 * times), BF16),
-            pltpu.SemaphoreType.DMA((2,)),
+            pltpu.SemaphoreType.DMA((3,)),
             pltpu.SemaphoreType.DMA((2 * planes * count,)),
         ],
         compiler_params=pltpu.CompilerParams(vmem_limit_bytes=(16 if teams <= 8 else 48) * 2**20),
         name="products",
-    )(place, pattern, own, other, *weights)
+    )(place, pattern, own, *other, *weights)
     received = [
         swap(partial[mx * chips + my], mx, 2 * my) if mx + my else partial[0]
         for mx in range(LOW)

time: 127 us -> 112 us (0.88)
  blocking collectives: 29.2 us -> 0 us
  waiting for transfers between devices: 66.1 us -> 75.2 us
  starting transfers between devices: 17.8 us -> 23.3 us
    all_to_all x1 -> x0, blocking collectives: 29.2 us -> none  [per_device(): own = lax.all_to_all(signals.reshape(teams, times, width), 'blk', 0, 0)]
    all_to_all x0 -> x1, waiting for transfers between devices: none -> 21.3 us  [per_device(): own = lax.all_to_all(signals.reshape(teams, times, width), 'blk', 0, 0)]
    ppermute x17 -> x18, waiting for transfers between devices: 66.1 us -> 53.9 us  [swap(): return lax.ppermute(array, ('blk', 'rep'), route)]
    all_to_all x0 -> x1, starting transfers between devices: none -> 4.73 us  [per_device(): own = lax.all_to_all(signals.reshape(teams, times, width), 'blk', 0, 0)]
    ppermute x17 -> x18, starting transfers between devices: 17.8 us -> 18.5 us  [swap(): return lax.ppermute(array, ('blk', 'rep'), route)]
  transfers between devices with their start and end apart: 17 -> 19, of which waited for: 11 -> 11; matrix products, arithmetic and copies ran while one was open for 0% -> 0% of each run, Pallas kernels for 0% -> 0%
where the time goes in v1:
time: 112 us
  waiting for transfers between devices  75.2 us (67%)
  starting transfers between devices  23.3 us (21%)
  Pallas kernels  11.8 us (11%)
  local copies, waits for them, and re-layouts  1.62 us (1%)
    ppermute x18, waiting for transfers between devices, swap(): return lax.ppermute(array, ('blk', 'rep'), route)  53.9 us
    all_to_all x1, waiting for transfers between devices, per_device(): own = lax.all_to_all(signals.reshape(teams, times, width), 'blk', 0, 0)  21.3 us
    ppermute x18, starting transfers between devices, swap(): return lax.ppermute(array, ('blk', 'rep'), route)  18.5 us
    pallas_call x1, Pallas kernels, per_device(): pl.pallas_call(functools.partial(product_kernel, teams, replicas, tile_ro...  8.88 us
    all_to_all x1, starting transfers between devices, per_device(): own = lax.all_to_all(signals.reshape(teams, times, width), 'blk', 0, 0)  4.73 us
  transfers between devices with their start and end apart: 19, of which 11 were waited for; matrix products, arithmetic and copies ran while one was open for 0% of the time, Pallas kernels for 0%

profile of v1, /device:TPU:0, one launch (start us, length us, event | category | flops | bytes accessed | tf_op | source)
XLA Modules:
  0.0 112.0 jit_solution(15145810072995697974)
XLA Ops:
  0.0 0.1 pad_add_fusion.place_ref
  0.1 0.6 copy-done.2
  0.7 1.0 copy-done
  1.6 0.6 prepare.1
  2.2 5.1 %collective-permute-start.2 = (bf16[3,64,256]{2,1,0:T(8,128)(2,1)S(1)}, bf16[3,64,256]{2,1,0:T(8,128)(2,1)S(1)}, u32[]{:S(2)}, u32[]{:S(2)}) collective-permute-start(bf16[3,64,256]{2,1,0:T(8,128)(2,1)S(1)} %prepare.1), channel_id=1, source_target_pairs={{0,24},{1,25},{2,26},{3,27},{4,28},{5,29},{6,30},{7,31},{8,16},{9,... | collective-permute-start | bytes 294920 | tf_op jit(solution)/shard_map/ppermute | solution.py:162
  7.3 0.0 collective-permute-start.1
  7.3 0.6 collective-permute-start
  8.0 3.1 %collective-permute-done.2 = bf16[3,64,256]{2,1,0:T(8,128)(2,1)S(1)} collective-permute-done((bf16[3,64,256]{2,1,0:T(8,128)(2,1)S(1)}, bf16[3,64,256]{2,1,0:T(8,128)(2,1)S(1)}, u32[]{:S(2)}, u32[]{:S(2)}) %collective-permute-start.2) | collective-permute-done | bytes 98336 | tf_op jit(solution)/shard_map/ppermute | solution.py:162
  11.0 4.6 %collective-permute-done.1 = bf16[3,64,256]{2,1,0:T(8,128)(2,1)S(1)} collective-permute-done((bf16[3,64,256]{2,1,0:T(8,128)(2,1)S(1)}, bf16[3,64,256]{2,1,0:T(8,128)(2,1)S(1)}, u32[]{:S(2)}, u32[]{:S(2)}) %collective-permute-start.1) | collective-permute-done | bytes 98336 | tf_op jit(solution)/shard_map/ppermute | solution.py:162
  15.6 0.0 collective-permute-done
  15.6 0.1 pad_maximum_fusion.rest_0_
  15.7 4.7 %all-to-all-start = ((bf16[8,256,256]{2,1,0:T(8,128)(2,1)}), bf16[8,256,256]{2,1,0:T(8,128)(2,1)S(1)}, u32[]{:S(2)}, u32[]{:S(2)}) async-start(bf16[8,256,256]{2,1,0:T(8,128)(2,1)} %bitcast.6), calls=%async_computation | async-start | bytes 2097152 | tf_op jit(solution)/shard_map/all_to_all | solution.py:180
  20.4 0.0 collective-permute-start.8
  20.4 3.0 %collective-permute-start.7 = (bf16[4,3,64,256]{3,2,1,0:T(8,128)(2,1)S(1)}, bf16[4,3,64,256]{3,2,1,0:T(8,128)(2,1)S(1)}, u32[]{:S(2)}, u32[]{:S(2)}) collective-permute-start(bf16[4,3,64,256]{3,2,1,0:T(8,128)(2,1)S(1)} %pad_maximum_fusion.rest_0_), channel_id=1, source_target_pairs={{0,6},{1,7},{2,4},{3,5},{4,2},{5,3},{6,0},{7,1},{8,14},{9,15},{10,... | collective-permute-start | bytes 1179656 | tf_op jit(solution)/shard_map/ppermute | solution.py:162
  23.4 0.1 collective-permute-start.6
  23.4 0.6 collective-permute-start.5
  24.0 21.3 %all-to-all-done.own_ref = bf16[8,256,256]{2,1,0:T(8,128)(2,1)S(1)} async-done(((bf16[8,256,256]{2,1,0:T(8,128)(2,1)}), bf16[8,256,256]{2,1,0:T(8,128)(2,1)S(1)}, u32[]{:S(2)}, u32[]{:S(2)}) %all-to-all-start) | async-done | bytes 1048608 | tf_op jit(solution)/shard_map/all_to_all | solution.py:180
  45.3 0.1 fusion
  45.3 0.1 collective-permute-start.4
  45.4 0.0 collective-permute-done.8.rest_4_
  45.4 0.5 collective-permute-start.3
  45.9 0.0 collective-permute-done.7.rest_3_
  45.9 0.1 collective-permute-start.11
  46.0 4.2 %collective-permute-done.6.rest_2_ = bf16[4,3,64,256]{3,2,1,0:T(8,128)(2,1)S(1)} collective-permute-done((bf16[4,3,64,256]{3,2,1,0:T(8,128)(2,1)S(1)}, bf16[4,3,64,256]{3,2,1,0:T(8,128)(2,1)S(1)}, u32[]{:S(2)}, u32[]{:S(2)}) %collective-permute-start.6) | collective-permute-done | bytes 393248 | tf_op jit(solution)/shard_map/ppermute | solution.py:162
  50.2 0.0 collective-permute-start.10
  50.2 0.0 collective-permute-done.5.rest_1_
  50.2 0.5 collective-permute-start.9
  50.7 0.0 collective-permute-done.11.rest_7_
  50.7 1.2 %collective-permute-done.10.rest_6_ = bf16[4,3,64,256]{3,2,1,0:T(8,128)(2,1)S(1)} collective-permute-done((bf16[4,3,64,256]{3,2,1,0:T(8,128)(2,1)S(1)}, bf16[4,3,64,256]{3,2,1,0:T(8,128)(2,1)S(1)}, u32[]{:S(2)}, u32[]{:S(2)}) %collective-permute-start.10) | collective-permute-done | bytes 393248 | tf_op jit(solution)/shard_map/ppermute | solution.py:162
  51.9 0.6 collective-permute-done.9.rest_5_
  52.5 0.0 collective-permute-done.4.high_ref
  52.5 0.0 collective-permute-done.3.low_ref
  52.5 8.9 %products.1 = (bf16[4,5,64,256]{3,2,1,0:T(8,128)(2,1)S(1)}, bf16[4,5,64,256]{3,2,1,0:T(8,128)(2,1)S(1)}, bf16[4,5,64,256]{3,2,1,0:T(8,128)(2,1)S(1)}, bf16[4,5,64,256]{3,2,1,0:T(8,128)(2,1)S(1)}) custom-call(s32[2]{0:T(128)S(1)} %pad_add_fusion.place_ref, s32[1,5]{1,0:T(1,128)S(1)} %copy-done.2, bf16[8,256,256]{2,1,0:T(8,128)(2,1)S(1)} %all-to-all-done.own_ref, ...), custom_call_target="tpu_custom_call" | custom-call | tf_op jit(solution)/shard_map/products/pallas_call | solution.py:184
  61.4 1.6 %collective-permute-start.12 = (bf16[4,5,64,256]{3,2,1,0:T(8,128)(2,1)S(1)}, bf16[4,5,64,256]{3,2,1,0:T(8,128)(2,1)S(1)}, u32[]{:S(2)}, u32[]{:S(2)}) collective-permute-start(bf16[4,5,64,256]{3,2,1,0:T(8,128)(2,1)S(1)} %get-tuple-element.18), channel_id=1, source_target_pairs={{0,2},{1,3},{2,0},{3,1},{4,6},{5,7},{6,4},{7,5},{8,10},{9,11},{10,... | collective-permute-start | bytes 1966088 | tf_op jit(solution)/shard_map/ppermute | solution.py:162
  63.0 0.0 collective-permute-start.13
  63.0 2.0 %collective-permute-start.14 = (bf16[4,5,64,256]{3,2,1,0:T(8,128)(2,1)S(1)}, bf16[4,5,64,256]{3,2,1,0:T(8,128)(2,1)S(1)}, u32[]{:S(2)}, u32[]{:S(2)}) collective-permute-start(bf16[4,5,64,256]{3,2,1,0:T(8,128)(2,1)S(1)} %get-tuple-element.20), channel_id=1, source_target_pairs={{0,6},{1,7},{2,4},{3,5},{4,2},{5,3},{6,0},{7,1},{8,14},{9,15},{10,... | collective-permute-start | bytes 1966088 | tf_op jit(solution)/shard_map/ppermute | solution.py:162
  64.9 13.3 %collective-permute-done.12.rest_1_ = bf16[4,5,64,256]{3,2,1,0:T(8,128)(2,1)S(1)} collective-permute-done((bf16[4,5,64,256]{3,2,1,0:T(8,128)(2,1)S(1)}, bf16[4,5,64,256]{3,2,1,0:T(8,128)(2,1)S(1)}, u32[]{:S(2)}, u32[]{:S(2)}) %collective-permute-start.12) | collective-permute-done | bytes 655392 | tf_op jit(solution)/shard_map/ppermute | solution.py:162
  78.2 2.4 %collective-permute-done.13.rest_2_ = bf16[4,5,64,256]{3,2,1,0:T(8,128)(2,1)S(1)} collective-permute-done((bf16[4,5,64,256]{3,2,1,0:T(8,128)(2,1)S(1)}, bf16[4,5,64,256]{3,2,1,0:T(8,128)(2,1)S(1)}, u32[]{:S(2)}, u32[]{:S(2)}) %collective-permute-start.13) | collective-permute-done | bytes 655392 | tf_op jit(solution)/shard_map/ppermute | solution.py:162
  80.6 12.9 %collective-permute-done.14.rest_3_ = bf16[4,5,64,256]{3,2,1,0:T(8,128)(2,1)S(1)} collective-permute-done((bf16[4,5,64,256]{3,2,1,0:T(8,128)(2,1)S(1)}, bf16[4,5,64,256]{3,2,1,0:T(8,128)(2,1)S(1)}, u32[]{:S(2)}, u32[]{:S(2)}) %collective-permute-start.14) | collective-permute-done | bytes 655392 | tf_op jit(solution)/shard_map/ppermute | solution.py:162
  93.5 0.9 plane_sum.1
  94.3 1.7 %collective-permute-start.15 = (bf16[5,64,256]{2,1,0:T(8,128)(2,1)S(1)}, bf16[5,64,256]{2,1,0:T(8,128)(2,1)S(1)}, u32[]{:S(2)}, u32[]{:S(2)}) collective-permute-start(bf16[5,64,256]{2,1,0:T(8,128)(2,1)S(1)} %get-tuple-element.22), channel_id=1, source_target_pairs={{0,8},{1,9},{2,10},{3,11},{4,12},{5,13},{6,14},{7,15},{8,0},{9,1},... | collective-permute-start | bytes 491528 | tf_op jit(solution)/shard_map/ppermute | solution.py:162
  96.0 2.7 %collective-permute-start.16 = (bf16[5,64,256]{2,1,0:T(8,128)(2,1)S(1)}, bf16[5,64,256]{2,1,0:T(8,128)(2,1)S(1)}, u32[]{:S(2)}, u32[]{:S(2)}) collective-permute-start(bf16[5,64,256]{2,1,0:T(8,128)(2,1)S(1)} %get-tuple-element.23), channel_id=1, source_target_pairs={{0,16},{1,17},{2,18},{3,19},{4,20},{5,21},{6,22},{7,23},{8,24},{9,... | collective-permute-start | bytes 491528 | tf_op jit(solution)/shard_map/ppermute | solution.py:162
  98.7 0.1 collective-permute-start.17
  98.8 3.0 %collective-permute-done.15.rest_1_ = bf16[5,64,256]{2,1,0:T(8,128)(2,1)S(1)} collective-permute-done((bf16[5,64,256]{2,1,0:T(8,128)(2,1)S(1)}, bf16[5,64,256]{2,1,0:T(8,128)(2,1)S(1)}, u32[]{:S(2)}, u32[]{:S(2)}) %collective-permute-start.15) | collective-permute-done | bytes 163872 | tf_op jit(solution)/shard_map/ppermute | solution.py:162
  101.8 8.8 %collective-permute-done.16.rest_2_ = bf16[5,64,256]{2,1,0:T(8,128)(2,1)S(1)} collective-permute-done((bf16[5,64,256]{2,1,0:T(8,128)(2,1)S(1)}, bf16[5,64,256]{2,1,0:T(8,128)(2,1)S(1)}, u32[]{:S(2)}, u32[]{:S(2)}) %collective-permute-start.16) | collective-permute-done | bytes 163872 | tf_op jit(solution)/shard_map/ppermute | solution.py:162
  110.6 0.0 collective-permute-done.17.rest_3_
  110.6 0.0 copy-done.1
  110.6 1.5 %update.1 = f32[1,5,64,256]{3,2,1,0:T(8,128)} custom-call(s32[2]{0:T(128)S(1)} %pad_add_fusion.place_ref, s32[1,5]{1,0:T(1,128)S(1)} %copy-done.2, f32[1,5,64,256]{3,2,1,0:T(8,128)S(1)} %copy-done.1, f32[5,64,256]{2,1,0:T(8,128)S(1)} %get-tuple-element.21.rest_0_, bf16[5,64,256]{2,1,0:T(8,128)(2,1)S(1)} %collective-permute-done.15.rest_1_, ...), custom_call_target="tpu_custom_call" | custom-call | tf_op jit(solution)/shard_map/update/pallas_call | solution.py:220
  (3 shorter events, 0.0 us)
Async XLA Ops:
  0.0 0.7 copy-start.2
  0.7 1.0 copy-start
  2.2 8.8 %collective-permute-start.2 = (bf16[3,64,256]{2,1,0:T(8,128)(2,1)S(1)}, bf16[3,64,256]{2,1,0:T(8,128)(2,1)S(1)}, u32[]{:S(2)}, u32[]{:S(2)}) collective-permute-start(bf16[3,64,256]{2,1,0:T(8,128)(2,1)S(1)} %prepare.1), channel_id=1, source_target_pairs={{0,24},{1,25},{2,26},{3,27},{4,28},{5,29},{6,30},{7,31},{8,16},{9,... | collective-permute-start | bytes 294920 | tf_op jit(solution)/shard_map/ppermute | solution.py:162
  7.3 8.3 %collective-permute-start.1 = (bf16[3,64,256]{2,1,0:T(8,128)(2,1)S(1)}, bf16[3,64,256]{2,1,0:T(8,128)(2,1)S(1)}, u32[]{:S(2)}, u32[]{:S(2)}) collective-permute-start(bf16[3,64,256]{2,1,0:T(8,128)(2,1)S(1)} %prepare.1), channel_id=1, source_target_pairs={{0,16},{1,17},{2,18},{3,19},{4,20},{5,21},{6,22},{7,23},{8,24},{9,... | collective-permute-start | bytes 294920 | tf_op jit(solution)/shard_map/ppermute | solution.py:162
  7.3 8.3 %collective-permute-start = (bf16[3,64,256]{2,1,0:T(8,128)(2,1)S(1)}, bf16[3,64,256]{2,1,0:T(8,128)(2,1)S(1)}, u32[]{:S(2)}, u32[]{:S(2)}) collective-permute-start(bf16[3,64,256]{2,1,0:T(8,128)(2,1)S(1)} %prepare.1), channel_id=1, source_target_pairs={{0,8},{1,9},{2,10},{3,11},{4,12},{5,13},{6,14},{7,15},{8,0},{9,1},... | collective-permute-start | bytes 294920 | tf_op jit(solution)/shard_map/ppermute | solution.py:162
  15.7 29.6 %all-to-all-start = ((bf16[8,256,256]{2,1,0:T(8,128)(2,1)}), bf16[8,256,256]{2,1,0:T(8,128)(2,1)S(1)}, u32[]{:S(2)}, u32[]{:S(2)}) async-start(bf16[8,256,256]{2,1,0:T(8,128)(2,1)} %bitcast.6), calls=%async_computation | async-start | bytes 2097152 | tf_op jit(solution)/shard_map/all_to_all | solution.py:180
  20.4 25.0 %collective-permute-start.8 = (bf16[4,3,64,256]{3,2,1,0:T(8,128)(2,1)S(1)}, bf16[4,3,64,256]{3,2,1,0:T(8,128)(2,1)S(1)}, u32[]{:S(2)}, u32[]{:S(2)}) collective-permute-start(bf16[4,3,64,256]{3,2,1,0:T(8,128)(2,1)S(1)} %pad_maximum_fusion.rest_0_), channel_id=1, source_target_pairs={{0,1},{1,0},{2,3},{3,2},{4,5},{5,4},{6,7},{7,6},{8,9},{9,8},{10,11... | collective-permute-start | bytes 1179656 | tf_op jit(solution)/shard_map/ppermute | solution.py:162
  20.4 25.5 %collective-permute-start.7 = (bf16[4,3,64,256]{3,2,1,0:T(8,128)(2,1)S(1)}, bf16[4,3,64,256]{3,2,1,0:T(8,128)(2,1)S(1)}, u32[]{:S(2)}, u32[]{:S(2)}) collective-permute-start(bf16[4,3,64,256]{3,2,1,0:T(8,128)(2,1)S(1)} %pad_maximum_fusion.rest_0_), channel_id=1, source_target_pairs={{0,6},{1,7},{2,4},{3,5},{4,2},{5,3},{6,0},{7,1},{8,14},{9,15},{10,... | collective-permute-start | bytes 1179656 | tf_op jit(solution)/shard_map/ppermute | solution.py:162
  23.4 26.8 %collective-permute-start.6 = (bf16[4,3,64,256]{3,2,1,0:T(8,128)(2,1)S(1)}, bf16[4,3,64,256]{3,2,1,0:T(8,128)(2,1)S(1)}, u32[]{:S(2)}, u32[]{:S(2)}) collective-permute-start(bf16[4,3,64,256]{3,2,1,0:T(8,128)(2,1)S(1)} %pad_maximum_fusion.rest_0_), channel_id=1, source_target_pairs={{0,4},{1,5},{2,6},{3,7},{4,0},{5,1},{6,2},{7,3},{8,12},{9,13},{10,... | collective-permute-start | bytes 1179656 | tf_op jit(solution)/shard_map/ppermute | solution.py:162
  23.4 26.8 %collective-permute-start.5 = (bf16[4,3,64,256]{3,2,1,0:T(8,128)(2,1)S(1)}, bf16[4,3,64,256]{3,2,1,0:T(8,128)(2,1)S(1)}, u32[]{:S(2)}, u32[]{:S(2)}) collective-permute-start(bf16[4,3,64,256]{3,2,1,0:T(8,128)(2,1)S(1)} %pad_maximum_fusion.rest_0_), channel_id=1, source_target_pairs={{0,2},{1,3},{2,0},{3,1},{4,6},{5,7},{6,4},{7,5},{8,10},{9,11},{10,... | collective-permute-start | bytes 1179656 | tf_op jit(solution)/shard_map/ppermute | solution.py:162
  45.3 7.2 %collective-permute-start.4 = (bf16[4,256,256]{2,1,0:T(8,128)(2,1)S(1)}, bf16[4,256,256]{2,1,0:T(8,128)(2,1)S(1)}, u32[]{:S(2)}, u32[]{:S(2)}) collective-permute-start(bf16[4,256,256]{2,1,0:T(8,128)(2,1)S(1)} %get-tuple-element.25), channel_id=1, source_target_pairs={{0,1},{1,0},{2,3},{3,2},{4,5},{5,4},{6,7},{7,6},{8,9},{9,8},{10,11... | collective-permute-start | bytes 1572872 | tf_op jit(solution)/shard_map/ppermute | solution.py:162
  45.4 7.1 %collective-permute-start.3 = (bf16[4,256,256]{2,1,0:T(8,128)(2,1)S(1)}, bf16[4,256,256]{2,1,0:T(8,128)(2,1)S(1)}, u32[]{:S(2)}, u32[]{:S(2)}) collective-permute-start(bf16[4,256,256]{2,1,0:T(8,128)(2,1)S(1)} %get-tuple-element.26), channel_id=1, source_target_pairs={{0,1},{1,0},{2,3},{3,2},{4,5},{5,4},{6,7},{7,6},{8,9},{9,8},{10,11... | collective-permute-start | bytes 1572872 | tf_op jit(solution)/shard_map/ppermute | solution.py:162
  45.9 4.8 %collective-permute-start.11 = (bf16[4,3,64,256]{3,2,1,0:T(8,128)(2,1)S(1)}, bf16[4,3,64,256]{3,2,1,0:T(8,128)(2,1)S(1)}, u32[]{:S(2)}, u32[]{:S(2)}) collective-permute-start(bf16[4,3,64,256]{3,2,1,0:T(8,128)(2,1)S(1)} %collective-permute-done.7.rest_3_), channel_id=1, source_target_pairs={{0,1},{1,0},{2,3},{3,2},{4,5},{5,4},{6,7},{7,6},{8,9},{9,8},{10,11... | collective-permute-start | bytes 1179656 | tf_op jit(solution)/shard_map/ppermute | solution.py:162
  50.2 1.7 %collective-permute-start.10 = (bf16[4,3,64,256]{3,2,1,0:T(8,128)(2,1)S(1)}, bf16[4,3,64,256]{3,2,1,0:T(8,128)(2,1)S(1)}, u32[]{:S(2)}, u32[]{:S(2)}) collective-permute-start(bf16[4,3,64,256]{3,2,1,0:T(8,128)(2,1)S(1)} %collective-permute-done.6.rest_2_), channel_id=1, source_target_pairs={{0,1},{1,0},{2,3},{3,2},{4,5},{5,4},{6,7},{7,6},{8,9},{9,8},{10,11... | collective-permute-start | bytes 1179656 | tf_op jit(solution)/shard_map/ppermute | solution.py:162
  50.2 2.3 %collective-permute-start.9 = (bf16[4,3,64,256]{3,2,1,0:T(8,128)(2,1)S(1)}, bf16[4,3,64,256]{3,2,1,0:T(8,128)(2,1)S(1)}, u32[]{:S(2)}, u32[]{:S(2)}) collective-permute-start(bf16[4,3,64,256]{3,2,1,0:T(8,128)(2,1)S(1)} %collective-permute-done.5.rest_1_), channel_id=1, source_target_pairs={{0,1},{1,0},{2,3},{3,2},{4,5},{5,4},{6,7},{7,6},{8,9},{9,8},{10,11... | collective-permute-start | bytes 1179656 | tf_op jit(solution)/shard_map/ppermute | solution.py:162
  61.4 16.8 %collective-permute-start.12 = (bf16[4,5,64,256]{3,2,1,0:T(8,128)(2,1)S(1)}, bf16[4,5,64,256]{3,2,1,0:T(8,128)(2,1)S(1)}, u32[]{:S(2)}, u32[]{:S(2)}) collective-permute-start(bf16[4,5,64,256]{3,2,1,0:T(8,128)(2,1)S(1)} %get-tuple-element.18), channel_id=1, source_target_pairs={{0,2},{1,3},{2,0},{3,1},{4,6},{5,7},{6,4},{7,5},{8,10},{9,11},{10,... | collective-permute-start | bytes 1966088 | tf_op jit(solution)/shard_map/ppermute | solution.py:162
  63.0 17.6 %collective-permute-start.13 = (bf16[4,5,64,256]{3,2,1,0:T(8,128)(2,1)S(1)}, bf16[4,5,64,256]{3,2,1,0:T(8,128)(2,1)S(1)}, u32[]{:S(2)}, u32[]{:S(2)}) collective-permute-start(bf16[4,5,64,256]{3,2,1,0:T(8,128)(2,1)S(1)} %get-tuple-element.19), channel_id=1, source_target_pairs={{0,4},{1,5},{2,6},{3,7},{4,0},{5,1},{6,2},{7,3},{8,12},{9,13},{10,... | collective-permute-start | bytes 1966088 | tf_op jit(solution)/shard_map/ppermute | solution.py:162
  63.0 30.5 %collective-permute-start.14 = (bf16[4,5,64,256]{3,2,1,0:T(8,128)(2,1)S(1)}, bf16[4,5,64,256]{3,2,1,0:T(8,128)(2,1)S(1)}, u32[]{:S(2)}, u32[]{:S(2)}) collective-permute-start(bf16[4,5,64,256]{3,2,1,0:T(8,128)(2,1)S(1)} %get-tuple-element.20), channel_id=1, source_target_pairs={{0,6},{1,7},{2,4},{3,5},{4,2},{5,3},{6,0},{7,1},{8,14},{9,15},{10,... | collective-permute-start | bytes 1966088 | tf_op jit(solution)/shard_map/ppermute | solution.py:162
  93.4 17.1 %copy-start.1 = (f32[1,5,64,256]{3,2,1,0:T(8,128)S(1)}, f32[1,5,64,256]{3,2,1,0:T(8,128)}, u32[]{:S(2)}) copy-start(f32[1,5,64,256]{3,2,1,0:T(8,128)} %omega_ref.3) | copy-start | bytes 983044
  94.3 7.4 %collective-permute-start.15 = (bf16[5,64,256]{2,1,0:T(8,128)(2,1)S(1)}, bf16[5,64,256]{2,1,0:T(8,128)(2,1)S(1)}, u32[]{:S(2)}, u32[]{:S(2)}) collective-permute-start(bf16[5,64,256]{2,1,0:T(8,128)(2,1)S(1)} %get-tuple-element.22), channel_id=1, source_target_pairs={{0,8},{1,9},{2,10},{3,11},{4,12},{5,13},{6,14},{7,15},{8,0},{9,1},... | collective-permute-start | bytes 491528 | tf_op jit(solution)/shard_map/ppermute | solution.py:162
  96.0 14.6 %collective-permute-start.16 = (bf16[5,64,256]{2,1,0:T(8,128)(2,1)S(1)}, bf16[5,64,256]{2,1,0:T(8,128)(2,1)S(1)}, u32[]{:S(2)}, u32[]{:S(2)}) collective-permute-start(bf16[5,64,256]{2,1,0:T(8,128)(2,1)S(1)} %get-tuple-element.23), channel_id=1, source_target_pairs={{0,16},{1,17},{2,18},{3,19},{4,20},{5,21},{6,22},{7,23},{8,24},{9,... | collective-permute-start | bytes 491528 | tf_op jit(solution)/shard_map/ppermute | solution.py:162
  98.7 11.9 %collective-permute-start.17 = (bf16[5,64,256]{2,1,0:T(8,128)(2,1)S(1)}, bf16[5,64,256]{2,1,0:T(8,128)(2,1)S(1)}, u32[]{:S(2)}, u32[]{:S(2)}) collective-permute-start(bf16[5,64,256]{2,1,0:T(8,128)(2,1)S(1)} %get-tuple-element.24), channel_id=1, source_target_pairs={{0,24},{1,25},{2,26},{3,27},{4,28},{5,29},{6,30},{7,31},{8,16},{9,... | collective-permute-start | bytes 491528 | tf_op jit(solution)/shard_map/ppermute | solution.py:162

commit v2 on v1

v2 whole, which is shorter than its diff:
```python
import functools

import jax
import jax.numpy as jnp
from jax import lax
from jax.experimental import pallas as pl
from jax.experimental.pallas import tpu as pltpu
from jax.sharding import Mesh, PartitionSpec as P

STEP_SIZE = 0.5
PENALTY = 0.1
LOW = 2
LINE_FIRST = (3, 4)
PLANE_FIRST = (0, 1, 2)
AXES = ("line", "low", "chip", "core")
BLK, REP = AXES[:2], AXES[2:]
F32 = jnp.float32
BF16 = jnp.bfloat16

VMEM = pl.BlockSpec(memory_space=pltpu.VMEM)
ANY = pl.BlockSpec(memory_space=pl.ANY)
SMEM = pl.BlockSpec(memory_space=pltpu.SMEM)


def stored_offsets(pattern_ref, team, teams):
    drawn = [lax.rem(pattern_ref[0, k] - team + teams, teams) for k in range(1, 5)]
    a = functools.reduce(jnp.minimum, drawn)
    b = functools.reduce(jnp.minimum, [jnp.where(d == a, teams, d) for d in drawn])
    offsets = [jnp.int32(0), a, b, teams - b, teams - a]
    slots = [jnp.int32(0)]
    for offset in offsets[1:]:
        slots.append(sum(jnp.where(d == offset, k + 1, 0) for k, d in enumerate(drawn)))
    return offsets, slots


def prepare_kernel(teams, place_ref, pattern_ref, omega_ref, signals_ref, upper_ref, across_ref, sem):
    team = place_ref[0]
    rows = across_ref.shape[0]
    first = pl.multiple_of((lax.rem(team, LOW) ^ 1) * rows, rows)
    copy = pltpu.make_async_copy(signals_ref.at[pl.ds(first, rows)], across_ref, sem)
    copy.start()
    _, slots = stored_offsets(pattern_ref, team, teams)
    for k in range(3):
        upper_ref[k] = omega_ref[0, slots[k]].astype(BF16)
    copy.wait()


def deal_kernel(place_ref, signals_ref, across_ref, out_ref, sems):
    rows = across_ref.shape[0]
    first = pl.multiple_of(lax.rem(place_ref[0], LOW) * rows, rows)
    sources = [signals_ref.at[pl.ds(first, rows)], across_ref]
    copies = [
        pltpu.make_async_copy(source.reshape(out_ref.shape[0], *out_ref.shape[2:]), out_ref.at[:, n], sems.at[n])
        for n, source in enumerate(sources)
    ]
    for copy in copies:
        copy.start()
    for copy in copies:
        copy.wait()


def product_kernel(teams, replicas, tile_rows, place_ref, pattern_ref, *rest):
    chips = replicas // 2
    planes = LOW * chips
    depth = teams // LOW
    block_refs, rest = rest[:3], rest[3:]
    weight_refs, rest = rest[: 2 * planes], rest[2 * planes :]
    plane_outs, line_out, rest = rest[:planes], rest[planes], rest[planes + 1 :]
    data_ref, omega_ref, mixed_ref, flip_ref, left_ref, data_sems, omega_sems = rest
    team, replica = place_ref[0], place_ref[1]
    core, chip = lax.rem(replica, 2), lax.div(replica, 2)
    high, low = lax.div(team, LOW), lax.rem(team, LOW)
    offsets, _ = stored_offsets(pattern_ref, team, teams)
    times, width = data_ref.shape[1] // 2, data_ref.shape[2]

    copies = []
    for half in range(2):
        for z in range(depth):
            source = block_refs[half + (z >= depth // 2) * half].at[z % (depth // 2) if half else z]
            for n in range(LOW):
                copies.append(
                    pltpu.make_async_copy(
                        source.at[n],
                        data_ref.at[z * LOW + (low ^ n), pl.ds(half * times, times)],
                        data_sems.at[(half * depth + z) * LOW + n],
                    )
                )
    for half in range(2):
        for mx in range(LOW):
            for my in range(chips):
                plane = mx * chips + my
                row = (2 * (chip ^ my) + (core ^ half)) * tile_rows
                for mz in range(depth):
                    i = (high ^ mz) * LOW + (low ^ mx)
                    target = omega_ref.at[i, :, pl.ds(pl.multiple_of(row, tile_rows), tile_rows)]
                    copies.append(
                        pltpu.make_async_copy(
                            weight_refs[half * planes + plane].at[mz],
                            target,
                            omega_sems.at[(half * planes + plane) * depth + mz],
                        )
                    )
    for copy in copies:
        copy.start()
    for copy in copies:
        copy.wait()

    nn = (((1,), (0,)), ((), ()))
    nt = (((1,), (1,)), ((), ()))

    def mix(i, carry):
        total = None
        for k, offset in enumerate(offsets):
            c = lax.rem(i + offset, teams)
            if k < 3:
                term = lax.dot_general(data_ref[c], omega_ref[i, k], nt, preferred_element_type=F32)
            else:
                term = lax.dot_general(data_ref[c], omega_ref[c, 5 - k], nn, preferred_element_type=F32)
            total = term if total is None else total + term
        mixed = total.astype(BF16)
        mixed_ref[i] = mixed
        flip_ref[:, : 2 * times] = mixed.T
        flip_ref[:, 2 * times :] = data_ref[i].T
        for m in range(chips):
            row = (2 * (chip ^ m) + core) * tile_rows
            left_ref[i, m * tile_rows : (m + 1) * tile_rows] = flip_ref[
                pl.ds(pl.multiple_of(row, tile_rows), tile_rows)
            ]
        return carry

    unroll = teams <= 8
    lax.fori_loop(0, teams, mix, 0, unroll=unroll)

    def part(i, k):
        c = lax.rem(i + offsets[k], teams)
        right = jnp.concatenate([data_ref[c], mixed_ref[c]], axis=0)
        product = lax.dot_general(left_ref[i], right, nn, preferred_element_type=F32).astype(BF16)
        return [product[m * tile_rows : (m + 1) * tile_rows] for m in range(chips)]

    for mx in range(LOW):

        def outer(z, carry):
            i = z * LOW + (low ^ mx)
            for n, k in enumerate(LINE_FIRST):
                for m, rows in enumerate(part(i, k)):
                    line_out[z, mx * chips + m, n] = rows
            for n, k in enumerate(PLANE_FIRST):
                for m, rows in enumerate(part(i, k)):
                    plane_outs[mx * chips + m][z, n] = rows
            return carry

        lax.fori_loop(0, depth, outer, 0, unroll=unroll)


def line_sum_kernel(parts_ref, *outs):
    for m, out in enumerate(outs):
        total = parts_ref[0, m].astype(F32)
        for z in range(1, parts_ref.shape[0]):
            total = total + parts_ref[z, m].astype(F32)
        out[...] = total.astype(out.dtype)


def plane_sum_kernel(teams, place_ref, *rest):
    count = teams // LOW
    parts, outs = rest[:-count], rest[-count:]
    z = lax.div(place_ref[0], LOW)
    for m in range(count):
        total = parts[0][z ^ m].astype(F32)
        for part in parts[1:]:
            total = total + part[z ^ m].astype(F32)
        outs[m][...] = total.astype(outs[m].dtype)


def update_kernel(teams, scale, place_ref, pattern_ref, omega_ref, *rest):
    depth = teams // LOW
    plane_first, line_first, out_ref = rest[:depth], rest[depth:-1], rest[-1]
    _, slots = stored_offsets(pattern_ref, place_ref[0], teams)
    rows, width = out_ref.shape[2:]
    first = place_ref[1] * rows
    row_ids = first + lax.broadcasted_iota(jnp.int32, (rows, width), 0)
    diagonal = row_ids == lax.broadcasted_iota(jnp.int32, (rows, width), 1)
    for k in range(5):
        parts, n = (line_first, LINE_FIRST.index(k)) if k in LINE_FIRST else (plane_first, PLANE_FIRST.index(k))
        total = parts[0][n].astype(F32)
        for part in parts[1:]:
            total = total + part[n].astype(F32)
        current = omega_ref[0, slots[k]]
        gradient = total * scale
        if k == 0:
            gradient = gradient - jnp.where(diagonal, 1.0 / current, 0.0)
        value = current - STEP_SIZE * gradient
        bound = STEP_SIZE * PENALTY
        shrunk = jnp.where(value > bound, value - bound, jnp.where(value < -bound, value + bound, 0.0))
        if k == 0:
            shrunk = jnp.where(diagonal, value, shrunk)
        out_ref[0, slots[k]] = shrunk


def per_device(teams, replicas, signals, omega, pattern):
    chips = replicas // 2
    slots, tile_rows, width = omega.shape[1:]
    times = signals.shape[0] // teams
    place = jnp.stack([lax.axis_index(BLK), lax.axis_index(REP)]).astype(jnp.int32)

    def swap(array, blk_mask, rep_mask):
        route = [
            (b * replicas + r, (b ^ blk_mask) * replicas + (r ^ rep_mask))
            for b in range(teams)
            for r in range(replicas)
        ]
        return lax.ppermute(array, AXES, route)

    planes = LOW * chips
    count = teams // LOW
    planes = LOW * chips
    count = teams // LOW
    small = pltpu.CompilerParams(vmem_limit_bytes=(8 if teams <= 8 else 48) * 2**20)
    large = pltpu.CompilerParams(vmem_limit_bytes=(18 if teams <= 8 else 56) * 2**20)

    def across_plane(arrays):
        return [
            swap(arrays[mx * chips + my], mx, 2 * my) if mx + my else arrays[0]
            for mx in range(LOW)
            for my in range(chips)
        ]

    def along_line(arrays):
        return [swap(array, m * LOW, 0) if m else array for m, array in enumerate(arrays)]

    upper, across = pl.pallas_call(
        functools.partial(prepare_kernel, teams),
        out_shape=[
            jax.ShapeDtypeStruct((3, tile_rows, width), BF16),
            jax.ShapeDtypeStruct((count * times, width), BF16),
        ],
        in_specs=[SMEM, SMEM, VMEM, ANY],
        out_specs=[VMEM, VMEM],
        scratch_shapes=[pltpu.SemaphoreType.DMA],
        compiler_params=small,
        name="prepare",
    )(place, pattern, omega, signals)

    across = swap(across, 1, 0)
    line = jnp.stack(along_line([upper] * count))
    weights = across_plane([line] * planes)
    weights += [swap(array, 0, 1) for array in weights]
    dealt = pl.pallas_call(
        deal_kernel,
        out_shape=jax.ShapeDtypeStruct((count, LOW, times, width), BF16),
        in_specs=[SMEM, ANY, VMEM],
        out_specs=VMEM,
        scratch_shapes=[pltpu.SemaphoreType.DMA((2,))],
        compiler_params=small,
        name="deal",
    )(place, signals, across)
    own = lax.all_to_all(dealt, "line", 0, 0)
    blocks = [own] + [swap(array, 0, 1) for array in jnp.split(own, 2)]

    partial = pl.pallas_call(
        functools.partial(product_kernel, teams, replicas, tile_rows),
        out_shape=[jax.ShapeDtypeStruct((count, len(PLANE_FIRST), tile_rows, width), BF16)] * planes
        + [jax.ShapeDtypeStruct((count, planes, len(LINE_FIRST), tile_rows, width), BF16)],
        in_specs=[SMEM, SMEM] + [ANY] * (3 + 2 * planes),
        out_specs=[VMEM] * (planes + 1),
        scratch_shapes=[
            pltpu.VMEM((teams, 2 * times, width), BF16),
            pltpu.VMEM((teams, 3, width, width), BF16),
            pltpu.VMEM((teams, 2 * times, width), BF16),
            pltpu.VMEM((width, 4 * times), BF16),
            pltpu.VMEM((teams, chips * tile_rows, 4 * times), BF16),
            pltpu.SemaphoreType.DMA((2 * teams,)),
            pltpu.SemaphoreType.DMA((2 * planes * count,)),
        ],
        compiler_params=large,
        name="products",
    )(place, pattern, *blocks, *weights)

    line_parts = lax.all_to_all(partial[planes], "line", 0, 0)
    plane_parts = across_plane(partial[:planes])
    plane_sums = pl.pallas_call(
        functools.partial(plane_sum_kernel, teams),
        out_shape=[
            jax.ShapeDtypeStruct((len(PLANE_FIRST), tile_rows, width), BF16 if m else F32) for m in range(count)
        ],
        in_specs=[SMEM] + [VMEM] * planes,
        out_specs=[VMEM] * count,
        compiler_params=small,
        name="plane_sum",
    )(place, *plane_parts)
    plane_sums = along_line(plane_sums)
    line_parts, plane_sums[1] = lax.optimization_barrier((line_parts, plane_sums[1]))
    line_sums = pl.pallas_call(
        line_sum_kernel,
        out_shape=[
            jax.ShapeDtypeStruct((len(LINE_FIRST), tile_rows, width), BF16 if m else F32) for m in range(planes)
        ],
        in_specs=[VMEM],
        out_specs=[VMEM] * planes,
        compiler_params=small,
        name="line_sum",
    )(line_parts)

    scale = 1.0 / (2.0 * signals.shape[0] * replicas)
    return pl.pallas_call(
        functools.partial(update_kernel, teams, scale),
        out_shape=jax.ShapeDtypeStruct(omega.shape, F32),
        in_specs=[SMEM, SMEM, VMEM] + [VMEM] * (count + planes),
        out_specs=VMEM,
        compiler_params=small,
        name="update",
    )(place, pattern, omega, *plane_sums, *across_plane(line_sums))


def solution(mesh):
    teams, replicas = mesh.shape["blk"], mesh.shape["rep"]
    fine = Mesh(mesh.devices.reshape(teams // LOW, LOW, replicas // 2, 2), AXES)
    return jax.shard_map(
        functools.partial(per_device, teams, replicas),
        mesh=fine,
        in_specs=(P(REP, BLK), P(BLK, None, REP, None), P(BLK, None)),
        out_specs=P(BLK, None, REP, None),
        check_vma=False,
    )
```

time: 112 us -> 140 us (1.25)
  waiting for transfers between devices: 75.2 us -> 84.9 us
  starting transfers between devices: 23.3 us -> 32.5 us
  Pallas kernels: 11.8 us -> 17 us
  local copies, waits for them, and re-layouts: 1.62 us -> 5.11 us
    ppermute x18 -> x22, waiting for transfers between devices: 53.9 us -> 84.9 us  [swap(): return lax.ppermute(array, AXES, route)]
    all_to_all x1 -> x2, waiting for transfers between devices: 21.3 us -> 0.01 us  [the longest x1 0.01 us: per_device(): own = lax.all_to_all(dealt, 'line', 0, 0)]
    ppermute x18 -> x22, starting transfers between devices: 18.5 us -> 23.7 us  [swap(): return lax.ppermute(array, AXES, route)]
    all_to_all x1 -> x2, starting transfers between devices: 4.73 us -> 8.78 us  [the longest x1 5.13 us: per_device(): own = lax.all_to_all(dealt, 'line', 0, 0)]
    unnamed x6 -> x22, local copies, waits for them, and re-layouts: 1.56 us -> 5.04 us
    pallas_call x1, Pallas kernels: 8.88 us -> 12.4 us  [per_device(): pl.pallas_call(functools.partial(product_kernel, teams, replicas, tile_ro...]
    pallas_call x2 -> x4, Pallas kernels: 1.44 us -> 3.14 us  [the longest x1 1.63 us: per_device(): pl.pallas_call(deal_kernel, out_shape=jax.ShapeDtypeStruct((count, LOW, t...]
  transfers between devices with their start and end apart: 19 -> 24, of which waited for: 11 -> 14; matrix products, arithmetic and copies ran while one was open for 0% -> 0% of each run, Pallas kernels for 0% -> 1%
where the time goes in v2:
time: 140 us
  waiting for transfers between devices  84.9 us (61%)
  starting transfers between devices  32.5 us (23%)
  Pallas kernels  17 us (12%)
  local copies, waits for them, and re-layouts  5.11 us (4%)
    ppermute x22, waiting for transfers between devices, swap(): return lax.ppermute(array, AXES, route)  84.9 us
    ppermute x22, starting transfers between devices, swap(): return lax.ppermute(array, AXES, route)  23.7 us
    pallas_call x1, Pallas kernels, per_device(): pl.pallas_call(functools.partial(product_kernel, teams, replicas, tile_ro...  12.4 us
    all_to_all x1, starting transfers between devices, per_device(): own = lax.all_to_all(dealt, 'line', 0, 0)  5.13 us
    unnamed x22, local copies, waits for them, and re-layouts  5.04 us
    all_to_all x1, starting transfers between devices, per_device(): line_parts = lax.all_to_all(partial[planes], 'line', 0, 0)  3.65 us
  transfers between devices with their start and end apart: 24, of which 14 were waited for; matrix products, arithmetic and copies ran while one was open for 0% of the time, Pallas kernels for 1%

profile of v2, /device:TPU:0, one launch (start us, length us, event | category | flops | bytes accessed | tf_op | source)
XLA Modules:
  0.0 139.6 jit_solution(5653237993617652840)
XLA Ops:
  0.0 0.1 pad_add_fusion.place_ref
  0.1 0.6 copy-done.4
  0.7 1.2 copy-done
  1.9 1.0 copy-done.2
  2.9 0.6 prepare.1
  3.5 3.0 %collective-permute-start = (bf16[1024,256]{1,0:T(8,128)(2,1)S(1)}, bf16[1024,256]{1,0:T(8,128)(2,1)S(1)}, u32[]{:S(2)}, u32[]{:S(2)}) collective-permute-start(bf16[1024,256]{1,0:T(8,128)(2,1)S(1)} %get-tuple-element.22), channel_id=1, source_target_pairs={{0,4},{1,5},{2,6},{3,7},{4,0},{5,1},{6,2},{7,3},{8,12},{9,13},{10,... | collective-permute-start | bytes 1572872 | tf_op jit(solution)/shard_map/ppermute | solution.py:211
  6.5 11.9 %collective-permute-done.across_ref = bf16[1024,256]{1,0:T(8,128)(2,1)S(1)} collective-permute-done((bf16[1024,256]{1,0:T(8,128)(2,1)S(1)}, bf16[1024,256]{1,0:T(8,128)(2,1)S(1)}, u32[]{:S(2)}, u32[]{:S(2)}) %collective-permute-start) | collective-permute-done | bytes 524320 | tf_op jit(solution)/shard_map/ppermute | solution.py:211
  18.4 1.6 %deal.1 = bf16[4,2,256,256]{3,2,1,0:T(8,128)(2,1)} custom-call(s32[2]{0:T(128)S(1)} %pad_add_fusion.place_ref, bf16[2048,256]{1,0:T(8,128)(2,1)S(1)} %copy-done.1, bf16[1024,256]{1,0:T(8,128)(2,1)S(1)} %collective-permute-done.across_ref), custom_call_target="tpu_custom_call" | custom-call | tf_op jit(solution)/shard_map/deal/pallas_call | solution.py:247
  20.1 5.1 %all-to-all-start = ((bf16[4,2,256,256]{3,2,1,0:T(8,128)(2,1)}), bf16[4,2,256,256]{3,2,1,0:T(8,128)(2,1)S(1)}, u32[]{:S(2)}, u32[]{:S(2)}) async-start(bf16[4,2,256,256]{3,2,1,0:T(8,128)(2,1)} %deal.1), calls=%async_computation | async-start | bytes 2097152 | tf_op jit(solution)/shard_map/all_to_all | solution.py:256
  25.2 3.8 %collective-permute-start.5 = (bf16[3,64,256]{2,1,0:T(8,128)(2,1)S(1)}, bf16[3,64,256]{2,1,0:T(8,128)(2,1)S(1)}, u32[]{:S(2)}, u32[]{:S(2)}) collective-permute-start(bf16[3,64,256]{2,1,0:T(8,128)(2,1)S(1)} %get-tuple-element.23), channel_id=1, source_target_pairs={{0,24},{1,25},{2,26},{3,27},{4,28},{5,29},{6,30},{7,31},{8,16},{9,... | collective-permute-start | bytes 294920 | tf_op jit(solution)/shard_map/ppermute | solution.py:211
  29.0 0.6 collective-permute-start.3
  29.6 20.0 %collective-permute-done.5 = bf16[3,64,256]{2,1,0:T(8,128)(2,1)S(1)} collective-permute-done((bf16[3,64,256]{2,1,0:T(8,128)(2,1)S(1)}, bf16[3,64,256]{2,1,0:T(8,128)(2,1)S(1)}, u32[]{:S(2)}, u32[]{:S(2)}) %collective-permute-start.5) | collective-permute-done | bytes 98336 | tf_op jit(solution)/shard_map/ppermute | solution.py:211
  49.6 8.8 %collective-permute-done.4 = bf16[3,64,256]{2,1,0:T(8,128)(2,1)S(1)} collective-permute-done((bf16[3,64,256]{2,1,0:T(8,128)(2,1)S(1)}, bf16[3,64,256]{2,1,0:T(8,128)(2,1)S(1)}, u32[]{:S(2)}, u32[]{:S(2)}) %collective-permute-start.4) | collective-permute-done | bytes 98336 | tf_op jit(solution)/shard_map/ppermute | solution.py:211
  58.5 0.1 collective-permute-start.9
  58.6 2.5 %collective-permute-start.8 = (bf16[4,3,64,256]{3,2,1,0:T(8,128)(2,1)S(1)}, bf16[4,3,64,256]{3,2,1,0:T(8,128)(2,1)S(1)}, u32[]{:S(2)}, u32[]{:S(2)}) collective-permute-start(bf16[4,3,64,256]{3,2,1,0:T(8,128)(2,1)S(1)} %pad_maximum_fusion.rest_3_), channel_id=1, source_target_pairs={{0,6},{1,7},{2,4},{3,5},{4,2},{5,3},{6,0},{7,1},{8,14},{9,15},{10,... | collective-permute-start | bytes 1179656 | tf_op jit(solution)/shard_map/ppermute | solution.py:211
  61.1 0.5 collective-permute-start.7
  61.7 0.5 collective-permute-start.6
  62.2 0.1 collective-permute-start.2
  62.3 0.5 collective-permute-start.1
  62.8 8.7 %collective-permute-done.8.rest_6_ = bf16[4,3,64,256]{3,2,1,0:T(8,128)(2,1)S(1)} collective-permute-done((bf16[4,3,64,256]{3,2,1,0:T(8,128)(2,1)S(1)}, bf16[4,3,64,256]{3,2,1,0:T(8,128)(2,1)S(1)}, u32[]{:S(2)}, u32[]{:S(2)}) %collective-permute-start.8) | collective-permute-done | bytes 393248 | tf_op jit(solution)/shard_map/ppermute | solution.py:211
  71.5 8.0 %collective-permute-done.7.rest_5_ = bf16[4,3,64,256]{3,2,1,0:T(8,128)(2,1)S(1)} collective-permute-done((bf16[4,3,64,256]{3,2,1,0:T(8,128)(2,1)S(1)}, bf16[4,3,64,256]{3,2,1,0:T(8,128)(2,1)S(1)}, u32[]{:S(2)}, u32[]{:S(2)}) %collective-permute-start.7) | collective-permute-done | bytes 393248 | tf_op jit(solution)/shard_map/ppermute | solution.py:211
  79.6 0.5 collective-permute-start.10
  80.1 1.2 collective-permute-done.11.rest_9_
  81.3 0.6 collective-permute-done.10.rest_8_
  81.9 12.4 %products.1 = (bf16[4,3,64,256]{3,2,1,0:T(8,128)(2,1)S(1)}, bf16[4,3,64,256]{3,2,1,0:T(8,128)(2,1)S(1)}, bf16[4,3,64,256]{3,2,1,0:T(8,128)(2,1)S(1)}, bf16[4,3,6...) custom-call(s32[2]{0:T(128)S(1)} %pad_add_fusion.place_ref, s32[1,5]{1,0:T(1,128)S(1)} %copy-done.4, ...), custom_call_target="tpu_custom_call" | custom-call | tf_op jit(solution)/shard_map/products/pallas_call | solution.py:259
  94.2 0.7 copy-done.5
  95.0 0.7 copy-done.7
  95.7 0.8 copy-done.9
  96.5 3.6 %all-to-all-start.1 = ((bf16[4,4,2,64,256]{4,3,2,1,0:T(8,128)(2,1)}), bf16[4,4,2,64,256]{4,3,2,1,0:T(8,128)(2,1)S(1)}, u32[]{:S(2)}, u32[]{:S(2)}) async-start(bf16[4,4,2,64,256]{4,3,2,1,0:T(8,128)(2,1)} %get-tuple-element.29), calls=%async_computation.1 | async-start | bytes 2097152 | tf_op jit(solution)/shard_map/all_to_all | solution.py:278
  100.1 0.9 collective-permute-start.13
  101.1 1.5 %collective-permute-start.14 = (bf16[4,3,64,256]{3,2,1,0:T(8,128)(2,1)S(1)}, bf16[4,3,64,256]{3,2,1,0:T(8,128)(2,1)S(1)}, u32[]{:S(2)}, u32[]{:S(2)}) collective-permute-start(bf16[4,3,64,256]{3,2,1,0:T(8,128)(2,1)S(1)} %copy-done.8), channel_id=1, source_target_pairs={{0,4},{1,5},{2,6},{3,7},{4,0},{5,1},{6,2},{7,3},{8,12},{9,13},{10,... | collective-permute-start | bytes 1179656 | tf_op jit(solution)/shard_map/ppermute | solution.py:211
  102.6 1.1 collective-permute-start.15
  103.7 7.7 %collective-permute-done.13.rest_1_ = bf16[4,3,64,256]{3,2,1,0:T(8,128)(2,1)S(1)} collective-permute-done((bf16[4,3,64,256]{3,2,1,0:T(8,128)(2,1)S(1)}, bf16[4,3,64,256]{3,2,1,0:T(8,128)(2,1)S(1)}, u32[]{:S(2)}, u32[]{:S(2)}) %collective-permute-start.13) | collective-permute-done | bytes 393248 | tf_op jit(solution)/shard_map/ppermute | solution.py:211
  111.4 1.7 %collective-permute-done.14.rest_2_ = bf16[4,3,64,256]{3,2,1,0:T(8,128)(2,1)S(1)} collective-permute-done((bf16[4,3,64,256]{3,2,1,0:T(8,128)(2,1)S(1)}, bf16[4,3,64,256]{3,2,1,0:T(8,128)(2,1)S(1)}, u32[]{:S(2)}, u32[]{:S(2)}) %collective-permute-start.14) | collective-permute-done | bytes 393248 | tf_op jit(solution)/shard_map/ppermute | solution.py:211
  113.1 7.9 %collective-permute-done.15.rest_3_ = bf16[4,3,64,256]{3,2,1,0:T(8,128)(2,1)S(1)} collective-permute-done((bf16[4,3,64,256]{3,2,1,0:T(8,128)(2,1)S(1)}, bf16[4,3,64,256]{3,2,1,0:T(8,128)(2,1)S(1)}, u32[]{:S(2)}, u32[]{:S(2)}) %collective-permute-start.15) | collective-permute-done | bytes 393248 | tf_op jit(solution)/shard_map/ppermute | solution.py:211
  121.0 0.8 plane_sum.1
  121.8 1.7 %collective-permute-start.16 = (bf16[3,64,256]{2,1,0:T(8,128)(2,1)S(1)}, bf16[3,64,256]{2,1,0:T(8,128)(2,1)S(1)}, u32[]{:S(2)}, u32[]{:S(2)}) collective-permute-start(bf16[3,64,256]{2,1,0:T(8,128)(2,1)S(1)} %get-tuple-element.30), channel_id=1, source_target_pairs={{0,8},{1,9},{2,10},{3,11},{4,12},{5,13},{6,14},{7,15},{8,0},{9,1},... | collective-permute-start | bytes 294920 | tf_op jit(solution)/shard_map/ppermute | solution.py:211
  123.5 2.4 %collective-permute-start.17 = (bf16[3,64,256]{2,1,0:T(8,128)(2,1)S(1)}, bf16[3,64,256]{2,1,0:T(8,128)(2,1)S(1)}, u32[]{:S(2)}, u32[]{:S(2)}) collective-permute-start(bf16[3,64,256]{2,1,0:T(8,128)(2,1)S(1)} %get-tuple-element.32), channel_id=1, source_target_pairs={{0,16},{1,17},{2,18},{3,19},{4,20},{5,21},{6,22},{7,23},{8,24},{9,... | collective-permute-start | bytes 294920 | tf_op jit(solution)/shard_map/ppermute | solution.py:211
  125.8 0.4 collective-permute-start.18
  126.2 4.2 %collective-permute-done.16.rest_1_ = bf16[3,64,256]{2,1,0:T(8,128)(2,1)S(1)} collective-permute-done((bf16[3,64,256]{2,1,0:T(8,128)(2,1)S(1)}, bf16[3,64,256]{2,1,0:T(8,128)(2,1)S(1)}, u32[]{:S(2)}, u32[]{:S(2)}) %collective-permute-start.16) | collective-permute-done | bytes 98336 | tf_op jit(solution)/shard_map/ppermute | solution.py:211
  130.5 0.1 line_sum.1
  130.6 0.9 collective-permute-start.19
  131.5 1.5 %collective-permute-start.20 = (bf16[2,64,256]{2,1,0:T(8,128)(2,1)S(1)}, bf16[2,64,256]{2,1,0:T(8,128)(2,1)S(1)}, u32[]{:S(2)}, u32[]{:S(2)}) collective-permute-start(bf16[2,64,256]{2,1,0:T(8,128)(2,1)S(1)} %get-tuple-element.37), channel_id=1, source_target_pairs={{0,4},{1,5},{2,6},{3,7},{4,0},{5,1},{6,2},{7,3},{8,12},{9,13},{10,... | collective-permute-start | bytes 196616 | tf_op jit(solution)/shard_map/ppermute | solution.py:211
  133.0 1.1 collective-permute-start.21
  134.1 0.8 collective-permute-done.19.rest_5_
  134.9 1.1 collective-permute-done.20.rest_6_
  136.0 2.1 %collective-permute-done.21.rest_7_ = bf16[2,64,256]{2,1,0:T(8,128)(2,1)S(1)} collective-permute-done((bf16[2,64,256]{2,1,0:T(8,128)(2,1)S(1)}, bf16[2,64,256]{2,1,0:T(8,128)(2,1)S(1)}, u32[]{:S(2)}, u32[]{:S(2)}) %collective-permute-start.21) | collective-permute-done | bytes 65568 | tf_op jit(solution)/shard_map/ppermute | solution.py:211
  138.2 1.5 %update.1 = f32[1,5,64,256]{3,2,1,0:T(8,128)} custom-call(s32[2]{0:T(128)S(1)} %pad_add_fusion.place_ref, s32[1,5]{1,0:T(1,128)S(1)} %copy-done.4, f32[1,5,64,256]{3,2,1,0:T(8,128)S(1)} %copy-done.3, f32[3,64,256]{2,1,0:T(8,128)S(1)} %get-tuple-element.28.rest_0_, bf16[3,64,256]{2,1,0:T(8,128)(2,1)S(1)} %collective-permute-done.16.rest_1_, ...), custom_call_target="tpu_custom_call" | custom-call | tf_op jit(solution)/shard_map/update/pallas_call | solution.py:304
  (31 shorter events, 0.2 us)
Async XLA Ops:
  0.0 0.7 copy-start.4
  0.7 1.2 copy-start
  1.9 1.0 copy-start.2
  2.9 15.6 %copy-start.1 = (bf16[2048,256]{1,0:T(8,128)(2,1)S(1)}, bf16[2048,256]{1,0:T(8,128)(2,1)}, u32[]{:S(2)}) copy-start(bf16[2048,256]{1,0:T(8,128)(2,1)} %signals_ref.3) | copy-start | bytes 3145732
  3.5 14.9 %collective-permute-start = (bf16[1024,256]{1,0:T(8,128)(2,1)S(1)}, bf16[1024,256]{1,0:T(8,128)(2,1)S(1)}, u32[]{:S(2)}, u32[]{:S(2)}) collective-permute-start(bf16[1024,256]{1,0:T(8,128)(2,1)S(1)} %get-tuple-element.22), channel_id=1, source_target_pairs={{0,4},{1,5},{2,6},{3,7},{4,0},{5,1},{6,2},{7,3},{8,12},{9,13},{10,... | collective-permute-start | bytes 1572872 | tf_op jit(solution)/shard_map/ppermute | solution.py:211
  20.1 42.1 %all-to-all-start = ((bf16[4,2,256,256]{3,2,1,0:T(8,128)(2,1)}), bf16[4,2,256,256]{3,2,1,0:T(8,128)(2,1)S(1)}, u32[]{:S(2)}, u32[]{:S(2)}) async-start(bf16[4,2,256,256]{3,2,1,0:T(8,128)(2,1)} %deal.1), calls=%async_computation | async-start | bytes 2097152 | tf_op jit(solution)/shard_map/all_to_all | solution.py:256
  25.2 24.4 %collective-permute-start.5 = (bf16[3,64,256]{2,1,0:T(8,128)(2,1)S(1)}, bf16[3,64,256]{2,1,0:T(8,128)(2,1)S(1)}, u32[]{:S(2)}, u32[]{:S(2)}) collective-permute-start(bf16[3,64,256]{2,1,0:T(8,128)(2,1)S(1)} %get-tuple-element.23), channel_id=1, source_target_pairs={{0,24},{1,25},{2,26},{3,27},{4,28},{5,29},{6,30},{7,31},{8,16},{9,... | collective-permute-start | bytes 294920 | tf_op jit(solution)/shard_map/ppermute | solution.py:211
  29.0 29.5 %collective-permute-start.4 = (bf16[3,64,256]{2,1,0:T(8,128)(2,1)S(1)}, bf16[3,64,256]{2,1,0:T(8,128)(2,1)S(1)}, u32[]{:S(2)}, u32[]{:S(2)}) collective-permute-start(bf16[3,64,256]{2,1,0:T(8,128)(2,1)S(1)} %get-tuple-element.23), channel_id=1, source_target_pairs={{0,16},{1,17},{2,18},{3,19},{4,20},{5,21},{6,22},{7,23},{8,24},{9,... | collective-permute-start | bytes 294920 | tf_op jit(solution)/shard_map/ppermute | solution.py:211
  29.0 29.5 %collective-permute-start.3 = (bf16[3,64,256]{2,1,0:T(8,128)(2,1)S(1)}, bf16[3,64,256]{2,1,0:T(8,128)(2,1)S(1)}, u32[]{:S(2)}, u32[]{:S(2)}) collective-permute-start(bf16[3,64,256]{2,1,0:T(8,128)(2,1)S(1)} %get-tuple-element.23), channel_id=1, source_target_pairs={{0,8},{1,9},{2,10},{3,11},{4,12},{5,13},{6,14},{7,15},{8,0},{9,1},... | collective-permute-start | bytes 294920 | tf_op jit(solution)/shard_map/ppermute | solution.py:211
  58.5 3.8 %collective-permute-start.9 = (bf16[4,3,64,256]{3,2,1,0:T(8,128)(2,1)S(1)}, bf16[4,3,64,256]{3,2,1,0:T(8,128)(2,1)S(1)}, u32[]{:S(2)}, u32[]{:S(2)}) collective-permute-start(bf16[4,3,64,256]{3,2,1,0:T(8,128)(2,1)S(1)} %pad_maximum_fusion.rest_3_), channel_id=1, source_target_pairs={{0,1},{1,0},{2,3},{3,2},{4,5},{5,4},{6,7},{7,6},{8,9},{9,8},{10,11... | collective-permute-start | bytes 1179656 | tf_op jit(solution)/shard_map/ppermute | solution.py:211
  58.6 12.9 %collective-permute-start.8 = (bf16[4,3,64,256]{3,2,1,0:T(8,128)(2,1)S(1)}, bf16[4,3,64,256]{3,2,1,0:T(8,128)(2,1)S(1)}, u32[]{:S(2)}, u32[]{:S(2)}) collective-permute-start(bf16[4,3,64,256]{3,2,1,0:T(8,128)(2,1)S(1)} %pad_maximum_fusion.rest_3_), channel_id=1, source_target_pairs={{0,6},{1,7},{2,4},{3,5},{4,2},{5,3},{6,0},{7,1},{8,14},{9,15},{10,... | collective-permute-start | bytes 1179656 | tf_op jit(solution)/shard_map/ppermute | solution.py:211
  61.1 18.4 %collective-permute-start.7 = (bf16[4,3,64,256]{3,2,1,0:T(8,128)(2,1)S(1)}, bf16[4,3,64,256]{3,2,1,0:T(8,128)(2,1)S(1)}, u32[]{:S(2)}, u32[]{:S(2)}) collective-permute-start(bf16[4,3,64,256]{3,2,1,0:T(8,128)(2,1)S(1)} %pad_maximum_fusion.rest_3_), channel_id=1, source_target_pairs={{0,4},{1,5},{2,6},{3,7},{4,0},{5,1},{6,2},{7,3},{8,12},{9,13},{10,... | collective-permute-start | bytes 1179656 | tf_op jit(solution)/shard_map/ppermute | solution.py:211
  61.7 17.9 %collective-permute-start.6 = (bf16[4,3,64,256]{3,2,1,0:T(8,128)(2,1)S(1)}, bf16[4,3,64,256]{3,2,1,0:T(8,128)(2,1)S(1)}, u32[]{:S(2)}, u32[]{:S(2)}) collective-permute-start(bf16[4,3,64,256]{3,2,1,0:T(8,128)(2,1)S(1)} %pad_maximum_fusion.rest_3_), channel_id=1, source_target_pairs={{0,2},{1,3},{2,0},{3,1},{4,6},{5,7},{6,4},{7,5},{8,10},{9,11},{10,... | collective-permute-start | bytes 1179656 | tf_op jit(solution)/shard_map/ppermute | solution.py:211
  62.2 19.6 %collective-permute-start.2 = (bf16[2,2,256,256]{3,2,1,0:T(8,128)(2,1)S(1)}, bf16[2,2,256,256]{3,2,1,0:T(8,128)(2,1)S(1)}, u32[]{:S(2)}, u32[]{:S(2)}) collective-permute-start(bf16[2,2,256,256]{3,2,1,0:T(8,128)(2,1)S(1)} %get-tuple-element.39), channel_id=1, source_target_pairs={{0,1},{1,0},{2,3},{3,2},{4,5},{5,4},{6,7},{7,6},{8,9},{9,8},{10,11... | collective-permute-start | bytes 1572872 | tf_op jit(solution)/shard_map/ppermute | solution.py:211
  62.3 19.5 %collective-permute-start.1 = (bf16[2,2,256,256]{3,2,1,0:T(8,128)(2,1)S(1)}, bf16[2,2,256,256]{3,2,1,0:T(8,128)(2,1)S(1)}, u32[]{:S(2)}, u32[]{:S(2)}) collective-permute-start(bf16[2,2,256,256]{3,2,1,0:T(8,128)(2,1)S(1)} %get-tuple-element.40), channel_id=1, source_target_pairs={{0,1},{1,0},{2,3},{3,2},{4,5},{5,4},{6,7},{7,6},{8,9},{9,8},{10,11... | collective-permute-start | bytes 1572872 | tf_op jit(solution)/shard_map/ppermute | solution.py:211
  71.5 8.6 %collective-permute-start.12 = (bf16[4,3,64,256]{3,2,1,0:T(8,128)(2,1)S(1)}, bf16[4,3,64,256]{3,2,1,0:T(8,128)(2,1)S(1)}, u32[]{:S(2)}, u32[]{:S(2)}) collective-permute-start(bf16[4,3,64,256]{3,2,1,0:T(8,128)(2,1)S(1)} %collective-permute-done.8.rest_6_), channel_id=1, source_target_pairs={{0,1},{1,0},{2,3},{3,2},{4,5},{5,4},{6,7},{7,6},{8,9},{9,8},{10,11... | collective-permute-start | bytes 1179656 | tf_op jit(solution)/shard_map/ppermute | solution.py:211
  79.6 1.7 %collective-permute-start.11 = (bf16[4,3,64,256]{3,2,1,0:T(8,128)(2,1)S(1)}, bf16[4,3,64,256]{3,2,1,0:T(8,128)(2,1)S(1)}, u32[]{:S(2)}, u32[]{:S(2)}) collective-permute-start(bf16[4,3,64,256]{3,2,1,0:T(8,128)(2,1)S(1)} %collective-permute-done.7.rest_5_), channel_id=1, source_target_pairs={{0,1},{1,0},{2,3},{3,2},{4,5},{5,4},{6,7},{7,6},{8,9},{9,8},{10,11... | collective-permute-start | bytes 1179656 | tf_op jit(solution)/shard_map/ppermute | solution.py:211
  79.6 2.3 %collective-permute-start.10 = (bf16[4,3,64,256]{3,2,1,0:T(8,128)(2,1)S(1)}, bf16[4,3,64,256]{3,2,1,0:T(8,128)(2,1)S(1)}, u32[]{:S(2)}, u32[]{:S(2)}) collective-permute-start(bf16[4,3,64,256]{3,2,1,0:T(8,128)(2,1)S(1)} %collective-permute-done.6.rest_4_), channel_id=1, source_target_pairs={{0,1},{1,0},{2,3},{3,2},{4,5},{5,4},{6,7},{7,6},{8,9},{9,8},{10,11... | collective-permute-start | bytes 1179656 | tf_op jit(solution)/shard_map/ppermute | solution.py:211
  94.2 0.7 copy-start.5
  95.0 0.8 copy-start.7
  95.7 0.8 copy-start.9
  96.5 3.7 %copy-start.10 = (bf16[4,3,64,256]{3,2,1,0:T(8,128)(2,1)S(1)}, bf16[4,3,64,256]{3,2,1,0:T(8,128)(2,1)}, u32[]{:S(2)}) copy-start(bf16[4,3,64,256]{3,2,1,0:T(8,128)(2,1)} %copy-done.9) | copy-start | bytes 1179652
  96.5 4.6 %copy-start.8 = (bf16[4,3,64,256]{3,2,1,0:T(8,128)(2,1)S(1)}, bf16[4,3,64,256]{3,2,1,0:T(8,128)(2,1)}, u32[]{:S(2)}) copy-start(bf16[4,3,64,256]{3,2,1,0:T(8,128)(2,1)} %copy-done.7) | copy-start | bytes 1179652
  96.5 6.1 %copy-start.6 = (bf16[4,3,64,256]{3,2,1,0:T(8,128)(2,1)S(1)}, bf16[4,3,64,256]{3,2,1,0:T(8,128)(2,1)}, u32[]{:S(2)}) copy-start(bf16[4,3,64,256]{3,2,1,0:T(8,128)(2,1)} %copy-done.5) | copy-start | bytes 1179652
  96.5 34.0 %all-to-all-start.1 = ((bf16[4,4,2,64,256]{4,3,2,1,0:T(8,128)(2,1)}), bf16[4,4,2,64,256]{4,3,2,1,0:T(8,128)(2,1)S(1)}, u32[]{:S(2)}, u32[]{:S(2)}) async-start(bf16[4,4,2,64,256]{4,3,2,1,0:T(8,128)(2,1)} %get-tuple-element.29), calls=%async_computation.1 | async-start | bytes 2097152 | tf_op jit(solution)/shard_map/all_to_all | solution.py:278
  100.1 11.2 %collective-permute-start.13 = (bf16[4,3,64,256]{3,2,1,0:T(8,128)(2,1)S(1)}, bf16[4,3,64,256]{3,2,1,0:T(8,128)(2,1)S(1)}, u32[]{:S(2)}, u32[]{:S(2)}) collective-permute-start(bf16[4,3,64,256]{3,2,1,0:T(8,128)(2,1)S(1)} %copy-done.10), channel_id=1, source_target_pairs={{0,2},{1,3},{2,0},{3,1},{4,6},{5,7},{6,4},{7,5},{8,10},{9,11},{10,... | collective-permute-start | bytes 1179656 | tf_op jit(solution)/shard_map/ppermute | solution.py:211
  101.1 12.0 %collective-permute-start.14 = (bf16[4,3,64,256]{3,2,1,0:T(8,128)(2,1)S(1)}, bf16[4,3,64,256]{3,2,1,0:T(8,128)(2,1)S(1)}, u32[]{:S(2)}, u32[]{:S(2)}) collective-permute-start(bf16[4,3,64,256]{3,2,1,0:T(8,128)(2,1)S(1)} %copy-done.8), channel_id=1, source_target_pairs={{0,4},{1,5},{2,6},{3,7},{4,0},{5,1},{6,2},{7,3},{8,12},{9,13},{10,... | collective-permute-start | bytes 1179656 | tf_op jit(solution)/shard_map/ppermute | solution.py:211
  102.6 18.4 %collective-permute-start.15 = (bf16[4,3,64,256]{3,2,1,0:T(8,128)(2,1)S(1)}, bf16[4,3,64,256]{3,2,1,0:T(8,128)(2,1)S(1)}, u32[]{:S(2)}, u32[]{:S(2)}) collective-permute-start(bf16[4,3,64,256]{3,2,1,0:T(8,128)(2,1)S(1)} %copy-done.6), channel_id=1, source_target_pairs={{0,6},{1,7},{2,4},{3,5},{4,2},{5,3},{6,0},{7,1},{8,14},{9,15},{10,... | collective-permute-start | bytes 1179656 | tf_op jit(solution)/shard_map/ppermute | solution.py:211
  121.8 8.7 %collective-permute-start.16 = (bf16[3,64,256]{2,1,0:T(8,128)(2,1)S(1)}, bf16[3,64,256]{2,1,0:T(8,128)(2,1)S(1)}, u32[]{:S(2)}, u32[]{:S(2)}) collective-permute-start(bf16[3,64,256]{2,1,0:T(8,128)(2,1)S(1)} %get-tuple-element.30), channel_id=1, source_target_pairs={{0,8},{1,9},{2,10},{3,11},{4,12},{5,13},{6,14},{7,15},{8,0},{9,1},... | collective-permute-start | bytes 294920 | tf_op jit(solution)/shard_map/ppermute | solution.py:211
  123.5 10.7 %collective-permute-start.17 = (bf16[3,64,256]{2,1,0:T(8,128)(2,1)S(1)}, bf16[3,64,256]{2,1,0:T(8,128)(2,1)S(1)}, u32[]{:S(2)}, u32[]{:S(2)}) collective-permute-start(bf16[3,64,256]{2,1,0:T(8,128)(2,1)S(1)} %get-tuple-element.32), channel_id=1, source_target_pairs={{0,16},{1,17},{2,18},{3,19},{4,20},{5,21},{6,22},{7,23},{8,24},{9,... | collective-permute-start | bytes 294920 | tf_op jit(solution)/shard_map/ppermute | solution.py:211
  125.8 12.3 %copy-start.3 = (f32[1,5,64,256]{3,2,1,0:T(8,128)S(1)}, f32[1,5,64,256]{3,2,1,0:T(8,128)}, u32[]{:S(2)}) copy-start(f32[1,5,64,256]{3,2,1,0:T(8,128)} %omega_ref.3) | copy-start | bytes 983044
  125.8 8.3 %collective-permute-start.18 = (bf16[3,64,256]{2,1,0:T(8,128)(2,1)S(1)}, bf16[3,64,256]{2,1,0:T(8,128)(2,1)S(1)}, u32[]{:S(2)}, u32[]{:S(2)}) collective-permute-start(bf16[3,64,256]{2,1,0:T(8,128)(2,1)S(1)} %get-tuple-element.33), channel_id=1, source_target_pairs={{0,24},{1,25},{2,26},{3,27},{4,28},{5,29},{6,30},{7,31},{8,16},{9,... | collective-permute-start | bytes 294920 | tf_op jit(solution)/shard_map/ppermute | solution.py:211
  130.6 4.3 %collective-permute-start.19 = (bf16[2,64,256]{2,1,0:T(8,128)(2,1)S(1)}, bf16[2,64,256]{2,1,0:T(8,128)(2,1)S(1)}, u32[]{:S(2)}, u32[]{:S(2)}) collective-permute-start(bf16[2,64,256]{2,1,0:T(8,128)(2,1)S(1)} %get-tuple-element.36), channel_id=1, source_target_pairs={{0,2},{1,3},{2,0},{3,1},{4,6},{5,7},{6,4},{7,5},{8,10},{9,11},{10,... | collective-permute-start | bytes 196616 | tf_op jit(solution)/shard_map/ppermute | solution.py:211
  131.5 4.5 %collective-permute-start.20 = (bf16[2,64,256]{2,1,0:T(8,128)(2,1)S(1)}, bf16[2,64,256]{2,1,0:T(8,128)(2,1)S(1)}, u32[]{:S(2)}, u32[]{:S(2)}) collective-permute-start(bf16[2,64,256]{2,1,0:T(8,128)(2,1)S(1)} %get-tuple-element.37), channel_id=1, source_target_pairs={{0,4},{1,5},{2,6},{3,7},{4,0},{5,1},{6,2},{7,3},{8,12},{9,13},{10,... | collective-permute-start | bytes 196616 | tf_op jit(solution)/shard_map/ppermute | solution.py:211
  133.0 5.2 %collective-permute-start.21 = (bf16[2,64,256]{2,1,0:T(8,128)(2,1)S(1)}, bf16[2,64,256]{2,1,0:T(8,128)(2,1)S(1)}, u32[]{:S(2)}, u32[]{:S(2)}) collective-permute-start(bf16[2,64,256]{2,1,0:T(8,128)(2,1)S(1)} %get-tuple-element.38), channel_id=1, source_target_pairs={{0,6},{1,7},{2,4},{3,5},{4,2},{5,3},{6,0},{7,1},{8,14},{9,15},{10,... | collective-permute-start | bytes 196616 | tf_op jit(solution)/shard_map/ppermute | solution.py:211

commit v3 on v1

--- a/solution.py
+++ b/solution.py
@@ -10,13 +10,14 @@
 STEP_SIZE = 0.5
 PENALTY = 0.1
 LOW = 2
+LINE_FIRST = (3, 4)
+PLANE_FIRST = (0, 1, 2)
 F32 = jnp.float32
 BF16 = jnp.bfloat16
 
 VMEM = pl.BlockSpec(memory_space=pltpu.VMEM)
 ANY = pl.BlockSpec(memory_space=pl.ANY)
 SMEM = pl.BlockSpec(memory_space=pltpu.SMEM)
-SMALL = pltpu.CompilerParams(vmem_limit_bytes=8 * 2**20)
 
 
 def stored_offsets(pattern_ref, team, teams):
@@ -36,12 +37,13 @@
         out_ref[k] = omega_ref[0, slots[k]].astype(BF16)
 
 
-def product_kernel(teams, replicas, tile_rows, place_ref, pattern_ref, own_ref, low_ref, high_ref, *rest):
+def product_kernel(teams, replicas, tile_rows, place_ref, pattern_ref, *rest):
     chips = replicas // 2
     planes = LOW * chips
     depth = teams // LOW
+    own_ref, low_ref, high_ref, *rest = rest
     weight_refs, rest = rest[: 2 * planes], rest[2 * planes :]
-    outs, rest = rest[:planes], rest[planes:]
+    plane_outs, line_outs, rest = rest[:planes], rest[planes : planes + depth], rest[planes + depth :]
     data_ref, omega_ref, mixed_ref, flip_ref, left_ref, data_sems, omega_sems = rest
     team, replica = place_ref[0], place_ref[1]
     core, chip = lax.rem(replica, 2), lax.div(replica, 2)
@@ -98,22 +100,41 @@
 
     unroll = teams <= 8
     lax.fori_loop(0, teams, mix, 0, unroll=unroll)
+
+    def part(i, k):
+        c = lax.rem(i + offsets[k], teams)
+        right = jnp.concatenate([data_ref[c], mixed_ref[c]], axis=0)
+        product = lax.dot_general(left_ref[i], right, nn, preferred_element_type=F32).astype(BF16)
+        return [product[m * tile_rows : (m + 1) * tile_rows] for m in range(chips)]
+
+    for mx in range(LOW):
+        for mz in range(depth):
+            i = (high ^ mz) * LOW + (low ^ mx)
+            for n, k in enumerate(LINE_FIRST):
+                for m, rows in enumerate(part(i, k)):
+                    line_outs[mz][mx * chips + m, n] = rows
     for mx in range(LOW):
 
         def outer(z, carry):
             i = z * LOW + (low ^ mx)
-            for k, offset in enumerate(offsets):
-                c = lax.rem(i + offset, teams)
-                right = jnp.concatenate([data_ref[c], mixed_ref[c]], axis=0)
-                part = lax.dot_general(left_ref[i], right, nn, preferred_element_type=F32).astype(BF16)
-                for m in range(chips):
-                    outs[mx * chips + m][z, k] = part[m * tile_rows : (m + 1) * tile_rows]
+            for n, k in enumerate(PLANE_FIRST):
+                for m, rows in enumerate(part(i, k)):
+                    plane_outs[mx * chips + m][z, n] = rows
             return carry
 
         lax.fori_loop(0, depth, outer, 0, unroll=unroll)
 
 
-def add_kernel(teams, place_ref, *rest):
+def line_sum_kernel(planes, *rest):
+    parts, outs = rest[:-planes], rest[-planes:]
+    for m in range(planes):
+        total = parts[0][m].astype(F32)
+        for part in parts[1:]:
+            total = total + part[m].astype(F32)
+        outs[m][...] = total.astype(outs[m].dtype)
+
+
+def plane_sum_kernel(teams, place_ref, *rest):
     count = teams // LOW
     parts, outs = rest[:-count], rest[-count:]
     z = lax.div(place_ref[0], LOW)
@@ -125,16 +146,18 @@
 
 
 def update_kernel(teams, scale, place_ref, pattern_ref, omega_ref, *rest):
-    parts, out_ref = rest[:-1], rest[-1]
+    depth = teams // LOW
+    plane_first, line_first, out_ref = rest[:depth], rest[depth:-1], rest[-1]
     _, slots = stored_offsets(pattern_ref, place_ref[0], teams)
     rows, width = out_ref.shape[2:]
     first = place_ref[1] * rows
     row_ids = first + lax.broadcasted_iota(jnp.int32, (rows, width), 0)
     diagonal = row_ids == lax.broadcasted_iota(jnp.int32, (rows, width), 1)
     for k in range(5):
-        total = parts[0][k].astype(F32)
+        parts, n = (line_first, LINE_FIRST.index(k)) if k in LINE_FIRST else (plane_first, PLANE_FIRST.index(k))
+        total = parts[0][n].astype(F32)
         for part in parts[1:]:
-            total = total + part[k].astype(F32)
+            total = total + part[n].astype(F32)
         current = omega_ref[0, slots[k]]
         gradient = total * scale
         if k == 0:
@@ -163,29 +186,45 @@
 
     planes = LOW * chips
     count = teams // LOW
+    planes = LOW * chips
+    count = teams // LOW
+    small = pltpu.CompilerParams(vmem_limit_bytes=(8 if teams <= 8 else 48) * 2**20)
+    large = pltpu.CompilerParams(vmem_limit_bytes=(14 if teams <= 8 else 56) * 2**20)
+
+    def across_plane(arrays):
+        return [
+            swap(arrays[mx * chips + my], mx, 2 * my) if mx + my else arrays[0]
+            for mx in range(LOW)
+            for my in range(chips)
+        ]
+
+    def along_line(arrays):
+        return [swap(array, m * LOW, 0) if m else array for m, array in enumerate(arrays)]
+
     upper = pl.pallas_call(
         functools.partial(prepare_kernel, teams),
         out_shape=jax.ShapeDtypeStruct((3, tile_rows, width), BF16),
         in_specs=[SMEM, SMEM, VMEM],
         out_specs=VMEM,
-        compiler_params=SMALL,
+        compiler_params=small,
         name="prepare",
     )(place, pattern, omega)
 
-    line = jnp.stack([upper] + [swap(upper, m * LOW, 0) for m in range(1, count)])
+    line = jnp.stack(along_line([upper] * count))
     line, signals = lax.optimization_barrier((line, signals))
-    weights = [
-        swap(line, mx, 2 * my) if mx + my else line for mx in range(LOW) for my in range(chips)
-    ]
+    rows = [line, swap(line, 1, 0)]
+    weights = [swap(row, 0, 2 * my) if my else row for row in rows for my in range(chips)]
     own = lax.all_to_all(signals.reshape(teams, times, width), "blk", 0, 0)
+    weights[-1], own = lax.optimization_barrier((weights[-1], own))
     other = [swap(part, 0, 1) for part in jnp.split(own, 2)]
     weights += [swap(array, 0, 1) for array in weights]
 
     partial = pl.pallas_call(
         functools.partial(product_kernel, teams, replicas, tile_rows),
-        out_shape=[jax.ShapeDtypeStruct((count, slots, tile_rows, width), BF16)] * planes,
+        out_shape=[jax.ShapeDtypeStruct((count, len(PLANE_FIRST), tile_rows, width), BF16)] * planes
+        + [jax.ShapeDtypeStruct((planes, len(LINE_FIRST), tile_rows, width), BF16)] * count,
         in_specs=[SMEM, SMEM] + [ANY] * (3 + 2 * planes),
-        out_specs=[VMEM] * planes,
+        out_specs=[VMEM] * (planes + count),
         scratch_shapes=[
             pltpu.VMEM((teams, 2 * times, width), BF16),
             pltpu.VMEM((teams, 3, width, width), BF16),
@@ -195,36 +234,46 @@
             pltpu.SemaphoreType.DMA((3,)),
             pltpu.SemaphoreType.DMA((2 * planes * count,)),
         ],
-        compiler_params=pltpu.CompilerParams(vmem_limit_bytes=(16 if teams <= 8 else 48) * 2**20),
+        compiler_params=large,
         name="products",
     )(place, pattern, own, *other, *weights)
-    received = [
-        swap(partial[mx * chips + my], mx, 2 * my) if mx + my else partial[0]
-        for mx in range(LOW)
-        for my in range(chips)
-    ]
-
-    summed = pl.pallas_call(
-        functools.partial(add_kernel, teams),
+
+    partial = list(partial)
+    line_parts = along_line(partial[planes:])
+    partial[planes - 1], line_parts[2] = lax.optimization_barrier((partial[planes - 1], line_parts[2]))
+    plane_parts = across_plane(partial[:planes])
+    plane_sums = pl.pallas_call(
+        functools.partial(plane_sum_kernel, teams),
         out_shape=[
-            jax.ShapeDtypeStruct((slots, tile_rows, width), BF16 if m else F32) for m in range(count)
+            jax.ShapeDtypeStruct((len(PLANE_FIRST), tile_rows, width), BF16 if m else F32) for m in range(count)
         ],
         in_specs=[SMEM] + [VMEM] * planes,
         out_specs=[VMEM] * count,
-        compiler_params=pltpu.CompilerParams(vmem_limit_bytes=(8 if teams <= 8 else 48) * 2**20),
+        compiler_params=small,
         name="plane_sum",
-    )(place, *received)
-    arrived = [swap(summed[m], m * LOW, 0) if m else summed[0] for m in range(count)]
+    )(place, *plane_parts)
+    plane_sums = along_line(plane_sums)
+    line_parts[1], plane_sums[1] = lax.optimization_barrier((line_parts[1], plane_sums[1]))
+    line_sums = pl.pallas_call(
+        functools.partial(line_sum_kernel, planes),
+        out_shape=[
+            jax.ShapeDtypeStruct((len(LINE_FIRST), tile_rows, width), BF16 if m else F32) for m in range(planes)
+        ],
+        in_specs=[VMEM] * count,
+        out_specs=[VMEM] * planes,
+        compiler_params=small,
+        name="line_sum",
+    )(*line_parts)
 
     scale = 1.0 / (2.0 * signals.shape[0] * replicas)
     return pl.pallas_call(
         functools.partial(update_kernel, teams, scale),
         out_shape=jax.ShapeDtypeStruct(omega.shape, F32),
-        in_specs=[SMEM, SMEM, VMEM] + [VMEM] * count,
+        in_specs=[SMEM, SMEM, VMEM] + [VMEM] * (count + planes),
         out_specs=VMEM,
-        compiler_params=pltpu.CompilerParams(vmem_limit_bytes=(8 if teams <= 8 else 48) * 2**20),
+        compiler_params=small,
         name="update",
-    )(place, pattern, omega, *arrived)
+    )(place, pattern, omega, *plane_sums, *across_plane(line_sums))
 
 
 def solution(mesh):

time: 112 us -> 114 us (1.018)
  starting transfers between devices: 23.3 us -> 36.5 us
  waiting for transfers between devices: 75.2 us -> 63.6 us
    all_to_all x1, waiting for transfers between devices: 21.3 us -> 0.01 us  [per_device(): own = lax.all_to_all(signals.reshape(teams, times, width), 'blk', 0, 0)]
    ppermute x18 -> x24, starting transfers between devices: 18.5 us -> 31.7 us  [swap(): return lax.ppermute(array, ('blk', 'rep'), route)]
    ppermute x18 -> x24, waiting for transfers between devices: 53.9 us -> 63.6 us  [swap(): return lax.ppermute(array, ('blk', 'rep'), route)]
  transfers between devices with their start and end apart: 19 -> 25, of which waited for: 11 -> 14; matrix products, arithmetic and copies ran while one was open for 0% -> 0% of each run, Pallas kernels for 0% -> 1%
where the time goes in v3:
time: 114 us
  waiting for transfers between devices  63.6 us (56%)
  starting transfers between devices  36.5 us (32%)
  Pallas kernels  11.9 us (10%)
  local copies, waits for them, and re-layouts  1.62 us (1%)
    ppermute x24, waiting for transfers between devices, swap(): return lax.ppermute(array, ('blk', 'rep'), route)  63.6 us
    ppermute x24, starting transfers between devices, swap(): return lax.ppermute(array, ('blk', 'rep'), route)  31.7 us
    pallas_call x1, Pallas kernels, per_device(): pl.pallas_call(functools.partial(product_kernel, teams, replicas, tile_ro...  8.95 us
    all_to_all x1, starting transfers between devices, per_device(): own = lax.all_to_all(signals.reshape(teams, times, width), 'blk', 0, 0)  4.73 us
  transfers between devices with their start and end apart: 25, of which 14 were waited for; matrix products, arithmetic and copies ran while one was open for 0% of the time, Pallas kernels for 1%

profile of v3, /device:TPU:0, one launch (start us, length us, event | category | flops | bytes accessed | tf_op | source)
XLA Modules:
  0.0 113.7 jit_solution(4513818218772200655)
XLA Ops:
  0.0 0.1 pad_add_fusion.place_ref
  0.1 0.6 copy-done.2
  0.7 1.0 copy-done
  1.6 0.6 prepare.1
  2.2 5.1 %collective-permute-start.2 = (bf16[3,64,256]{2,1,0:T(8,128)(2,1)S(1)}, bf16[3,64,256]{2,1,0:T(8,128)(2,1)S(1)}, u32[]{:S(2)}, u32[]{:S(2)}) collective-permute-start(bf16[3,64,256]{2,1,0:T(8,128)(2,1)S(1)} %prepare.1), channel_id=1, source_target_pairs={{0,24},{1,25},{2,26},{3,27},{4,28},{5,29},{6,30},{7,31},{8,16},{9,... | collective-permute-start | bytes 294920 | tf_op jit(solution)/shard_map/ppermute | solution.py:185
  7.3 0.0 collective-permute-start.1
  7.3 0.6 collective-permute-start
  8.0 3.1 %collective-permute-done.2 = bf16[3,64,256]{2,1,0:T(8,128)(2,1)S(1)} collective-permute-done((bf16[3,64,256]{2,1,0:T(8,128)(2,1)S(1)}, bf16[3,64,256]{2,1,0:T(8,128)(2,1)S(1)}, u32[]{:S(2)}, u32[]{:S(2)}) %collective-permute-start.2) | collective-permute-done | bytes 98336 | tf_op jit(solution)/shard_map/ppermute | solution.py:185
  11.0 4.6 %collective-permute-done.1 = bf16[3,64,256]{2,1,0:T(8,128)(2,1)S(1)} collective-permute-done((bf16[3,64,256]{2,1,0:T(8,128)(2,1)S(1)}, bf16[3,64,256]{2,1,0:T(8,128)(2,1)S(1)}, u32[]{:S(2)}, u32[]{:S(2)}) %collective-permute-start.1) | collective-permute-done | bytes 98336 | tf_op jit(solution)/shard_map/ppermute | solution.py:185
  15.6 0.1 pad_maximum_fusion.rest_3_
  15.7 4.7 %all-to-all-start = ((bf16[8,256,256]{2,1,0:T(8,128)(2,1)}), bf16[8,256,256]{2,1,0:T(8,128)(2,1)S(1)}, u32[]{:S(2)}, u32[]{:S(2)}) async-start(bf16[8,256,256]{2,1,0:T(8,128)(2,1)} %bitcast.6), calls=%async_computation | async-start | bytes 2097152 | tf_op jit(solution)/shard_map/all_to_all | solution.py:217
  20.4 2.0 %collective-permute-start.3 = (bf16[4,3,64,256]{3,2,1,0:T(8,128)(2,1)S(1)}, bf16[4,3,64,256]{3,2,1,0:T(8,128)(2,1)S(1)}, u32[]{:S(2)}, u32[]{:S(2)}) collective-permute-start(bf16[4,3,64,256]{3,2,1,0:T(8,128)(2,1)S(1)} %pad_maximum_fusion.rest_3_), channel_id=1, source_target_pairs={{0,4},{1,5},{2,6},{3,7},{4,0},{5,1},{6,2},{7,3},{8,12},{9,13},{10,... | collective-permute-start | bytes 1179656 | tf_op jit(solution)/shard_map/ppermute | solution.py:185
  22.4 18.9 %collective-permute-done.3.rest_5_ = bf16[4,3,64,256]{3,2,1,0:T(8,128)(2,1)S(1)} collective-permute-done((bf16[4,3,64,256]{3,2,1,0:T(8,128)(2,1)S(1)}, bf16[4,3,64,256]{3,2,1,0:T(8,128)(2,1)S(1)}, u32[]{:S(2)}, u32[]{:S(2)}) %collective-permute-start.3) | collective-permute-done | bytes 393248 | tf_op jit(solution)/shard_map/ppermute | solution.py:185
  41.3 1.5 %collective-permute-start.4 = (bf16[4,3,64,256]{3,2,1,0:T(8,128)(2,1)S(1)}, bf16[4,3,64,256]{3,2,1,0:T(8,128)(2,1)S(1)}, u32[]{:S(2)}, u32[]{:S(2)}) collective-permute-start(bf16[4,3,64,256]{3,2,1,0:T(8,128)(2,1)S(1)} %collective-permute-done.3.rest_5_), channel_id=1, source_target_pairs={{0,2},{1,3},{2,0},{3,1},{4,6},{5,7},{6,4},{7,5},{8,10},{9,11},{10,... | collective-permute-start | bytes 1179656 | tf_op jit(solution)/shard_map/ppermute | solution.py:185
  42.8 0.0 collective-permute-start.8
  42.8 0.5 collective-permute-start.7
  43.3 8.9 %collective-permute-done.4.rest_6_ = bf16[4,3,64,256]{3,2,1,0:T(8,128)(2,1)S(1)} collective-permute-done((bf16[4,3,64,256]{3,2,1,0:T(8,128)(2,1)S(1)}, bf16[4,3,64,256]{3,2,1,0:T(8,128)(2,1)S(1)}, u32[]{:S(2)}, u32[]{:S(2)}) %collective-permute-start.4) | collective-permute-done | bytes 393248 | tf_op jit(solution)/shard_map/ppermute | solution.py:185
  52.3 0.1 fusion
  52.3 0.1 collective-permute-start.6
  52.4 0.5 collective-permute-start.5
  52.9 0.1 collective-permute-start.10
  53.0 4.5 %collective-permute-done.7.rest_4_ = bf16[4,3,64,256]{3,2,1,0:T(8,128)(2,1)S(1)} collective-permute-done((bf16[4,3,64,256]{3,2,1,0:T(8,128)(2,1)S(1)}, bf16[4,3,64,256]{3,2,1,0:T(8,128)(2,1)S(1)}, u32[]{:S(2)}, u32[]{:S(2)}) %collective-permute-start.7) | collective-permute-done | bytes 393248 | tf_op jit(solution)/shard_map/ppermute | solution.py:185
  57.5 0.0 collective-permute-start.9
  57.5 0.5 collective-permute-start.11
  58.0 1.2 %collective-permute-done.9.rest_8_ = bf16[4,3,64,256]{3,2,1,0:T(8,128)(2,1)S(1)} collective-permute-done((bf16[4,3,64,256]{3,2,1,0:T(8,128)(2,1)S(1)}, bf16[4,3,64,256]{3,2,1,0:T(8,128)(2,1)S(1)}, u32[]{:S(2)}, u32[]{:S(2)}) %collective-permute-start.9) | collective-permute-done | bytes 393248 | tf_op jit(solution)/shard_map/ppermute | solution.py:185
  59.2 0.6 collective-permute-done.11.rest_10_
  59.8 8.9 %products.1 = (bf16[4,3,64,256]{3,2,1,0:T(8,128)(2,1)S(1)}, bf16[4,3,64,256]{3,2,1,0:T(8,128)(2,1)S(1)}, bf16[4,3,64,256]{3,2,1,0:T(8,128)(2,1)S(1)}, bf16[4,3,6...) custom-call(s32[2]{0:T(128)S(1)} %pad_add_fusion.place_ref, ...), custom_call_target="tpu_custom_call" | custom-call | tf_op jit(solution)/shard_map/products/pallas_call | solution.py:222
  68.7 2.9 %collective-permute-start.14 = (bf16[4,2,64,256]{3,2,1,0:T(8,128)(2,1)S(1)}, bf16[4,2,64,256]{3,2,1,0:T(8,128)(2,1)S(1)}, u32[]{:S(2)}, u32[]{:S(2)}) collective-permute-start(bf16[4,2,64,256]{3,2,1,0:T(8,128)(2,1)S(1)} %get-tuple-element.37), channel_id=1, source_target_pairs={{0,16},{1,17},{2,18},{3,19},{4,20},{5,21},{6,22},{7,23},{8,24},{9,... | collective-permute-start | bytes 786440 | tf_op jit(solution)/shard_map/ppermute | solution.py:185
  71.6 1.5 %collective-permute-start.12 = (bf16[4,3,64,256]{3,2,1,0:T(8,128)(2,1)S(1)}, bf16[4,3,64,256]{3,2,1,0:T(8,128)(2,1)S(1)}, u32[]{:S(2)}, u32[]{:S(2)}) collective-permute-start(bf16[4,3,64,256]{3,2,1,0:T(8,128)(2,1)S(1)} %get-tuple-element.34), channel_id=1, source_target_pairs={{0,2},{1,3},{2,0},{3,1},{4,6},{5,7},{6,4},{7,5},{8,10},{9,11},{10,... | collective-permute-start | bytes 1179656 | tf_op jit(solution)/shard_map/ppermute | solution.py:185
  73.1 2.5 %collective-permute-start.13 = (bf16[4,3,64,256]{3,2,1,0:T(8,128)(2,1)S(1)}, bf16[4,3,64,256]{3,2,1,0:T(8,128)(2,1)S(1)}, u32[]{:S(2)}, u32[]{:S(2)}) collective-permute-start(bf16[4,3,64,256]{3,2,1,0:T(8,128)(2,1)S(1)} %get-tuple-element.35), channel_id=1, source_target_pairs={{0,4},{1,5},{2,6},{3,7},{4,0},{5,1},{6,2},{7,3},{8,12},{9,13},{10,... | collective-permute-start | bytes 1179656 | tf_op jit(solution)/shard_map/ppermute | solution.py:185
  75.6 8.2 %collective-permute-done.14.rest_2_ = bf16[4,2,64,256]{3,2,1,0:T(8,128)(2,1)S(1)} collective-permute-done((bf16[4,2,64,256]{3,2,1,0:T(8,128)(2,1)S(1)}, bf16[4,2,64,256]{3,2,1,0:T(8,128)(2,1)S(1)}, u32[]{:S(2)}, u32[]{:S(2)}) %collective-permute-start.14) | collective-permute-done | bytes 262176 | tf_op jit(solution)/shard_map/ppermute | solution.py:185
  83.9 3.4 %collective-permute-start.15 = (bf16[4,3,64,256]{3,2,1,0:T(8,128)(2,1)S(1)}, bf16[4,3,64,256]{3,2,1,0:T(8,128)(2,1)S(1)}, u32[]{:S(2)}, u32[]{:S(2)}) collective-permute-start(bf16[4,3,64,256]{3,2,1,0:T(8,128)(2,1)S(1)} %get-tuple-element.38), channel_id=1, source_target_pairs={{0,6},{1,7},{2,4},{3,5},{4,2},{5,3},{6,0},{7,1},{8,14},{9,15},{10,... | collective-permute-start | bytes 1179656 | tf_op jit(solution)/shard_map/ppermute | solution.py:185
  87.3 2.4 %collective-permute-start.20 = (bf16[4,2,64,256]{3,2,1,0:T(8,128)(2,1)S(1)}, bf16[4,2,64,256]{3,2,1,0:T(8,128)(2,1)S(1)}, u32[]{:S(2)}, u32[]{:S(2)}) collective-permute-start(bf16[4,2,64,256]{3,2,1,0:T(8,128)(2,1)S(1)} %get-tuple-element.48), channel_id=1, source_target_pairs={{0,24},{1,25},{2,26},{3,27},{4,28},{5,29},{6,30},{7,31},{8,16},{9,... | collective-permute-start | bytes 786440 | tf_op jit(solution)/shard_map/ppermute | solution.py:185
  89.7 6.5 %collective-permute-done.15.rest_3_ = bf16[4,3,64,256]{3,2,1,0:T(8,128)(2,1)S(1)} collective-permute-done((bf16[4,3,64,256]{3,2,1,0:T(8,128)(2,1)S(1)}, bf16[4,3,64,256]{3,2,1,0:T(8,128)(2,1)S(1)}, u32[]{:S(2)}, u32[]{:S(2)}) %collective-permute-start.15) | collective-permute-done | bytes 393248 | tf_op jit(solution)/shard_map/ppermute | solution.py:185
  96.2 0.7 plane_sum.1
  97.0 0.4 collective-permute-start.17
  97.3 3.4 %collective-permute-start.18 = (bf16[3,64,256]{2,1,0:T(8,128)(2,1)S(1)}, bf16[3,64,256]{2,1,0:T(8,128)(2,1)S(1)}, u32[]{:S(2)}, u32[]{:S(2)}) collective-permute-start(bf16[3,64,256]{2,1,0:T(8,128)(2,1)S(1)} %get-tuple-element.43), channel_id=1, source_target_pairs={{0,16},{1,17},{2,18},{3,19},{4,20},{5,21},{6,22},{7,23},{8,24},{9,... | collective-permute-start | bytes 294920 | tf_op jit(solution)/shard_map/ppermute | solution.py:185
  100.7 0.7 collective-permute-start.19
  101.4 3.2 %collective-permute-done.17.rest_1_ = bf16[3,64,256]{2,1,0:T(8,128)(2,1)S(1)} collective-permute-done((bf16[3,64,256]{2,1,0:T(8,128)(2,1)S(1)}, bf16[3,64,256]{2,1,0:T(8,128)(2,1)S(1)}, u32[]{:S(2)}, u32[]{:S(2)}) %collective-permute-start.17) | collective-permute-done | bytes 98336 | tf_op jit(solution)/shard_map/ppermute | solution.py:185
  104.6 0.1 line_sum.1
  104.8 0.5 collective-permute-start.21
  105.3 1.9 %collective-permute-start.22 = (bf16[2,64,256]{2,1,0:T(8,128)(2,1)S(1)}, bf16[2,64,256]{2,1,0:T(8,128)(2,1)S(1)}, u32[]{:S(2)}, u32[]{:S(2)}) collective-permute-start(bf16[2,64,256]{2,1,0:T(8,128)(2,1)S(1)} %get-tuple-element.51), channel_id=1, source_target_pairs={{0,4},{1,5},{2,6},{3,7},{4,0},{5,1},{6,2},{7,3},{8,12},{9,13},{10,... | collective-permute-start | bytes 196616 | tf_op jit(solution)/shard_map/ppermute | solution.py:185
  107.1 1.2 %collective-permute-start.23 = (bf16[2,64,256]{2,1,0:T(8,128)(2,1)S(1)}, bf16[2,64,256]{2,1,0:T(8,128)(2,1)S(1)}, u32[]{:S(2)}, u32[]{:S(2)}) collective-permute-start(bf16[2,64,256]{2,1,0:T(8,128)(2,1)S(1)} %get-tuple-element.52), channel_id=1, source_target_pairs={{0,6},{1,7},{2,4},{3,5},{4,2},{5,3},{6,0},{7,1},{8,14},{9,15},{10,... | collective-permute-start | bytes 196616 | tf_op jit(solution)/shard_map/ppermute | solution.py:185
  108.3 0.3 collective-permute-done.18.rest_2_
  108.6 0.5 collective-permute-done.21.rest_5_
  109.1 0.4 collective-permute-done.22.rest_6_
  109.5 2.8 %collective-permute-done.23.rest_7_ = bf16[2,64,256]{2,1,0:T(8,128)(2,1)S(1)} collective-permute-done((bf16[2,64,256]{2,1,0:T(8,128)(2,1)S(1)}, bf16[2,64,256]{2,1,0:T(8,128)(2,1)S(1)}, u32[]{:S(2)}, u32[]{:S(2)}) %collective-permute-start.23) | collective-permute-done | bytes 65568 | tf_op jit(solution)/shard_map/ppermute | solution.py:185
  112.3 1.5 %update.1 = f32[1,5,64,256]{3,2,1,0:T(8,128)} custom-call(s32[2]{0:T(128)S(1)} %pad_add_fusion.place_ref, s32[1,5]{1,0:T(1,128)S(1)} %copy-done.2, f32[1,5,64,256]{3,2,1,0:T(8,128)S(1)} %copy-done.1, f32[3,64,256]{2,1,0:T(8,128)S(1)} %get-tuple-element.39.rest_0_, bf16[3,64,256]{2,1,0:T(8,128)(2,1)S(1)} %collective-permute-done.17.rest_1_, ...), custom_call_target="tpu_custom_call" | custom-call | tf_op jit(solution)/shard_map/update/pallas_call | solution.py:269
  (16 shorter events, 0.0 us)
Async XLA Ops:
  0.0 0.7 copy-start.2
  0.7 1.0 copy-start
  2.2 8.8 %collective-permute-start.2 = (bf16[3,64,256]{2,1,0:T(8,128)(2,1)S(1)}, bf16[3,64,256]{2,1,0:T(8,128)(2,1)S(1)}, u32[]{:S(2)}, u32[]{:S(2)}) collective-permute-start(bf16[3,64,256]{2,1,0:T(8,128)(2,1)S(1)} %prepare.1), channel_id=1, source_target_pairs={{0,24},{1,25},{2,26},{3,27},{4,28},{5,29},{6,30},{7,31},{8,16},{9,... | collective-permute-start | bytes 294920 | tf_op jit(solution)/shard_map/ppermute | solution.py:185
  7.3 8.3 %collective-permute-start.1 = (bf16[3,64,256]{2,1,0:T(8,128)(2,1)S(1)}, bf16[3,64,256]{2,1,0:T(8,128)(2,1)S(1)}, u32[]{:S(2)}, u32[]{:S(2)}) collective-permute-start(bf16[3,64,256]{2,1,0:T(8,128)(2,1)S(1)} %prepare.1), channel_id=1, source_target_pairs={{0,16},{1,17},{2,18},{3,19},{4,20},{5,21},{6,22},{7,23},{8,24},{9,... | collective-permute-start | bytes 294920 | tf_op jit(solution)/shard_map/ppermute | solution.py:185
  7.3 8.3 %collective-permute-start = (bf16[3,64,256]{2,1,0:T(8,128)(2,1)S(1)}, bf16[3,64,256]{2,1,0:T(8,128)(2,1)S(1)}, u32[]{:S(2)}, u32[]{:S(2)}) collective-permute-start(bf16[3,64,256]{2,1,0:T(8,128)(2,1)S(1)} %prepare.1), channel_id=1, source_target_pairs={{0,8},{1,9},{2,10},{3,11},{4,12},{5,13},{6,14},{7,15},{8,0},{9,1},... | collective-permute-start | bytes 294920 | tf_op jit(solution)/shard_map/ppermute | solution.py:185
  15.7 36.6 %all-to-all-start = ((bf16[8,256,256]{2,1,0:T(8,128)(2,1)}), bf16[8,256,256]{2,1,0:T(8,128)(2,1)S(1)}, u32[]{:S(2)}, u32[]{:S(2)}) async-start(bf16[8,256,256]{2,1,0:T(8,128)(2,1)} %bitcast.6), calls=%async_computation | async-start | bytes 2097152 | tf_op jit(solution)/shard_map/all_to_all | solution.py:217
  20.4 20.9 %collective-permute-start.3 = (bf16[4,3,64,256]{3,2,1,0:T(8,128)(2,1)S(1)}, bf16[4,3,64,256]{3,2,1,0:T(8,128)(2,1)S(1)}, u32[]{:S(2)}, u32[]{:S(2)}) collective-permute-start(bf16[4,3,64,256]{3,2,1,0:T(8,128)(2,1)S(1)} %pad_maximum_fusion.rest_3_), channel_id=1, source_target_pairs={{0,4},{1,5},{2,6},{3,7},{4,0},{5,1},{6,2},{7,3},{8,12},{9,13},{10,... | collective-permute-start | bytes 1179656 | tf_op jit(solution)/shard_map/ppermute | solution.py:185
  41.3 11.0 %collective-permute-start.4 = (bf16[4,3,64,256]{3,2,1,0:T(8,128)(2,1)S(1)}, bf16[4,3,64,256]{3,2,1,0:T(8,128)(2,1)S(1)}, u32[]{:S(2)}, u32[]{:S(2)}) collective-permute-start(bf16[4,3,64,256]{3,2,1,0:T(8,128)(2,1)S(1)} %collective-permute-done.3.rest_5_), channel_id=1, source_target_pairs={{0,2},{1,3},{2,0},{3,1},{4,6},{5,7},{6,4},{7,5},{8,10},{9,11},{10,... | collective-permute-start | bytes 1179656 | tf_op jit(solution)/shard_map/ppermute | solution.py:185
  42.8 14.7 %collective-permute-start.8 = (bf16[4,3,64,256]{3,2,1,0:T(8,128)(2,1)S(1)}, bf16[4,3,64,256]{3,2,1,0:T(8,128)(2,1)S(1)}, u32[]{:S(2)}, u32[]{:S(2)}) collective-permute-start(bf16[4,3,64,256]{3,2,1,0:T(8,128)(2,1)S(1)} %pad_maximum_fusion.rest_3_), channel_id=1, source_target_pairs={{0,1},{1,0},{2,3},{3,2},{4,5},{5,4},{6,7},{7,6},{8,9},{9,8},{10,11... | collective-permute-start | bytes 1179656 | tf_op jit(solution)/shard_map/ppermute | solution.py:185
  42.8 14.7 %collective-permute-start.7 = (bf16[4,3,64,256]{3,2,1,0:T(8,128)(2,1)S(1)}, bf16[4,3,64,256]{3,2,1,0:T(8,128)(2,1)S(1)}, u32[]{:S(2)}, u32[]{:S(2)}) collective-permute-start(bf16[4,3,64,256]{3,2,1,0:T(8,128)(2,1)S(1)} %pad_maximum_fusion.rest_3_), channel_id=1, source_target_pairs={{0,2},{1,3},{2,0},{3,1},{4,6},{5,7},{6,4},{7,5},{8,10},{9,11},{10,... | collective-permute-start | bytes 1179656 | tf_op jit(solution)/shard_map/ppermute | solution.py:185
  52.3 7.4 %collective-permute-start.6 = (bf16[4,256,256]{2,1,0:T(8,128)(2,1)S(1)}, bf16[4,256,256]{2,1,0:T(8,128)(2,1)S(1)}, u32[]{:S(2)}, u32[]{:S(2)}) collective-permute-start(bf16[4,256,256]{2,1,0:T(8,128)(2,1)S(1)} %get-tuple-element.53), channel_id=1, source_target_pairs={{0,1},{1,0},{2,3},{3,2},{4,5},{5,4},{6,7},{7,6},{8,9},{9,8},{10,11... | collective-permute-start | bytes 1572872 | tf_op jit(solution)/shard_map/ppermute | solution.py:185
  52.4 7.4 %collective-permute-start.5 = (bf16[4,256,256]{2,1,0:T(8,128)(2,1)S(1)}, bf16[4,256,256]{2,1,0:T(8,128)(2,1)S(1)}, u32[]{:S(2)}, u32[]{:S(2)}) collective-permute-start(bf16[4,256,256]{2,1,0:T(8,128)(2,1)S(1)} %get-tuple-element.54), channel_id=1, source_target_pairs={{0,1},{1,0},{2,3},{3,2},{4,5},{5,4},{6,7},{7,6},{8,9},{9,8},{10,11... | collective-permute-start | bytes 1572872 | tf_op jit(solution)/shard_map/ppermute | solution.py:185
  52.9 6.3 %collective-permute-start.10 = (bf16[4,3,64,256]{3,2,1,0:T(8,128)(2,1)S(1)}, bf16[4,3,64,256]{3,2,1,0:T(8,128)(2,1)S(1)}, u32[]{:S(2)}, u32[]{:S(2)}) collective-permute-start(bf16[4,3,64,256]{3,2,1,0:T(8,128)(2,1)S(1)} %collective-permute-done.3.rest_5_), channel_id=1, source_target_pairs={{0,1},{1,0},{2,3},{3,2},{4,5},{5,4},{6,7},{7,6},{8,9},{9,8},{10,11... | collective-permute-start | bytes 1179656 | tf_op jit(solution)/shard_map/ppermute | solution.py:185
  57.5 1.7 %collective-permute-start.9 = (bf16[4,3,64,256]{3,2,1,0:T(8,128)(2,1)S(1)}, bf16[4,3,64,256]{3,2,1,0:T(8,128)(2,1)S(1)}, u32[]{:S(2)}, u32[]{:S(2)}) collective-permute-start(bf16[4,3,64,256]{3,2,1,0:T(8,128)(2,1)S(1)} %collective-permute-done.7.rest_4_), channel_id=1, source_target_pairs={{0,1},{1,0},{2,3},{3,2},{4,5},{5,4},{6,7},{7,6},{8,9},{9,8},{10,11... | collective-permute-start | bytes 1179656 | tf_op jit(solution)/shard_map/ppermute | solution.py:185
  57.5 2.3 %collective-permute-start.11 = (bf16[4,3,64,256]{3,2,1,0:T(8,128)(2,1)S(1)}, bf16[4,3,64,256]{3,2,1,0:T(8,128)(2,1)S(1)}, u32[]{:S(2)}, u32[]{:S(2)}) collective-permute-start(bf16[4,3,64,256]{3,2,1,0:T(8,128)(2,1)S(1)} %collective-permute-done.4.rest_6_), channel_id=1, source_target_pairs={{0,1},{1,0},{2,3},{3,2},{4,5},{5,4},{6,7},{7,6},{8,9},{9,8},{10,11... | collective-permute-start | bytes 1179656 | tf_op jit(solution)/shard_map/ppermute | solution.py:185
  68.7 15.1 %collective-permute-start.14 = (bf16[4,2,64,256]{3,2,1,0:T(8,128)(2,1)S(1)}, bf16[4,2,64,256]{3,2,1,0:T(8,128)(2,1)S(1)}, u32[]{:S(2)}, u32[]{:S(2)}) collective-permute-start(bf16[4,2,64,256]{3,2,1,0:T(8,128)(2,1)S(1)} %get-tuple-element.37), channel_id=1, source_target_pairs={{0,16},{1,17},{2,18},{3,19},{4,20},{5,21},{6,22},{7,23},{8,24},{9,... | collective-permute-start | bytes 786440 | tf_op jit(solution)/shard_map/ppermute | solution.py:185
  71.6 18.1 %collective-permute-start.12 = (bf16[4,3,64,256]{3,2,1,0:T(8,128)(2,1)S(1)}, bf16[4,3,64,256]{3,2,1,0:T(8,128)(2,1)S(1)}, u32[]{:S(2)}, u32[]{:S(2)}) collective-permute-start(bf16[4,3,64,256]{3,2,1,0:T(8,128)(2,1)S(1)} %get-tuple-element.34), channel_id=1, source_target_pairs={{0,2},{1,3},{2,0},{3,1},{4,6},{5,7},{6,4},{7,5},{8,10},{9,11},{10,... | collective-permute-start | bytes 1179656 | tf_op jit(solution)/shard_map/ppermute | solution.py:185
  73.1 16.6 %collective-permute-start.13 = (bf16[4,3,64,256]{3,2,1,0:T(8,128)(2,1)S(1)}, bf16[4,3,64,256]{3,2,1,0:T(8,128)(2,1)S(1)}, u32[]{:S(2)}, u32[]{:S(2)}) collective-permute-start(bf16[4,3,64,256]{3,2,1,0:T(8,128)(2,1)S(1)} %get-tuple-element.35), channel_id=1, source_target_pairs={{0,4},{1,5},{2,6},{3,7},{4,0},{5,1},{6,2},{7,3},{8,12},{9,13},{10,... | collective-permute-start | bytes 1179656 | tf_op jit(solution)/shard_map/ppermute | solution.py:185
  83.9 12.4 %collective-permute-start.15 = (bf16[4,3,64,256]{3,2,1,0:T(8,128)(2,1)S(1)}, bf16[4,3,64,256]{3,2,1,0:T(8,128)(2,1)S(1)}, u32[]{:S(2)}, u32[]{:S(2)}) collective-permute-start(bf16[4,3,64,256]{3,2,1,0:T(8,128)(2,1)S(1)} %get-tuple-element.38), channel_id=1, source_target_pairs={{0,6},{1,7},{2,4},{3,5},{4,2},{5,3},{6,0},{7,1},{8,14},{9,15},{10,... | collective-permute-start | bytes 1179656 | tf_op jit(solution)/shard_map/ppermute | solution.py:185
  87.3 14.1 %collective-permute-start.16 = (bf16[4,2,64,256]{3,2,1,0:T(8,128)(2,1)S(1)}, bf16[4,2,64,256]{3,2,1,0:T(8,128)(2,1)S(1)}, u32[]{:S(2)}, u32[]{:S(2)}) collective-permute-start(bf16[4,2,64,256]{3,2,1,0:T(8,128)(2,1)S(1)} %get-tuple-element.40), channel_id=1, source_target_pairs={{0,8},{1,9},{2,10},{3,11},{4,12},{5,13},{6,14},{7,15},{8,0},{9,1},... | collective-permute-start | bytes 786440 | tf_op jit(solution)/shard_map/ppermute | solution.py:185
  87.3 17.3 %collective-permute-start.20 = (bf16[4,2,64,256]{3,2,1,0:T(8,128)(2,1)S(1)}, bf16[4,2,64,256]{3,2,1,0:T(8,128)(2,1)S(1)}, u32[]{:S(2)}, u32[]{:S(2)}) collective-permute-start(bf16[4,2,64,256]{3,2,1,0:T(8,128)(2,1)S(1)} %get-tuple-element.48), channel_id=1, source_target_pairs={{0,24},{1,25},{2,26},{3,27},{4,28},{5,29},{6,30},{7,31},{8,16},{9,... | collective-permute-start | bytes 786440 | tf_op jit(solution)/shard_map/ppermute | solution.py:185
  97.0 7.7 %collective-permute-start.17 = (bf16[3,64,256]{2,1,0:T(8,128)(2,1)S(1)}, bf16[3,64,256]{2,1,0:T(8,128)(2,1)S(1)}, u32[]{:S(2)}, u32[]{:S(2)}) collective-permute-start(bf16[3,64,256]{2,1,0:T(8,128)(2,1)S(1)} %get-tuple-element.41), channel_id=1, source_target_pairs={{0,8},{1,9},{2,10},{3,11},{4,12},{5,13},{6,14},{7,15},{8,0},{9,1},... | collective-permute-start | bytes 294920 | tf_op jit(solution)/shard_map/ppermute | solution.py:185
  97.3 11.2 %collective-permute-start.18 = (bf16[3,64,256]{2,1,0:T(8,128)(2,1)S(1)}, bf16[3,64,256]{2,1,0:T(8,128)(2,1)S(1)}, u32[]{:S(2)}, u32[]{:S(2)}) collective-permute-start(bf16[3,64,256]{2,1,0:T(8,128)(2,1)S(1)} %get-tuple-element.43), channel_id=1, source_target_pairs={{0,16},{1,17},{2,18},{3,19},{4,20},{5,21},{6,22},{7,23},{8,24},{9,... | collective-permute-start | bytes 294920 | tf_op jit(solution)/shard_map/ppermute | solution.py:185
  100.7 7.9 %collective-permute-start.19 = (bf16[3,64,256]{2,1,0:T(8,128)(2,1)S(1)}, bf16[3,64,256]{2,1,0:T(8,128)(2,1)S(1)}, u32[]{:S(2)}, u32[]{:S(2)}) collective-permute-start(bf16[3,64,256]{2,1,0:T(8,128)(2,1)S(1)} %get-tuple-element.44), channel_id=1, source_target_pairs={{0,24},{1,25},{2,26},{3,27},{4,28},{5,29},{6,30},{7,31},{8,16},{9,... | collective-permute-start | bytes 294920 | tf_op jit(solution)/shard_map/ppermute | solution.py:185
  104.6 7.6 %copy-start.1 = (f32[1,5,64,256]{3,2,1,0:T(8,128)S(1)}, f32[1,5,64,256]{3,2,1,0:T(8,128)}, u32[]{:S(2)}) copy-start(f32[1,5,64,256]{3,2,1,0:T(8,128)} %omega_ref.3) | copy-start | bytes 983044
  104.8 4.3 %collective-permute-start.21 = (bf16[2,64,256]{2,1,0:T(8,128)(2,1)S(1)}, bf16[2,64,256]{2,1,0:T(8,128)(2,1)S(1)}, u32[]{:S(2)}, u32[]{:S(2)}) collective-permute-start(bf16[2,64,256]{2,1,0:T(8,128)(2,1)S(1)} %get-tuple-element.50), channel_id=1, source_target_pairs={{0,2},{1,3},{2,0},{3,1},{4,6},{5,7},{6,4},{7,5},{8,10},{9,11},{10,... | collective-permute-start | bytes 196616 | tf_op jit(solution)/shard_map/ppermute | solution.py:185
  105.3 4.3 %collective-permute-start.22 = (bf16[2,64,256]{2,1,0:T(8,128)(2,1)S(1)}, bf16[2,64,256]{2,1,0:T(8,128)(2,1)S(1)}, u32[]{:S(2)}, u32[]{:S(2)}) collective-permute-start(bf16[2,64,256]{2,1,0:T(8,128)(2,1)S(1)} %get-tuple-element.51), channel_id=1, source_target_pairs={{0,4},{1,5},{2,6},{3,7},{4,0},{5,1},{6,2},{7,3},{8,12},{9,13},{10,... | collective-permute-start | bytes 196616 | tf_op jit(solution)/shard_map/ppermute | solution.py:185
  107.1 5.2 %collective-permute-start.23 = (bf16[2,64,256]{2,1,0:T(8,128)(2,1)S(1)}, bf16[2,64,256]{2,1,0:T(8,128)(2,1)S(1)}, u32[]{:S(2)}, u32[]{:S(2)}) collective-permute-start(bf16[2,64,256]{2,1,0:T(8,128)(2,1)S(1)} %get-tuple-element.52), channel_id=1, source_target_pairs={{0,6},{1,7},{2,4},{3,5},{4,2},{5,3},{6,0},{7,1},{8,14},{9,15},{10,... | collective-permute-start | bytes 196616 | tf_op jit(solution)/shard_map/ppermute | solution.py:185

commit v4 on v3

--- a/solution.py
+++ b/solution.py
@@ -10,8 +10,8 @@
 STEP_SIZE = 0.5
 PENALTY = 0.1
 LOW = 2
-LINE_FIRST = (3, 4)
-PLANE_FIRST = (0, 1, 2)
+LINE_FIRST = (4,)
+PLANE_FIRST = (0, 1, 2, 3)
 F32 = jnp.float32
 BF16 = jnp.bfloat16
 
@@ -37,24 +37,28 @@
         out_ref[k] = omega_ref[0, slots[k]].astype(BF16)
 
 
-def product_kernel(teams, replicas, tile_rows, place_ref, pattern_ref, *rest):
+NN = (((1,), (0,)), ((), ()))
+NT = (((1,), (1,)), ((), ()))
+
+
+def block(data_refs, c):
+    return jnp.concatenate([ref[c] for ref in data_refs], axis=0)
+
+
+def mix_kernel(teams, replicas, tile_rows, place_ref, pattern_ref, *rest):
     chips = replicas // 2
     planes = LOW * chips
     depth = teams // LOW
-    own_ref, low_ref, high_ref, *rest = rest
+    data_refs, rest = rest[:3], rest[3:]
     weight_refs, rest = rest[: 2 * planes], rest[2 * planes :]
-    plane_outs, line_outs, rest = rest[:planes], rest[planes : planes + depth], rest[planes + depth :]
-    data_ref, omega_ref, mixed_ref, flip_ref, left_ref, data_sems, omega_sems = rest
+    mixed_ref, left_ref, omega_ref, flip_ref, sems = rest
     team, replica = place_ref[0], place_ref[1]
     core, chip = lax.rem(replica, 2), lax.div(replica, 2)
     high, low = lax.div(team, LOW), lax.rem(team, LOW)
     offsets, _ = stored_offsets(pattern_ref, team, teams)
-    times, width = data_ref.shape[1] // 2, data_ref.shape[2]
+    times = mixed_ref.shape[1]
 
     copies = []
-    for n, (source, first, half) in enumerate([(own_ref, 0, 0), (low_ref, 0, 1), (high_ref, teams // 2, 1)]):
-        target = data_ref.at[pl.ds(first, source.shape[0]), pl.ds(half * times, times)]
-        copies.append(pltpu.make_async_copy(source, target, data_sems.at[n]))
     for half in range(2):
         for mx in range(LOW):
             for my in range(chips):
@@ -67,62 +71,77 @@
                         pltpu.make_async_copy(
                             weight_refs[half * planes + plane].at[mz],
                             target,
-                            omega_sems.at[(half * planes + plane) * depth + mz],
+                            sems.at[(half * planes + plane) * depth + mz],
                         )
                     )
     for copy in copies:
         copy.start()
-    for copy in copies:
-        copy.wait()
-
-    nn = (((1,), (0,)), ((), ()))
-    nt = (((1,), (1,)), ((), ()))
+
+    def keep(i, first, array):
+        flip_ref[...] = array.T
+        for m in range(chips):
+            row = (2 * (chip ^ m) + core) * tile_rows
+            left_ref[i, m * tile_rows : (m + 1) * tile_rows, first : first + times] = flip_ref[
+                pl.ds(pl.multiple_of(row, tile_rows), tile_rows)
+            ]
+
+    def turn(i, carry):
+        keep(i, times, block(data_refs, i))
+        return carry
 
     def mix(i, carry):
         total = None
         for k, offset in enumerate(offsets):
             c = lax.rem(i + offset, teams)
             if k < 3:
-                term = lax.dot_general(data_ref[c], omega_ref[i, k], nt, preferred_element_type=F32)
+                term = lax.dot_general(block(data_refs, c), omega_ref[i, k], NT, preferred_element_type=F32)
             else:
-                term = lax.dot_general(data_ref[c], omega_ref[c, 5 - k], nn, preferred_element_type=F32)
+                term = lax.dot_general(block(data_refs, c), omega_ref[c, 5 - k], NN, preferred_element_type=F32)
             total = term if total is None else total + term
         mixed = total.astype(BF16)
         mixed_ref[i] = mixed
-        flip_ref[:, : 2 * times] = mixed.T
-        flip_ref[:, 2 * times :] = data_ref[i].T
-        for m in range(chips):
-            row = (2 * (chip ^ m) + core) * tile_rows
-            left_ref[i, m * tile_rows : (m + 1) * tile_rows] = flip_ref[
-                pl.ds(pl.multiple_of(row, tile_rows), tile_rows)
-            ]
+        keep(i, 0, mixed)
         return carry
 
     unroll = teams <= 8
+    lax.fori_loop(0, teams, turn, 0, unroll=unroll)
+    for copy in copies:
+        copy.wait()
     lax.fori_loop(0, teams, mix, 0, unroll=unroll)
+
+
+def product_kernel(teams, chips, far, place_ref, pattern_ref, *rest):
+    depth = teams // LOW
+    data_refs, mixed_ref, left_ref, outs = rest[:3], rest[3], rest[4], rest[5:]
+    plane_outs, line_outs = outs[: chips * len(far)], outs[chips * len(far) :]
+    team = place_ref[0]
+    high, low = lax.div(team, LOW), lax.rem(team, LOW)
+    offsets, _ = stored_offsets(pattern_ref, team, teams)
+    tile_rows = left_ref.shape[1] // chips
 
     def part(i, k):
         c = lax.rem(i + offsets[k], teams)
-        right = jnp.concatenate([data_ref[c], mixed_ref[c]], axis=0)
-        product = lax.dot_general(left_ref[i], right, nn, preferred_element_type=F32).astype(BF16)
+        right = jnp.concatenate([block(data_refs, c), mixed_ref[c]], axis=0)
+        product = lax.dot_general(left_ref[i], right, NN, preferred_element_type=F32).astype(BF16)
         return [product[m * tile_rows : (m + 1) * tile_rows] for m in range(chips)]
 
-    for mx in range(LOW):
-        for mz in range(depth):
-            i = (high ^ mz) * LOW + (low ^ mx)
-            for n, k in enumerate(LINE_FIRST):
-                for m, rows in enumerate(part(i, k)):
-                    line_outs[mz][mx * chips + m, n] = rows
-    for mx in range(LOW):
+    if line_outs:
+        for mx in range(LOW):
+            for mz in range(depth):
+                i = (high ^ mz) * LOW + (low ^ mx)
+                for n, k in enumerate(LINE_FIRST):
+                    for m, rows in enumerate(part(i, k)):
+                        line_outs[mz][mx * chips + m, n] = rows
+    for index, mx in enumerate(far):
 
         def outer(z, carry):
             i = z * LOW + (low ^ mx)
             for n, k in enumerate(PLANE_FIRST):
                 for m, rows in enumerate(part(i, k)):
-                    plane_outs[mx * chips + m][z, n] = rows
+                    plane_outs[index * chips + m][z, n] = rows
             return carry
 
-        lax.fori_loop(0, depth, outer, 0, unroll=unroll)
+        lax.fori_loop(0, depth, outer, 0, unroll=teams <= 8)
 
 
 def line_sum_kernel(planes, *rest):
@@ -188,8 +207,8 @@
     count = teams // LOW
     planes = LOW * chips
     count = teams // LOW
-    small = pltpu.CompilerParams(vmem_limit_bytes=(8 if teams <= 8 else 48) * 2**20)
-    large = pltpu.CompilerParams(vmem_limit_bytes=(14 if teams <= 8 else 56) * 2**20)
+    small = pltpu.CompilerParams(vmem_limit_bytes=(6 if teams <= 8 else 24) * 2**20)
+    large = pltpu.CompilerParams(vmem_limit_bytes=(8 if teams <= 8 else 32) * 2**20)
 
     def across_plane(arrays):
         return [
@@ -212,36 +231,55 @@
 
     line = jnp.stack(along_line([upper] * count))
     line, signals = lax.optimization_barrier((line, signals))
-    rows = [line, swap(line, 1, 0)]
-    weights = [swap(row, 0, 2 * my) if my else row for row in rows for my in range(chips)]
+    weights = across_plane([line] * planes)
     own = lax.all_to_all(signals.reshape(teams, times, width), "blk", 0, 0)
-    weights[-1], own = lax.optimization_barrier((weights[-1], own))
-    other = [swap(part, 0, 1) for part in jnp.split(own, 2)]
+    data = [own] + [swap(part, 0, 1) for part in jnp.split(own, 2, axis=1)]
     weights += [swap(array, 0, 1) for array in weights]
 
-    partial = pl.pallas_call(
-        functools.partial(product_kernel, teams, replicas, tile_rows),
-        out_shape=[jax.ShapeDtypeStruct((count, len(PLANE_FIRST), tile_rows, width), BF16)] * planes
-        + [jax.ShapeDtypeStruct((planes, len(LINE_FIRST), tile_rows, width), BF16)] * count,
-        in_specs=[SMEM, SMEM] + [ANY] * (3 + 2 * planes),
-        out_specs=[VMEM] * (planes + count),
+    mixed, left = pl.pallas_call(
+        functools.partial(mix_kernel, teams, replicas, tile_rows),
+        out_shape=[
+            jax.ShapeDtypeStruct((teams, 2 * times, width), BF16),
+            jax.ShapeDtypeStruct((teams, chips * tile_rows, 4 * times), BF16),
+        ],
+        in_specs=[SMEM, SMEM] + [VMEM] * 3 + [ANY] * (2 * planes),
+        out_specs=[VMEM, VMEM],
         scratch_shapes=[
-            pltpu.VMEM((teams, 2 * times, width), BF16),
             pltpu.VMEM((teams, 3, width, width), BF16),
-            pltpu.VMEM((teams, 2 * times, width), BF16),
-            pltpu.VMEM((width, 4 * times), BF16),
-            pltpu.VMEM((teams, chips * tile_rows, 4 * times), BF16),
-            pltpu.SemaphoreType.DMA((3,)),
+            pltpu.VMEM((width, 2 * times), BF16),
             pltpu.SemaphoreType.DMA((2 * planes * count,)),
         ],
         compiler_params=large,
-        name="products",
-    )(place, pattern, own, *other, *weights)
-
-    partial = list(partial)
-    line_parts = along_line(partial[planes:])
-    partial[planes - 1], line_parts[2] = lax.optimization_barrier((partial[planes - 1], line_parts[2]))
-    plane_parts = across_plane(partial[:planes])
+        name="mix",
+    )(place, pattern, *data, *weights)
+
+    def products(far, lines):
+        return pl.pallas_call(
+            functools.partial(product_kernel, teams, chips, far),
+            out_shape=[jax.ShapeDtypeStruct((count, len(PLANE_FIRST), tile_rows, width), BF16)] * (chips * len(far))
+            + [jax.ShapeDtypeStruct((planes, len(LINE_FIRST), tile_rows, width), BF16)] * lines,
+            in_specs=[SMEM, SMEM] + [VMEM] * 5,
+            out_specs=[VMEM] * (chips * len(far) + lines),
+            compiler_params=small,
+            name="products",
+        )(place, pattern, *data, mixed, left)
+
+    far_parts = products((1,), 0)
+    near_parts = products((0,), count)
+    plane_parts = across_plane(list(near_parts[:chips]) + list(far_parts))
+    line_parts = along_line(near_parts[chips:])
+    line_sums = pl.pallas_call(
+        functools.partial(line_sum_kernel, planes),
+        out_shape=[
+            jax.ShapeDtypeStruct((len(LINE_FIRST), tile_rows, width), BF16 if m else F32) for m in range(planes)
+        ],
+        in_specs=[VMEM] * count,
+        out_specs=[VMEM] * planes,
+        compiler_params=small,
+        name="line_sum",
+    )(*line_parts)
+    line_sums = across_plane(line_sums)
+    plane_parts, line_sums = lax.optimization_barrier((plane_parts, line_sums))
     plane_sums = pl.pallas_call(
         functools.partial(plane_sum_kernel, teams),
         out_shape=[
@@ -253,17 +291,6 @@
         name="plane_sum",
     )(place, *plane_parts)
     plane_sums = along_line(plane_sums)
-    line_parts[1], plane_sums[1] = lax.optimization_barrier((line_parts[1], plane_sums[1]))
-    line_sums = pl.pallas_call(
-        functools.partial(line_sum_kernel, planes),
-        out_shape=[
-            jax.ShapeDtypeStruct((len(LINE_FIRST), tile_rows, width), BF16 if m else F32) for m in range(planes)
-        ],
-        in_specs=[VMEM] * count,
-        out_specs=[VMEM] * planes,
-        compiler_params=small,
-        name="line_sum",
-    )(*line_parts)
 
     scale = 1.0 / (2.0 * signals.shape[0] * replicas)
     return pl.pallas_call(
@@ -273,7 +300,7 @@
         out_specs=VMEM,
         compiler_params=small,
         name="update",
-    )(place, pattern, omega, *plane_sums, *across_plane(line_sums))
+    )(place, pattern, omega, *plane_sums, *line_sums)
 
 
 def solution(mesh):

time: 114 us -> 111 us (0.974)
  starting transfers between devices: 36.5 us -> 33.1 us
  Pallas kernels: 11.9 us -> 13.2 us
  waiting for transfers between devices: 63.6 us -> 62.4 us
    ppermute x24, waiting for transfers between devices: 63.6 us -> 41.1 us  [swap(): return lax.ppermute(array, ('blk', 'rep'), route)]
    all_to_all x1, waiting for transfers between devices: 0.01 us -> 21.3 us  [per_device(): own = lax.all_to_all(signals.reshape(teams, times, width), 'blk', 0, 0)]
    ppermute x24, starting transfers between devices: 31.7 us -> 28.4 us  [swap(): return lax.ppermute(array, ('blk', 'rep'), route)]
    pallas_call x1 -> x3, Pallas kernels: 8.95 us -> 10.3 us  [the longest x1 6.14 us: per_device(): pl.pallas_call(functools.partial(mix_kernel, teams, replicas, tile_rows),...]
  transfers between devices with their start and end apart: 25 -> 25, of which waited for: 14 -> 13; matrix products, arithmetic and copies ran while one was open for 0% -> 0% of each run, Pallas kernels for 1% -> 2%
where the time goes in v4:
time: 111 us
  waiting for transfers between devices  62.4 us (56%)
  starting transfers between devices  33.1 us (30%)
  Pallas kernels  13.2 us (12%)
  local copies, waits for them, and re-layouts  1.73 us (2%)
    ppermute x24, waiting for transfers between devices, swap(): return lax.ppermute(array, ('blk', 'rep'), route)  41.1 us
    ppermute x24, starting transfers between devices, swap(): return lax.ppermute(array, ('blk', 'rep'), route)  28.4 us
    all_to_all x1, waiting for transfers between devices, per_device(): own = lax.all_to_all(signals.reshape(teams, times, width), 'blk', 0, 0)  21.3 us
    pallas_call x1, Pallas kernels, per_device(): pl.pallas_call(functools.partial(mix_kernel, teams, replicas, tile_rows),...  6.14 us
    all_to_all x1, starting transfers between devices, per_device(): own = lax.all_to_all(signals.reshape(teams, times, width), 'blk', 0, 0)  4.73 us
    pallas_call x2, Pallas kernels, products(): pl.pallas_call(functools.partial(product_kernel, teams, chips, far), out_...  4.19 us
  transfers between devices with their start and end apart: 25, of which 13 were waited for; matrix products, arithmetic and copies ran while one was open for 0% of the time, Pallas kernels for 2%

profile of v4, /device:TPU:0, one launch (start us, length us, event | category | flops | bytes accessed | tf_op | source)
XLA Modules:
  0.0 110.7 jit_solution(7959827633813222950)
XLA Ops:
  0.0 0.1 pad_add_fusion.place_ref
  0.1 1.0 copy-done
  1.1 0.7 copy-done.2
  1.7 0.6 prepare.1
  2.3 5.1 %collective-permute-start.2 = (bf16[3,64,256]{2,1,0:T(8,128)(2,1)S(1)}, bf16[3,64,256]{2,1,0:T(8,128)(2,1)S(1)}, u32[]{:S(2)}, u32[]{:S(2)}) collective-permute-start(bf16[3,64,256]{2,1,0:T(8,128)(2,1)S(1)} %prepare.1), channel_id=1, source_target_pairs={{0,24},{1,25},{2,26},{3,27},{4,28},{5,29},{6,30},{7,31},{8,16},{9,... | collective-permute-start | bytes 294920 | tf_op jit(solution)/shard_map/ppermute | solution.py:204
  7.4 0.6 collective-permute-start
  8.1 3.1 %collective-permute-done.2 = bf16[3,64,256]{2,1,0:T(8,128)(2,1)S(1)} collective-permute-done((bf16[3,64,256]{2,1,0:T(8,128)(2,1)S(1)}, bf16[3,64,256]{2,1,0:T(8,128)(2,1)S(1)}, u32[]{:S(2)}, u32[]{:S(2)}) %collective-permute-start.2) | collective-permute-done | bytes 98336 | tf_op jit(solution)/shard_map/ppermute | solution.py:204
  11.1 4.6 %collective-permute-done.1 = bf16[3,64,256]{2,1,0:T(8,128)(2,1)S(1)} collective-permute-done((bf16[3,64,256]{2,1,0:T(8,128)(2,1)S(1)}, bf16[3,64,256]{2,1,0:T(8,128)(2,1)S(1)}, u32[]{:S(2)}, u32[]{:S(2)}) %collective-permute-start.1) | collective-permute-done | bytes 98336 | tf_op jit(solution)/shard_map/ppermute | solution.py:204
  15.7 0.1 pad_maximum_fusion.rest_3_
  15.7 0.0 copy-start.3
  15.7 4.7 %all-to-all-start = ((bf16[8,256,256]{2,1,0:T(8,128)(2,1)}), bf16[8,256,256]{2,1,0:T(8,128)(2,1)S(1)}, u32[]{:S(2)}, u32[]{:S(2)}) async-start(bf16[8,256,256]{2,1,0:T(8,128)(2,1)} %bitcast.8), calls=%async_computation | async-start | bytes 2097152 | tf_op jit(solution)/shard_map/all_to_all | solution.py:235
  20.5 3.0 %collective-permute-start.7 = (bf16[4,3,64,256]{3,2,1,0:T(8,128)(2,1)S(1)}, bf16[4,3,64,256]{3,2,1,0:T(8,128)(2,1)S(1)}, u32[]{:S(2)}, u32[]{:S(2)}) collective-permute-start(bf16[4,3,64,256]{3,2,1,0:T(8,128)(2,1)S(1)} %pad_maximum_fusion.rest_3_), channel_id=1, source_target_pairs={{0,6},{1,7},{2,4},{3,5},{4,2},{5,3},{6,0},{7,1},{8,14},{9,15},{10,... | collective-permute-start | bytes 1179656 | tf_op jit(solution)/shard_map/ppermute | solution.py:204
  23.5 0.1 collective-permute-start.6
  23.5 0.6 collective-permute-start.5
  24.1 21.3 %all-to-all-done.rest_0_ = bf16[8,256,256]{2,1,0:T(8,128)(2,1)S(1)} async-done(((bf16[8,256,256]{2,1,0:T(8,128)(2,1)}), bf16[8,256,256]{2,1,0:T(8,128)(2,1)S(1)}, u32[]{:S(2)}, u32[]{:S(2)}) %all-to-all-start) | async-done | bytes 1048608 | tf_op jit(solution)/shard_map/all_to_all | solution.py:235
  45.3 0.1 fusion
  45.4 0.1 collective-permute-start.4
  45.5 0.5 collective-permute-start.3
  46.0 0.1 collective-permute-start.11
  46.1 4.2 %collective-permute-done.6.rest_5_ = bf16[4,3,64,256]{3,2,1,0:T(8,128)(2,1)S(1)} collective-permute-done((bf16[4,3,64,256]{3,2,1,0:T(8,128)(2,1)S(1)}, bf16[4,3,64,256]{3,2,1,0:T(8,128)(2,1)S(1)}, u32[]{:S(2)}, u32[]{:S(2)}) %collective-permute-start.6) | collective-permute-done | bytes 393248 | tf_op jit(solution)/shard_map/ppermute | solution.py:204
  50.3 0.5 collective-permute-start.9
  50.8 1.2 %collective-permute-done.10.rest_9_ = bf16[4,3,64,256]{3,2,1,0:T(8,128)(2,1)S(1)} collective-permute-done((bf16[4,3,64,256]{3,2,1,0:T(8,128)(2,1)S(1)}, bf16[4,3,64,256]{3,2,1,0:T(8,128)(2,1)S(1)}, u32[]{:S(2)}, u32[]{:S(2)}) %collective-permute-start.10) | collective-permute-done | bytes 393248 | tf_op jit(solution)/shard_map/ppermute | solution.py:204
  52.0 0.6 collective-permute-done.9.rest_8_
  52.6 6.1 %mix.1 = (bf16[8,512,256]{2,1,0:T(8,128)(2,1)S(1)}, bf16[8,128,1024]{2,1,0:T(8,128)(2,1)S(1)}) custom-call(s32[2]{0:T(128)S(1)} %pad_add_fusion.place_ref, s32[1,5]{1,0:T(1,128)S(1)} %copy-done.3, bf16[8,256,256]{2,1,0:T(8,128)(2,1)S(1)} %all-to-all-done.rest_0_, bf16[8,128,256]{2,1,0:T(8,128)(2,1)S(1)} %collective-permute-done.3.rest_1_, ...), custom_call_target="tpu_custom_call" | custom-call | tf_op jit(solution)/shard_map/mix/pallas_call | solution.py:239
  58.7 1.8 %products.3 = (bf16[4,4,64,256]{3,2,1,0:T(8,128)(2,1)S(1)}, bf16[4,4,64,256]{3,2,1,0:T(8,128)(2,1)S(1)}) custom-call(s32[2]{0:T(128)S(1)} %pad_add_fusion.place_ref, s32[1,5]{1,0:T(1,128)S(1)} %copy-done.3, bf16[8,256,256]{2,1,0:T(8,128)(2,1)S(1)} %all-to-all-done.rest_0_, bf16[8,128,256]{2,1,0:T(8,128)(2,1)S(1)} %collective-permute-done.3.rest_1_, ...), custom_call_target="tpu_custom_call" | custom-call | tf_op jit(solution)/shard_map/products/pallas_call | solution.py:257
  60.6 0.1 collective-permute-start.13
  60.6 3.0 %collective-permute-start.14 = (bf16[4,4,64,256]{3,2,1,0:T(8,128)(2,1)S(1)}, bf16[4,4,64,256]{3,2,1,0:T(8,128)(2,1)S(1)}, u32[]{:S(2)}, u32[]{:S(2)}) collective-permute-start(bf16[4,4,64,256]{3,2,1,0:T(8,128)(2,1)S(1)} %get-tuple-element.40), channel_id=1, source_target_pairs={{0,6},{1,7},{2,4},{3,5},{4,2},{5,3},{6,0},{7,1},{8,14},{9,15},{10,... | collective-permute-start | bytes 1572872 | tf_op jit(solution)/shard_map/ppermute | solution.py:204
  63.6 2.4 %products.2 = (bf16[4,4,64,256]{3,2,1,0:T(8,128)(2,1)S(1)}, bf16[4,4,64,256]{3,2,1,0:T(8,128)(2,1)S(1)}, bf16[4,1,64,256]{3,2,1,0:T(8,128)(2,1)S(1)}, bf16[4,1,6...) custom-call(s32[2]{0:T(128)S(1)} %pad_add_fusion.place_ref, ...), custom_call_target="tpu_custom_call" | custom-call | tf_op jit(solution)/shard_map/products/pallas_call | solution.py:257
  66.0 0.0 copy-start.1
  66.0 0.6 collective-permute-start.12
  66.6 1.6 %collective-permute-start.15 = (bf16[4,1,64,256]{3,2,1,0:T(8,128)(2,1)S(1)}, bf16[4,1,64,256]{3,2,1,0:T(8,128)(2,1)S(1)}, u32[]{:S(2)}, u32[]{:S(2)}) collective-permute-start(bf16[4,1,64,256]{3,2,1,0:T(8,128)(2,1)S(1)} %get-tuple-element.42), channel_id=1, source_target_pairs={{0,8},{1,9},{2,10},{3,11},{4,12},{5,13},{6,14},{7,15},{8,0},{9,1},... | collective-permute-start | bytes 393224 | tf_op jit(solution)/shard_map/ppermute | solution.py:204
  68.2 2.7 %collective-permute-start.16 = (bf16[4,1,64,256]{3,2,1,0:T(8,128)(2,1)S(1)}, bf16[4,1,64,256]{3,2,1,0:T(8,128)(2,1)S(1)}, u32[]{:S(2)}, u32[]{:S(2)}) collective-permute-start(bf16[4,1,64,256]{3,2,1,0:T(8,128)(2,1)S(1)} %get-tuple-element.43), channel_id=1, source_target_pairs={{0,16},{1,17},{2,18},{3,19},{4,20},{5,21},{6,22},{7,23},{8,24},{9,... | collective-permute-start | bytes 393224 | tf_op jit(solution)/shard_map/ppermute | solution.py:204
  70.9 2.4 %collective-permute-done.15.rest_1_ = bf16[4,1,64,256]{3,2,1,0:T(8,128)(2,1)S(1)} collective-permute-done((bf16[4,1,64,256]{3,2,1,0:T(8,128)(2,1)S(1)}, bf16[4,1,64,256]{3,2,1,0:T(8,128)(2,1)S(1)}, u32[]{:S(2)}, u32[]{:S(2)}) %collective-permute-start.15) | collective-permute-done | bytes 131104 | tf_op jit(solution)/shard_map/ppermute | solution.py:204
  73.2 3.6 %collective-permute-start.17 = (bf16[4,1,64,256]{3,2,1,0:T(8,128)(2,1)S(1)}, bf16[4,1,64,256]{3,2,1,0:T(8,128)(2,1)S(1)}, u32[]{:S(2)}, u32[]{:S(2)}) collective-permute-start(bf16[4,1,64,256]{3,2,1,0:T(8,128)(2,1)S(1)} %get-tuple-element.44), channel_id=1, source_target_pairs={{0,24},{1,25},{2,26},{3,27},{4,28},{5,29},{6,30},{7,31},{8,16},{9,... | collective-permute-start | bytes 393224 | tf_op jit(solution)/shard_map/ppermute | solution.py:204
  76.8 1.5 %collective-permute-done.16.rest_2_ = bf16[4,1,64,256]{3,2,1,0:T(8,128)(2,1)S(1)} collective-permute-done((bf16[4,1,64,256]{3,2,1,0:T(8,128)(2,1)S(1)}, bf16[4,1,64,256]{3,2,1,0:T(8,128)(2,1)S(1)}, u32[]{:S(2)}, u32[]{:S(2)}) %collective-permute-start.16) | collective-permute-done | bytes 131104 | tf_op jit(solution)/shard_map/ppermute | solution.py:204
  78.3 1.8 %collective-permute-done.17.rest_3_ = bf16[4,1,64,256]{3,2,1,0:T(8,128)(2,1)S(1)} collective-permute-done((bf16[4,1,64,256]{3,2,1,0:T(8,128)(2,1)S(1)}, bf16[4,1,64,256]{3,2,1,0:T(8,128)(2,1)S(1)}, u32[]{:S(2)}, u32[]{:S(2)}) %collective-permute-start.17) | collective-permute-done | bytes 131104 | tf_op jit(solution)/shard_map/ppermute | solution.py:204
  80.1 0.1 line_sum.1
  80.1 1.7 %collective-permute-start.18 = (bf16[1,64,256]{2,1,0:T(8,128)(2,1)S(1)}, bf16[1,64,256]{2,1,0:T(8,128)(2,1)S(1)}, u32[]{:S(2)}, u32[]{:S(2)}) collective-permute-start(bf16[1,64,256]{2,1,0:T(8,128)(2,1)S(1)} %get-tuple-element.46), channel_id=1, source_target_pairs={{0,2},{1,3},{2,0},{3,1},{4,6},{5,7},{6,4},{7,5},{8,10},{9,11},{10,... | collective-permute-start | bytes 98312 | tf_op jit(solution)/shard_map/ppermute | solution.py:204
  81.8 9.6 %collective-permute-done.18.rest_5_ = bf16[1,64,256]{2,1,0:T(8,128)(2,1)S(1)} collective-permute-done((bf16[1,64,256]{2,1,0:T(8,128)(2,1)S(1)}, bf16[1,64,256]{2,1,0:T(8,128)(2,1)S(1)}, u32[]{:S(2)}, u32[]{:S(2)}) %collective-permute-start.18) | collective-permute-done | bytes 32800 | tf_op jit(solution)/shard_map/ppermute | solution.py:204
  91.4 0.3 collective-permute-start.20
  91.7 4.5 %collective-permute-done.20.rest_7_ = bf16[1,64,256]{2,1,0:T(8,128)(2,1)S(1)} collective-permute-done((bf16[1,64,256]{2,1,0:T(8,128)(2,1)S(1)}, bf16[1,64,256]{2,1,0:T(8,128)(2,1)S(1)}, u32[]{:S(2)}, u32[]{:S(2)}) %collective-permute-start.20) | collective-permute-done | bytes 32800 | tf_op jit(solution)/shard_map/ppermute | solution.py:204
  96.2 0.8 plane_sum.1
  97.1 1.7 %collective-permute-start.21 = (bf16[4,64,256]{2,1,0:T(8,128)(2,1)S(1)}, bf16[4,64,256]{2,1,0:T(8,128)(2,1)S(1)}, u32[]{:S(2)}, u32[]{:S(2)}) collective-permute-start(bf16[4,64,256]{2,1,0:T(8,128)(2,1)S(1)} %get-tuple-element.54), channel_id=1, source_target_pairs={{0,8},{1,9},{2,10},{3,11},{4,12},{5,13},{6,14},{7,15},{8,0},{9,1},... | collective-permute-start | bytes 393224 | tf_op jit(solution)/shard_map/ppermute | solution.py:204
  98.7 2.5 %collective-permute-start.22 = (bf16[4,64,256]{2,1,0:T(8,128)(2,1)S(1)}, bf16[4,64,256]{2,1,0:T(8,128)(2,1)S(1)}, u32[]{:S(2)}, u32[]{:S(2)}) collective-permute-start(bf16[4,64,256]{2,1,0:T(8,128)(2,1)S(1)} %get-tuple-element.55), channel_id=1, source_target_pairs={{0,16},{1,17},{2,18},{3,19},{4,20},{5,21},{6,22},{7,23},{8,24},{9,... | collective-permute-start | bytes 393224 | tf_op jit(solution)/shard_map/ppermute | solution.py:204
  101.2 0.3 collective-permute-start.23
  101.5 1.1 %collective-permute-done.21.rest_1_ = bf16[4,64,256]{2,1,0:T(8,128)(2,1)S(1)} collective-permute-done((bf16[4,64,256]{2,1,0:T(8,128)(2,1)S(1)}, bf16[4,64,256]{2,1,0:T(8,128)(2,1)S(1)}, u32[]{:S(2)}, u32[]{:S(2)}) %collective-permute-start.21) | collective-permute-done | bytes 131104 | tf_op jit(solution)/shard_map/ppermute | solution.py:204
  102.6 6.7 %collective-permute-done.22.rest_2_ = bf16[4,64,256]{2,1,0:T(8,128)(2,1)S(1)} collective-permute-done((bf16[4,64,256]{2,1,0:T(8,128)(2,1)S(1)}, bf16[4,64,256]{2,1,0:T(8,128)(2,1)S(1)}, u32[]{:S(2)}, u32[]{:S(2)}) %collective-permute-start.22) | collective-permute-done | bytes 131104 | tf_op jit(solution)/shard_map/ppermute | solution.py:204
  109.3 1.5 %update.1 = f32[1,5,64,256]{3,2,1,0:T(8,128)} custom-call(s32[2]{0:T(128)S(1)} %pad_add_fusion.place_ref, s32[1,5]{1,0:T(1,128)S(1)} %copy-done.3, f32[1,5,64,256]{3,2,1,0:T(8,128)S(1)} %copy-done.1, f32[4,64,256]{2,1,0:T(8,128)S(1)} %get-tuple-element.53.rest_0_, bf16[4,64,256]{2,1,0:T(8,128)(2,1)S(1)} %collective-permute-done.21.rest_1_, ...), custom_call_target="tpu_custom_call" | custom-call | tf_op jit(solution)/shard_map/update/pallas_call | solution.py:296
  (20 shorter events, 0.0 us)
Async XLA Ops:
  0.1 1.0 copy-start
  1.0 0.7 copy-start.2
  2.3 8.8 %collective-permute-start.2 = (bf16[3,64,256]{2,1,0:T(8,128)(2,1)S(1)}, bf16[3,64,256]{2,1,0:T(8,128)(2,1)S(1)}, u32[]{:S(2)}, u32[]{:S(2)}) collective-permute-start(bf16[3,64,256]{2,1,0:T(8,128)(2,1)S(1)} %prepare.1), channel_id=1, source_target_pairs={{0,24},{1,25},{2,26},{3,27},{4,28},{5,29},{6,30},{7,31},{8,16},{9,... | collective-permute-start | bytes 294920 | tf_op jit(solution)/shard_map/ppermute | solution.py:204
  7.4 8.3 %collective-permute-start.1 = (bf16[3,64,256]{2,1,0:T(8,128)(2,1)S(1)}, bf16[3,64,256]{2,1,0:T(8,128)(2,1)S(1)}, u32[]{:S(2)}, u32[]{:S(2)}) collective-permute-start(bf16[3,64,256]{2,1,0:T(8,128)(2,1)S(1)} %prepare.1), channel_id=1, source_target_pairs={{0,16},{1,17},{2,18},{3,19},{4,20},{5,21},{6,22},{7,23},{8,24},{9,... | collective-permute-start | bytes 294920 | tf_op jit(solution)/shard_map/ppermute | solution.py:204
  7.4 8.3 %collective-permute-start = (bf16[3,64,256]{2,1,0:T(8,128)(2,1)S(1)}, bf16[3,64,256]{2,1,0:T(8,128)(2,1)S(1)}, u32[]{:S(2)}, u32[]{:S(2)}) collective-permute-start(bf16[3,64,256]{2,1,0:T(8,128)(2,1)S(1)} %prepare.1), channel_id=1, source_target_pairs={{0,8},{1,9},{2,10},{3,11},{4,12},{5,13},{6,14},{7,15},{8,0},{9,1},... | collective-permute-start | bytes 294920 | tf_op jit(solution)/shard_map/ppermute | solution.py:204
  15.7 36.9 %copy-start.3 = (s32[1,5]{1,0:T(1,128)S(1)}, s32[1,5]{1,0:T(1,128)}, u32[]{:S(2)}) copy-start(s32[1,5]{1,0:T(1,128)} %pattern_ref.9) | copy-start | bytes 64
  15.7 29.6 %all-to-all-start = ((bf16[8,256,256]{2,1,0:T(8,128)(2,1)}), bf16[8,256,256]{2,1,0:T(8,128)(2,1)S(1)}, u32[]{:S(2)}, u32[]{:S(2)}) async-start(bf16[8,256,256]{2,1,0:T(8,128)(2,1)} %bitcast.8), calls=%async_computation | async-start | bytes 2097152 | tf_op jit(solution)/shard_map/all_to_all | solution.py:235
  20.5 25.1 %collective-permute-start.8 = (bf16[4,3,64,256]{3,2,1,0:T(8,128)(2,1)S(1)}, bf16[4,3,64,256]{3,2,1,0:T(8,128)(2,1)S(1)}, u32[]{:S(2)}, u32[]{:S(2)}) collective-permute-start(bf16[4,3,64,256]{3,2,1,0:T(8,128)(2,1)S(1)} %pad_maximum_fusion.rest_3_), channel_id=1, source_target_pairs={{0,1},{1,0},{2,3},{3,2},{4,5},{5,4},{6,7},{7,6},{8,9},{9,8},{10,11... | collective-permute-start | bytes 1179656 | tf_op jit(solution)/shard_map/ppermute | solution.py:204
  20.5 25.5 %collective-permute-start.7 = (bf16[4,3,64,256]{3,2,1,0:T(8,128)(2,1)S(1)}, bf16[4,3,64,256]{3,2,1,0:T(8,128)(2,1)S(1)}, u32[]{:S(2)}, u32[]{:S(2)}) collective-permute-start(bf16[4,3,64,256]{3,2,1,0:T(8,128)(2,1)S(1)} %pad_maximum_fusion.rest_3_), channel_id=1, source_target_pairs={{0,6},{1,7},{2,4},{3,5},{4,2},{5,3},{6,0},{7,1},{8,14},{9,15},{10,... | collective-permute-start | bytes 1179656 | tf_op jit(solution)/shard_map/ppermute | solution.py:204
  23.5 26.8 %collective-permute-start.6 = (bf16[4,3,64,256]{3,2,1,0:T(8,128)(2,1)S(1)}, bf16[4,3,64,256]{3,2,1,0:T(8,128)(2,1)S(1)}, u32[]{:S(2)}, u32[]{:S(2)}) collective-permute-start(bf16[4,3,64,256]{3,2,1,0:T(8,128)(2,1)S(1)} %pad_maximum_fusion.rest_3_), channel_id=1, source_target_pairs={{0,4},{1,5},{2,6},{3,7},{4,0},{5,1},{6,2},{7,3},{8,12},{9,13},{10,... | collective-permute-start | bytes 1179656 | tf_op jit(solution)/shard_map/ppermute | solution.py:204
  23.5 26.8 %collective-permute-start.5 = (bf16[4,3,64,256]{3,2,1,0:T(8,128)(2,1)S(1)}, bf16[4,3,64,256]{3,2,1,0:T(8,128)(2,1)S(1)}, u32[]{:S(2)}, u32[]{:S(2)}) collective-permute-start(bf16[4,3,64,256]{3,2,1,0:T(8,128)(2,1)S(1)} %pad_maximum_fusion.rest_3_), channel_id=1, source_target_pairs={{0,2},{1,3},{2,0},{3,1},{4,6},{5,7},{6,4},{7,5},{8,10},{9,11},{10,... | collective-permute-start | bytes 1179656 | tf_op jit(solution)/shard_map/ppermute | solution.py:204
  45.4 7.1 %collective-permute-start.4 = (bf16[8,128,256]{2,1,0:T(8,128)(2,1)S(1)}, bf16[8,128,256]{2,1,0:T(8,128)(2,1)S(1)}, u32[]{:S(2)}, u32[]{:S(2)}) collective-permute-start(bf16[8,128,256]{2,1,0:T(8,128)(2,1)S(1)} %get-tuple-element.61), channel_id=1, source_target_pairs={{0,1},{1,0},{2,3},{3,2},{4,5},{5,4},{6,7},{7,6},{8,9},{9,8},{10,11... | collective-permute-start | bytes 1572872 | tf_op jit(solution)/shard_map/ppermute | solution.py:204
  45.5 7.1 %collective-permute-start.3 = (bf16[8,128,256]{2,1,0:T(8,128)(2,1)S(1)}, bf16[8,128,256]{2,1,0:T(8,128)(2,1)S(1)}, u32[]{:S(2)}, u32[]{:S(2)}) collective-permute-start(bf16[8,128,256]{2,1,0:T(8,128)(2,1)S(1)} %get-tuple-element.62), channel_id=1, source_target_pairs={{0,1},{1,0},{2,3},{3,2},{4,5},{5,4},{6,7},{7,6},{8,9},{9,8},{10,11... | collective-permute-start | bytes 1572872 | tf_op jit(solution)/shard_map/ppermute | solution.py:204
  46.0 4.8 %collective-permute-start.11 = (bf16[4,3,64,256]{3,2,1,0:T(8,128)(2,1)S(1)}, bf16[4,3,64,256]{3,2,1,0:T(8,128)(2,1)S(1)}, u32[]{:S(2)}, u32[]{:S(2)}) collective-permute-start(bf16[4,3,64,256]{3,2,1,0:T(8,128)(2,1)S(1)} %collective-permute-done.7.rest_6_), channel_id=1, source_target_pairs={{0,1},{1,0},{2,3},{3,2},{4,5},{5,4},{6,7},{7,6},{8,9},{9,8},{10,11... | collective-permute-start | bytes 1179656 | tf_op jit(solution)/shard_map/ppermute | solution.py:204
  50.3 1.7 %collective-permute-start.10 = (bf16[4,3,64,256]{3,2,1,0:T(8,128)(2,1)S(1)}, bf16[4,3,64,256]{3,2,1,0:T(8,128)(2,1)S(1)}, u32[]{:S(2)}, u32[]{:S(2)}) collective-permute-start(bf16[4,3,64,256]{3,2,1,0:T(8,128)(2,1)S(1)} %collective-permute-done.6.rest_5_), channel_id=1, source_target_pairs={{0,1},{1,0},{2,3},{3,2},{4,5},{5,4},{6,7},{7,6},{8,9},{9,8},{10,11... | collective-permute-start | bytes 1179656 | tf_op jit(solution)/shard_map/ppermute | solution.py:204
  50.3 2.3 %collective-permute-start.9 = (bf16[4,3,64,256]{3,2,1,0:T(8,128)(2,1)S(1)}, bf16[4,3,64,256]{3,2,1,0:T(8,128)(2,1)S(1)}, u32[]{:S(2)}, u32[]{:S(2)}) collective-permute-start(bf16[4,3,64,256]{3,2,1,0:T(8,128)(2,1)S(1)} %collective-permute-done.5.rest_4_), channel_id=1, source_target_pairs={{0,1},{1,0},{2,3},{3,2},{4,5},{5,4},{6,7},{7,6},{8,9},{9,8},{10,11... | collective-permute-start | bytes 1179656 | tf_op jit(solution)/shard_map/ppermute | solution.py:204
  60.6 35.7 %collective-permute-start.13 = (bf16[4,4,64,256]{3,2,1,0:T(8,128)(2,1)S(1)}, bf16[4,4,64,256]{3,2,1,0:T(8,128)(2,1)S(1)}, u32[]{:S(2)}, u32[]{:S(2)}) collective-permute-start(bf16[4,4,64,256]{3,2,1,0:T(8,128)(2,1)S(1)} %get-tuple-element.39), channel_id=1, source_target_pairs={{0,4},{1,5},{2,6},{3,7},{4,0},{5,1},{6,2},{7,3},{8,12},{9,13},{10,... | collective-permute-start | bytes 1572872 | tf_op jit(solution)/shard_map/ppermute | solution.py:204
  60.6 35.6 %collective-permute-start.14 = (bf16[4,4,64,256]{3,2,1,0:T(8,128)(2,1)S(1)}, bf16[4,4,64,256]{3,2,1,0:T(8,128)(2,1)S(1)}, u32[]{:S(2)}, u32[]{:S(2)}) collective-permute-start(bf16[4,4,64,256]{3,2,1,0:T(8,128)(2,1)S(1)} %get-tuple-element.40), channel_id=1, source_target_pairs={{0,6},{1,7},{2,4},{3,5},{4,2},{5,3},{6,0},{7,1},{8,14},{9,15},{10,... | collective-permute-start | bytes 1572872 | tf_op jit(solution)/shard_map/ppermute | solution.py:204
  66.0 43.3 %copy-start.1 = (f32[1,5,64,256]{3,2,1,0:T(8,128)S(1)}, f32[1,5,64,256]{3,2,1,0:T(8,128)}, u32[]{:S(2)}) copy-start(f32[1,5,64,256]{3,2,1,0:T(8,128)} %omega_ref.3) | copy-start | bytes 983044
  66.0 30.2 %collective-permute-start.12 = (bf16[4,4,64,256]{3,2,1,0:T(8,128)(2,1)S(1)}, bf16[4,4,64,256]{3,2,1,0:T(8,128)(2,1)S(1)}, u32[]{:S(2)}, u32[]{:S(2)}) collective-permute-start(bf16[4,4,64,256]{3,2,1,0:T(8,128)(2,1)S(1)} %get-tuple-element.38), channel_id=1, source_target_pairs={{0,2},{1,3},{2,0},{3,1},{4,6},{5,7},{6,4},{7,5},{8,10},{9,11},{10,... | collective-permute-start | bytes 1572872 | tf_op jit(solution)/shard_map/ppermute | solution.py:204
  66.6 6.7 %collective-permute-start.15 = (bf16[4,1,64,256]{3,2,1,0:T(8,128)(2,1)S(1)}, bf16[4,1,64,256]{3,2,1,0:T(8,128)(2,1)S(1)}, u32[]{:S(2)}, u32[]{:S(2)}) collective-permute-start(bf16[4,1,64,256]{3,2,1,0:T(8,128)(2,1)S(1)} %get-tuple-element.42), channel_id=1, source_target_pairs={{0,8},{1,9},{2,10},{3,11},{4,12},{5,13},{6,14},{7,15},{8,0},{9,1},... | collective-permute-start | bytes 393224 | tf_op jit(solution)/shard_map/ppermute | solution.py:204
  68.2 10.1 %collective-permute-start.16 = (bf16[4,1,64,256]{3,2,1,0:T(8,128)(2,1)S(1)}, bf16[4,1,64,256]{3,2,1,0:T(8,128)(2,1)S(1)}, u32[]{:S(2)}, u32[]{:S(2)}) collective-permute-start(bf16[4,1,64,256]{3,2,1,0:T(8,128)(2,1)S(1)} %get-tuple-element.43), channel_id=1, source_target_pairs={{0,16},{1,17},{2,18},{3,19},{4,20},{5,21},{6,22},{7,23},{8,24},{9,... | collective-permute-start | bytes 393224 | tf_op jit(solution)/shard_map/ppermute | solution.py:204
  73.2 6.8 %collective-permute-start.17 = (bf16[4,1,64,256]{3,2,1,0:T(8,128)(2,1)S(1)}, bf16[4,1,64,256]{3,2,1,0:T(8,128)(2,1)S(1)}, u32[]{:S(2)}, u32[]{:S(2)}) collective-permute-start(bf16[4,1,64,256]{3,2,1,0:T(8,128)(2,1)S(1)} %get-tuple-element.44), channel_id=1, source_target_pairs={{0,24},{1,25},{2,26},{3,27},{4,28},{5,29},{6,30},{7,31},{8,16},{9,... | collective-permute-start | bytes 393224 | tf_op jit(solution)/shard_map/ppermute | solution.py:204
  80.1 11.3 %collective-permute-start.18 = (bf16[1,64,256]{2,1,0:T(8,128)(2,1)S(1)}, bf16[1,64,256]{2,1,0:T(8,128)(2,1)S(1)}, u32[]{:S(2)}, u32[]{:S(2)}) collective-permute-start(bf16[1,64,256]{2,1,0:T(8,128)(2,1)S(1)} %get-tuple-element.46), channel_id=1, source_target_pairs={{0,2},{1,3},{2,0},{3,1},{4,6},{5,7},{6,4},{7,5},{8,10},{9,11},{10,... | collective-permute-start | bytes 98312 | tf_op jit(solution)/shard_map/ppermute | solution.py:204
  81.8 9.9 %collective-permute-start.19 = (bf16[1,64,256]{2,1,0:T(8,128)(2,1)S(1)}, bf16[1,64,256]{2,1,0:T(8,128)(2,1)S(1)}, u32[]{:S(2)}, u32[]{:S(2)}) collective-permute-start(bf16[1,64,256]{2,1,0:T(8,128)(2,1)S(1)} %get-tuple-element.47), channel_id=1, source_target_pairs={{0,4},{1,5},{2,6},{3,7},{4,0},{5,1},{6,2},{7,3},{8,12},{9,13},{10,... | collective-permute-start | bytes 98312 | tf_op jit(solution)/shard_map/ppermute | solution.py:204
  91.4 4.8 %collective-permute-start.20 = (bf16[1,64,256]{2,1,0:T(8,128)(2,1)S(1)}, bf16[1,64,256]{2,1,0:T(8,128)(2,1)S(1)}, u32[]{:S(2)}, u32[]{:S(2)}) collective-permute-start(bf16[1,64,256]{2,1,0:T(8,128)(2,1)S(1)} %get-tuple-element.48), channel_id=1, source_target_pairs={{0,6},{1,7},{2,4},{3,5},{4,2},{5,3},{6,0},{7,1},{8,14},{9,15},{10,... | collective-permute-start | bytes 98312 | tf_op jit(solution)/shard_map/ppermute | solution.py:204
  97.1 5.6 %collective-permute-start.21 = (bf16[4,64,256]{2,1,0:T(8,128)(2,1)S(1)}, bf16[4,64,256]{2,1,0:T(8,128)(2,1)S(1)}, u32[]{:S(2)}, u32[]{:S(2)}) collective-permute-start(bf16[4,64,256]{2,1,0:T(8,128)(2,1)S(1)} %get-tuple-element.54), channel_id=1, source_target_pairs={{0,8},{1,9},{2,10},{3,11},{4,12},{5,13},{6,14},{7,15},{8,0},{9,1},... | collective-permute-start | bytes 393224 | tf_op jit(solution)/shard_map/ppermute | solution.py:204
  98.7 10.6 %collective-permute-start.22 = (bf16[4,64,256]{2,1,0:T(8,128)(2,1)S(1)}, bf16[4,64,256]{2,1,0:T(8,128)(2,1)S(1)}, u32[]{:S(2)}, u32[]{:S(2)}) collective-permute-start(bf16[4,64,256]{2,1,0:T(8,128)(2,1)S(1)} %get-tuple-element.55), channel_id=1, source_target_pairs={{0,16},{1,17},{2,18},{3,19},{4,20},{5,21},{6,22},{7,23},{8,24},{9,... | collective-permute-start | bytes 393224 | tf_op jit(solution)/shard_map/ppermute | solution.py:204
  101.2 8.1 %collective-permute-start.23 = (bf16[4,64,256]{2,1,0:T(8,128)(2,1)S(1)}, bf16[4,64,256]{2,1,0:T(8,128)(2,1)S(1)}, u32[]{:S(2)}, u32[]{:S(2)}) collective-permute-start(bf16[4,64,256]{2,1,0:T(8,128)(2,1)S(1)} %get-tuple-element.56), channel_id=1, source_target_pairs={{0,24},{1,25},{2,26},{3,27},{4,28},{5,29},{6,30},{7,31},{8,16},{9,... | collective-permute-start | bytes 393224 | tf_op jit(solution)/shard_map/ppermute | solution.py:204

commit v5 on v4

--- a/solution.py
+++ b/solution.py
@@ -10,8 +10,6 @@
 STEP_SIZE = 0.5
 PENALTY = 0.1
 LOW = 2
-LINE_FIRST = (4,)
-PLANE_FIRST = (0, 1, 2, 3)
 F32 = jnp.float32
 BF16 = jnp.bfloat16
 
@@ -110,73 +108,45 @@
     lax.fori_loop(0, teams, mix, 0, unroll=unroll)
 
 
-def product_kernel(teams, chips, far, place_ref, pattern_ref, *rest):
-    depth = teams // LOW
+def product_kernel(teams, chips, wanted, place_ref, pattern_ref, *rest):
     data_refs, mixed_ref, left_ref, outs = rest[:3], rest[3], rest[4], rest[5:]
-    plane_outs, line_outs = outs[: chips * len(far)], outs[chips * len(far) :]
     team = place_ref[0]
     high, low = lax.div(team, LOW), lax.rem(team, LOW)
     offsets, _ = stored_offsets(pattern_ref, team, teams)
     tile_rows = left_ref.shape[1] // chips
-
-    def part(i, k):
-        c = lax.rem(i + offsets[k], teams)
-        right = jnp.concatenate([block(data_refs, c), mixed_ref[c]], axis=0)
-        product = lax.dot_general(left_ref[i], right, NN, preferred_element_type=F32).astype(BF16)
-        return [product[m * tile_rows : (m + 1) * tile_rows] for m in range(chips)]
-
-    if line_outs:
-        for mx in range(LOW):
-            for mz in range(depth):
-                i = (high ^ mz) * LOW + (low ^ mx)
-                for n, k in enumerate(LINE_FIRST):
-                    for m, rows in enumerate(part(i, k)):
-                        line_outs[mz][mx * chips + m, n] = rows
-    for index, mx in enumerate(far):
-
-        def outer(z, carry):
-            i = z * LOW + (low ^ mx)
-            for n, k in enumerate(PLANE_FIRST):
-                for m, rows in enumerate(part(i, k)):
-                    plane_outs[index * chips + m][z, n] = rows
-            return carry
-
-        lax.fori_loop(0, depth, outer, 0, unroll=teams <= 8)
-
-
-def line_sum_kernel(planes, *rest):
-    parts, outs = rest[:-planes], rest[-planes:]
-    for m in range(planes):
-        total = parts[0][m].astype(F32)
-        for part in parts[1:]:
-            total = total + part[m].astype(F32)
-        outs[m][...] = total.astype(outs[m].dtype)
-
-
-def plane_sum_kernel(teams, place_ref, *rest):
-    count = teams // LOW
-    parts, outs = rest[:-count], rest[-count:]
-    z = lax.div(place_ref[0], LOW)
-    for m in range(count):
-        total = parts[0][z ^ m].astype(F32)
-        for part in parts[1:]:
-            total = total + part[z ^ m].astype(F32)
-        outs[m][...] = total.astype(outs[m].dtype)
+    for mz, mx in sorted({key[:2] for key in wanted}):
+        i = (high ^ mz) * LOW + (low ^ mx)
+        for k, offset in enumerate(offsets):
+            c = lax.rem(i + offset, teams)
+            right = jnp.concatenate([block(data_refs, c), mixed_ref[c]], axis=0)
+            product = lax.dot_general(left_ref[i], right, NN, preferred_element_type=F32)
+            for m in range(chips):
+                if (mz, mx, m) in wanted:
+                    out, place = wanted[mz, mx, m]
+                    outs[out][place + (k,)] = product[m * tile_rows : (m + 1) * tile_rows].astype(outs[out].dtype)
+
+
+def add_kernel(groups, *refs):
+    outs = refs[len(refs) - len(groups) :]
+    for out, terms in zip(outs, groups):
+        total = None
+        for source, index in terms:
+            term = (refs[source][...] if index is None else refs[source][index]).astype(F32)
+            total = term if total is None else total + term
+        out[...] = total.astype(out.dtype)
 
 
 def update_kernel(teams, scale, place_ref, pattern_ref, omega_ref, *rest):
-    depth = teams // LOW
-    plane_first, line_first, out_ref = rest[:depth], rest[depth:-1], rest[-1]
+    parts, out_ref = rest[:-1], rest[-1]
     _, slots = stored_offsets(pattern_ref, place_ref[0], teams)
     rows, width = out_ref.shape[2:]
     first = place_ref[1] * rows
     row_ids = first + lax.broadcasted_iota(jnp.int32, (rows, width), 0)
     diagonal = row_ids == lax.broadcasted_iota(jnp.int32, (rows, width), 1)
     for k in range(5):
-        parts, n = (line_first, LINE_FIRST.index(k)) if k in LINE_FIRST else (plane_first, PLANE_FIRST.index(k))
-        total = parts[0][n].astype(F32)
+        total = parts[0][k].astype(F32)
         for part in parts[1:]:
-            total = total + part[n].astype(F32)
+            total = total + part[k].astype(F32)
         current = omega_ref[0, slots[k]]
         gradient = total * scale
         if k == 0:
@@ -253,54 +223,76 @@
         name="mix",
     )(place, pattern, *data, *weights)
 
-    def products(far, lines):
+    tile = (slots, tile_rows, width)
+
+    def shape(lead, dtype):
+        return jax.ShapeDtypeStruct(tuple(lead) + tile, dtype)
+
+    def products(wanted, shapes):
         return pl.pallas_call(
-            functools.partial(product_kernel, teams, chips, far),
-            out_shape=[jax.ShapeDtypeStruct((count, len(PLANE_FIRST), tile_rows, width), BF16)] * (chips * len(far))
-            + [jax.ShapeDtypeStruct((planes, len(LINE_FIRST), tile_rows, width), BF16)] * lines,
+            functools.partial(product_kernel, teams, chips, wanted),
+            out_shape=shapes,
             in_specs=[SMEM, SMEM] + [VMEM] * 5,
-            out_specs=[VMEM] * (chips * len(far) + lines),
+            out_specs=[VMEM] * len(shapes),
             compiler_params=small,
             name="products",
         )(place, pattern, *data, mixed, left)
 
-    far_parts = products((1,), 0)
-    near_parts = products((0,), count)
-    plane_parts = across_plane(list(near_parts[:chips]) + list(far_parts))
-    line_parts = along_line(near_parts[chips:])
-    line_sums = pl.pallas_call(
-        functools.partial(line_sum_kernel, planes),
-        out_shape=[
-            jax.ShapeDtypeStruct((len(LINE_FIRST), tile_rows, width), BF16 if m else F32) for m in range(planes)
-        ],
-        in_specs=[VMEM] * count,
-        out_specs=[VMEM] * planes,
-        compiler_params=small,
-        name="line_sum",
-    )(*line_parts)
-    line_sums = across_plane(line_sums)
-    plane_parts, line_sums = lax.optimization_barrier((plane_parts, line_sums))
-    plane_sums = pl.pallas_call(
-        functools.partial(plane_sum_kernel, teams),
-        out_shape=[
-            jax.ShapeDtypeStruct((len(PLANE_FIRST), tile_rows, width), BF16 if m else F32) for m in range(count)
-        ],
-        in_specs=[SMEM] + [VMEM] * planes,
-        out_specs=[VMEM] * count,
-        compiler_params=small,
-        name="plane_sum",
-    )(place, *plane_parts)
-    plane_sums = along_line(plane_sums)
+    def add(groups, shapes, *arrays):
+        return pl.pallas_call(
+            functools.partial(add_kernel, groups),
+            out_shape=shapes,
+            in_specs=[VMEM] * len(arrays),
+            out_specs=[VMEM] * len(shapes),
+            compiler_params=small,
+            name="add",
+        )(*arrays)
+
+    half = count // 2
+    outer, inner = range(half, count), range(half)
+    chip_range = range(chips)
+    (outer_sent,) = products(
+        {(mz, 1, my): (0, (my, mz - half)) for mz in outer for my in chip_range}, [shape((chips, half), BF16)]
+    )
+    outer_sent = swap(outer_sent, 1, 0)
+    inner_parts = products(
+        {(mz, mx, my): (my, (mx, mz)) for mz in inner for mx in range(LOW) for my in chip_range},
+        [shape((LOW, half), BF16 if my else F32) for my in chip_range],
+    )
+    inner_parts = [swap(array, 0, 2 * my) if my else array for my, array in enumerate(inner_parts)]
+    (outer_kept,) = products(
+        {(mz, 0, my): (0, (my, mz - half)) for mz in outer for my in chip_range}, [shape((chips, half), F32)]
+    )
+    outer_parts = add(
+        [[(0, my), (1, my)] for my in chip_range],
+        [shape((half,), BF16 if my else F32) for my in chip_range],
+        outer_kept,
+        outer_sent,
+    )
+    outer_parts = [swap(array, 0, 2 * my) if my else array for my, array in enumerate(outer_parts)]
+    inner_parts = add(
+        [[(n, mx) for n in chip_range] for mx in range(LOW)],
+        [shape((half,), BF16 if mx else F32) for mx in range(LOW)],
+        *inner_parts,
+    )
+    inner_parts = [inner_parts[0], swap(inner_parts[1], 1, 0)]
+    outer_sums = add(
+        [[(n, mz - half) for n in chip_range] for mz in outer], [shape((), BF16) for _ in outer], *outer_parts
+    )
+    inner_sums = add(
+        [[(n, mz) for n in range(LOW)] for mz in inner], [shape((), BF16 if mz else F32) for mz in inner], *inner_parts
+    )
+    sums = along_line(list(inner_sums) + list(outer_sums))
 
     scale = 1.0 / (2.0 * signals.shape[0] * replicas)
     return pl.pallas_call(
         functools.partial(update_kernel, teams, scale),
         out_shape=jax.ShapeDtypeStruct(omega.shape, F32),
-        in_specs=[SMEM, SMEM, VMEM] + [VMEM] * (count + planes),
+        in_specs=[SMEM, SMEM, VMEM] + [VMEM] * count,
         out_specs=VMEM,
         compiler_params=small,
         name="update",
-    )(place, pattern, omega, *plane_sums, *line_sums)
+    )(place, pattern, omega, *sums)
 
 
 def solution(mesh):

time: 111 us -> 104 us (0.937)
  starting transfers between devices: 33.1 us -> 23.8 us
  waiting for transfers between devices: 62.4 us -> 64 us
    ppermute x24 -> x19, starting transfers between devices: 28.4 us -> 19 us  [swap(): return lax.ppermute(array, ('blk', 'rep'), route)]
    ppermute x24 -> x19, waiting for transfers between devices: 41.1 us -> 42.7 us  [swap(): return lax.ppermute(array, ('blk', 'rep'), route)]
    pallas_call x4 -> x7, Pallas kernels: 5.06 us -> 5.23 us  [the longest x3 4.9 us: products(): pl.pallas_call(functools.partial(product_kernel, teams, chips, wanted), o...]
  transfers between devices with their start and end apart: 25 -> 20, of which waited for: 13 -> 12; matrix products, arithmetic and copies ran while one was open for 0% -> 0% of each run, Pallas kernels for 2% -> 4%
where the time goes in v5:
time: 104 us; the launch traced here: 103 us
  waiting for transfers between devices  64 us (62%)
  starting transfers between devices  23.8 us (23%)
  Pallas kernels  13.4 us (13%)
  local copies, waits for them, and re-layouts  1.73 us (2%)
    ppermute x19, waiting for transfers between devices, swap(): return lax.ppermute(array, ('blk', 'rep'), route)  42.7 us
    all_to_all x1, waiting for transfers between devices, per_device(): own = lax.all_to_all(signals.reshape(teams, times, width), 'blk', 0, 0)  21.3 us
    ppermute x19, starting transfers between devices, swap(): return lax.ppermute(array, ('blk', 'rep'), route)  19 us
    pallas_call x1, Pallas kernels, per_device(): pl.pallas_call(functools.partial(mix_kernel, teams, replicas, tile_rows),...  6.14 us
    pallas_call x3, Pallas kernels, products(): pl.pallas_call(functools.partial(product_kernel, teams, chips, wanted), o...  4.9 us
    all_to_all x1, starting transfers between devices, per_device(): own = lax.all_to_all(signals.reshape(teams, times, width), 'blk', 0, 0)  4.84 us
  transfers between devices with their start and end apart: 20, of which 12 were waited for; matrix products, arithmetic and copies ran while one was open for 0% of the time, Pallas kernels for 4%

profile of v5, /device:TPU:0, one launch (start us, length us, event | category | flops | bytes accessed | tf_op | source)
XLA Modules:
  0.0 103.2 jit_solution(5895215832798164208)
XLA Ops:
  0.0 0.1 pad_add_fusion.place_ref
  0.1 1.0 copy-done
  1.1 0.7 copy-done.2
  1.7 0.6 prepare.1
  2.3 3.1 %collective-permute-start = (bf16[3,64,256]{2,1,0:T(8,128)(2,1)S(1)}, bf16[3,64,256]{2,1,0:T(8,128)(2,1)S(1)}, u32[]{:S(2)}, u32[]{:S(2)}) collective-permute-start(bf16[3,64,256]{2,1,0:T(8,128)(2,1)S(1)} %prepare.1), channel_id=1, source_target_pairs={{0,8},{1,9},{2,10},{3,11},{4,12},{5,13},{6,14},{7,15},{8,0},{9,1},... | collective-permute-start | bytes 294920 | tf_op jit(solution)/shard_map/ppermute | solution.py:174
  5.4 2.6 %collective-permute-start.1 = (bf16[3,64,256]{2,1,0:T(8,128)(2,1)S(1)}, bf16[3,64,256]{2,1,0:T(8,128)(2,1)S(1)}, u32[]{:S(2)}, u32[]{:S(2)}) collective-permute-start(bf16[3,64,256]{2,1,0:T(8,128)(2,1)S(1)} %prepare.1), channel_id=1, source_target_pairs={{0,16},{1,17},{2,18},{3,19},{4,20},{5,21},{6,22},{7,23},{8,24},{9,... | collective-permute-start | bytes 294920 | tf_op jit(solution)/shard_map/ppermute | solution.py:174
  8.0 0.0 collective-permute-start.2
  8.0 0.2 collective-permute-done
  8.2 7.6 %collective-permute-done.1 = bf16[3,64,256]{2,1,0:T(8,128)(2,1)S(1)} collective-permute-done((bf16[3,64,256]{2,1,0:T(8,128)(2,1)S(1)}, bf16[3,64,256]{2,1,0:T(8,128)(2,1)S(1)}, u32[]{:S(2)}, u32[]{:S(2)}) %collective-permute-start.1) | collective-permute-done | bytes 98336 | tf_op jit(solution)/shard_map/ppermute | solution.py:174
  15.8 0.0 collective-permute-done.2
  15.8 0.1 pad_maximum_fusion.rest_3_
  15.9 0.0 copy-start.3
  15.9 4.8 %all-to-all-start = ((bf16[8,256,256]{2,1,0:T(8,128)(2,1)}), bf16[8,256,256]{2,1,0:T(8,128)(2,1)S(1)}, u32[]{:S(2)}, u32[]{:S(2)}) async-start(bf16[8,256,256]{2,1,0:T(8,128)(2,1)} %bitcast.8), calls=%async_computation | async-start | bytes 2097152 | tf_op jit(solution)/shard_map/all_to_all | solution.py:205
  20.7 2.0 %collective-permute-start.6 = (bf16[4,3,64,256]{3,2,1,0:T(8,128)(2,1)S(1)}, bf16[4,3,64,256]{3,2,1,0:T(8,128)(2,1)S(1)}, u32[]{:S(2)}, u32[]{:S(2)}) collective-permute-start(bf16[4,3,64,256]{3,2,1,0:T(8,128)(2,1)S(1)} %pad_maximum_fusion.rest_3_), channel_id=1, source_target_pairs={{0,4},{1,5},{2,6},{3,7},{4,0},{5,1},{6,2},{7,3},{8,12},{9,13},{10,... | collective-permute-start | bytes 1179656 | tf_op jit(solution)/shard_map/ppermute | solution.py:174
  22.7 1.0 collective-permute-start.7
  23.7 0.5 collective-permute-start.5
  24.3 21.3 %all-to-all-done.rest_0_ = bf16[8,256,256]{2,1,0:T(8,128)(2,1)S(1)} async-done(((bf16[8,256,256]{2,1,0:T(8,128)(2,1)}), bf16[8,256,256]{2,1,0:T(8,128)(2,1)S(1)}, u32[]{:S(2)}, u32[]{:S(2)}) %all-to-all-start) | async-done | bytes 1048608 | tf_op jit(solution)/shard_map/all_to_all | solution.py:205
  45.6 0.1 fusion
  45.7 0.1 collective-permute-start.3
  45.8 0.5 collective-permute-start.4
  46.2 4.7 %collective-permute-done.7.rest_6_ = bf16[4,3,64,256]{3,2,1,0:T(8,128)(2,1)S(1)} collective-permute-done((bf16[4,3,64,256]{3,2,1,0:T(8,128)(2,1)S(1)}, bf16[4,3,64,256]{3,2,1,0:T(8,128)(2,1)S(1)}, u32[]{:S(2)}, u32[]{:S(2)}) %collective-permute-start.7) | collective-permute-done | bytes 393248 | tf_op jit(solution)/shard_map/ppermute | solution.py:174
  50.9 0.5 collective-permute-start.11
  51.4 0.1 collective-permute-start.9
  51.5 1.1 %collective-permute-done.10.rest_9_ = bf16[4,3,64,256]{3,2,1,0:T(8,128)(2,1)S(1)} collective-permute-done((bf16[4,3,64,256]{3,2,1,0:T(8,128)(2,1)S(1)}, bf16[4,3,64,256]{3,2,1,0:T(8,128)(2,1)S(1)}, u32[]{:S(2)}, u32[]{:S(2)}) %collective-permute-start.10) | collective-permute-done | bytes 393248 | tf_op jit(solution)/shard_map/ppermute | solution.py:174
  52.7 0.6 collective-permute-done.11.rest_10_
  53.2 0.6 collective-permute-done.9.rest_8_
  53.8 6.1 %mix.1 = (bf16[8,512,256]{2,1,0:T(8,128)(2,1)S(1)}, bf16[8,128,1024]{2,1,0:T(8,128)(2,1)S(1)}) custom-call(s32[2]{0:T(128)S(1)} %pad_add_fusion.place_ref, s32[1,5]{1,0:T(1,128)S(1)} %copy-done.3, bf16[8,256,256]{2,1,0:T(8,128)(2,1)S(1)} %all-to-all-done.rest_0_, bf16[8,128,256]{2,1,0:T(8,128)(2,1)S(1)} %collective-permute-done.3.rest_1_, ...), custom_call_target="tpu_custom_call" | custom-call | tf_op jit(solution)/shard_map/mix/pallas_call | solution.py:209
  59.9 1.4 %products.5 = bf16[2,2,5,64,256]{4,3,2,1,0:T(8,128)(2,1)S(1)} custom-call(s32[2]{0:T(128)S(1)} %pad_add_fusion.place_ref, s32[1,5]{1,0:T(1,128)S(1)} %copy-done.3, bf16[8,256,256]{2,1,0:T(8,128)(2,1)S(1)} %all-to-all-done.rest_0_, bf16[8,128,256]{2,1,0:T(8,128)(2,1)S(1)} %collective-permute-done.3.rest_1_, ...), custom_call_target="tpu_custom_call" | custom-call | tf_op jit(solution)/shard_map/products/pallas_call | solution.py:232
  61.4 0.3 collective-permute-start.15
  61.7 2.1 %products.3 = (f32[2,2,5,64,256]{4,3,2,1,0:T(8,128)S(1)}, bf16[2,2,5,64,256]{4,3,2,1,0:T(8,128)(2,1)S(1)}) custom-call(s32[2]{0:T(128)S(1)} %pad_add_fusion.place_ref, s32[1,5]{1,0:T(1,128)S(1)} %copy-done.3, bf16[8,256,256]{2,1,0:T(8,128)(2,1)S(1)} %all-to-all-done.rest_0_, bf16[8,128,256]{2,1,0:T(8,128)(2,1)S(1)} %collective-permute-done.3.rest_1_, ...), custom_call_target="tpu_custom_call" | custom-call | tf_op jit(solution)/shard_map/products/pallas_call | solution.py:232
  63.8 0.6 collective-permute-start.12
  64.4 1.4 %products.4.refs_0_ = f32[2,2,5,64,256]{4,3,2,1,0:T(8,128)S(1)} custom-call(s32[2]{0:T(128)S(1)} %pad_add_fusion.place_ref, s32[1,5]{1,0:T(1,128)S(1)} %copy-done.3, bf16[8,256,256]{2,1,0:T(8,128)(2,1)S(1)} %all-to-all-done.rest_0_, bf16[8,128,256]{2,1,0:T(8,128)(2,1)S(1)} %collective-permute-done.3.rest_1_, ...), custom_call_target="tpu_custom_call" | custom-call | tf_op jit(solution)/shard_map/products/pallas_call | solution.py:232
  65.8 12.4 %collective-permute-done.15.refs_1_ = bf16[2,2,5,64,256]{4,3,2,1,0:T(8,128)(2,1)S(1)} collective-permute-done((bf16[2,2,5,64,256]{4,3,2,1,0:T(8,128)(2,1)S(1)}, bf16[2,2,5,64,256]{4,3,2,1,0:T(8,128)(2,1)S(1)}, u32[]{:S(2)}, u32[]{:S(2)}) %collective-permute-start.15) | collective-permute-done | bytes 655392 | tf_op jit(solution)/shard_map/ppermute | solution.py:174
  78.2 0.1 add.8
  78.3 0.0 copy-start.1
  78.3 0.6 collective-permute-start.16
  78.9 1.5 %collective-permute-done.12.refs_1_ = bf16[2,2,5,64,256]{4,3,2,1,0:T(8,128)(2,1)S(1)} collective-permute-done((bf16[2,2,5,64,256]{4,3,2,1,0:T(8,128)(2,1)S(1)}, bf16[2,2,5,64,256]{4,3,2,1,0:T(8,128)(2,1)S(1)}, u32[]{:S(2)}, u32[]{:S(2)}) %collective-permute-start.12) | collective-permute-done | bytes 655392 | tf_op jit(solution)/shard_map/ppermute | solution.py:174
  80.4 0.1 add.6
  80.5 2.9 %collective-permute-start.13 = (bf16[2,5,64,256]{3,2,1,0:T(8,128)(2,1)S(1)}, bf16[2,5,64,256]{3,2,1,0:T(8,128)(2,1)S(1)}, u32[]{:S(2)}, u32[]{:S(2)}) collective-permute-start(bf16[2,5,64,256]{3,2,1,0:T(8,128)(2,1)S(1)} %get-tuple-element.26), channel_id=1, source_target_pairs={{0,4},{1,5},{2,6},{3,7},{4,0},{5,1},{6,2},{7,3},{8,12},{9,13},{10,... | collective-permute-start | bytes 983048 | tf_op jit(solution)/shard_map/ppermute | solution.py:174
  83.4 4.0 %collective-permute-done.16.refs_1_ = bf16[2,5,64,256]{3,2,1,0:T(8,128)(2,1)S(1)} collective-permute-done((bf16[2,5,64,256]{3,2,1,0:T(8,128)(2,1)S(1)}, bf16[2,5,64,256]{3,2,1,0:T(8,128)(2,1)S(1)}, u32[]{:S(2)}, u32[]{:S(2)}) %collective-permute-start.16) | collective-permute-done | bytes 327712 | tf_op jit(solution)/shard_map/ppermute | solution.py:174
  87.4 0.1 add.9
  87.5 2.7 %collective-permute-start.17 = (bf16[5,64,256]{2,1,0:T(8,128)(2,1)S(1)}, bf16[5,64,256]{2,1,0:T(8,128)(2,1)S(1)}, u32[]{:S(2)}, u32[]{:S(2)}) collective-permute-start(bf16[5,64,256]{2,1,0:T(8,128)(2,1)S(1)} %get-tuple-element.31), channel_id=1, source_target_pairs={{0,16},{1,17},{2,18},{3,19},{4,20},{5,21},{6,22},{7,23},{8,24},{9,... | collective-permute-start | bytes 491528 | tf_op jit(solution)/shard_map/ppermute | solution.py:174
  90.2 1.5 %collective-permute-start.18 = (bf16[5,64,256]{2,1,0:T(8,128)(2,1)S(1)}, bf16[5,64,256]{2,1,0:T(8,128)(2,1)S(1)}, u32[]{:S(2)}, u32[]{:S(2)}) collective-permute-start(bf16[5,64,256]{2,1,0:T(8,128)(2,1)S(1)} %get-tuple-element.32), channel_id=1, source_target_pairs={{0,24},{1,25},{2,26},{3,27},{4,28},{5,29},{6,30},{7,31},{8,16},{9,... | collective-permute-start | bytes 491528 | tf_op jit(solution)/shard_map/ppermute | solution.py:174
  91.6 0.1 add.7
  91.7 0.1 collective-permute-start.14
  91.8 9.8 %collective-permute-done.17.rest_2_ = bf16[5,64,256]{2,1,0:T(8,128)(2,1)S(1)} collective-permute-done((bf16[5,64,256]{2,1,0:T(8,128)(2,1)S(1)}, bf16[5,64,256]{2,1,0:T(8,128)(2,1)S(1)}, u32[]{:S(2)}, u32[]{:S(2)}) %collective-permute-start.17) | collective-permute-done | bytes 163872 | tf_op jit(solution)/shard_map/ppermute | solution.py:174
  101.6 0.2 collective-permute-done.14.rest_1_
  101.8 1.5 %update.1 = f32[1,5,64,256]{3,2,1,0:T(8,128)} custom-call(s32[2]{0:T(128)S(1)} %pad_add_fusion.place_ref, s32[1,5]{1,0:T(1,128)S(1)} %copy-done.3, f32[1,5,64,256]{3,2,1,0:T(8,128)S(1)} %copy-done.1, f32[5,64,256]{2,1,0:T(8,128)S(1)} %get-tuple-element.27.rest_0_, bf16[5,64,256]{2,1,0:T(8,128)(2,1)S(1)} %collective-permute-done.14.rest_1_, ...), custom_call_target="tpu_custom_call" | custom-call | tf_op jit(solution)/shard_map/update/pallas_call | solution.py:288
  (13 shorter events, 0.0 us)
Async XLA Ops:
  0.1 1.0 copy-start
  1.0 0.7 copy-start.2
  2.3 5.9 %collective-permute-start = (bf16[3,64,256]{2,1,0:T(8,128)(2,1)S(1)}, bf16[3,64,256]{2,1,0:T(8,128)(2,1)S(1)}, u32[]{:S(2)}, u32[]{:S(2)}) collective-permute-start(bf16[3,64,256]{2,1,0:T(8,128)(2,1)S(1)} %prepare.1), channel_id=1, source_target_pairs={{0,8},{1,9},{2,10},{3,11},{4,12},{5,13},{6,14},{7,15},{8,0},{9,1},... | collective-permute-start | bytes 294920 | tf_op jit(solution)/shard_map/ppermute | solution.py:174
  5.4 10.4 %collective-permute-start.1 = (bf16[3,64,256]{2,1,0:T(8,128)(2,1)S(1)}, bf16[3,64,256]{2,1,0:T(8,128)(2,1)S(1)}, u32[]{:S(2)}, u32[]{:S(2)}) collective-permute-start(bf16[3,64,256]{2,1,0:T(8,128)(2,1)S(1)} %prepare.1), channel_id=1, source_target_pairs={{0,16},{1,17},{2,18},{3,19},{4,20},{5,21},{6,22},{7,23},{8,24},{9,... | collective-permute-start | bytes 294920 | tf_op jit(solution)/shard_map/ppermute | solution.py:174
  8.0 7.8 %collective-permute-start.2 = (bf16[3,64,256]{2,1,0:T(8,128)(2,1)S(1)}, bf16[3,64,256]{2,1,0:T(8,128)(2,1)S(1)}, u32[]{:S(2)}, u32[]{:S(2)}) collective-permute-start(bf16[3,64,256]{2,1,0:T(8,128)(2,1)S(1)} %prepare.1), channel_id=1, source_target_pairs={{0,24},{1,25},{2,26},{3,27},{4,28},{5,29},{6,30},{7,31},{8,16},{9,... | collective-permute-start | bytes 294920 | tf_op jit(solution)/shard_map/ppermute | solution.py:174
  15.9 37.9 %copy-start.3 = (s32[1,5]{1,0:T(1,128)S(1)}, s32[1,5]{1,0:T(1,128)}, u32[]{:S(2)}) copy-start(s32[1,5]{1,0:T(1,128)} %pattern_ref.11) | copy-start | bytes 64
  15.9 29.7 %all-to-all-start = ((bf16[8,256,256]{2,1,0:T(8,128)(2,1)}), bf16[8,256,256]{2,1,0:T(8,128)(2,1)S(1)}, u32[]{:S(2)}, u32[]{:S(2)}) async-start(bf16[8,256,256]{2,1,0:T(8,128)(2,1)} %bitcast.8), calls=%async_computation | async-start | bytes 2097152 | tf_op jit(solution)/shard_map/all_to_all | solution.py:205
  20.7 25.0 %collective-permute-start.6 = (bf16[4,3,64,256]{3,2,1,0:T(8,128)(2,1)S(1)}, bf16[4,3,64,256]{3,2,1,0:T(8,128)(2,1)S(1)}, u32[]{:S(2)}, u32[]{:S(2)}) collective-permute-start(bf16[4,3,64,256]{3,2,1,0:T(8,128)(2,1)S(1)} %pad_maximum_fusion.rest_3_), channel_id=1, source_target_pairs={{0,4},{1,5},{2,6},{3,7},{4,0},{5,1},{6,2},{7,3},{8,12},{9,13},{10,... | collective-permute-start | bytes 1179656 | tf_op jit(solution)/shard_map/ppermute | solution.py:174
  22.7 28.2 %collective-permute-start.7 = (bf16[4,3,64,256]{3,2,1,0:T(8,128)(2,1)S(1)}, bf16[4,3,64,256]{3,2,1,0:T(8,128)(2,1)S(1)}, u32[]{:S(2)}, u32[]{:S(2)}) collective-permute-start(bf16[4,3,64,256]{3,2,1,0:T(8,128)(2,1)S(1)} %pad_maximum_fusion.rest_3_), channel_id=1, source_target_pairs={{0,6},{1,7},{2,4},{3,5},{4,2},{5,3},{6,0},{7,1},{8,14},{9,15},{10,... | collective-permute-start | bytes 1179656 | tf_op jit(solution)/shard_map/ppermute | solution.py:174
  23.7 27.2 %collective-permute-start.5 = (bf16[4,3,64,256]{3,2,1,0:T(8,128)(2,1)S(1)}, bf16[4,3,64,256]{3,2,1,0:T(8,128)(2,1)S(1)}, u32[]{:S(2)}, u32[]{:S(2)}) collective-permute-start(bf16[4,3,64,256]{3,2,1,0:T(8,128)(2,1)S(1)} %pad_maximum_fusion.rest_3_), channel_id=1, source_target_pairs={{0,2},{1,3},{2,0},{3,1},{4,6},{5,7},{6,4},{7,5},{8,10},{9,11},{10,... | collective-permute-start | bytes 1179656 | tf_op jit(solution)/shard_map/ppermute | solution.py:174
  24.3 27.2 %collective-permute-start.8 = (bf16[4,3,64,256]{3,2,1,0:T(8,128)(2,1)S(1)}, bf16[4,3,64,256]{3,2,1,0:T(8,128)(2,1)S(1)}, u32[]{:S(2)}, u32[]{:S(2)}) collective-permute-start(bf16[4,3,64,256]{3,2,1,0:T(8,128)(2,1)S(1)} %pad_maximum_fusion.rest_3_), channel_id=1, source_target_pairs={{0,1},{1,0},{2,3},{3,2},{4,5},{5,4},{6,7},{7,6},{8,9},{9,8},{10,11... | collective-permute-start | bytes 1179656 | tf_op jit(solution)/shard_map/ppermute | solution.py:174
  45.7 8.1 %collective-permute-start.3 = (bf16[8,128,256]{2,1,0:T(8,128)(2,1)S(1)}, bf16[8,128,256]{2,1,0:T(8,128)(2,1)S(1)}, u32[]{:S(2)}, u32[]{:S(2)}) collective-permute-start(bf16[8,128,256]{2,1,0:T(8,128)(2,1)S(1)} %get-tuple-element.34), channel_id=1, source_target_pairs={{0,1},{1,0},{2,3},{3,2},{4,5},{5,4},{6,7},{7,6},{8,9},{9,8},{10,11... | collective-permute-start | bytes 1572872 | tf_op jit(solution)/shard_map/ppermute | solution.py:174
  45.8 8.0 %collective-permute-start.4 = (bf16[8,128,256]{2,1,0:T(8,128)(2,1)S(1)}, bf16[8,128,256]{2,1,0:T(8,128)(2,1)S(1)}, u32[]{:S(2)}, u32[]{:S(2)}) collective-permute-start(bf16[8,128,256]{2,1,0:T(8,128)(2,1)S(1)} %get-tuple-element.33), channel_id=1, source_target_pairs={{0,1},{1,0},{2,3},{3,2},{4,5},{5,4},{6,7},{7,6},{8,9},{9,8},{10,11... | collective-permute-start | bytes 1572872 | tf_op jit(solution)/shard_map/ppermute | solution.py:174
  50.9 1.7 %collective-permute-start.10 = (bf16[4,3,64,256]{3,2,1,0:T(8,128)(2,1)S(1)}, bf16[4,3,64,256]{3,2,1,0:T(8,128)(2,1)S(1)}, u32[]{:S(2)}, u32[]{:S(2)}) collective-permute-start(bf16[4,3,64,256]{3,2,1,0:T(8,128)(2,1)S(1)} %collective-permute-done.6.rest_5_), channel_id=1, source_target_pairs={{0,1},{1,0},{2,3},{3,2},{4,5},{5,4},{6,7},{7,6},{8,9},{9,8},{10,11... | collective-permute-start | bytes 1179656 | tf_op jit(solution)/shard_map/ppermute | solution.py:174
  50.9 2.3 %collective-permute-start.11 = (bf16[4,3,64,256]{3,2,1,0:T(8,128)(2,1)S(1)}, bf16[4,3,64,256]{3,2,1,0:T(8,128)(2,1)S(1)}, u32[]{:S(2)}, u32[]{:S(2)}) collective-permute-start(bf16[4,3,64,256]{3,2,1,0:T(8,128)(2,1)S(1)} %collective-permute-done.7.rest_6_), channel_id=1, source_target_pairs={{0,1},{1,0},{2,3},{3,2},{4,5},{5,4},{6,7},{7,6},{8,9},{9,8},{10,11... | collective-permute-start | bytes 1179656 | tf_op jit(solution)/shard_map/ppermute | solution.py:174
  51.4 2.3 %collective-permute-start.9 = (bf16[4,3,64,256]{3,2,1,0:T(8,128)(2,1)S(1)}, bf16[4,3,64,256]{3,2,1,0:T(8,128)(2,1)S(1)}, u32[]{:S(2)}, u32[]{:S(2)}) collective-permute-start(bf16[4,3,64,256]{3,2,1,0:T(8,128)(2,1)S(1)} %collective-permute-done.5.rest_4_), channel_id=1, source_target_pairs={{0,1},{1,0},{2,3},{3,2},{4,5},{5,4},{6,7},{7,6},{8,9},{9,8},{10,11... | collective-permute-start | bytes 1179656 | tf_op jit(solution)/shard_map/ppermute | solution.py:174
  61.4 16.8 %collective-permute-start.15 = (bf16[2,2,5,64,256]{4,3,2,1,0:T(8,128)(2,1)S(1)}, bf16[2,2,5,64,256]{4,3,2,1,0:T(8,128)(2,1)S(1)}, u32[]{:S(2)}, u32[]{:S(2)}) collective-permute-start(bf16[2,2,5,64,256]{4,3,2,1,0:T(8,128)(2,1)S(1)} %products.5), channel_id=1, source_target_pairs={{0,4},{1,5},{2,6},{3,7},{4,0},{5,1},{6,2},{7,3},{8,12},{9,13},{10,... | collective-permute-start | bytes 1966088 | tf_op jit(solution)/shard_map/ppermute | solution.py:174
  63.8 16.6 %collective-permute-start.12 = (bf16[2,2,5,64,256]{4,3,2,1,0:T(8,128)(2,1)S(1)}, bf16[2,2,5,64,256]{4,3,2,1,0:T(8,128)(2,1)S(1)}, u32[]{:S(2)}, u32[]{:S(2)}) collective-permute-start(bf16[2,2,5,64,256]{4,3,2,1,0:T(8,128)(2,1)S(1)} %get-tuple-element.24), channel_id=1, source_target_pairs={{0,2},{1,3},{2,0},{3,1},{4,6},{5,7},{6,4},{7,5},{8,10},{9,11},{10,... | collective-permute-start | bytes 1966088 | tf_op jit(solution)/shard_map/ppermute | solution.py:174
  78.3 23.5 %copy-start.1 = (f32[1,5,64,256]{3,2,1,0:T(8,128)S(1)}, f32[1,5,64,256]{3,2,1,0:T(8,128)}, u32[]{:S(2)}) copy-start(f32[1,5,64,256]{3,2,1,0:T(8,128)} %omega_ref.3) | copy-start | bytes 983044
  78.3 9.1 %collective-permute-start.16 = (bf16[2,5,64,256]{3,2,1,0:T(8,128)(2,1)S(1)}, bf16[2,5,64,256]{3,2,1,0:T(8,128)(2,1)S(1)}, u32[]{:S(2)}, u32[]{:S(2)}) collective-permute-start(bf16[2,5,64,256]{3,2,1,0:T(8,128)(2,1)S(1)} %get-tuple-element.30), channel_id=1, source_target_pairs={{0,2},{1,3},{2,0},{3,1},{4,6},{5,7},{6,4},{7,5},{8,10},{9,11},{10,... | collective-permute-start | bytes 983048 | tf_op jit(solution)/shard_map/ppermute | solution.py:174
  80.5 11.1 %collective-permute-start.13 = (bf16[2,5,64,256]{3,2,1,0:T(8,128)(2,1)S(1)}, bf16[2,5,64,256]{3,2,1,0:T(8,128)(2,1)S(1)}, u32[]{:S(2)}, u32[]{:S(2)}) collective-permute-start(bf16[2,5,64,256]{3,2,1,0:T(8,128)(2,1)S(1)} %get-tuple-element.26), channel_id=1, source_target_pairs={{0,4},{1,5},{2,6},{3,7},{4,0},{5,1},{6,2},{7,3},{8,12},{9,13},{10,... | collective-permute-start | bytes 983048 | tf_op jit(solution)/shard_map/ppermute | solution.py:174
  87.5 14.1 %collective-permute-start.17 = (bf16[5,64,256]{2,1,0:T(8,128)(2,1)S(1)}, bf16[5,64,256]{2,1,0:T(8,128)(2,1)S(1)}, u32[]{:S(2)}, u32[]{:S(2)}) collective-permute-start(bf16[5,64,256]{2,1,0:T(8,128)(2,1)S(1)} %get-tuple-element.31), channel_id=1, source_target_pairs={{0,16},{1,17},{2,18},{3,19},{4,20},{5,21},{6,22},{7,23},{8,24},{9,... | collective-permute-start | bytes 491528 | tf_op jit(solution)/shard_map/ppermute | solution.py:174
  90.2 11.5 %collective-permute-start.18 = (bf16[5,64,256]{2,1,0:T(8,128)(2,1)S(1)}, bf16[5,64,256]{2,1,0:T(8,128)(2,1)S(1)}, u32[]{:S(2)}, u32[]{:S(2)}) collective-permute-start(bf16[5,64,256]{2,1,0:T(8,128)(2,1)S(1)} %get-tuple-element.32), channel_id=1, source_target_pairs={{0,24},{1,25},{2,26},{3,27},{4,28},{5,29},{6,30},{7,31},{8,16},{9,... | collective-permute-start | bytes 491528 | tf_op jit(solution)/shard_map/ppermute | solution.py:174
  91.7 10.1 %collective-permute-start.14 = (bf16[5,64,256]{2,1,0:T(8,128)(2,1)S(1)}, bf16[5,64,256]{2,1,0:T(8,128)(2,1)S(1)}, u32[]{:S(2)}, u32[]{:S(2)}) collective-permute-start(bf16[5,64,256]{2,1,0:T(8,128)(2,1)S(1)} %get-tuple-element.28), channel_id=1, source_target_pairs={{0,8},{1,9},{2,10},{3,11},{4,12},{5,13},{6,14},{7,15},{8,0},{9,1},... | collective-permute-start | bytes 491528 | tf_op jit(solution)/shard_map/ppermute | solution.py:174

commit v6 on v5

--- a/solution.py
+++ b/solution.py
@@ -5,11 +5,13 @@
 from jax import lax
 from jax.experimental import pallas as pl
 from jax.experimental.pallas import tpu as pltpu
-from jax.sharding import PartitionSpec as P
+from jax.sharding import Mesh, PartitionSpec as P
 
 STEP_SIZE = 0.5
 PENALTY = 0.1
 LOW = 2
+AXES = ("line", "low", "chip", "core")
+BLK, REP = AXES[:2], AXES[2:]
 F32 = jnp.float32
 BF16 = jnp.bfloat16
 
@@ -29,33 +31,43 @@
     return offsets, slots
 
 
-def prepare_kernel(teams, place_ref, pattern_ref, omega_ref, out_ref):
-    _, slots = stored_offsets(pattern_ref, place_ref[0], teams)
+def prepare_kernel(teams, place_ref, pattern_ref, omega_ref, signals_ref, upper_ref, across_ref, sem):
+    team = place_ref[0]
+    rows = across_ref.shape[0]
+    first = pl.multiple_of((lax.rem(team, LOW) ^ 1) * rows, rows)
+    copy = pltpu.make_async_copy(signals_ref.at[pl.ds(first, rows)], across_ref, sem)
+    copy.start()
+    _, slots = stored_offsets(pattern_ref, team, teams)
     for k in range(3):
-        out_ref[k] = omega_ref[0, slots[k]].astype(BF16)
+        upper_ref[k] = omega_ref[0, slots[k]].astype(BF16)
+    copy.wait()
+
+
+def deal_kernel(place_ref, signals_ref, across_ref, out_ref, sems):
+    rows = across_ref.shape[0]
+    first = pl.multiple_of(lax.rem(place_ref[0], LOW) * rows, rows)
+    sources = [signals_ref.at[pl.ds(first, rows)], across_ref]
+    copies = [
+        pltpu.make_async_copy(source.reshape(out_ref.shape[0], *out_ref.shape[2:]), out_ref.at[:, n], sems.at[n])
+        for n, source in enumerate(sources)
+    ]
+    for copy in copies:
+        copy.start()
+    for copy in copies:
+        copy.wait()
 
 
 NN = (((1,), (0,)), ((), ()))
 NT = (((1,), (1,)), ((), ()))
 
 
-def block(data_refs, c):
-    return jnp.concatenate([ref[c] for ref in data_refs], axis=0)
-
-
-def mix_kernel(teams, replicas, tile_rows, place_ref, pattern_ref, *rest):
-    chips = replicas // 2
+def gather_kernel(teams, chips, tile_rows, place_ref, *rest):
+    weight_refs, omega_ref, sems = rest[:-2], rest[-2], rest[-1]
     planes = LOW * chips
     depth = teams // LOW
-    data_refs, rest = rest[:3], rest[3:]
-    weight_refs, rest = rest[: 2 * planes], rest[2 * planes :]
-    mixed_ref, left_ref, omega_ref, flip_ref, sems = rest
     team, replica = place_ref[0], place_ref[1]
     core, chip = lax.rem(replica, 2), lax.div(replica, 2)
     high, low = lax.div(team, LOW), lax.rem(team, LOW)
-    offsets, _ = stored_offsets(pattern_ref, team, teams)
-    times = mixed_ref.shape[1]
-
     copies = []
     for half in range(2):
         for mx in range(LOW):
@@ -74,52 +86,58 @@
                     )
     for copy in copies:
         copy.start()
-
-    def keep(i, first, array):
-        flip_ref[...] = array.T
-        for m in range(chips):
-            row = (2 * (chip ^ m) + core) * tile_rows
-            left_ref[i, m * tile_rows : (m + 1) * tile_rows, first : first + times] = flip_ref[
-                pl.ds(pl.multiple_of(row, tile_rows), tile_rows)
-            ]
-
-    def turn(i, carry):
-        keep(i, times, block(data_refs, i))
-        return carry
+    for copy in copies:
+        copy.wait()
+
+
+def block(data_ref, low, c):
+    return data_ref[lax.div(c, LOW), lax.rem(c, LOW) ^ low]
+
+
+def mix_kernel(teams, replicas, tile_rows, place_ref, pattern_ref, data_ref, omega_ref, mixed_ref, left_ref, flip_ref):
+    chips = replicas // 2
+    team, replica = place_ref[0], place_ref[1]
+    core, chip = lax.rem(replica, 2), lax.div(replica, 2)
+    low = lax.rem(team, LOW)
+    offsets, _ = stored_offsets(pattern_ref, team, teams)
+    times = mixed_ref.shape[1]
 
     def mix(i, carry):
         total = None
         for k, offset in enumerate(offsets):
             c = lax.rem(i + offset, teams)
-            if k < 3:
-                term = lax.dot_general(block(data_refs, c), omega_ref[i, k], NT, preferred_element_type=F32)
-            else:
-                term = lax.dot_general(block(data_refs, c), omega_ref[c, 5 - k], NN, preferred_element_type=F32)
+            right, dims = (omega_ref[i, k], NT) if k < 3 else (omega_ref[c, 5 - k], NN)
+            term = lax.dot_general(block(data_ref, low, c), right, dims, preferred_element_type=F32)
             total = term if total is None else total + term
         mixed = total.astype(BF16)
         mixed_ref[i] = mixed
-        keep(i, 0, mixed)
+        for n, array in enumerate([mixed, block(data_ref, low, i)]):
+            flip_ref[n] = array.T
+            for m in range(chips):
+                row = (2 * (chip ^ m) + core) * tile_rows
+                left_ref[i, m * tile_rows : (m + 1) * tile_rows, n * times : (n + 1) * times] = flip_ref[
+                    n, pl.ds(pl.multiple_of(row, tile_rows), tile_rows)
+                ]
         return carry
 
-    unroll = teams <= 8
-    lax.fori_loop(0, teams, turn, 0, unroll=unroll)
-    for copy in copies:
-        copy.wait()
-    lax.fori_loop(0, teams, mix, 0, unroll=unroll)
+    lax.fori_loop(0, teams, mix, 0, unroll=teams <= 8)
 
 
 def product_kernel(teams, chips, wanted, place_ref, pattern_ref, *rest):
-    data_refs, mixed_ref, left_ref, outs = rest[:3], rest[3], rest[4], rest[5:]
+    cores, outs = [rest[:3], rest[3:6]], rest[6:]
     team = place_ref[0]
     high, low = lax.div(team, LOW), lax.rem(team, LOW)
     offsets, _ = stored_offsets(pattern_ref, team, teams)
-    tile_rows = left_ref.shape[1] // chips
+    tile_rows = cores[0][2].shape[1] // chips
     for mz, mx in sorted({key[:2] for key in wanted}):
         i = (high ^ mz) * LOW + (low ^ mx)
         for k, offset in enumerate(offsets):
             c = lax.rem(i + offset, teams)
-            right = jnp.concatenate([block(data_refs, c), mixed_ref[c]], axis=0)
-            product = lax.dot_general(left_ref[i], right, NN, preferred_element_type=F32)
+            left = jnp.concatenate([left_ref[i] for _, _, left_ref in cores], axis=1)
+            right = jnp.concatenate(
+                [part for data_ref, mixed_ref, _ in cores for part in (block(data_ref, low, c), mixed_ref[c])], axis=0
+            )
+            product = lax.dot_general(left, right, NN, preferred_element_type=F32)
             for m in range(chips):
                 if (mz, mx, m) in wanted:
                     out, place = wanted[mz, mx, m]
@@ -163,7 +181,7 @@
     chips = replicas // 2
     slots, tile_rows, width = omega.shape[1:]
     times = signals.shape[0] // teams
-    place = jnp.stack([lax.axis_index("blk"), lax.axis_index("rep")]).astype(jnp.int32)
+    place = jnp.stack([lax.axis_index(BLK), lax.axis_index(REP)]).astype(jnp.int32)
 
     def swap(array, blk_mask, rep_mask):
         route = [
@@ -171,14 +189,13 @@
             for b in range(teams)
             for r in range(replicas)
         ]
-        return lax.ppermute(array, ("blk", "rep"), route)
+        return lax.ppermute(array, AXES, route)
 
     planes = LOW * chips
     count = teams // LOW
     planes = LOW * chips
     count = teams // LOW
     small = pltpu.CompilerParams(vmem_limit_bytes=(6 if teams <= 8 else 24) * 2**20)
-    large = pltpu.CompilerParams(vmem_limit_bytes=(8 if teams <= 8 else 32) * 2**20)
 
     def across_plane(arrays):
         return [
@@ -190,38 +207,61 @@
     def along_line(arrays):
         return [swap(array, m * LOW, 0) if m else array for m, array in enumerate(arrays)]
 
-    upper = pl.pallas_call(
+    upper, across = pl.pallas_call(
         functools.partial(prepare_kernel, teams),
-        out_shape=jax.ShapeDtypeStruct((3, tile_rows, width), BF16),
-        in_specs=[SMEM, SMEM, VMEM],
-        out_specs=VMEM,
+        out_shape=[
+            jax.ShapeDtypeStruct((3, tile_rows, width), BF16),
+            jax.ShapeDtypeStruct((count * times, width), BF16),
+        ],
+        in_specs=[SMEM, SMEM, VMEM, ANY],
+        out_specs=[VMEM, VMEM],
+        scratch_shapes=[pltpu.SemaphoreType.DMA],
         compiler_params=small,
         name="prepare",
-    )(place, pattern, omega)
+    )(place, pattern, omega, signals)
 
     line = jnp.stack(along_line([upper] * count))
-    line, signals = lax.optimization_barrier((line, signals))
+    across = swap(across, 1, 0)
+    line, across = lax.optimization_barrier((line, across))
     weights = across_plane([line] * planes)
-    own = lax.all_to_all(signals.reshape(teams, times, width), "blk", 0, 0)
-    data = [own] + [swap(part, 0, 1) for part in jnp.split(own, 2, axis=1)]
+    dealt = pl.pallas_call(
+        deal_kernel,
+        out_shape=jax.ShapeDtypeStruct((count, LOW, times, width), BF16),
+        in_specs=[SMEM, ANY, VMEM],
+        out_specs=VMEM,
+        scratch_shapes=[pltpu.SemaphoreType.DMA((2,))],
+        compiler_params=small,
+        name="deal",
+    )(place, signals, across)
+    own = lax.all_to_all(dealt, "line", 0, 0)
     weights += [swap(array, 0, 1) for array in weights]
-
-    mixed, left = pl.pallas_call(
-        functools.partial(mix_kernel, teams, replicas, tile_rows),
-        out_shape=[
-            jax.ShapeDtypeStruct((teams, 2 * times, width), BF16),
-            jax.ShapeDtypeStruct((teams, chips * tile_rows, 4 * times), BF16),
-        ],
-        in_specs=[SMEM, SMEM] + [VMEM] * 3 + [ANY] * (2 * planes),
-        out_specs=[VMEM, VMEM],
-        scratch_shapes=[
-            pltpu.VMEM((teams, 3, width, width), BF16),
-            pltpu.VMEM((width, 2 * times), BF16),
-            pltpu.SemaphoreType.DMA((2 * planes * count,)),
-        ],
-        compiler_params=large,
-        name="mix",
-    )(place, pattern, *data, *weights)
+    tiles = pl.pallas_call(
+        functools.partial(gather_kernel, teams, chips, tile_rows),
+        out_shape=jax.ShapeDtypeStruct((teams, 3, width, width), BF16),
+        in_specs=[SMEM] + [ANY] * (2 * planes),
+        out_specs=VMEM,
+        scratch_shapes=[pltpu.SemaphoreType.DMA((2 * planes * count,))],
+        compiler_params=small,
+        name="gather",
+    )(place, *weights)
+    own, tiles = lax.optimization_barrier((own, tiles))
+
+    def mix(data):
+        return pl.pallas_call(
+            functools.partial(mix_kernel, teams, replicas, tile_rows),
+            out_shape=[
+                jax.ShapeDtypeStruct((teams, times, width), BF16),
+                jax.ShapeDtypeStruct((teams, chips * tile_rows, 2 * times), BF16),
+            ],
+            in_specs=[SMEM, SMEM, VMEM, VMEM],
+            out_specs=[VMEM, VMEM],
+            scratch_shapes=[pltpu.VMEM((2, width, times), BF16)],
+            compiler_params=small,
+            name="mix",
+        )(place, pattern, data, tiles)
+
+    other = swap(own, 0, 1)
+    cores = [own, *mix(own), other, *mix(other)]
 
     tile = (slots, tile_rows, width)
 
@@ -232,11 +272,11 @@
         return pl.pallas_call(
             functools.partial(product_kernel, teams, chips, wanted),
             out_shape=shapes,
-            in_specs=[SMEM, SMEM] + [VMEM] * 5,
+            in_specs=[SMEM, SMEM] + [VMEM] * 6,
             out_specs=[VMEM] * len(shapes),
             compiler_params=small,
             name="products",
-        )(place, pattern, *data, mixed, left)
+        )(place, pattern, *cores)
 
     def add(groups, shapes, *arrays):
         return pl.pallas_call(
@@ -296,10 +336,12 @@
 
 
 def solution(mesh):
+    teams, replicas = mesh.shape["blk"], mesh.shape["rep"]
+    fine = Mesh(mesh.devices.reshape(teams // LOW, LOW, replicas // 2, 2), AXES)
     return jax.shard_map(
-        functools.partial(per_device, mesh.shape["blk"], mesh.shape["rep"]),
-        mesh=mesh,
-        in_specs=(P("rep", "blk"), P("blk", None, "rep", None), P("blk", None)),
-        out_specs=P("blk", None, "rep", None),
+        functools.partial(per_device, teams, replicas),
+        mesh=fine,
+        in_specs=(P(REP, BLK), P(BLK, None, REP, None), P(BLK, None)),
+        out_specs=P(BLK, None, REP, None),
         check_vma=False,
     )

time: 104 us -> 103 us (level)
  waiting for transfers between devices: 64 us -> 55.2 us
  Pallas kernels: 13.4 us -> 18.9 us
  starting transfers between devices: 23.8 us -> 25.3 us
  local copies, waits for them, and re-layouts: 1.73 us -> 2.86 us
    all_to_all x1, waiting for transfers between devices: 21.3 us -> 1.19 us  [per_device(): own = lax.all_to_all(dealt, 'line', 0, 0)]
    ppermute x19, waiting for transfers between devices: 42.7 us -> 54 us  [swap(): return lax.ppermute(array, AXES, route)]
    pallas_call x2 -> x5, Pallas kernels: 6.72 us -> 9.99 us  [the longest x2 5.32 us: mix(): pl.pallas_call(functools.partial(mix_kernel, teams, replicas, tile_rows),...]
    pallas_call x3, Pallas kernels: 4.9 us -> 7.06 us  [products(): pl.pallas_call(functools.partial(product_kernel, teams, chips, wanted), o...]
    unnamed x8 -> x12, local copies, waits for them, and re-layouts: 1.64 us -> 2.86 us
    ppermute x19, starting transfers between devices: 19 us -> 20.2 us  [swap(): return lax.ppermute(array, AXES, route)]
  transfers between devices with their start and end apart: 20 -> 20, of which waited for: 12 -> 14; matrix products, arithmetic and copies ran while one was open for 0% -> 0% of each run, Pallas kernels for 4% -> 10%
where the time goes in v6:
time: 103 us; the launch traced here: 102 us
  waiting for transfers between devices  55.2 us (54%)
  starting transfers between devices  25.3 us (25%)
  Pallas kernels  18.9 us (18%)
  local copies, waits for them, and re-layouts  2.86 us (3%)
    ppermute x19, waiting for transfers between devices, swap(): return lax.ppermute(array, AXES, route)  54 us
    ppermute x19, starting transfers between devices, swap(): return lax.ppermute(array, AXES, route)  20.2 us
    pallas_call x3, Pallas kernels, products(): pl.pallas_call(functools.partial(product_kernel, teams, chips, wanted), o...  7.06 us
    pallas_call x2, Pallas kernels, mix(): pl.pallas_call(functools.partial(mix_kernel, teams, replicas, tile_rows),...  5.32 us
    all_to_all x1, starting transfers between devices, per_device(): own = lax.all_to_all(dealt, 'line', 0, 0)  5.13 us
    unnamed x12, local copies, waits for them, and re-layouts  2.86 us
    pallas_call x1, Pallas kernels, per_device(): pl.pallas_call(functools.partial(gather_kernel, teams, chips, tile_rows),...  2.44 us
  transfers between devices with their start and end apart: 20, of which 14 were waited for; matrix products, arithmetic and copies ran while one was open for 0% of the time, Pallas kernels for 10%

profile of v6, /device:TPU:0, one launch (start us, length us, event | category | flops | bytes accessed | tf_op | source)
XLA Modules:
  0.0 102.5 jit_solution(10314627906443659908)
XLA Ops:
  0.0 0.1 pad_add_fusion.place_ref
  0.1 1.2 %copy-done = bf16[2048,256]{1,0:T(8,128)(2,1)S(1)} copy-done((bf16[2048,256]{1,0:T(8,128)(2,1)S(1)}, bf16[2048,256]{1,0:T(8,128)(2,1)}, u32[]{:S(2)}) %copy-start) | copy-done | bytes 1048600
  1.3 1.0 copy-done.2
  2.3 0.7 copy-done.4
  2.9 0.6 prepare.1
  3.6 3.0 %collective-permute-start.3 = (bf16[1024,256]{1,0:T(8,128)(2,1)S(1)}, bf16[1024,256]{1,0:T(8,128)(2,1)S(1)}, u32[]{:S(2)}, u32[]{:S(2)}) collective-permute-start(bf16[1024,256]{1,0:T(8,128)(2,1)S(1)} %get-tuple-element.26), channel_id=1, source_target_pairs={{0,4},{1,5},{2,6},{3,7},{4,0},{5,1},{6,2},{7,3},{8,12},{9,13},{10,... | collective-permute-start | bytes 1572872 | tf_op jit(solution)/shard_map/ppermute | solution.py:192
  6.6 1.6 %collective-permute-start = (bf16[3,64,256]{2,1,0:T(8,128)(2,1)S(1)}, bf16[3,64,256]{2,1,0:T(8,128)(2,1)S(1)}, u32[]{:S(2)}, u32[]{:S(2)}) collective-permute-start(bf16[3,64,256]{2,1,0:T(8,128)(2,1)S(1)} %get-tuple-element.25), channel_id=1, source_target_pairs={{0,8},{1,9},{2,10},{3,11},{4,12},{5,13},{6,14},{7,15},{8,0},{9,1},... | collective-permute-start | bytes 294920 | tf_op jit(solution)/shard_map/ppermute | solution.py:192
  8.2 2.6 %collective-permute-start.1 = (bf16[3,64,256]{2,1,0:T(8,128)(2,1)S(1)}, bf16[3,64,256]{2,1,0:T(8,128)(2,1)S(1)}, u32[]{:S(2)}, u32[]{:S(2)}) collective-permute-start(bf16[3,64,256]{2,1,0:T(8,128)(2,1)S(1)} %get-tuple-element.25), channel_id=1, source_target_pairs={{0,16},{1,17},{2,18},{3,19},{4,20},{5,21},{6,22},{7,23},{8,24},{9,... | collective-permute-start | bytes 294920 | tf_op jit(solution)/shard_map/ppermute | solution.py:192
  10.7 0.2 collective-permute-start.2
  11.0 1.2 %collective-permute-done = bf16[3,64,256]{2,1,0:T(8,128)(2,1)S(1)} collective-permute-done((bf16[3,64,256]{2,1,0:T(8,128)(2,1)S(1)}, bf16[3,64,256]{2,1,0:T(8,128)(2,1)S(1)}, u32[]{:S(2)}, u32[]{:S(2)}) %collective-permute-start) | collective-permute-done | bytes 98336 | tf_op jit(solution)/shard_map/ppermute | solution.py:192
  12.2 6.1 %collective-permute-done.1 = bf16[3,64,256]{2,1,0:T(8,128)(2,1)S(1)} collective-permute-done((bf16[3,64,256]{2,1,0:T(8,128)(2,1)S(1)}, bf16[3,64,256]{2,1,0:T(8,128)(2,1)S(1)}, u32[]{:S(2)}, u32[]{:S(2)}) %collective-permute-start.1) | collective-permute-done | bytes 98336 | tf_op jit(solution)/shard_map/ppermute | solution.py:192
  18.3 0.1 pad_maximum_fusion.rest_0_
  18.4 0.1 collective-permute-done.3.across_ref
  18.5 1.6 %deal.1 = bf16[4,2,256,256]{3,2,1,0:T(8,128)(2,1)} custom-call(s32[2]{0:T(128)S(1)} %pad_add_fusion.place_ref, bf16[2048,256]{1,0:T(8,128)(2,1)S(1)} %copy-done.1, bf16[1024,256]{1,0:T(8,128)(2,1)S(1)} %collective-permute-done.3.across_ref), custom_call_target="tpu_custom_call" | custom-call | tf_op jit(solution)/shard_map/deal/pallas_call | solution.py:227
  20.1 5.1 %all-to-all-start = ((bf16[4,2,256,256]{3,2,1,0:T(8,128)(2,1)}), bf16[4,2,256,256]{3,2,1,0:T(8,128)(2,1)}, u32[]{:S(2)}, u32[]{:S(2)}) async-start(bf16[4,2,256,256]{3,2,1,0:T(8,128)(2,1)} %deal.1), calls=%async_computation | async-start | bytes 2097152 | tf_op jit(solution)/shard_map/all_to_all | solution.py:236
  25.3 2.4 %collective-permute-start.6 = (bf16[4,3,64,256]{3,2,1,0:T(8,128)(2,1)S(1)}, bf16[4,3,64,256]{3,2,1,0:T(8,128)(2,1)S(1)}, u32[]{:S(2)}, u32[]{:S(2)}) collective-permute-start(bf16[4,3,64,256]{3,2,1,0:T(8,128)(2,1)S(1)} %pad_maximum_fusion.rest_0_), channel_id=1, source_target_pairs={{0,6},{1,7},{2,4},{3,5},{4,2},{5,3},{6,0},{7,1},{8,14},{9,15},{10,... | collective-permute-start | bytes 1179656 | tf_op jit(solution)/shard_map/ppermute | solution.py:192
  27.7 0.5 collective-permute-start.4
  28.2 0.5 collective-permute-start.5
  28.7 9.5 %collective-permute-done.6.rest_3_ = bf16[4,3,64,256]{3,2,1,0:T(8,128)(2,1)S(1)} collective-permute-done((bf16[4,3,64,256]{3,2,1,0:T(8,128)(2,1)S(1)}, bf16[4,3,64,256]{3,2,1,0:T(8,128)(2,1)S(1)}, u32[]{:S(2)}, u32[]{:S(2)}) %collective-permute-start.6) | collective-permute-done | bytes 393248 | tf_op jit(solution)/shard_map/ppermute | solution.py:192
  38.2 6.0 %collective-permute-done.4.rest_1_ = bf16[4,3,64,256]{3,2,1,0:T(8,128)(2,1)S(1)} collective-permute-done((bf16[4,3,64,256]{3,2,1,0:T(8,128)(2,1)S(1)}, bf16[4,3,64,256]{3,2,1,0:T(8,128)(2,1)S(1)}, u32[]{:S(2)}, u32[]{:S(2)}) %collective-permute-start.4) | collective-permute-done | bytes 393248 | tf_op jit(solution)/shard_map/ppermute | solution.py:192
  44.3 0.1 collective-permute-done.5.rest_2_
  44.4 0.4 collective-permute-start.9
  44.8 1.2 %collective-permute-done.8.rest_5_ = bf16[4,3,64,256]{3,2,1,0:T(8,128)(2,1)S(1)} collective-permute-done((bf16[4,3,64,256]{3,2,1,0:T(8,128)(2,1)S(1)}, bf16[4,3,64,256]{3,2,1,0:T(8,128)(2,1)S(1)}, u32[]{:S(2)}, u32[]{:S(2)}) %collective-permute-start.8) | collective-permute-done | bytes 393248 | tf_op jit(solution)/shard_map/ppermute | solution.py:192
  46.0 0.6 collective-permute-done.9.rest_6_
  46.6 2.4 %gather.1.omega_ref = bf16[8,3,256,256]{3,2,1,0:T(8,128)(2,1)S(1)} custom-call(s32[2]{0:T(128)S(1)} %pad_add_fusion.place_ref, bf16[4,3,64,256]{3,2,1,0:T(8,128)(2,1)S(1)} %pad_maximum_fusion.rest_0_, bf16[4,3,64,256]{3,2,1,0:T(8,128)(2,1)S(1)} %collective-permute-done.4.rest_1_, bf16[4,3,64,256]{3,2,1,0:T(8,128)(2,1)S(1)} %collective-permute-done.5.rest_2_, ...), custom_call_target="tpu_custom_call" | custom-call | tf_op jit(solution)/shard_map/gather/pallas_call | solution.py:238
  49.0 1.2 %all-to-all-done.data_ref.rest_0_ = bf16[4,2,256,256]{3,2,1,0:T(8,128)(2,1)} async-done(((bf16[4,2,256,256]{3,2,1,0:T(8,128)(2,1)}), bf16[4,2,256,256]{3,2,1,0:T(8,128)(2,1)}, u32[]{:S(2)}, u32[]{:S(2)}) %all-to-all-start) | async-done | bytes 1048608 | tf_op jit(solution)/shard_map/all_to_all | solution.py:236
  50.2 3.0 %mix.2 = (bf16[8,256,256]{2,1,0:T(8,128)(2,1)S(1)}, bf16[8,128,512]{2,1,0:T(8,128)(2,1)S(1)}) custom-call(s32[2]{0:T(128)S(1)} %pad_add_fusion.place_ref, s32[1,5]{1,0:T(1,128)S(1)} %copy-done.5, bf16[4,2,256,256]{3,2,1,0:T(8,128)(2,1)} %all-to-all-done.data_ref.rest_0_, bf16[8,3,256,256]{3,2,1,0:T(8,128)(2,1)S(1)} %gather.1.omega_ref), custom_call_target="tpu_custom_call" | custom-call | tf_op jit(solution)/shard_map/mix/pallas_call | solution.py:250
  53.2 2.3 %mix.3 = (bf16[8,256,256]{2,1,0:T(8,128)(2,1)S(1)}, bf16[8,128,512]{2,1,0:T(8,128)(2,1)S(1)}) custom-call(s32[2]{0:T(128)S(1)} %pad_add_fusion.place_ref, s32[1,5]{1,0:T(1,128)S(1)} %copy-done.5, bf16[4,2,256,256]{3,2,1,0:T(8,128)(2,1)S(1)} %collective-permute-done.11.data_ref.rest_3_, bf16[8,3,256,256]{3,2,1,0:T(8,128)(2,1)S(1)} %gather.1.omega_ref), custom_call_target="tpu_custom_call" | custom-call | tf_op jit(solution)/shard_map/mix/pallas_call | solution.py:250
  55.6 2.1 %products.5 = bf16[2,2,5,64,256]{4,3,2,1,0:T(8,128)(2,1)S(1)} custom-call(s32[2]{0:T(128)S(1)} %pad_add_fusion.place_ref, s32[1,5]{1,0:T(1,128)S(1)} %copy-done.5, bf16[4,2,256,256]{3,2,1,0:T(8,128)(2,1)} %all-to-all-done.data_ref.rest_0_, bf16[8,256,256]{2,1,0:T(8,128)(2,1)S(1)} %get-tuple-element.31.rest_1_, ...), custom_call_target="tpu_custom_call" | custom-call | tf_op jit(solution)/shard_map/products/pallas_call | solution.py:272
  57.7 1.6 %collective-permute-start.15 = (bf16[2,2,5,64,256]{4,3,2,1,0:T(8,128)(2,1)S(1)}, bf16[2,2,5,64,256]{4,3,2,1,0:T(8,128)(2,1)S(1)}, u32[]{:S(2)}, u32[]{:S(2)}) collective-permute-start(bf16[2,2,5,64,256]{4,3,2,1,0:T(8,128)(2,1)S(1)} %products.5), channel_id=1, source_target_pairs={{0,4},{1,5},{2,6},{3,7},{4,0},{5,1},{6,2},{7,3},{8,12},{9,13},{10,... | collective-permute-start | bytes 1966088 | tf_op jit(solution)/shard_map/ppermute | solution.py:192
  59.3 2.8 %products.3 = (f32[2,2,5,64,256]{4,3,2,1,0:T(8,128)S(1)}, bf16[2,2,5,64,256]{4,3,2,1,0:T(8,128)(2,1)S(1)}) custom-call(s32[2]{0:T(128)S(1)} %pad_add_fusion.place_ref, s32[1,5]{1,0:T(1,128)S(1)} %copy-done.5, bf16[4,2,256,256]{3,2,1,0:T(8,128)(2,1)} %all-to-all-done.data_ref.rest_0_, bf16[8,256,256]{2,1,0:T(8,128)(2,1)S(1)} %get-tuple-element.31.rest_1_, ...), custom_call_target="tpu_custom_call" | custom-call | tf_op jit(solution)/shard_map/products/pallas_call | solution.py:272
  62.1 1.6 %collective-permute-start.12 = (bf16[2,2,5,64,256]{4,3,2,1,0:T(8,128)(2,1)S(1)}, bf16[2,2,5,64,256]{4,3,2,1,0:T(8,128)(2,1)S(1)}, u32[]{:S(2)}, u32[]{:S(2)}) collective-permute-start(bf16[2,2,5,64,256]{4,3,2,1,0:T(8,128)(2,1)S(1)} %get-tuple-element.36), channel_id=1, source_target_pairs={{0,2},{1,3},{2,0},{3,1},{4,6},{5,7},{6,4},{7,5},{8,10},{9,11},{10,... | collective-permute-start | bytes 1966088 | tf_op jit(solution)/shard_map/ppermute | solution.py:192
  63.7 2.1 %products.4.refs_0_ = f32[2,2,5,64,256]{4,3,2,1,0:T(8,128)S(1)} custom-call(s32[2]{0:T(128)S(1)} %pad_add_fusion.place_ref, s32[1,5]{1,0:T(1,128)S(1)} %copy-done.5, bf16[4,2,256,256]{3,2,1,0:T(8,128)(2,1)} %all-to-all-done.data_ref.rest_0_, bf16[8,256,256]{2,1,0:T(8,128)(2,1)S(1)} %get-tuple-element.31.rest_1_, ...), custom_call_target="tpu_custom_call" | custom-call | tf_op jit(solution)/shard_map/products/pallas_call | solution.py:272
  65.8 9.1 %collective-permute-done.15.refs_1_ = bf16[2,2,5,64,256]{4,3,2,1,0:T(8,128)(2,1)S(1)} collective-permute-done((bf16[2,2,5,64,256]{4,3,2,1,0:T(8,128)(2,1)S(1)}, bf16[2,2,5,64,256]{4,3,2,1,0:T(8,128)(2,1)S(1)}, u32[]{:S(2)}, u32[]{:S(2)}) %collective-permute-start.15) | collective-permute-done | bytes 655392 | tf_op jit(solution)/shard_map/ppermute | solution.py:192
  74.9 0.1 add.16
  75.0 1.6 %collective-permute-start.16 = (bf16[2,5,64,256]{3,2,1,0:T(8,128)(2,1)S(1)}, bf16[2,5,64,256]{3,2,1,0:T(8,128)(2,1)S(1)}, u32[]{:S(2)}, u32[]{:S(2)}) collective-permute-start(bf16[2,5,64,256]{3,2,1,0:T(8,128)(2,1)S(1)} %get-tuple-element.42), channel_id=1, source_target_pairs={{0,2},{1,3},{2,0},{3,1},{4,6},{5,7},{6,4},{7,5},{8,10},{9,11},{10,... | collective-permute-start | bytes 983048 | tf_op jit(solution)/shard_map/ppermute | solution.py:192
  76.6 3.1 %collective-permute-done.12.refs_1_ = bf16[2,2,5,64,256]{4,3,2,1,0:T(8,128)(2,1)S(1)} collective-permute-done((bf16[2,2,5,64,256]{4,3,2,1,0:T(8,128)(2,1)S(1)}, bf16[2,2,5,64,256]{4,3,2,1,0:T(8,128)(2,1)S(1)}, u32[]{:S(2)}, u32[]{:S(2)}) %collective-permute-start.12) | collective-permute-done | bytes 655392 | tf_op jit(solution)/shard_map/ppermute | solution.py:192
  79.7 0.1 add.14
  79.8 0.5 collective-permute-start.13
  80.3 5.7 %collective-permute-done.16.refs_1_ = bf16[2,5,64,256]{3,2,1,0:T(8,128)(2,1)S(1)} collective-permute-done((bf16[2,5,64,256]{3,2,1,0:T(8,128)(2,1)S(1)}, bf16[2,5,64,256]{3,2,1,0:T(8,128)(2,1)S(1)}, u32[]{:S(2)}, u32[]{:S(2)}) %collective-permute-start.16) | collective-permute-done | bytes 327712 | tf_op jit(solution)/shard_map/ppermute | solution.py:192
  86.0 0.1 add.17
  86.1 1.6 %collective-permute-start.17 = (bf16[5,64,256]{2,1,0:T(8,128)(2,1)S(1)}, bf16[5,64,256]{2,1,0:T(8,128)(2,1)S(1)}, u32[]{:S(2)}, u32[]{:S(2)}) collective-permute-start(bf16[5,64,256]{2,1,0:T(8,128)(2,1)S(1)} %get-tuple-element.43), channel_id=1, source_target_pairs={{0,16},{1,17},{2,18},{3,19},{4,20},{5,21},{6,22},{7,23},{8,24},{9,... | collective-permute-start | bytes 491528 | tf_op jit(solution)/shard_map/ppermute | solution.py:192
  87.7 1.5 %collective-permute-start.18 = (bf16[5,64,256]{2,1,0:T(8,128)(2,1)S(1)}, bf16[5,64,256]{2,1,0:T(8,128)(2,1)S(1)}, u32[]{:S(2)}, u32[]{:S(2)}) collective-permute-start(bf16[5,64,256]{2,1,0:T(8,128)(2,1)S(1)} %get-tuple-element.44), channel_id=1, source_target_pairs={{0,24},{1,25},{2,26},{3,27},{4,28},{5,29},{6,30},{7,31},{8,16},{9,... | collective-permute-start | bytes 491528 | tf_op jit(solution)/shard_map/ppermute | solution.py:192
  89.2 0.1 add.15
  89.2 0.6 collective-permute-start.14
  89.8 9.8 %collective-permute-done.17.rest_2_ = bf16[5,64,256]{2,1,0:T(8,128)(2,1)S(1)} collective-permute-done((bf16[5,64,256]{2,1,0:T(8,128)(2,1)S(1)}, bf16[5,64,256]{2,1,0:T(8,128)(2,1)S(1)}, u32[]{:S(2)}, u32[]{:S(2)}) %collective-permute-start.17) | collective-permute-done | bytes 163872 | tf_op jit(solution)/shard_map/ppermute | solution.py:192
  99.6 1.4 %collective-permute-done.14.rest_1_ = bf16[5,64,256]{2,1,0:T(8,128)(2,1)S(1)} collective-permute-done((bf16[5,64,256]{2,1,0:T(8,128)(2,1)S(1)}, bf16[5,64,256]{2,1,0:T(8,128)(2,1)S(1)}, u32[]{:S(2)}, u32[]{:S(2)}) %collective-permute-start.14) | collective-permute-done | bytes 163872 | tf_op jit(solution)/shard_map/ppermute | solution.py:192
  101.0 1.5 %update.1 = f32[1,5,64,256]{3,2,1,0:T(8,128)} custom-call(s32[2]{0:T(128)S(1)} %pad_add_fusion.place_ref, s32[1,5]{1,0:T(1,128)S(1)} %copy-done.5, f32[1,5,64,256]{3,2,1,0:T(8,128)S(1)} %copy-done.3, f32[5,64,256]{2,1,0:T(8,128)S(1)} %get-tuple-element.39.rest_0_, bf16[5,64,256]{2,1,0:T(8,128)(2,1)S(1)} %collective-permute-done.14.rest_1_, ...), custom_call_target="tpu_custom_call" | custom-call | tf_op jit(solution)/shard_map/update/pallas_call | solution.py:328
  (19 shorter events, 0.1 us)
Async XLA Ops:
  0.1 1.2 %copy-start = (bf16[2048,256]{1,0:T(8,128)(2,1)S(1)}, bf16[2048,256]{1,0:T(8,128)(2,1)}, u32[]{:S(2)}) copy-start(bf16[2048,256]{1,0:T(8,128)(2,1)} %signals_ref.3) | copy-start | bytes 3145732
  1.3 1.0 copy-start.2
  2.3 0.7 copy-start.4
  2.9 15.6 %copy-start.1 = (bf16[2048,256]{1,0:T(8,128)(2,1)S(1)}, bf16[2048,256]{1,0:T(8,128)(2,1)}, u32[]{:S(2)}) copy-start(bf16[2048,256]{1,0:T(8,128)(2,1)} %signals_ref.3) | copy-start | bytes 3145732
  3.6 14.9 %collective-permute-start.3 = (bf16[1024,256]{1,0:T(8,128)(2,1)S(1)}, bf16[1024,256]{1,0:T(8,128)(2,1)S(1)}, u32[]{:S(2)}, u32[]{:S(2)}) collective-permute-start(bf16[1024,256]{1,0:T(8,128)(2,1)S(1)} %get-tuple-element.26), channel_id=1, source_target_pairs={{0,4},{1,5},{2,6},{3,7},{4,0},{5,1},{6,2},{7,3},{8,12},{9,13},{10,... | collective-permute-start | bytes 1572872 | tf_op jit(solution)/shard_map/ppermute | solution.py:192
  6.6 5.6 %collective-permute-start = (bf16[3,64,256]{2,1,0:T(8,128)(2,1)S(1)}, bf16[3,64,256]{2,1,0:T(8,128)(2,1)S(1)}, u32[]{:S(2)}, u32[]{:S(2)}) collective-permute-start(bf16[3,64,256]{2,1,0:T(8,128)(2,1)S(1)} %get-tuple-element.25), channel_id=1, source_target_pairs={{0,8},{1,9},{2,10},{3,11},{4,12},{5,13},{6,14},{7,15},{8,0},{9,1},... | collective-permute-start | bytes 294920 | tf_op jit(solution)/shard_map/ppermute | solution.py:192
  8.2 10.1 %collective-permute-start.1 = (bf16[3,64,256]{2,1,0:T(8,128)(2,1)S(1)}, bf16[3,64,256]{2,1,0:T(8,128)(2,1)S(1)}, u32[]{:S(2)}, u32[]{:S(2)}) collective-permute-start(bf16[3,64,256]{2,1,0:T(8,128)(2,1)S(1)} %get-tuple-element.25), channel_id=1, source_target_pairs={{0,16},{1,17},{2,18},{3,19},{4,20},{5,21},{6,22},{7,23},{8,24},{9,... | collective-permute-start | bytes 294920 | tf_op jit(solution)/shard_map/ppermute | solution.py:192
  10.7 7.6 %collective-permute-start.2 = (bf16[3,64,256]{2,1,0:T(8,128)(2,1)S(1)}, bf16[3,64,256]{2,1,0:T(8,128)(2,1)S(1)}, u32[]{:S(2)}, u32[]{:S(2)}) collective-permute-start(bf16[3,64,256]{2,1,0:T(8,128)(2,1)S(1)} %get-tuple-element.25), channel_id=1, source_target_pairs={{0,24},{1,25},{2,26},{3,27},{4,28},{5,29},{6,30},{7,31},{8,16},{9,... | collective-permute-start | bytes 294920 | tf_op jit(solution)/shard_map/ppermute | solution.py:192
  20.1 30.1 %all-to-all-start = ((bf16[4,2,256,256]{3,2,1,0:T(8,128)(2,1)}), bf16[4,2,256,256]{3,2,1,0:T(8,128)(2,1)}, u32[]{:S(2)}, u32[]{:S(2)}) async-start(bf16[4,2,256,256]{3,2,1,0:T(8,128)(2,1)} %deal.1), calls=%async_computation | async-start | bytes 2097152 | tf_op jit(solution)/shard_map/all_to_all | solution.py:236
  25.2 25.0 %copy-start.5 = (s32[1,5]{1,0:T(1,128)S(1)}, s32[1,5]{1,0:T(1,128)}, u32[]{:S(2)}) copy-start(s32[1,5]{1,0:T(1,128)} %pattern_ref.13) | copy-start | bytes 64
  25.3 13.0 %collective-permute-start.6 = (bf16[4,3,64,256]{3,2,1,0:T(8,128)(2,1)S(1)}, bf16[4,3,64,256]{3,2,1,0:T(8,128)(2,1)S(1)}, u32[]{:S(2)}, u32[]{:S(2)}) collective-permute-start(bf16[4,3,64,256]{3,2,1,0:T(8,128)(2,1)S(1)} %pad_maximum_fusion.rest_0_), channel_id=1, source_target_pairs={{0,6},{1,7},{2,4},{3,5},{4,2},{5,3},{6,0},{7,1},{8,14},{9,15},{10,... | collective-permute-start | bytes 1179656 | tf_op jit(solution)/shard_map/ppermute | solution.py:192
  27.7 16.6 %collective-permute-start.4 = (bf16[4,3,64,256]{3,2,1,0:T(8,128)(2,1)S(1)}, bf16[4,3,64,256]{3,2,1,0:T(8,128)(2,1)S(1)}, u32[]{:S(2)}, u32[]{:S(2)}) collective-permute-start(bf16[4,3,64,256]{3,2,1,0:T(8,128)(2,1)S(1)} %pad_maximum_fusion.rest_0_), channel_id=1, source_target_pairs={{0,2},{1,3},{2,0},{3,1},{4,6},{5,7},{6,4},{7,5},{8,10},{9,11},{10,... | collective-permute-start | bytes 1179656 | tf_op jit(solution)/shard_map/ppermute | solution.py:192
  28.2 16.2 %collective-permute-start.5 = (bf16[4,3,64,256]{3,2,1,0:T(8,128)(2,1)S(1)}, bf16[4,3,64,256]{3,2,1,0:T(8,128)(2,1)S(1)}, u32[]{:S(2)}, u32[]{:S(2)}) collective-permute-start(bf16[4,3,64,256]{3,2,1,0:T(8,128)(2,1)S(1)} %pad_maximum_fusion.rest_0_), channel_id=1, source_target_pairs={{0,4},{1,5},{2,6},{3,7},{4,0},{5,1},{6,2},{7,3},{8,12},{9,13},{10,... | collective-permute-start | bytes 1179656 | tf_op jit(solution)/shard_map/ppermute | solution.py:192
  28.7 16.1 %collective-permute-start.7 = (bf16[4,3,64,256]{3,2,1,0:T(8,128)(2,1)S(1)}, bf16[4,3,64,256]{3,2,1,0:T(8,128)(2,1)S(1)}, u32[]{:S(2)}, u32[]{:S(2)}) collective-permute-start(bf16[4,3,64,256]{3,2,1,0:T(8,128)(2,1)S(1)} %pad_maximum_fusion.rest_0_), channel_id=1, source_target_pairs={{0,1},{1,0},{2,3},{3,2},{4,5},{5,4},{6,7},{7,6},{8,9},{9,8},{10,11... | collective-permute-start | bytes 1179656 | tf_op jit(solution)/shard_map/ppermute | solution.py:192
  38.2 6.6 %collective-permute-start.10 = (bf16[4,3,64,256]{3,2,1,0:T(8,128)(2,1)S(1)}, bf16[4,3,64,256]{3,2,1,0:T(8,128)(2,1)S(1)}, u32[]{:S(2)}, u32[]{:S(2)}) collective-permute-start(bf16[4,3,64,256]{3,2,1,0:T(8,128)(2,1)S(1)} %collective-permute-done.6.rest_3_), channel_id=1, source_target_pairs={{0,1},{1,0},{2,3},{3,2},{4,5},{5,4},{6,7},{7,6},{8,9},{9,8},{10,11... | collective-permute-start | bytes 1179656 | tf_op jit(solution)/shard_map/ppermute | solution.py:192
  44.3 1.7 %collective-permute-start.8 = (bf16[4,3,64,256]{3,2,1,0:T(8,128)(2,1)S(1)}, bf16[4,3,64,256]{3,2,1,0:T(8,128)(2,1)S(1)}, u32[]{:S(2)}, u32[]{:S(2)}) collective-permute-start(bf16[4,3,64,256]{3,2,1,0:T(8,128)(2,1)S(1)} %collective-permute-done.4.rest_1_), channel_id=1, source_target_pairs={{0,1},{1,0},{2,3},{3,2},{4,5},{5,4},{6,7},{7,6},{8,9},{9,8},{10,11... | collective-permute-start | bytes 1179656 | tf_op jit(solution)/shard_map/ppermute | solution.py:192
  44.4 2.2 %collective-permute-start.9 = (bf16[4,3,64,256]{3,2,1,0:T(8,128)(2,1)S(1)}, bf16[4,3,64,256]{3,2,1,0:T(8,128)(2,1)S(1)}, u32[]{:S(2)}, u32[]{:S(2)}) collective-permute-start(bf16[4,3,64,256]{3,2,1,0:T(8,128)(2,1)S(1)} %collective-permute-done.5.rest_2_), channel_id=1, source_target_pairs={{0,1},{1,0},{2,3},{3,2},{4,5},{5,4},{6,7},{7,6},{8,9},{9,8},{10,11... | collective-permute-start | bytes 1179656 | tf_op jit(solution)/shard_map/ppermute | solution.py:192
  50.2 3.0 %collective-permute-start.11 = (bf16[4,2,256,256]{3,2,1,0:T(8,128)(2,1)}, bf16[4,2,256,256]{3,2,1,0:T(8,128)(2,1)S(1)}, u32[]{:S(2)}, u32[]{:S(2)}) collective-permute-start(bf16[4,2,256,256]{3,2,1,0:T(8,128)(2,1)} %all-to-all-done.data_ref.rest_0_), channel_id=1, source_target_pairs={{0,1},{1,0},{2,3},{3,2},{4,5},{5,4},{6,7},{7,6},{8,9},{9,8},{10,11... | collective-permute-start | bytes 3145736 | tf_op jit(solution)/shard_map/ppermute | solution.py:192
  57.7 17.2 %collective-permute-start.15 = (bf16[2,2,5,64,256]{4,3,2,1,0:T(8,128)(2,1)S(1)}, bf16[2,2,5,64,256]{4,3,2,1,0:T(8,128)(2,1)S(1)}, u32[]{:S(2)}, u32[]{:S(2)}) collective-permute-start(bf16[2,2,5,64,256]{4,3,2,1,0:T(8,128)(2,1)S(1)} %products.5), channel_id=1, source_target_pairs={{0,4},{1,5},{2,6},{3,7},{4,0},{5,1},{6,2},{7,3},{8,12},{9,13},{10,... | collective-permute-start | bytes 1966088 | tf_op jit(solution)/shard_map/ppermute | solution.py:192
  62.1 17.6 %collective-permute-start.12 = (bf16[2,2,5,64,256]{4,3,2,1,0:T(8,128)(2,1)S(1)}, bf16[2,2,5,64,256]{4,3,2,1,0:T(8,128)(2,1)S(1)}, u32[]{:S(2)}, u32[]{:S(2)}) collective-permute-start(bf16[2,2,5,64,256]{4,3,2,1,0:T(8,128)(2,1)S(1)} %get-tuple-element.36), channel_id=1, source_target_pairs={{0,2},{1,3},{2,0},{3,1},{4,6},{5,7},{6,4},{7,5},{8,10},{9,11},{10,... | collective-permute-start | bytes 1966088 | tf_op jit(solution)/shard_map/ppermute | solution.py:192
  75.0 11.0 %collective-permute-start.16 = (bf16[2,5,64,256]{3,2,1,0:T(8,128)(2,1)S(1)}, bf16[2,5,64,256]{3,2,1,0:T(8,128)(2,1)S(1)}, u32[]{:S(2)}, u32[]{:S(2)}) collective-permute-start(bf16[2,5,64,256]{3,2,1,0:T(8,128)(2,1)S(1)} %get-tuple-element.42), channel_id=1, source_target_pairs={{0,2},{1,3},{2,0},{3,1},{4,6},{5,7},{6,4},{7,5},{8,10},{9,11},{10,... | collective-permute-start | bytes 983048 | tf_op jit(solution)/shard_map/ppermute | solution.py:192
  79.8 21.2 %copy-start.3 = (f32[1,5,64,256]{3,2,1,0:T(8,128)S(1)}, f32[1,5,64,256]{3,2,1,0:T(8,128)}, u32[]{:S(2)}) copy-start(f32[1,5,64,256]{3,2,1,0:T(8,128)} %omega_ref.3) | copy-start | bytes 983044
  79.8 9.3 %collective-permute-start.13 = (bf16[2,5,64,256]{3,2,1,0:T(8,128)(2,1)S(1)}, bf16[2,5,64,256]{3,2,1,0:T(8,128)(2,1)S(1)}, u32[]{:S(2)}, u32[]{:S(2)}) collective-permute-start(bf16[2,5,64,256]{3,2,1,0:T(8,128)(2,1)S(1)} %get-tuple-element.38), channel_id=1, source_target_pairs={{0,4},{1,5},{2,6},{3,7},{4,0},{5,1},{6,2},{7,3},{8,12},{9,13},{10,... | collective-permute-start | bytes 983048 | tf_op jit(solution)/shard_map/ppermute | solution.py:192
  86.1 13.5 %collective-permute-start.17 = (bf16[5,64,256]{2,1,0:T(8,128)(2,1)S(1)}, bf16[5,64,256]{2,1,0:T(8,128)(2,1)S(1)}, u32[]{:S(2)}, u32[]{:S(2)}) collective-permute-start(bf16[5,64,256]{2,1,0:T(8,128)(2,1)S(1)} %get-tuple-element.43), channel_id=1, source_target_pairs={{0,16},{1,17},{2,18},{3,19},{4,20},{5,21},{6,22},{7,23},{8,24},{9,... | collective-permute-start | bytes 491528 | tf_op jit(solution)/shard_map/ppermute | solution.py:192
  87.7 11.9 %collective-permute-start.18 = (bf16[5,64,256]{2,1,0:T(8,128)(2,1)S(1)}, bf16[5,64,256]{2,1,0:T(8,128)(2,1)S(1)}, u32[]{:S(2)}, u32[]{:S(2)}) collective-permute-start(bf16[5,64,256]{2,1,0:T(8,128)(2,1)S(1)} %get-tuple-element.44), channel_id=1, source_target_pairs={{0,24},{1,25},{2,26},{3,27},{4,28},{5,29},{6,30},{7,31},{8,16},{9,... | collective-permute-start | bytes 491528 | tf_op jit(solution)/shard_map/ppermute | solution.py:192
  89.2 11.8 %collective-permute-start.14 = (bf16[5,64,256]{2,1,0:T(8,128)(2,1)S(1)}, bf16[5,64,256]{2,1,0:T(8,128)(2,1)S(1)}, u32[]{:S(2)}, u32[]{:S(2)}) collective-permute-start(bf16[5,64,256]{2,1,0:T(8,128)(2,1)S(1)} %get-tuple-element.40), channel_id=1, source_target_pairs={{0,8},{1,9},{2,10},{3,11},{4,12},{5,13},{6,14},{7,15},{8,0},{9,1},... | collective-permute-start | bytes 491528 | tf_op jit(solution)/shard_map/ppermute | solution.py:192

commit v7 on v6

--- a/solution.py
+++ b/solution.py
@@ -17,11 +17,12 @@
 
 VMEM = pl.BlockSpec(memory_space=pltpu.VMEM)
 ANY = pl.BlockSpec(memory_space=pl.ANY)
+HBM = pl.BlockSpec(memory_space=pltpu.HBM)
 SMEM = pl.BlockSpec(memory_space=pltpu.SMEM)
 
 
-def stored_offsets(pattern_ref, team, teams):
-    drawn = [lax.rem(pattern_ref[0, k] - team + teams, teams) for k in range(1, 5)]
+def stored_offsets(place_ref, teams):
+    drawn = [lax.rem(place_ref[2 + k] - place_ref[0] + teams, teams) for k in range(1, 5)]
     a = functools.reduce(jnp.minimum, drawn)
     b = functools.reduce(jnp.minimum, [jnp.where(d == a, teams, d) for d in drawn])
     offsets = [jnp.int32(0), a, b, teams - b, teams - a]
@@ -31,25 +32,17 @@
     return offsets, slots
 
 
-def prepare_kernel(teams, place_ref, pattern_ref, omega_ref, signals_ref, upper_ref, across_ref, sem):
-    team = place_ref[0]
-    rows = across_ref.shape[0]
-    first = pl.multiple_of((lax.rem(team, LOW) ^ 1) * rows, rows)
-    copy = pltpu.make_async_copy(signals_ref.at[pl.ds(first, rows)], across_ref, sem)
-    copy.start()
-    _, slots = stored_offsets(pattern_ref, team, teams)
+def prepare_kernel(teams, place_ref, omega_ref, out_ref):
+    _, slots = stored_offsets(place_ref, teams)
     for k in range(3):
-        upper_ref[k] = omega_ref[0, slots[k]].astype(BF16)
-    copy.wait()
-
-
-def deal_kernel(place_ref, signals_ref, across_ref, out_ref, sems):
-    rows = across_ref.shape[0]
-    first = pl.multiple_of(lax.rem(place_ref[0], LOW) * rows, rows)
-    sources = [signals_ref.at[pl.ds(first, rows)], across_ref]
+        out_ref[k] = omega_ref[0, slots[k]].astype(BF16)
+
+
+def deal_kernel(kept_ref, across_ref, out_ref, sems):
+    shape = (out_ref.shape[0],) + out_ref.shape[2:]
     copies = [
-        pltpu.make_async_copy(source.reshape(out_ref.shape[0], *out_ref.shape[2:]), out_ref.at[:, n], sems.at[n])
-        for n, source in enumerate(sources)
+        pltpu.make_async_copy(source.reshape(shape), out_ref.at[:, n], sems.at[n])
+        for n, source in enumerate([kept_ref, across_ref])
     ]
     for copy in copies:
         copy.start()
@@ -94,13 +87,13 @@
     return data_ref[lax.div(c, LOW), lax.rem(c, LOW) ^ low]
 
 
-def mix_kernel(teams, replicas, tile_rows, place_ref, pattern_ref, data_ref, omega_ref, mixed_ref, left_ref, flip_ref):
+def mix_kernel(teams, replicas, tile_rows, place_ref, data_ref, omega_ref, right_ref, left_ref, flip_ref):
     chips = replicas // 2
     team, replica = place_ref[0], place_ref[1]
     core, chip = lax.rem(replica, 2), lax.div(replica, 2)
     low = lax.rem(team, LOW)
-    offsets, _ = stored_offsets(pattern_ref, team, teams)
-    times = mixed_ref.shape[1]
+    offsets, _ = stored_offsets(place_ref, teams)
+    times = right_ref.shape[1] // 2
 
     def mix(i, carry):
         total = None
@@ -110,8 +103,10 @@
             term = lax.dot_general(block(data_ref, low, c), right, dims, preferred_element_type=F32)
             total = term if total is None else total + term
         mixed = total.astype(BF16)
-        mixed_ref[i] = mixed
-        for n, array in enumerate([mixed, block(data_ref, low, i)]):
+        data = block(data_ref, low, i)
+        right_ref[i, :times] = data
+        right_ref[i, times:] = mixed
+        for n, array in enumerate([mixed, data]):
             flip_ref[n] = array.T
             for m in range(chips):
                 row = (2 * (chip ^ m) + core) * tile_rows
@@ -123,20 +118,18 @@
     lax.fori_loop(0, teams, mix, 0, unroll=teams <= 8)
 
 
-def product_kernel(teams, chips, wanted, place_ref, pattern_ref, *rest):
-    cores, outs = [rest[:3], rest[3:6]], rest[6:]
+def product_kernel(teams, chips, wanted, place_ref, *rest):
+    rights, lefts, outs = rest[0:4:2], rest[1:4:2], rest[4:]
     team = place_ref[0]
     high, low = lax.div(team, LOW), lax.rem(team, LOW)
-    offsets, _ = stored_offsets(pattern_ref, team, teams)
-    tile_rows = cores[0][2].shape[1] // chips
+    offsets, _ = stored_offsets(place_ref, teams)
+    tile_rows = lefts[0].shape[1] // chips
     for mz, mx in sorted({key[:2] for key in wanted}):
         i = (high ^ mz) * LOW + (low ^ mx)
         for k, offset in enumerate(offsets):
             c = lax.rem(i + offset, teams)
-            left = jnp.concatenate([left_ref[i] for _, _, left_ref in cores], axis=1)
-            right = jnp.concatenate(
-                [part for data_ref, mixed_ref, _ in cores for part in (block(data_ref, low, c), mixed_ref[c])], axis=0
-            )
+            left = jnp.concatenate([ref[i] for ref in lefts], axis=1)
+            right = jnp.concatenate([ref[c] for ref in rights], axis=0)
             product = lax.dot_general(left, right, NN, preferred_element_type=F32)
             for m in range(chips):
                 if (mz, mx, m) in wanted:
@@ -154,9 +147,9 @@
         out[...] = total.astype(out.dtype)
 
 
-def update_kernel(teams, scale, place_ref, pattern_ref, omega_ref, *rest):
+def update_kernel(teams, scale, place_ref, omega_ref, *rest):
     parts, out_ref = rest[:-1], rest[-1]
-    _, slots = stored_offsets(pattern_ref, place_ref[0], teams)
+    _, slots = stored_offsets(place_ref, teams)
     rows, width = out_ref.shape[2:]
     first = place_ref[1] * rows
     row_ids = first + lax.broadcasted_iota(jnp.int32, (rows, width), 0)
@@ -181,7 +174,7 @@
     chips = replicas // 2
     slots, tile_rows, width = omega.shape[1:]
     times = signals.shape[0] // teams
-    place = jnp.stack([lax.axis_index(BLK), lax.axis_index(REP)]).astype(jnp.int32)
+    place = jnp.concatenate([jnp.stack([lax.axis_index(BLK), lax.axis_index(REP)]).astype(jnp.int32), pattern[0]])
 
     def swap(array, blk_mask, rep_mask):
         route = [
@@ -207,32 +200,29 @@
     def along_line(arrays):
         return [swap(array, m * LOW, 0) if m else array for m, array in enumerate(arrays)]
 
-    upper, across = pl.pallas_call(
+    low = lax.axis_index("low")
+    across = swap(lax.dynamic_slice_in_dim(signals, (low ^ 1) * count * times, count * times, 0), 1, 0)
+    upper = pl.pallas_call(
         functools.partial(prepare_kernel, teams),
-        out_shape=[
-            jax.ShapeDtypeStruct((3, tile_rows, width), BF16),
-            jax.ShapeDtypeStruct((count * times, width), BF16),
-        ],
-        in_specs=[SMEM, SMEM, VMEM, ANY],
-        out_specs=[VMEM, VMEM],
-        scratch_shapes=[pltpu.SemaphoreType.DMA],
+        out_shape=jax.ShapeDtypeStruct((3, tile_rows, width), BF16),
+        in_specs=[SMEM, VMEM],
+        out_specs=VMEM,
         compiler_params=small,
         name="prepare",
-    )(place, pattern, omega, signals)
-
+    )(place, omega)
     line = jnp.stack(along_line([upper] * count))
-    across = swap(across, 1, 0)
-    line, across = lax.optimization_barrier((line, across))
+    line, across, signals = lax.optimization_barrier((line, across, signals))
+    kept = lax.dynamic_slice_in_dim(signals, low * count * times, count * times, 0)
     weights = across_plane([line] * planes)
     dealt = pl.pallas_call(
         deal_kernel,
         out_shape=jax.ShapeDtypeStruct((count, LOW, times, width), BF16),
-        in_specs=[SMEM, ANY, VMEM],
-        out_specs=VMEM,
+        in_specs=[VMEM, VMEM],
+        out_specs=HBM,
         scratch_shapes=[pltpu.SemaphoreType.DMA((2,))],
         compiler_params=small,
         name="deal",
-    )(place, signals, across)
+    )(kept, across)
     own = lax.all_to_all(dealt, "line", 0, 0)
     weights += [swap(array, 0, 1) for array in weights]
     tiles = pl.pallas_call(
@@ -250,18 +240,18 @@
         return pl.pallas_call(
             functools.partial(mix_kernel, teams, replicas, tile_rows),
             out_shape=[
-                jax.ShapeDtypeStruct((teams, times, width), BF16),
+                jax.ShapeDtypeStruct((teams, 2 * times, width), BF16),
                 jax.ShapeDtypeStruct((teams, chips * tile_rows, 2 * times), BF16),
             ],
-            in_specs=[SMEM, SMEM, VMEM, VMEM],
+            in_specs=[SMEM, VMEM, VMEM],
             out_specs=[VMEM, VMEM],
             scratch_shapes=[pltpu.VMEM((2, width, times), BF16)],
             compiler_params=small,
             name="mix",
-        )(place, pattern, data, tiles)
+        )(place, data, tiles)
 
     other = swap(own, 0, 1)
-    cores = [own, *mix(own), other, *mix(other)]
+    cores = [*mix(own), *mix(other)]
 
     tile = (slots, tile_rows, width)
 
@@ -272,11 +262,11 @@
         return pl.pallas_call(
             functools.partial(product_kernel, teams, chips, wanted),
             out_shape=shapes,
-            in_specs=[SMEM, SMEM] + [VMEM] * 6,
+            in_specs=[SMEM] + [VMEM] * 4,
             out_specs=[VMEM] * len(shapes),
             compiler_params=small,
             name="products",
-        )(place, pattern, *cores)
+        )(place, *cores)
 
     def add(groups, shapes, *arrays):
         return pl.pallas_call(
@@ -324,15 +314,15 @@
     )
     sums = along_line(list(inner_sums) + list(outer_sums))
 
-    scale = 1.0 / (2.0 * signals.shape[0] * replicas)
+    scale = 1.0 / (2.0 * teams * times * replicas)
     return pl.pallas_call(
         functools.partial(update_kernel, teams, scale),
         out_shape=jax.ShapeDtypeStruct(omega.shape, F32),
-        in_specs=[SMEM, SMEM, VMEM] + [VMEM] * count,
+        in_specs=[SMEM, VMEM] + [VMEM] * count,
         out_specs=VMEM,
         compiler_params=small,
         name="update",
-    )(place, pattern, omega, *sums)
+    )(place, omega, *sums)
 
 
 def solution(mesh):

time: 103 us -> 101 us (0.981)
  Pallas kernels: 18.9 us -> 15.3 us
  local copies, waits for them, and re-layouts: 2.86 us -> 5.8 us
  waiting for transfers between devices: 55.2 us -> 52.5 us
    unnamed x12 -> x10, local copies, waits for them, and re-layouts: 2.86 us -> 5.72 us
    pallas_call x3, Pallas kernels: 7.06 us -> 4.89 us  [products(): pl.pallas_call(functools.partial(product_kernel, teams, chips, wanted), o...]
    ppermute x19, waiting for transfers between devices: 54 us -> 52.5 us  [swap(): return lax.ppermute(array, AXES, route)]
    all_to_all x1, starting transfers between devices: 5.13 us -> 3.91 us  [per_device(): own = lax.all_to_all(dealt, 'line', 0, 0)]
    all_to_all x1, waiting for transfers between devices: 1.19 us -> 0.01 us  [per_device(): own = lax.all_to_all(dealt, 'line', 0, 0)]
  transfers between devices with their start and end apart: 20 -> 20, of which waited for: 14 -> 12; matrix products, arithmetic and copies ran while one was open for 0% -> 1% of each run, Pallas kernels for 10% -> 9%
where the time goes in v7:
time: 101 us; the launch traced here: 99.5 us
  waiting for transfers between devices  52.5 us (52%)
  starting transfers between devices  24.9 us (25%)
  Pallas kernels  15.3 us (15%)
  local copies, waits for them, and re-layouts  5.8 us (6%)
    ppermute x19, waiting for transfers between devices, swap(): return lax.ppermute(array, AXES, route)  52.5 us
    ppermute x19, starting transfers between devices, swap(): return lax.ppermute(array, AXES, route)  21 us
    unnamed x10, local copies, waits for them, and re-layouts  5.72 us
    pallas_call x3, Pallas kernels, products(): pl.pallas_call(functools.partial(product_kernel, teams, chips, wanted), o...  4.89 us
    pallas_call x2, Pallas kernels, mix(): pl.pallas_call(functools.partial(mix_kernel, teams, replicas, tile_rows),...  4.59 us
    all_to_all x1, starting transfers between devices, per_device(): own = lax.all_to_all(dealt, 'line', 0, 0)  3.91 us
    pallas_call x1, Pallas kernels, per_device(): pl.pallas_call(functools.partial(gather_kernel, teams, chips, tile_rows),...  2.44 us
  transfers between devices with their start and end apart: 20, of which 12 were waited for; matrix products, arithmetic and copies ran while one was open for 1% of the time, Pallas kernels for 9%

profile of v7, /device:TPU:0, one launch (start us, length us, event | category | flops | bytes accessed | tf_op | source)
XLA Modules:
  0.0 99.5 jit_solution(465052530759984745)
XLA Ops:
  0.0 1.2 %copy-done = bf16[2048,256]{1,0:T(8,128)(2,1)S(1)} copy-done((bf16[2048,256]{1,0:T(8,128)(2,1)S(1)}, bf16[2048,256]{1,0:T(8,128)(2,1)}, u32[]{:S(2)}) %copy-start) | copy-done | bytes 1048600
  1.3 3.0 %collective-permute-start.3 = (bf16[1024,256]{1,0:T(8,128)(2,1)S(1)}, bf16[1024,256]{1,0:T(8,128)(2,1)S(1)}, u32[]{:S(2)}, u32[]{:S(2)}) collective-permute-start(bf16[1024,256]{1,0:T(8,128)(2,1)S(1)} %constant_dynamic-slice_fusion.1), channel_id=1, source_target_pairs={{0,4},{1,5},{2,6},{3,7},{4,0},{5,1},{6,2},{7,3},{8,12},{9,13},{10,... | collective-permute-start | bytes 1572872 | tf_op jit(solution)/shard_map/ppermute | solution.py:185
  4.3 0.7 pad_add_fusion.place_ref
  5.0 1.0 copy-done.3
  6.0 0.6 prepare.1
  6.6 1.6 %collective-permute-start = (bf16[3,64,256]{2,1,0:T(8,128)(2,1)S(1)}, bf16[3,64,256]{2,1,0:T(8,128)(2,1)S(1)}, u32[]{:S(2)}, u32[]{:S(2)}) collective-permute-start(bf16[3,64,256]{2,1,0:T(8,128)(2,1)S(1)} %prepare.1), channel_id=1, source_target_pairs={{0,8},{1,9},{2,10},{3,11},{4,12},{5,13},{6,14},{7,15},{8,0},{9,1},... | collective-permute-start | bytes 294920 | tf_op jit(solution)/shard_map/ppermute | solution.py:185
  8.2 2.6 %collective-permute-start.1 = (bf16[3,64,256]{2,1,0:T(8,128)(2,1)S(1)}, bf16[3,64,256]{2,1,0:T(8,128)(2,1)S(1)}, u32[]{:S(2)}, u32[]{:S(2)}) collective-permute-start(bf16[3,64,256]{2,1,0:T(8,128)(2,1)S(1)} %prepare.1), channel_id=1, source_target_pairs={{0,16},{1,17},{2,18},{3,19},{4,20},{5,21},{6,22},{7,23},{8,24},{9,... | collective-permute-start | bytes 294920 | tf_op jit(solution)/shard_map/ppermute | solution.py:185
  10.8 0.2 collective-permute-start.2
  11.0 1.2 %collective-permute-done = bf16[3,64,256]{2,1,0:T(8,128)(2,1)S(1)} collective-permute-done((bf16[3,64,256]{2,1,0:T(8,128)(2,1)S(1)}, bf16[3,64,256]{2,1,0:T(8,128)(2,1)S(1)}, u32[]{:S(2)}, u32[]{:S(2)}) %collective-permute-start) | collective-permute-done | bytes 98336 | tf_op jit(solution)/shard_map/ppermute | solution.py:185
  12.2 6.1 %collective-permute-done.1 = bf16[3,64,256]{2,1,0:T(8,128)(2,1)S(1)} collective-permute-done((bf16[3,64,256]{2,1,0:T(8,128)(2,1)S(1)}, bf16[3,64,256]{2,1,0:T(8,128)(2,1)S(1)}, u32[]{:S(2)}, u32[]{:S(2)}) %collective-permute-start.1) | collective-permute-done | bytes 98336 | tf_op jit(solution)/shard_map/ppermute | solution.py:185
  18.3 0.1 pad_maximum_fusion.rest_0_
  18.5 1.0 deal.1
  19.5 3.9 %all-to-all-start = ((bf16[4,2,256,256]{3,2,1,0:T(8,128)(2,1)}), bf16[4,2,256,256]{3,2,1,0:T(8,128)(2,1)S(1)}, u32[]{:S(2)}, u32[]{:S(2)}) async-start(bf16[4,2,256,256]{3,2,1,0:T(8,128)(2,1)} %deal.1), calls=%async_computation | async-start | bytes 2097152 | tf_op jit(solution)/shard_map/all_to_all | solution.py:226
  23.4 1.5 %collective-permute-start.6 = (bf16[4,3,64,256]{3,2,1,0:T(8,128)(2,1)S(1)}, bf16[4,3,64,256]{3,2,1,0:T(8,128)(2,1)S(1)}, u32[]{:S(2)}, u32[]{:S(2)}) collective-permute-start(bf16[4,3,64,256]{3,2,1,0:T(8,128)(2,1)S(1)} %pad_maximum_fusion.rest_0_), channel_id=1, source_target_pairs={{0,6},{1,7},{2,4},{3,5},{4,2},{5,3},{6,0},{7,1},{8,14},{9,15},{10,... | collective-permute-start | bytes 1179656 | tf_op jit(solution)/shard_map/ppermute | solution.py:185
  24.9 0.5 collective-permute-start.4
  25.4 1.5 %collective-permute-start.5 = (bf16[4,3,64,256]{3,2,1,0:T(8,128)(2,1)S(1)}, bf16[4,3,64,256]{3,2,1,0:T(8,128)(2,1)S(1)}, u32[]{:S(2)}, u32[]{:S(2)}) collective-permute-start(bf16[4,3,64,256]{3,2,1,0:T(8,128)(2,1)S(1)} %pad_maximum_fusion.rest_0_), channel_id=1, source_target_pairs={{0,4},{1,5},{2,6},{3,7},{4,0},{5,1},{6,2},{7,3},{8,12},{9,13},{10,... | collective-permute-start | bytes 1179656 | tf_op jit(solution)/shard_map/ppermute | solution.py:185
  26.9 9.5 %collective-permute-done.6.rest_3_ = bf16[4,3,64,256]{3,2,1,0:T(8,128)(2,1)S(1)} collective-permute-done((bf16[4,3,64,256]{3,2,1,0:T(8,128)(2,1)S(1)}, bf16[4,3,64,256]{3,2,1,0:T(8,128)(2,1)S(1)}, u32[]{:S(2)}, u32[]{:S(2)}) %collective-permute-start.6) | collective-permute-done | bytes 393248 | tf_op jit(solution)/shard_map/ppermute | solution.py:185
  36.3 5.7 %collective-permute-done.4.rest_1_ = bf16[4,3,64,256]{3,2,1,0:T(8,128)(2,1)S(1)} collective-permute-done((bf16[4,3,64,256]{3,2,1,0:T(8,128)(2,1)S(1)}, bf16[4,3,64,256]{3,2,1,0:T(8,128)(2,1)S(1)}, u32[]{:S(2)}, u32[]{:S(2)}) %collective-permute-start.4) | collective-permute-done | bytes 393248 | tf_op jit(solution)/shard_map/ppermute | solution.py:185
  42.0 0.1 collective-permute-done.5.rest_2_
  42.1 0.4 collective-permute-start.9
  42.5 1.2 %collective-permute-done.8.rest_5_ = bf16[4,3,64,256]{3,2,1,0:T(8,128)(2,1)S(1)} collective-permute-done((bf16[4,3,64,256]{3,2,1,0:T(8,128)(2,1)S(1)}, bf16[4,3,64,256]{3,2,1,0:T(8,128)(2,1)S(1)}, u32[]{:S(2)}, u32[]{:S(2)}) %collective-permute-start.8) | collective-permute-done | bytes 393248 | tf_op jit(solution)/shard_map/ppermute | solution.py:185
  43.7 0.6 collective-permute-done.9.rest_6_
  44.3 2.4 %gather.1.omega_ref = bf16[8,3,256,256]{3,2,1,0:T(8,128)(2,1)S(1)} custom-call(s32[7]{0:T(128)S(1)} %pad_add_fusion.place_ref, bf16[4,3,64,256]{3,2,1,0:T(8,128)(2,1)S(1)} %pad_maximum_fusion.rest_0_, bf16[4,3,64,256]{3,2,1,0:T(8,128)(2,1)S(1)} %collective-permute-done.4.rest_1_, bf16[4,3,64,256]{3,2,1,0:T(8,128)(2,1)S(1)} %collective-permute-done.5.rest_2_, ...), custom_call_target="tpu_custom_call" | custom-call | tf_op jit(solution)/shard_map/gather/pallas_call | solution.py:228
  46.7 1.6 %copy-done.1 = bf16[8,3,256,256]{3,2,1,0:T(8,128)(2,1)} copy-done((bf16[8,3,256,256]{3,2,1,0:T(8,128)(2,1)}, bf16[8,3,256,256]{3,2,1,0:T(8,128)(2,1)S(1)}, u32[]{:S(2)}) %copy-start.1) | copy-done | bytes 3145752
  48.4 0.1 collective-permute-start.11
  48.5 1.9 %copy-done.2 = bf16[8,3,256,256]{3,2,1,0:T(8,128)(2,1)S(1)} copy-done((bf16[8,3,256,256]{3,2,1,0:T(8,128)(2,1)S(1)}, bf16[8,3,256,256]{3,2,1,0:T(8,128)(2,1)}, u32[]{:S(2)}) %copy-start.2) | copy-done | bytes 3145752
  50.4 2.3 %mix.2 = (bf16[8,512,256]{2,1,0:T(8,128)(2,1)S(1)}, bf16[8,128,512]{2,1,0:T(8,128)(2,1)S(1)}) custom-call(s32[7]{0:T(128)S(1)} %pad_add_fusion.place_ref, bf16[4,2,256,256]{3,2,1,0:T(8,128)(2,1)S(1)} %all-to-all-done.data_ref, bf16[8,3,256,256]{3,2,1,0:T(8,128)(2,1)S(1)} %copy-done.2), custom_call_target="tpu_custom_call" | custom-call | tf_op jit(solution)/shard_map/mix/pallas_call | solution.py:240
  52.7 2.3 %mix.3 = (bf16[8,512,256]{2,1,0:T(8,128)(2,1)S(1)}, bf16[8,128,512]{2,1,0:T(8,128)(2,1)S(1)}) custom-call(s32[7]{0:T(128)S(1)} %pad_add_fusion.place_ref, bf16[4,2,256,256]{3,2,1,0:T(8,128)(2,1)S(1)} %collective-permute-done.11.data_ref, bf16[8,3,256,256]{3,2,1,0:T(8,128)(2,1)S(1)} %copy-done.2), custom_call_target="tpu_custom_call" | custom-call | tf_op jit(solution)/shard_map/mix/pallas_call | solution.py:240
  55.0 1.4 %products.5 = bf16[2,2,5,64,256]{4,3,2,1,0:T(8,128)(2,1)S(1)} custom-call(s32[7]{0:T(128)S(1)} %pad_add_fusion.place_ref, bf16[8,512,256]{2,1,0:T(8,128)(2,1)S(1)} %get-tuple-element.29.rest_0_, bf16[8,128,512]{2,1,0:T(8,128)(2,1)S(1)} %get-tuple-element.30.rest_1_, bf16[8,512,256]{2,1,0:T(8,128)(2,1)S(1)} %get-tuple-element.31.rest_2_, ...), custom_call_target="tpu_custom_call" | custom-call | tf_op jit(solution)/shard_map/products/pallas_call | solution.py:262
  56.4 1.0 %collective-permute-start.15 = (bf16[2,2,5,64,256]{4,3,2,1,0:T(8,128)(2,1)S(1)}, bf16[2,2,5,64,256]{4,3,2,1,0:T(8,128)(2,1)S(1)}, u32[]{:S(2)}, u32[]{:S(2)}) collective-permute-start(bf16[2,2,5,64,256]{4,3,2,1,0:T(8,128)(2,1)S(1)} %products.5), channel_id=1, source_target_pairs={{0,4},{1,5},{2,6},{3,7},{4,0},{5,1},{6,2},{7,3},{8,12},{9,13},{10,... | collective-permute-start | bytes 1966088 | tf_op jit(solution)/shard_map/ppermute | solution.py:185
  57.4 2.1 %products.3 = (f32[2,2,5,64,256]{4,3,2,1,0:T(8,128)S(1)}, bf16[2,2,5,64,256]{4,3,2,1,0:T(8,128)(2,1)S(1)}) custom-call(s32[7]{0:T(128)S(1)} %pad_add_fusion.place_ref, bf16[8,512,256]{2,1,0:T(8,128)(2,1)S(1)} %get-tuple-element.29.rest_0_, bf16[8,128,512]{2,1,0:T(8,128)(2,1)S(1)} %get-tuple-element.30.rest_1_, ...), custom_call_target="tpu_custom_call" | custom-call | tf_op jit(solution)/shard_map/products/pallas_call | solution.py:262
  59.5 1.5 %collective-permute-start.12 = (bf16[2,2,5,64,256]{4,3,2,1,0:T(8,128)(2,1)S(1)}, bf16[2,2,5,64,256]{4,3,2,1,0:T(8,128)(2,1)S(1)}, u32[]{:S(2)}, u32[]{:S(2)}) collective-permute-start(bf16[2,2,5,64,256]{4,3,2,1,0:T(8,128)(2,1)S(1)} %get-tuple-element.34), channel_id=1, source_target_pairs={{0,2},{1,3},{2,0},{3,1},{4,6},{5,7},{6,4},{7,5},{8,10},{9,11},{10,... | collective-permute-start | bytes 1966088 | tf_op jit(solution)/shard_map/ppermute | solution.py:185
  61.0 1.4 %products.4.refs_0_ = f32[2,2,5,64,256]{4,3,2,1,0:T(8,128)S(1)} custom-call(s32[7]{0:T(128)S(1)} %pad_add_fusion.place_ref, bf16[8,512,256]{2,1,0:T(8,128)(2,1)S(1)} %get-tuple-element.29.rest_0_, bf16[8,128,512]{2,1,0:T(8,128)(2,1)S(1)} %get-tuple-element.30.rest_1_, bf16[8,512,256]{2,1,0:T(8,128)(2,1)S(1)} %get-tuple-element.31.rest_2_, ...), custom_call_target="tpu_custom_call" | custom-call | tf_op jit(solution)/shard_map/products/pallas_call | solution.py:262
  62.4 11.1 %collective-permute-done.15.refs_1_ = bf16[2,2,5,64,256]{4,3,2,1,0:T(8,128)(2,1)S(1)} collective-permute-done((bf16[2,2,5,64,256]{4,3,2,1,0:T(8,128)(2,1)S(1)}, bf16[2,2,5,64,256]{4,3,2,1,0:T(8,128)(2,1)S(1)}, u32[]{:S(2)}, u32[]{:S(2)}) %collective-permute-start.15) | collective-permute-done | bytes 655392 | tf_op jit(solution)/shard_map/ppermute | solution.py:185
  73.5 0.1 add.26
  73.7 1.3 %collective-permute-start.16 = (bf16[2,5,64,256]{3,2,1,0:T(8,128)(2,1)S(1)}, bf16[2,5,64,256]{3,2,1,0:T(8,128)(2,1)S(1)}, u32[]{:S(2)}, u32[]{:S(2)}) collective-permute-start(bf16[2,5,64,256]{3,2,1,0:T(8,128)(2,1)S(1)} %get-tuple-element.40), channel_id=1, source_target_pairs={{0,2},{1,3},{2,0},{3,1},{4,6},{5,7},{6,4},{7,5},{8,10},{9,11},{10,... | collective-permute-start | bytes 983048 | tf_op jit(solution)/shard_map/ppermute | solution.py:185
  75.0 1.6 %collective-permute-done.12.refs_1_ = bf16[2,2,5,64,256]{4,3,2,1,0:T(8,128)(2,1)S(1)} collective-permute-done((bf16[2,2,5,64,256]{4,3,2,1,0:T(8,128)(2,1)S(1)}, bf16[2,2,5,64,256]{4,3,2,1,0:T(8,128)(2,1)S(1)}, u32[]{:S(2)}, u32[]{:S(2)}) %collective-permute-start.12) | collective-permute-done | bytes 655392 | tf_op jit(solution)/shard_map/ppermute | solution.py:185
  76.6 0.1 add.24
  76.7 1.4 %collective-permute-start.13 = (bf16[2,5,64,256]{3,2,1,0:T(8,128)(2,1)S(1)}, bf16[2,5,64,256]{3,2,1,0:T(8,128)(2,1)S(1)}, u32[]{:S(2)}, u32[]{:S(2)}) collective-permute-start(bf16[2,5,64,256]{3,2,1,0:T(8,128)(2,1)S(1)} %get-tuple-element.36), channel_id=1, source_target_pairs={{0,4},{1,5},{2,6},{3,7},{4,0},{5,1},{6,2},{7,3},{8,12},{9,13},{10,... | collective-permute-start | bytes 983048 | tf_op jit(solution)/shard_map/ppermute | solution.py:185
  78.2 5.1 %collective-permute-done.16.refs_1_ = bf16[2,5,64,256]{3,2,1,0:T(8,128)(2,1)S(1)} collective-permute-done((bf16[2,5,64,256]{3,2,1,0:T(8,128)(2,1)S(1)}, bf16[2,5,64,256]{3,2,1,0:T(8,128)(2,1)S(1)}, u32[]{:S(2)}, u32[]{:S(2)}) %collective-permute-start.16) | collective-permute-done | bytes 327712 | tf_op jit(solution)/shard_map/ppermute | solution.py:185
  83.3 0.1 add.27
  83.4 2.7 %collective-permute-start.17 = (bf16[5,64,256]{2,1,0:T(8,128)(2,1)S(1)}, bf16[5,64,256]{2,1,0:T(8,128)(2,1)S(1)}, u32[]{:S(2)}, u32[]{:S(2)}) collective-permute-start(bf16[5,64,256]{2,1,0:T(8,128)(2,1)S(1)} %get-tuple-element.41), channel_id=1, source_target_pairs={{0,16},{1,17},{2,18},{3,19},{4,20},{5,21},{6,22},{7,23},{8,24},{9,... | collective-permute-start | bytes 491528 | tf_op jit(solution)/shard_map/ppermute | solution.py:185
  86.1 1.5 %collective-permute-start.18 = (bf16[5,64,256]{2,1,0:T(8,128)(2,1)S(1)}, bf16[5,64,256]{2,1,0:T(8,128)(2,1)S(1)}, u32[]{:S(2)}, u32[]{:S(2)}) collective-permute-start(bf16[5,64,256]{2,1,0:T(8,128)(2,1)S(1)} %get-tuple-element.42), channel_id=1, source_target_pairs={{0,24},{1,25},{2,26},{3,27},{4,28},{5,29},{6,30},{7,31},{8,16},{9,... | collective-permute-start | bytes 491528 | tf_op jit(solution)/shard_map/ppermute | solution.py:185
  87.5 0.1 add.25
  87.6 0.1 collective-permute-start.14
  87.7 10.2 %collective-permute-done.17.rest_2_ = bf16[5,64,256]{2,1,0:T(8,128)(2,1)S(1)} collective-permute-done((bf16[5,64,256]{2,1,0:T(8,128)(2,1)S(1)}, bf16[5,64,256]{2,1,0:T(8,128)(2,1)S(1)}, u32[]{:S(2)}, u32[]{:S(2)}) %collective-permute-start.17) | collective-permute-done | bytes 163872 | tf_op jit(solution)/shard_map/ppermute | solution.py:185
  97.8 0.2 collective-permute-done.14.rest_1_
  98.0 1.5 %update.1 = f32[1,5,64,256]{3,2,1,0:T(8,128)} custom-call(s32[7]{0:T(128)S(1)} %pad_add_fusion.place_ref, f32[1,5,64,256]{3,2,1,0:T(8,128)S(1)} %copy-done.4, f32[5,64,256]{2,1,0:T(8,128)S(1)} %get-tuple-element.37.rest_0_, bf16[5,64,256]{2,1,0:T(8,128)(2,1)S(1)} %collective-permute-done.14.rest_1_, bf16[5,64,256]{2,1,0:T(8,128)(2,1)S(1)} %collective-permute-done.17.rest_2_, ...), custom_call_target="tpu_custom_call" | custom-call | tf_op jit(solution)/shard_map/update/pallas_call | solution.py:318
  (19 shorter events, 0.1 us)
Async XLA Ops:
  0.0 1.2 %copy-start = (bf16[2048,256]{1,0:T(8,128)(2,1)S(1)}, bf16[2048,256]{1,0:T(8,128)(2,1)}, u32[]{:S(2)}) copy-start(bf16[2048,256]{1,0:T(8,128)(2,1)} %param.3) | copy-start | bytes 3145732
  1.3 17.1 %collective-permute-start.3 = (bf16[1024,256]{1,0:T(8,128)(2,1)S(1)}, bf16[1024,256]{1,0:T(8,128)(2,1)S(1)}, u32[]{:S(2)}, u32[]{:S(2)}) collective-permute-start(bf16[1024,256]{1,0:T(8,128)(2,1)S(1)} %constant_dynamic-slice_fusion.1), channel_id=1, source_target_pairs={{0,4},{1,5},{2,6},{3,7},{4,0},{5,1},{6,2},{7,3},{8,12},{9,13},{10,... | collective-permute-start | bytes 1572872 | tf_op jit(solution)/shard_map/ppermute | solution.py:185
  5.0 1.0 copy-start.3
  6.6 5.7 %collective-permute-start = (bf16[3,64,256]{2,1,0:T(8,128)(2,1)S(1)}, bf16[3,64,256]{2,1,0:T(8,128)(2,1)S(1)}, u32[]{:S(2)}, u32[]{:S(2)}) collective-permute-start(bf16[3,64,256]{2,1,0:T(8,128)(2,1)S(1)} %prepare.1), channel_id=1, source_target_pairs={{0,8},{1,9},{2,10},{3,11},{4,12},{5,13},{6,14},{7,15},{8,0},{9,1},... | collective-permute-start | bytes 294920 | tf_op jit(solution)/shard_map/ppermute | solution.py:185
  8.2 10.1 %collective-permute-start.1 = (bf16[3,64,256]{2,1,0:T(8,128)(2,1)S(1)}, bf16[3,64,256]{2,1,0:T(8,128)(2,1)S(1)}, u32[]{:S(2)}, u32[]{:S(2)}) collective-permute-start(bf16[3,64,256]{2,1,0:T(8,128)(2,1)S(1)} %prepare.1), channel_id=1, source_target_pairs={{0,16},{1,17},{2,18},{3,19},{4,20},{5,21},{6,22},{7,23},{8,24},{9,... | collective-permute-start | bytes 294920 | tf_op jit(solution)/shard_map/ppermute | solution.py:185
  10.8 7.6 %collective-permute-start.2 = (bf16[3,64,256]{2,1,0:T(8,128)(2,1)S(1)}, bf16[3,64,256]{2,1,0:T(8,128)(2,1)S(1)}, u32[]{:S(2)}, u32[]{:S(2)}) collective-permute-start(bf16[3,64,256]{2,1,0:T(8,128)(2,1)S(1)} %prepare.1), channel_id=1, source_target_pairs={{0,24},{1,25},{2,26},{3,27},{4,28},{5,29},{6,30},{7,31},{8,16},{9,... | collective-permute-start | bytes 294920 | tf_op jit(solution)/shard_map/ppermute | solution.py:185
  19.5 28.9 %all-to-all-start = ((bf16[4,2,256,256]{3,2,1,0:T(8,128)(2,1)}), bf16[4,2,256,256]{3,2,1,0:T(8,128)(2,1)S(1)}, u32[]{:S(2)}, u32[]{:S(2)}) async-start(bf16[4,2,256,256]{3,2,1,0:T(8,128)(2,1)} %deal.1), calls=%async_computation | async-start | bytes 2097152 | tf_op jit(solution)/shard_map/all_to_all | solution.py:226
  23.4 13.0 %collective-permute-start.6 = (bf16[4,3,64,256]{3,2,1,0:T(8,128)(2,1)S(1)}, bf16[4,3,64,256]{3,2,1,0:T(8,128)(2,1)S(1)}, u32[]{:S(2)}, u32[]{:S(2)}) collective-permute-start(bf16[4,3,64,256]{3,2,1,0:T(8,128)(2,1)S(1)} %pad_maximum_fusion.rest_0_), channel_id=1, source_target_pairs={{0,6},{1,7},{2,4},{3,5},{4,2},{5,3},{6,0},{7,1},{8,14},{9,15},{10,... | collective-permute-start | bytes 1179656 | tf_op jit(solution)/shard_map/ppermute | solution.py:185
  24.9 17.1 %collective-permute-start.4 = (bf16[4,3,64,256]{3,2,1,0:T(8,128)(2,1)S(1)}, bf16[4,3,64,256]{3,2,1,0:T(8,128)(2,1)S(1)}, u32[]{:S(2)}, u32[]{:S(2)}) collective-permute-start(bf16[4,3,64,256]{3,2,1,0:T(8,128)(2,1)S(1)} %pad_maximum_fusion.rest_0_), channel_id=1, source_target_pairs={{0,2},{1,3},{2,0},{3,1},{4,6},{5,7},{6,4},{7,5},{8,10},{9,11},{10,... | collective-permute-start | bytes 1179656 | tf_op jit(solution)/shard_map/ppermute | solution.py:185
  25.4 16.7 %collective-permute-start.5 = (bf16[4,3,64,256]{3,2,1,0:T(8,128)(2,1)S(1)}, bf16[4,3,64,256]{3,2,1,0:T(8,128)(2,1)S(1)}, u32[]{:S(2)}, u32[]{:S(2)}) collective-permute-start(bf16[4,3,64,256]{3,2,1,0:T(8,128)(2,1)S(1)} %pad_maximum_fusion.rest_0_), channel_id=1, source_target_pairs={{0,4},{1,5},{2,6},{3,7},{4,0},{5,1},{6,2},{7,3},{8,12},{9,13},{10,... | collective-permute-start | bytes 1179656 | tf_op jit(solution)/shard_map/ppermute | solution.py:185
  26.9 15.6 %collective-permute-start.7 = (bf16[4,3,64,256]{3,2,1,0:T(8,128)(2,1)S(1)}, bf16[4,3,64,256]{3,2,1,0:T(8,128)(2,1)S(1)}, u32[]{:S(2)}, u32[]{:S(2)}) collective-permute-start(bf16[4,3,64,256]{3,2,1,0:T(8,128)(2,1)S(1)} %pad_maximum_fusion.rest_0_), channel_id=1, source_target_pairs={{0,1},{1,0},{2,3},{3,2},{4,5},{5,4},{6,7},{7,6},{8,9},{9,8},{10,11... | collective-permute-start | bytes 1179656 | tf_op jit(solution)/shard_map/ppermute | solution.py:185
  36.3 6.2 %collective-permute-start.10 = (bf16[4,3,64,256]{3,2,1,0:T(8,128)(2,1)S(1)}, bf16[4,3,64,256]{3,2,1,0:T(8,128)(2,1)S(1)}, u32[]{:S(2)}, u32[]{:S(2)}) collective-permute-start(bf16[4,3,64,256]{3,2,1,0:T(8,128)(2,1)S(1)} %collective-permute-done.6.rest_3_), channel_id=1, source_target_pairs={{0,1},{1,0},{2,3},{3,2},{4,5},{5,4},{6,7},{7,6},{8,9},{9,8},{10,11... | collective-permute-start | bytes 1179656 | tf_op jit(solution)/shard_map/ppermute | solution.py:185
  42.0 1.7 %collective-permute-start.8 = (bf16[4,3,64,256]{3,2,1,0:T(8,128)(2,1)S(1)}, bf16[4,3,64,256]{3,2,1,0:T(8,128)(2,1)S(1)}, u32[]{:S(2)}, u32[]{:S(2)}) collective-permute-start(bf16[4,3,64,256]{3,2,1,0:T(8,128)(2,1)S(1)} %collective-permute-done.4.rest_1_), channel_id=1, source_target_pairs={{0,1},{1,0},{2,3},{3,2},{4,5},{5,4},{6,7},{7,6},{8,9},{9,8},{10,11... | collective-permute-start | bytes 1179656 | tf_op jit(solution)/shard_map/ppermute | solution.py:185
  42.1 2.2 %collective-permute-start.9 = (bf16[4,3,64,256]{3,2,1,0:T(8,128)(2,1)S(1)}, bf16[4,3,64,256]{3,2,1,0:T(8,128)(2,1)S(1)}, u32[]{:S(2)}, u32[]{:S(2)}) collective-permute-start(bf16[4,3,64,256]{3,2,1,0:T(8,128)(2,1)S(1)} %collective-permute-done.5.rest_2_), channel_id=1, source_target_pairs={{0,1},{1,0},{2,3},{3,2},{4,5},{5,4},{6,7},{7,6},{8,9},{9,8},{10,11... | collective-permute-start | bytes 1179656 | tf_op jit(solution)/shard_map/ppermute | solution.py:185
  46.7 1.6 %copy-start.1 = (bf16[8,3,256,256]{3,2,1,0:T(8,128)(2,1)}, bf16[8,3,256,256]{3,2,1,0:T(8,128)(2,1)S(1)}, u32[]{:S(2)}) copy-start(bf16[8,3,256,256]{3,2,1,0:T(8,128)(2,1)S(1)} %gather.1.omega_ref) | copy-start | bytes 9437188
  48.4 4.3 %collective-permute-start.11 = (bf16[4,2,256,256]{3,2,1,0:T(8,128)(2,1)S(1)}, bf16[4,2,256,256]{3,2,1,0:T(8,128)(2,1)S(1)}, u32[]{:S(2)}, u32[]{:S(2)}) collective-permute-start(bf16[4,2,256,256]{3,2,1,0:T(8,128)(2,1)S(1)} %all-to-all-done.data_ref), channel_id=1, source_target_pairs={{0,1},{1,0},{2,3},{3,2},{4,5},{5,4},{6,7},{7,6},{8,9},{9,8},{10,11... | collective-permute-start | bytes 3145736 | tf_op jit(solution)/shard_map/ppermute | solution.py:185
  48.5 1.9 %copy-start.2 = (bf16[8,3,256,256]{3,2,1,0:T(8,128)(2,1)S(1)}, bf16[8,3,256,256]{3,2,1,0:T(8,128)(2,1)}, u32[]{:S(2)}) copy-start(bf16[8,3,256,256]{3,2,1,0:T(8,128)(2,1)} %copy-done.1) | copy-start | bytes 9437188
  56.4 17.1 %collective-permute-start.15 = (bf16[2,2,5,64,256]{4,3,2,1,0:T(8,128)(2,1)S(1)}, bf16[2,2,5,64,256]{4,3,2,1,0:T(8,128)(2,1)S(1)}, u32[]{:S(2)}, u32[]{:S(2)}) collective-permute-start(bf16[2,2,5,64,256]{4,3,2,1,0:T(8,128)(2,1)S(1)} %products.5), channel_id=1, source_target_pairs={{0,4},{1,5},{2,6},{3,7},{4,0},{5,1},{6,2},{7,3},{8,12},{9,13},{10,... | collective-permute-start | bytes 1966088 | tf_op jit(solution)/shard_map/ppermute | solution.py:185
  59.5 17.1 %collective-permute-start.12 = (bf16[2,2,5,64,256]{4,3,2,1,0:T(8,128)(2,1)S(1)}, bf16[2,2,5,64,256]{4,3,2,1,0:T(8,128)(2,1)S(1)}, u32[]{:S(2)}, u32[]{:S(2)}) collective-permute-start(bf16[2,2,5,64,256]{4,3,2,1,0:T(8,128)(2,1)S(1)} %get-tuple-element.34), channel_id=1, source_target_pairs={{0,2},{1,3},{2,0},{3,1},{4,6},{5,7},{6,4},{7,5},{8,10},{9,11},{10,... | collective-permute-start | bytes 1966088 | tf_op jit(solution)/shard_map/ppermute | solution.py:185
  73.7 24.3 %copy-start.4 = (f32[1,5,64,256]{3,2,1,0:T(8,128)S(1)}, f32[1,5,64,256]{3,2,1,0:T(8,128)}, u32[]{:S(2)}) copy-start(f32[1,5,64,256]{3,2,1,0:T(8,128)} %omega_ref.3) | copy-start | bytes 983044
  73.7 9.6 %collective-permute-start.16 = (bf16[2,5,64,256]{3,2,1,0:T(8,128)(2,1)S(1)}, bf16[2,5,64,256]{3,2,1,0:T(8,128)(2,1)S(1)}, u32[]{:S(2)}, u32[]{:S(2)}) collective-permute-start(bf16[2,5,64,256]{3,2,1,0:T(8,128)(2,1)S(1)} %get-tuple-element.40), channel_id=1, source_target_pairs={{0,2},{1,3},{2,0},{3,1},{4,6},{5,7},{6,4},{7,5},{8,10},{9,11},{10,... | collective-permute-start | bytes 983048 | tf_op jit(solution)/shard_map/ppermute | solution.py:185
  76.7 10.8 %collective-permute-start.13 = (bf16[2,5,64,256]{3,2,1,0:T(8,128)(2,1)S(1)}, bf16[2,5,64,256]{3,2,1,0:T(8,128)(2,1)S(1)}, u32[]{:S(2)}, u32[]{:S(2)}) collective-permute-start(bf16[2,5,64,256]{3,2,1,0:T(8,128)(2,1)S(1)} %get-tuple-element.36), channel_id=1, source_target_pairs={{0,4},{1,5},{2,6},{3,7},{4,0},{5,1},{6,2},{7,3},{8,12},{9,13},{10,... | collective-permute-start | bytes 983048 | tf_op jit(solution)/shard_map/ppermute | solution.py:185
  83.4 14.5 %collective-permute-start.17 = (bf16[5,64,256]{2,1,0:T(8,128)(2,1)S(1)}, bf16[5,64,256]{2,1,0:T(8,128)(2,1)S(1)}, u32[]{:S(2)}, u32[]{:S(2)}) collective-permute-start(bf16[5,64,256]{2,1,0:T(8,128)(2,1)S(1)} %get-tuple-element.41), channel_id=1, source_target_pairs={{0,16},{1,17},{2,18},{3,19},{4,20},{5,21},{6,22},{7,23},{8,24},{9,... | collective-permute-start | bytes 491528 | tf_op jit(solution)/shard_map/ppermute | solution.py:185
  86.1 11.8 %collective-permute-start.18 = (bf16[5,64,256]{2,1,0:T(8,128)(2,1)S(1)}, bf16[5,64,256]{2,1,0:T(8,128)(2,1)S(1)}, u32[]{:S(2)}, u32[]{:S(2)}) collective-permute-start(bf16[5,64,256]{2,1,0:T(8,128)(2,1)S(1)} %get-tuple-element.42), channel_id=1, source_target_pairs={{0,24},{1,25},{2,26},{3,27},{4,28},{5,29},{6,30},{7,31},{8,16},{9,... | collective-permute-start | bytes 491528 | tf_op jit(solution)/shard_map/ppermute | solution.py:185
  87.6 10.4 %collective-permute-start.14 = (bf16[5,64,256]{2,1,0:T(8,128)(2,1)S(1)}, bf16[5,64,256]{2,1,0:T(8,128)(2,1)S(1)}, u32[]{:S(2)}, u32[]{:S(2)}) collective-permute-start(bf16[5,64,256]{2,1,0:T(8,128)(2,1)S(1)} %get-tuple-element.38), channel_id=1, source_target_pairs={{0,8},{1,9},{2,10},{3,11},{4,12},{5,13},{6,14},{7,15},{8,0},{9,1},... | collective-permute-start | bytes 491528 | tf_op jit(solution)/shard_map/ppermute | solution.py:185

commit v8 on v7

--- a/solution.py
+++ b/solution.py
@@ -188,7 +188,8 @@
     count = teams // LOW
     planes = LOW * chips
     count = teams // LOW
-    small = pltpu.CompilerParams(vmem_limit_bytes=(6 if teams <= 8 else 24) * 2**20)
+    small = pltpu.CompilerParams(vmem_limit_bytes=(4 if teams <= 8 else 16) * 2**20)
+    tiny = pltpu.CompilerParams(vmem_limit_bytes=2 * 2**20)
 
     def across_plane(arrays):
         return [
@@ -207,7 +208,7 @@
         out_shape=jax.ShapeDtypeStruct((3, tile_rows, width), BF16),
         in_specs=[SMEM, VMEM],
         out_specs=VMEM,
-        compiler_params=small,
+        compiler_params=tiny,
         name="prepare",
     )(place, omega)
     line = jnp.stack(along_line([upper] * count))
@@ -220,7 +221,7 @@
         in_specs=[VMEM, VMEM],
         out_specs=HBM,
         scratch_shapes=[pltpu.SemaphoreType.DMA((2,))],
-        compiler_params=small,
+        compiler_params=tiny,
         name="deal",
     )(kept, across)
     own = lax.all_to_all(dealt, "line", 0, 0)
@@ -231,7 +232,7 @@
         in_specs=[SMEM] + [ANY] * (2 * planes),
         out_specs=VMEM,
         scratch_shapes=[pltpu.SemaphoreType.DMA((2 * planes * count,))],
-        compiler_params=small,
+        compiler_params=tiny,
         name="gather",
     )(place, *weights)
     own, tiles = lax.optimization_barrier((own, tiles))
@@ -278,41 +279,45 @@
             name="add",
         )(*arrays)
 
-    half = count // 2
-    outer, inner = range(half, count), range(half)
     chip_range = range(chips)
-    (outer_sent,) = products(
-        {(mz, 1, my): (0, (my, mz - half)) for mz in outer for my in chip_range}, [shape((chips, half), BF16)]
-    )
-    outer_sent = swap(outer_sent, 1, 0)
-    inner_parts = products(
-        {(mz, mx, my): (my, (mx, mz)) for mz in inner for mx in range(LOW) for my in chip_range},
-        [shape((LOW, half), BF16 if my else F32) for my in chip_range],
-    )
-    inner_parts = [swap(array, 0, 2 * my) if my else array for my, array in enumerate(inner_parts)]
-    (outer_kept,) = products(
-        {(mz, 0, my): (0, (my, mz - half)) for mz in outer for my in chip_range}, [shape((chips, half), F32)]
-    )
-    outer_parts = add(
-        [[(0, my), (1, my)] for my in chip_range],
-        [shape((half,), BF16 if my else F32) for my in chip_range],
-        outer_kept,
-        outer_sent,
-    )
-    outer_parts = [swap(array, 0, 2 * my) if my else array for my, array in enumerate(outer_parts)]
-    inner_parts = add(
-        [[(n, mx) for n in chip_range] for mx in range(LOW)],
-        [shape((half,), BF16 if mx else F32) for mx in range(LOW)],
-        *inner_parts,
-    )
-    inner_parts = [inner_parts[0], swap(inner_parts[1], 1, 0)]
-    outer_sums = add(
-        [[(n, mz - half) for n in chip_range] for mz in outer], [shape((), BF16) for _ in outer], *outer_parts
-    )
-    inner_sums = add(
-        [[(n, mz) for n in range(LOW)] for mz in inner], [shape((), BF16 if mz else F32) for mz in inner], *inner_parts
-    )
-    sums = along_line(list(inner_sums) + list(outer_sums))
+
+    def plane_sums(group, x_first):
+        size = len(group)
+        if x_first:
+            (far,) = products(
+                {(mz, 1, my): (0, (my, n)) for n, mz in enumerate(group) for my in chip_range},
+                [shape((chips, size), BF16)],
+            )
+            far = swap(far, 1, 0)
+            (near,) = products(
+                {(mz, 0, my): (0, (my, n)) for n, mz in enumerate(group) for my in chip_range},
+                [shape((chips, size), F32)],
+            )
+            groups = [[(0, my), (1, my)] for my in chip_range]
+            parts = add(groups, [shape((size,), BF16 if my else F32) for my in chip_range], near, far)
+            parts = [swap(array, 0, 2 * my) if my else array for my, array in enumerate(parts)]
+        else:
+            parts = products(
+                {
+                    (mz, mx, my): (my, (mx, n))
+                    for n, mz in enumerate(group)
+                    for mx in range(LOW)
+                    for my in chip_range
+                },
+                [shape((LOW, size), BF16 if my else F32) for my in chip_range],
+            )
+            parts = [swap(array, 0, 2 * my) if my else array for my, array in enumerate(parts)]
+            groups = [[(m, mx) for m in chip_range] for mx in range(LOW)]
+            parts = add(groups, [shape((size,), BF16 if mx else F32) for mx in range(LOW)], *parts)
+            parts = [swap(array, mx, 0) if mx else array for mx, array in enumerate(parts)]
+        groups = [[(m, n) for m in range(len(parts))] for n in range(size)]
+        return add(groups, [shape((), BF16 if mz else F32) for mz in group], *parts)
+
+    quarter = count // 4
+    bounds = [range(n * quarter, (n + 1) * quarter) for n in range(4)]
+    far_sums = [*plane_sums(bounds[2], True), *plane_sums(bounds[3], False)]
+    near_sums = [*plane_sums(bounds[0], True), *plane_sums(bounds[1], False)]
+    sums = along_line(near_sums + far_sums)
 
     scale = 1.0 / (2.0 * teams * times * replicas)
     return pl.pallas_call(

time: 101 us -> 98.1 us (0.971); the launches traced: 99.5 us -> 97.8 us
  waiting for transfers between devices: 52.5 us -> 45.1 us
  starting transfers between devices: 24.9 us -> 28.4 us
  Pallas kernels: 15.3 us -> 17.5 us
    ppermute x19 -> x23, waiting for transfers between devices: 52.5 us -> 45.1 us  [swap(): return lax.ppermute(array, AXES, route)]
    ppermute x19 -> x23, starting transfers between devices: 21 us -> 24.5 us  [swap(): return lax.ppermute(array, AXES, route)]
    pallas_call x3 -> x6, Pallas kernels: 4.89 us -> 7.04 us  [products(): pl.pallas_call(functools.partial(product_kernel, teams, chips, wanted), o...]
  transfers between devices with their start and end apart: 20 -> 24, of which waited for: 12 -> 14; matrix products, arithmetic and copies ran while one was open for 1% -> 1% of each run, Pallas kernels for 9% -> 12%
where the time goes in v8:
time: 98.1 us; the launch traced here: 97.8 us
  waiting for transfers between devices  45.1 us (46%)
  starting transfers between devices  28.4 us (29%)
  Pallas kernels  17.5 us (18%)
  local copies, waits for them, and re-layouts  5.8 us (6%)
    ppermute x23, waiting for transfers between devices, swap(): return lax.ppermute(array, AXES, route)  45.1 us
    ppermute x23, starting transfers between devices, swap(): return lax.ppermute(array, AXES, route)  24.5 us
    pallas_call x6, Pallas kernels, products(): pl.pallas_call(functools.partial(product_kernel, teams, chips, wanted), o...  7.04 us
    unnamed x10, local copies, waits for them, and re-layouts  5.72 us
    pallas_call x2, Pallas kernels, mix(): pl.pallas_call(functools.partial(mix_kernel, teams, replicas, tile_rows),...  4.6 us
    all_to_all x1, starting transfers between devices, per_device(): own = lax.all_to_all(dealt, 'line', 0, 0)  3.91 us
    pallas_call x1, Pallas kernels, per_device(): pl.pallas_call(functools.partial(gather_kernel, teams, chips, tile_rows),...  2.44 us
  transfers between devices with their start and end apart: 24, of which 14 were waited for; matrix products, arithmetic and copies ran while one was open for 1% of the time, Pallas kernels for 12%

profile of v8, /device:TPU:0, one launch (start us, length us, event | category | flops | bytes accessed | tf_op | source)
XLA Modules:
  0.0 97.8 jit_solution(941892382273006986)
XLA Ops:
  0.0 1.2 %copy-done = bf16[2048,256]{1,0:T(8,128)(2,1)S(1)} copy-done((bf16[2048,256]{1,0:T(8,128)(2,1)S(1)}, bf16[2048,256]{1,0:T(8,128)(2,1)}, u32[]{:S(2)}) %copy-start) | copy-done | bytes 1048600
  1.3 3.0 %collective-permute-start.3 = (bf16[1024,256]{1,0:T(8,128)(2,1)S(1)}, bf16[1024,256]{1,0:T(8,128)(2,1)S(1)}, u32[]{:S(2)}, u32[]{:S(2)}) collective-permute-start(bf16[1024,256]{1,0:T(8,128)(2,1)S(1)} %constant_dynamic-slice_fusion.1), channel_id=1, source_target_pairs={{0,4},{1,5},{2,6},{3,7},{4,0},{5,1},{6,2},{7,3},{8,12},{9,13},{10,... | collective-permute-start | bytes 1572872 | tf_op jit(solution)/shard_map/ppermute | solution.py:185
  4.3 0.7 pad_add_fusion.place_ref
  5.0 1.0 copy-done.3
  6.0 0.6 prepare.1
  6.6 1.6 %collective-permute-start = (bf16[3,64,256]{2,1,0:T(8,128)(2,1)S(1)}, bf16[3,64,256]{2,1,0:T(8,128)(2,1)S(1)}, u32[]{:S(2)}, u32[]{:S(2)}) collective-permute-start(bf16[3,64,256]{2,1,0:T(8,128)(2,1)S(1)} %prepare.1), channel_id=1, source_target_pairs={{0,8},{1,9},{2,10},{3,11},{4,12},{5,13},{6,14},{7,15},{8,0},{9,1},... | collective-permute-start | bytes 294920 | tf_op jit(solution)/shard_map/ppermute | solution.py:185
  8.2 2.6 %collective-permute-start.1 = (bf16[3,64,256]{2,1,0:T(8,128)(2,1)S(1)}, bf16[3,64,256]{2,1,0:T(8,128)(2,1)S(1)}, u32[]{:S(2)}, u32[]{:S(2)}) collective-permute-start(bf16[3,64,256]{2,1,0:T(8,128)(2,1)S(1)} %prepare.1), channel_id=1, source_target_pairs={{0,16},{1,17},{2,18},{3,19},{4,20},{5,21},{6,22},{7,23},{8,24},{9,... | collective-permute-start | bytes 294920 | tf_op jit(solution)/shard_map/ppermute | solution.py:185
  10.8 0.2 collective-permute-start.2
  11.0 1.2 %collective-permute-done = bf16[3,64,256]{2,1,0:T(8,128)(2,1)S(1)} collective-permute-done((bf16[3,64,256]{2,1,0:T(8,128)(2,1)S(1)}, bf16[3,64,256]{2,1,0:T(8,128)(2,1)S(1)}, u32[]{:S(2)}, u32[]{:S(2)}) %collective-permute-start) | collective-permute-done | bytes 98336 | tf_op jit(solution)/shard_map/ppermute | solution.py:185
  12.2 6.1 %collective-permute-done.1 = bf16[3,64,256]{2,1,0:T(8,128)(2,1)S(1)} collective-permute-done((bf16[3,64,256]{2,1,0:T(8,128)(2,1)S(1)}, bf16[3,64,256]{2,1,0:T(8,128)(2,1)S(1)}, u32[]{:S(2)}, u32[]{:S(2)}) %collective-permute-start.1) | collective-permute-done | bytes 98336 | tf_op jit(solution)/shard_map/ppermute | solution.py:185
  18.5 1.0 %deal.1 = bf16[4,2,256,256]{3,2,1,0:T(8,128)(2,1)} custom-call(bf16[1024,256]{1,0:T(8,128)(2,1)S(1)} %constant_dynamic-slice_fusion.kept_ref, bf16[1024,256]{1,0:T(8,128)(2,1)S(1)} %collective-permute-done.3.across_ref), custom_call_target="tpu_custom_call" | custom-call | tf_op jit(solution)/shard_map/deal/pallas_call | solution.py:218
  19.5 3.9 %all-to-all-start = ((bf16[4,2,256,256]{3,2,1,0:T(8,128)(2,1)}), bf16[4,2,256,256]{3,2,1,0:T(8,128)(2,1)S(1)}, u32[]{:S(2)}, u32[]{:S(2)}) async-start(bf16[4,2,256,256]{3,2,1,0:T(8,128)(2,1)} %deal.1), calls=%async_computation | async-start | bytes 2097152 | tf_op jit(solution)/shard_map/all_to_all | solution.py:227
  23.4 1.5 %collective-permute-start.6 = (bf16[4,3,64,256]{3,2,1,0:T(8,128)(2,1)S(1)}, bf16[4,3,64,256]{3,2,1,0:T(8,128)(2,1)S(1)}, u32[]{:S(2)}, u32[]{:S(2)}) collective-permute-start(bf16[4,3,64,256]{3,2,1,0:T(8,128)(2,1)S(1)} %pad_maximum_fusion.rest_0_), channel_id=1, source_target_pairs={{0,6},{1,7},{2,4},{3,5},{4,2},{5,3},{6,0},{7,1},{8,14},{9,15},{10,... | collective-permute-start | bytes 1179656 | tf_op jit(solution)/shard_map/ppermute | solution.py:185
  24.9 0.5 collective-permute-start.4
  25.4 1.5 %collective-permute-start.5 = (bf16[4,3,64,256]{3,2,1,0:T(8,128)(2,1)S(1)}, bf16[4,3,64,256]{3,2,1,0:T(8,128)(2,1)S(1)}, u32[]{:S(2)}, u32[]{:S(2)}) collective-permute-start(bf16[4,3,64,256]{3,2,1,0:T(8,128)(2,1)S(1)} %pad_maximum_fusion.rest_0_), channel_id=1, source_target_pairs={{0,4},{1,5},{2,6},{3,7},{4,0},{5,1},{6,2},{7,3},{8,12},{9,13},{10,... | collective-permute-start | bytes 1179656 | tf_op jit(solution)/shard_map/ppermute | solution.py:185
  26.9 9.5 %collective-permute-done.6.rest_3_ = bf16[4,3,64,256]{3,2,1,0:T(8,128)(2,1)S(1)} collective-permute-done((bf16[4,3,64,256]{3,2,1,0:T(8,128)(2,1)S(1)}, bf16[4,3,64,256]{3,2,1,0:T(8,128)(2,1)S(1)}, u32[]{:S(2)}, u32[]{:S(2)}) %collective-permute-start.6) | collective-permute-done | bytes 393248 | tf_op jit(solution)/shard_map/ppermute | solution.py:185
  36.3 5.7 %collective-permute-done.4.rest_1_ = bf16[4,3,64,256]{3,2,1,0:T(8,128)(2,1)S(1)} collective-permute-done((bf16[4,3,64,256]{3,2,1,0:T(8,128)(2,1)S(1)}, bf16[4,3,64,256]{3,2,1,0:T(8,128)(2,1)S(1)}, u32[]{:S(2)}, u32[]{:S(2)}) %collective-permute-start.4) | collective-permute-done | bytes 393248 | tf_op jit(solution)/shard_map/ppermute | solution.py:185
  42.1 0.4 collective-permute-start.9
  42.5 1.2 %collective-permute-done.8.rest_5_ = bf16[4,3,64,256]{3,2,1,0:T(8,128)(2,1)S(1)} collective-permute-done((bf16[4,3,64,256]{3,2,1,0:T(8,128)(2,1)S(1)}, bf16[4,3,64,256]{3,2,1,0:T(8,128)(2,1)S(1)}, u32[]{:S(2)}, u32[]{:S(2)}) %collective-permute-start.8) | collective-permute-done | bytes 393248 | tf_op jit(solution)/shard_map/ppermute | solution.py:185
  43.7 0.6 collective-permute-done.9.rest_6_
  44.3 2.4 %gather.1.omega_ref = bf16[8,3,256,256]{3,2,1,0:T(8,128)(2,1)S(1)} custom-call(s32[7]{0:T(128)S(1)} %pad_add_fusion.place_ref, bf16[4,3,64,256]{3,2,1,0:T(8,128)(2,1)S(1)} %pad_maximum_fusion.rest_0_, bf16[4,3,64,256]{3,2,1,0:T(8,128)(2,1)S(1)} %collective-permute-done.4.rest_1_, bf16[4,3,64,256]{3,2,1,0:T(8,128)(2,1)S(1)} %collective-permute-done.5.rest_2_, ...), custom_call_target="tpu_custom_call" | custom-call | tf_op jit(solution)/shard_map/gather/pallas_call | solution.py:229
  46.7 1.6 %copy-done.1 = bf16[8,3,256,256]{3,2,1,0:T(8,128)(2,1)} copy-done((bf16[8,3,256,256]{3,2,1,0:T(8,128)(2,1)}, bf16[8,3,256,256]{3,2,1,0:T(8,128)(2,1)S(1)}, u32[]{:S(2)}) %copy-start.1) | copy-done | bytes 3145752
  48.5 1.9 %copy-done.2 = bf16[8,3,256,256]{3,2,1,0:T(8,128)(2,1)S(1)} copy-done((bf16[8,3,256,256]{3,2,1,0:T(8,128)(2,1)S(1)}, bf16[8,3,256,256]{3,2,1,0:T(8,128)(2,1)}, u32[]{:S(2)}) %copy-start.2) | copy-done | bytes 3145752
  50.4 2.3 %mix.2 = (bf16[8,512,256]{2,1,0:T(8,128)(2,1)S(1)}, bf16[8,128,512]{2,1,0:T(8,128)(2,1)S(1)}) custom-call(s32[7]{0:T(128)S(1)} %pad_add_fusion.place_ref, bf16[4,2,256,256]{3,2,1,0:T(8,128)(2,1)S(1)} %all-to-all-done.data_ref, bf16[8,3,256,256]{3,2,1,0:T(8,128)(2,1)S(1)} %copy-done.2), custom_call_target="tpu_custom_call" | custom-call | tf_op jit(solution)/shard_map/mix/pallas_call | solution.py:241
  52.7 2.3 %mix.3 = (bf16[8,512,256]{2,1,0:T(8,128)(2,1)S(1)}, bf16[8,128,512]{2,1,0:T(8,128)(2,1)S(1)}) custom-call(s32[7]{0:T(128)S(1)} %pad_add_fusion.place_ref, bf16[4,2,256,256]{3,2,1,0:T(8,128)(2,1)S(1)} %collective-permute-done.11.data_ref, bf16[8,3,256,256]{3,2,1,0:T(8,128)(2,1)S(1)} %copy-done.2), custom_call_target="tpu_custom_call" | custom-call | tf_op jit(solution)/shard_map/mix/pallas_call | solution.py:241
  55.0 1.4 %products.11 = (f32[2,1,5,64,256]{4,3,2,1,0:T(8,128)S(1)}, bf16[2,1,5,64,256]{4,3,2,1,0:T(8,128)(2,1)S(1)}) custom-call(s32[7]{0:T(128)S(1)} %pad_add_fusion.place_ref, bf16[8,512,256]{2,1,0:T(8,128)(2,1)S(1)} %get-tuple-element.31.rest_0_, bf16[8,128,512]{2,1,0:T(8,128)(2,1)S(1)} %get-tuple-element.32.rest_1_, ...), custom_call_target="tpu_custom_call" | custom-call | tf_op jit(solution)/shard_map/products/pallas_call | solution.py:263
  56.4 1.2 %collective-permute-start.20 = (bf16[2,1,5,64,256]{4,3,2,1,0:T(8,128)(2,1)S(1)}, bf16[2,1,5,64,256]{4,3,2,1,0:T(8,128)(2,1)S(1)}, u32[]{:S(2)}, u32[]{:S(2)}) collective-permute-start(bf16[2,1,5,64,256]{4,3,2,1,0:T(8,128)(2,1)S(1)} %get-tuple-element.44), channel_id=1, source_target_pairs={{0,2},{1,3},{2,0},{3,1},{4,6},{5,7},{6,4},{7,5},{8,10},{9,11},{10,... | collective-permute-start | bytes 983048 | tf_op jit(solution)/shard_map/ppermute | solution.py:185
  57.7 1.1 %products.10 = bf16[2,1,5,64,256]{4,3,2,1,0:T(8,128)(2,1)S(1)} custom-call(s32[7]{0:T(128)S(1)} %pad_add_fusion.place_ref, bf16[8,512,256]{2,1,0:T(8,128)(2,1)S(1)} %get-tuple-element.31.rest_0_, bf16[8,128,512]{2,1,0:T(8,128)(2,1)S(1)} %get-tuple-element.32.rest_1_, bf16[8,512,256]{2,1,0:T(8,128)(2,1)S(1)} %get-tuple-element.33.rest_2_, ...), custom_call_target="tpu_custom_call" | custom-call | tf_op jit(solution)/shard_map/products/pallas_call | solution.py:263
  58.8 1.2 %collective-permute-start.17 = (bf16[2,1,5,64,256]{4,3,2,1,0:T(8,128)(2,1)S(1)}, bf16[2,1,5,64,256]{4,3,2,1,0:T(8,128)(2,1)S(1)}, u32[]{:S(2)}, u32[]{:S(2)}) collective-permute-start(bf16[2,1,5,64,256]{4,3,2,1,0:T(8,128)(2,1)S(1)} %products.10), channel_id=1, source_target_pairs={{0,4},{1,5},{2,6},{3,7},{4,0},{5,1},{6,2},{7,3},{8,12},{9,13},{10,... | collective-permute-start | bytes 983048 | tf_op jit(solution)/shard_map/ppermute | solution.py:185
  60.0 1.4 %products.8 = (f32[2,1,5,64,256]{4,3,2,1,0:T(8,128)S(1)}, bf16[2,1,5,64,256]{4,3,2,1,0:T(8,128)(2,1)S(1)}) custom-call(s32[7]{0:T(128)S(1)} %pad_add_fusion.place_ref, bf16[8,512,256]{2,1,0:T(8,128)(2,1)S(1)} %get-tuple-element.31.rest_0_, bf16[8,128,512]{2,1,0:T(8,128)(2,1)S(1)} %get-tuple-element.32.rest_1_, ...), custom_call_target="tpu_custom_call" | custom-call | tf_op jit(solution)/shard_map/products/pallas_call | solution.py:263
  61.4 0.7 collective-permute-start.14
  62.1 1.1 %products.7 = bf16[2,1,5,64,256]{4,3,2,1,0:T(8,128)(2,1)S(1)} custom-call(s32[7]{0:T(128)S(1)} %pad_add_fusion.place_ref, bf16[8,512,256]{2,1,0:T(8,128)(2,1)S(1)} %get-tuple-element.31.rest_0_, bf16[8,128,512]{2,1,0:T(8,128)(2,1)S(1)} %get-tuple-element.32.rest_1_, bf16[8,512,256]{2,1,0:T(8,128)(2,1)S(1)} %get-tuple-element.33.rest_2_, ...), custom_call_target="tpu_custom_call" | custom-call | tf_op jit(solution)/shard_map/products/pallas_call | solution.py:263
  63.1 1.2 %collective-permute-start.12 = (bf16[2,1,5,64,256]{4,3,2,1,0:T(8,128)(2,1)S(1)}, bf16[2,1,5,64,256]{4,3,2,1,0:T(8,128)(2,1)S(1)}, u32[]{:S(2)}, u32[]{:S(2)}) collective-permute-start(bf16[2,1,5,64,256]{4,3,2,1,0:T(8,128)(2,1)S(1)} %products.7), channel_id=1, source_target_pairs={{0,4},{1,5},{2,6},{3,7},{4,0},{5,1},{6,2},{7,3},{8,12},{9,13},{10,... | collective-permute-start | bytes 983048 | tf_op jit(solution)/shard_map/ppermute | solution.py:185
  64.3 1.1 %products.9.refs_0_ = f32[2,1,5,64,256]{4,3,2,1,0:T(8,128)S(1)} custom-call(s32[7]{0:T(128)S(1)} %pad_add_fusion.place_ref, bf16[8,512,256]{2,1,0:T(8,128)(2,1)S(1)} %get-tuple-element.31.rest_0_, bf16[8,128,512]{2,1,0:T(8,128)(2,1)S(1)} %get-tuple-element.32.rest_1_, bf16[8,512,256]{2,1,0:T(8,128)(2,1)S(1)} %get-tuple-element.33.rest_2_, ...), custom_call_target="tpu_custom_call" | custom-call | tf_op jit(solution)/shard_map/products/pallas_call | solution.py:263
  65.4 1.7 %collective-permute-done.20.refs_1_ = bf16[2,1,5,64,256]{4,3,2,1,0:T(8,128)(2,1)S(1)} collective-permute-done((bf16[2,1,5,64,256]{4,3,2,1,0:T(8,128)(2,1)S(1)}, bf16[2,1,5,64,256]{4,3,2,1,0:T(8,128)(2,1)S(1)}, u32[]{:S(2)}, u32[]{:S(2)}) %collective-permute-start.20) | collective-permute-done | bytes 327712 | tf_op jit(solution)/shard_map/ppermute | solution.py:185
  67.1 1.0 collective-permute-start.21
  68.1 1.3 %collective-permute-done.17.refs_1_ = bf16[2,1,5,64,256]{4,3,2,1,0:T(8,128)(2,1)S(1)} collective-permute-done((bf16[2,1,5,64,256]{4,3,2,1,0:T(8,128)(2,1)S(1)}, bf16[2,1,5,64,256]{4,3,2,1,0:T(8,128)(2,1)S(1)}, u32[]{:S(2)}, u32[]{:S(2)}) %collective-permute-start.17) | collective-permute-done | bytes 327712 | tf_op jit(solution)/shard_map/ppermute | solution.py:185
  69.5 0.9 collective-permute-start.18
  70.4 3.7 %collective-permute-done.14.refs_1_ = bf16[2,1,5,64,256]{4,3,2,1,0:T(8,128)(2,1)S(1)} collective-permute-done((bf16[2,1,5,64,256]{4,3,2,1,0:T(8,128)(2,1)S(1)}, bf16[2,1,5,64,256]{4,3,2,1,0:T(8,128)(2,1)S(1)}, u32[]{:S(2)}, u32[]{:S(2)}) %collective-permute-start.14) | collective-permute-done | bytes 327712 | tf_op jit(solution)/shard_map/ppermute | solution.py:185
  74.2 1.0 collective-permute-start.15
  75.1 1.1 %products.6.refs_0_ = f32[2,1,5,64,256]{4,3,2,1,0:T(8,128)S(1)} custom-call(s32[7]{0:T(128)S(1)} %pad_add_fusion.place_ref, bf16[8,512,256]{2,1,0:T(8,128)(2,1)S(1)} %get-tuple-element.31.rest_0_, bf16[8,128,512]{2,1,0:T(8,128)(2,1)S(1)} %get-tuple-element.32.rest_1_, bf16[8,512,256]{2,1,0:T(8,128)(2,1)S(1)} %get-tuple-element.33.rest_2_, ...), custom_call_target="tpu_custom_call" | custom-call | tf_op jit(solution)/shard_map/products/pallas_call | solution.py:263
  76.5 1.2 %collective-permute-start.13 = (bf16[1,5,64,256]{3,2,1,0:T(8,128)(2,1)S(1)}, bf16[1,5,64,256]{3,2,1,0:T(8,128)(2,1)S(1)}, u32[]{:S(2)}, u32[]{:S(2)}) collective-permute-start(bf16[1,5,64,256]{3,2,1,0:T(8,128)(2,1)S(1)} %get-tuple-element.36), channel_id=1, source_target_pairs={{0,2},{1,3},{2,0},{3,1},{4,6},{5,7},{6,4},{7,5},{8,10},{9,11},{10,... | collective-permute-start | bytes 491528 | tf_op jit(solution)/shard_map/ppermute | solution.py:185
  77.7 2.2 %collective-permute-done.21.refs_1_ = bf16[1,5,64,256]{3,2,1,0:T(8,128)(2,1)S(1)} collective-permute-done((bf16[1,5,64,256]{3,2,1,0:T(8,128)(2,1)S(1)}, bf16[1,5,64,256]{3,2,1,0:T(8,128)(2,1)S(1)}, u32[]{:S(2)}, u32[]{:S(2)}) %collective-permute-start.21) | collective-permute-done | bytes 163872 | tf_op jit(solution)/shard_map/ppermute | solution.py:185
  80.0 3.6 %collective-permute-start.22 = (bf16[5,64,256]{2,1,0:T(8,128)(2,1)S(1)}, bf16[5,64,256]{2,1,0:T(8,128)(2,1)S(1)}, u32[]{:S(2)}, u32[]{:S(2)}) collective-permute-start(bf16[5,64,256]{2,1,0:T(8,128)(2,1)S(1)} %add.35), channel_id=1, source_target_pairs={{0,24},{1,25},{2,26},{3,27},{4,28},{5,29},{6,30},{7,31},{8,16},{9,... | collective-permute-start | bytes 491528 | tf_op jit(solution)/shard_map/ppermute | solution.py:185
  83.7 0.9 collective-permute-start.16
  84.7 4.3 %collective-permute-done.22.rest_3_ = bf16[5,64,256]{2,1,0:T(8,128)(2,1)S(1)} collective-permute-done((bf16[5,64,256]{2,1,0:T(8,128)(2,1)S(1)}, bf16[5,64,256]{2,1,0:T(8,128)(2,1)S(1)}, u32[]{:S(2)}, u32[]{:S(2)}) %collective-permute-start.22) | collective-permute-done | bytes 163872 | tf_op jit(solution)/shard_map/ppermute | solution.py:185
  89.0 7.4 %collective-permute-done.19.rest_2_ = bf16[5,64,256]{2,1,0:T(8,128)(2,1)S(1)} collective-permute-done((bf16[5,64,256]{2,1,0:T(8,128)(2,1)S(1)}, bf16[5,64,256]{2,1,0:T(8,128)(2,1)S(1)}, u32[]{:S(2)}, u32[]{:S(2)}) %collective-permute-start.19) | collective-permute-done | bytes 163872 | tf_op jit(solution)/shard_map/ppermute | solution.py:185
  96.4 1.5 %update.1 = f32[1,5,64,256]{3,2,1,0:T(8,128)} custom-call(s32[7]{0:T(128)S(1)} %pad_add_fusion.place_ref, f32[1,5,64,256]{3,2,1,0:T(8,128)S(1)} %copy-done.4, f32[5,64,256]{2,1,0:T(8,128)S(1)} %add.29.rest_0_, bf16[5,64,256]{2,1,0:T(8,128)(2,1)S(1)} %collective-permute-done.16.rest_1_, bf16[5,64,256]{2,1,0:T(8,128)(2,1)S(1)} %collective-permute-done.19.rest_2_, ...), custom_call_target="tpu_custom_call" | custom-call | tf_op jit(solution)/shard_map/update/pallas_call | solution.py:323
  (34 shorter events, 1.1 us)
Async XLA Ops:
  0.0 1.2 %copy-start = (bf16[2048,256]{1,0:T(8,128)(2,1)S(1)}, bf16[2048,256]{1,0:T(8,128)(2,1)}, u32[]{:S(2)}) copy-start(bf16[2048,256]{1,0:T(8,128)(2,1)} %param.3) | copy-start | bytes 3145732
  1.3 17.1 %collective-permute-start.3 = (bf16[1024,256]{1,0:T(8,128)(2,1)S(1)}, bf16[1024,256]{1,0:T(8,128)(2,1)S(1)}, u32[]{:S(2)}, u32[]{:S(2)}) collective-permute-start(bf16[1024,256]{1,0:T(8,128)(2,1)S(1)} %constant_dynamic-slice_fusion.1), channel_id=1, source_target_pairs={{0,4},{1,5},{2,6},{3,7},{4,0},{5,1},{6,2},{7,3},{8,12},{9,13},{10,... | collective-permute-start | bytes 1572872 | tf_op jit(solution)/shard_map/ppermute | solution.py:185
  5.0 1.0 copy-start.3
  6.6 5.7 %collective-permute-start = (bf16[3,64,256]{2,1,0:T(8,128)(2,1)S(1)}, bf16[3,64,256]{2,1,0:T(8,128)(2,1)S(1)}, u32[]{:S(2)}, u32[]{:S(2)}) collective-permute-start(bf16[3,64,256]{2,1,0:T(8,128)(2,1)S(1)} %prepare.1), channel_id=1, source_target_pairs={{0,8},{1,9},{2,10},{3,11},{4,12},{5,13},{6,14},{7,15},{8,0},{9,1},... | collective-permute-start | bytes 294920 | tf_op jit(solution)/shard_map/ppermute | solution.py:185
  8.2 10.1 %collective-permute-start.1 = (bf16[3,64,256]{2,1,0:T(8,128)(2,1)S(1)}, bf16[3,64,256]{2,1,0:T(8,128)(2,1)S(1)}, u32[]{:S(2)}, u32[]{:S(2)}) collective-permute-start(bf16[3,64,256]{2,1,0:T(8,128)(2,1)S(1)} %prepare.1), channel_id=1, source_target_pairs={{0,16},{1,17},{2,18},{3,19},{4,20},{5,21},{6,22},{7,23},{8,24},{9,... | collective-permute-start | bytes 294920 | tf_op jit(solution)/shard_map/ppermute | solution.py:185
  10.8 7.6 %collective-permute-start.2 = (bf16[3,64,256]{2,1,0:T(8,128)(2,1)S(1)}, bf16[3,64,256]{2,1,0:T(8,128)(2,1)S(1)}, u32[]{:S(2)}, u32[]{:S(2)}) collective-permute-start(bf16[3,64,256]{2,1,0:T(8,128)(2,1)S(1)} %prepare.1), channel_id=1, source_target_pairs={{0,24},{1,25},{2,26},{3,27},{4,28},{5,29},{6,30},{7,31},{8,16},{9,... | collective-permute-start | bytes 294920 | tf_op jit(solution)/shard_map/ppermute | solution.py:185
  19.5 28.9 %all-to-all-start = ((bf16[4,2,256,256]{3,2,1,0:T(8,128)(2,1)}), bf16[4,2,256,256]{3,2,1,0:T(8,128)(2,1)S(1)}, u32[]{:S(2)}, u32[]{:S(2)}) async-start(bf16[4,2,256,256]{3,2,1,0:T(8,128)(2,1)} %deal.1), calls=%async_computation | async-start | bytes 2097152 | tf_op jit(solution)/shard_map/all_to_all | solution.py:227
  23.4 13.0 %collective-permute-start.6 = (bf16[4,3,64,256]{3,2,1,0:T(8,128)(2,1)S(1)}, bf16[4,3,64,256]{3,2,1,0:T(8,128)(2,1)S(1)}, u32[]{:S(2)}, u32[]{:S(2)}) collective-permute-start(bf16[4,3,64,256]{3,2,1,0:T(8,128)(2,1)S(1)} %pad_maximum_fusion.rest_0_), channel_id=1, source_target_pairs={{0,6},{1,7},{2,4},{3,5},{4,2},{5,3},{6,0},{7,1},{8,14},{9,15},{10,... | collective-permute-start | bytes 1179656 | tf_op jit(solution)/shard_map/ppermute | solution.py:185
  24.9 17.1 %collective-permute-start.4 = (bf16[4,3,64,256]{3,2,1,0:T(8,128)(2,1)S(1)}, bf16[4,3,64,256]{3,2,1,0:T(8,128)(2,1)S(1)}, u32[]{:S(2)}, u32[]{:S(2)}) collective-permute-start(bf16[4,3,64,256]{3,2,1,0:T(8,128)(2,1)S(1)} %pad_maximum_fusion.rest_0_), channel_id=1, source_target_pairs={{0,2},{1,3},{2,0},{3,1},{4,6},{5,7},{6,4},{7,5},{8,10},{9,11},{10,... | collective-permute-start | bytes 1179656 | tf_op jit(solution)/shard_map/ppermute | solution.py:185
  25.4 16.7 %collective-permute-start.5 = (bf16[4,3,64,256]{3,2,1,0:T(8,128)(2,1)S(1)}, bf16[4,3,64,256]{3,2,1,0:T(8,128)(2,1)S(1)}, u32[]{:S(2)}, u32[]{:S(2)}) collective-permute-start(bf16[4,3,64,256]{3,2,1,0:T(8,128)(2,1)S(1)} %pad_maximum_fusion.rest_0_), channel_id=1, source_target_pairs={{0,4},{1,5},{2,6},{3,7},{4,0},{5,1},{6,2},{7,3},{8,12},{9,13},{10,... | collective-permute-start | bytes 1179656 | tf_op jit(solution)/shard_map/ppermute | solution.py:185
  26.9 15.6 %collective-permute-start.7 = (bf16[4,3,64,256]{3,2,1,0:T(8,128)(2,1)S(1)}, bf16[4,3,64,256]{3,2,1,0:T(8,128)(2,1)S(1)}, u32[]{:S(2)}, u32[]{:S(2)}) collective-permute-start(bf16[4,3,64,256]{3,2,1,0:T(8,128)(2,1)S(1)} %pad_maximum_fusion.rest_0_), channel_id=1, source_target_pairs={{0,1},{1,0},{2,3},{3,2},{4,5},{5,4},{6,7},{7,6},{8,9},{9,8},{10,11... | collective-permute-start | bytes 1179656 | tf_op jit(solution)/shard_map/ppermute | solution.py:185
  36.3 6.2 %collective-permute-start.10 = (bf16[4,3,64,256]{3,2,1,0:T(8,128)(2,1)S(1)}, bf16[4,3,64,256]{3,2,1,0:T(8,128)(2,1)S(1)}, u32[]{:S(2)}, u32[]{:S(2)}) collective-permute-start(bf16[4,3,64,256]{3,2,1,0:T(8,128)(2,1)S(1)} %collective-permute-done.6.rest_3_), channel_id=1, source_target_pairs={{0,1},{1,0},{2,3},{3,2},{4,5},{5,4},{6,7},{7,6},{8,9},{9,8},{10,11... | collective-permute-start | bytes 1179656 | tf_op jit(solution)/shard_map/ppermute | solution.py:185
  42.0 1.7 %collective-permute-start.8 = (bf16[4,3,64,256]{3,2,1,0:T(8,128)(2,1)S(1)}, bf16[4,3,64,256]{3,2,1,0:T(8,128)(2,1)S(1)}, u32[]{:S(2)}, u32[]{:S(2)}) collective-permute-start(bf16[4,3,64,256]{3,2,1,0:T(8,128)(2,1)S(1)} %collective-permute-done.4.rest_1_), channel_id=1, source_target_pairs={{0,1},{1,0},{2,3},{3,2},{4,5},{5,4},{6,7},{7,6},{8,9},{9,8},{10,11... | collective-permute-start | bytes 1179656 | tf_op jit(solution)/shard_map/ppermute | solution.py:185
  42.1 2.2 %collective-permute-start.9 = (bf16[4,3,64,256]{3,2,1,0:T(8,128)(2,1)S(1)}, bf16[4,3,64,256]{3,2,1,0:T(8,128)(2,1)S(1)}, u32[]{:S(2)}, u32[]{:S(2)}) collective-permute-start(bf16[4,3,64,256]{3,2,1,0:T(8,128)(2,1)S(1)} %collective-permute-done.5.rest_2_), channel_id=1, source_target_pairs={{0,1},{1,0},{2,3},{3,2},{4,5},{5,4},{6,7},{7,6},{8,9},{9,8},{10,11... | collective-permute-start | bytes 1179656 | tf_op jit(solution)/shard_map/ppermute | solution.py:185
  46.7 1.6 %copy-start.1 = (bf16[8,3,256,256]{3,2,1,0:T(8,128)(2,1)}, bf16[8,3,256,256]{3,2,1,0:T(8,128)(2,1)S(1)}, u32[]{:S(2)}) copy-start(bf16[8,3,256,256]{3,2,1,0:T(8,128)(2,1)S(1)} %gather.1.omega_ref) | copy-start | bytes 9437188
  48.4 4.4 %collective-permute-start.11 = (bf16[4,2,256,256]{3,2,1,0:T(8,128)(2,1)S(1)}, bf16[4,2,256,256]{3,2,1,0:T(8,128)(2,1)S(1)}, u32[]{:S(2)}, u32[]{:S(2)}) collective-permute-start(bf16[4,2,256,256]{3,2,1,0:T(8,128)(2,1)S(1)} %all-to-all-done.data_ref), channel_id=1, source_target_pairs={{0,1},{1,0},{2,3},{3,2},{4,5},{5,4},{6,7},{7,6},{8,9},{9,8},{10,11... | collective-permute-start | bytes 3145736 | tf_op jit(solution)/shard_map/ppermute | solution.py:185
  48.5 1.9 %copy-start.2 = (bf16[8,3,256,256]{3,2,1,0:T(8,128)(2,1)S(1)}, bf16[8,3,256,256]{3,2,1,0:T(8,128)(2,1)}, u32[]{:S(2)}) copy-start(bf16[8,3,256,256]{3,2,1,0:T(8,128)(2,1)} %copy-done.1) | copy-start | bytes 9437188
  56.4 10.6 %collective-permute-start.20 = (bf16[2,1,5,64,256]{4,3,2,1,0:T(8,128)(2,1)S(1)}, bf16[2,1,5,64,256]{4,3,2,1,0:T(8,128)(2,1)S(1)}, u32[]{:S(2)}, u32[]{:S(2)}) collective-permute-start(bf16[2,1,5,64,256]{4,3,2,1,0:T(8,128)(2,1)S(1)} %get-tuple-element.44), channel_id=1, source_target_pairs={{0,2},{1,3},{2,0},{3,1},{4,6},{5,7},{6,4},{7,5},{8,10},{9,11},{10,... | collective-permute-start | bytes 983048 | tf_op jit(solution)/shard_map/ppermute | solution.py:185
  58.8 10.6 %collective-permute-start.17 = (bf16[2,1,5,64,256]{4,3,2,1,0:T(8,128)(2,1)S(1)}, bf16[2,1,5,64,256]{4,3,2,1,0:T(8,128)(2,1)S(1)}, u32[]{:S(2)}, u32[]{:S(2)}) collective-permute-start(bf16[2,1,5,64,256]{4,3,2,1,0:T(8,128)(2,1)S(1)} %products.10), channel_id=1, source_target_pairs={{0,4},{1,5},{2,6},{3,7},{4,0},{5,1},{6,2},{7,3},{8,12},{9,13},{10,... | collective-permute-start | bytes 983048 | tf_op jit(solution)/shard_map/ppermute | solution.py:185
  61.4 12.7 %collective-permute-start.14 = (bf16[2,1,5,64,256]{4,3,2,1,0:T(8,128)(2,1)S(1)}, bf16[2,1,5,64,256]{4,3,2,1,0:T(8,128)(2,1)S(1)}, u32[]{:S(2)}, u32[]{:S(2)}) collective-permute-start(bf16[2,1,5,64,256]{4,3,2,1,0:T(8,128)(2,1)S(1)} %get-tuple-element.38), channel_id=1, source_target_pairs={{0,2},{1,3},{2,0},{3,1},{4,6},{5,7},{6,4},{7,5},{8,10},{9,11},{10,... | collective-permute-start | bytes 983048 | tf_op jit(solution)/shard_map/ppermute | solution.py:185
  63.1 13.3 %collective-permute-start.12 = (bf16[2,1,5,64,256]{4,3,2,1,0:T(8,128)(2,1)S(1)}, bf16[2,1,5,64,256]{4,3,2,1,0:T(8,128)(2,1)S(1)}, u32[]{:S(2)}, u32[]{:S(2)}) collective-permute-start(bf16[2,1,5,64,256]{4,3,2,1,0:T(8,128)(2,1)S(1)} %products.7), channel_id=1, source_target_pairs={{0,4},{1,5},{2,6},{3,7},{4,0},{5,1},{6,2},{7,3},{8,12},{9,13},{10,... | collective-permute-start | bytes 983048 | tf_op jit(solution)/shard_map/ppermute | solution.py:185
  67.1 12.8 %collective-permute-start.21 = (bf16[1,5,64,256]{3,2,1,0:T(8,128)(2,1)S(1)}, bf16[1,5,64,256]{3,2,1,0:T(8,128)(2,1)S(1)}, u32[]{:S(2)}, u32[]{:S(2)}) collective-permute-start(bf16[1,5,64,256]{3,2,1,0:T(8,128)(2,1)S(1)} %get-tuple-element.46), channel_id=1, source_target_pairs={{0,4},{1,5},{2,6},{3,7},{4,0},{5,1},{6,2},{7,3},{8,12},{9,13},{10,... | collective-permute-start | bytes 491528 | tf_op jit(solution)/shard_map/ppermute | solution.py:185
  69.5 14.1 %collective-permute-start.18 = (bf16[1,5,64,256]{3,2,1,0:T(8,128)(2,1)S(1)}, bf16[1,5,64,256]{3,2,1,0:T(8,128)(2,1)S(1)}, u32[]{:S(2)}, u32[]{:S(2)}) collective-permute-start(bf16[1,5,64,256]{3,2,1,0:T(8,128)(2,1)S(1)} %get-tuple-element.42), channel_id=1, source_target_pairs={{0,2},{1,3},{2,0},{3,1},{4,6},{5,7},{6,4},{7,5},{8,10},{9,11},{10,... | collective-permute-start | bytes 491528 | tf_op jit(solution)/shard_map/ppermute | solution.py:185
  74.2 9.5 %collective-permute-start.15 = (bf16[1,5,64,256]{3,2,1,0:T(8,128)(2,1)S(1)}, bf16[1,5,64,256]{3,2,1,0:T(8,128)(2,1)S(1)}, u32[]{:S(2)}, u32[]{:S(2)}) collective-permute-start(bf16[1,5,64,256]{3,2,1,0:T(8,128)(2,1)S(1)} %get-tuple-element.40), channel_id=1, source_target_pairs={{0,4},{1,5},{2,6},{3,7},{4,0},{5,1},{6,2},{7,3},{8,12},{9,13},{10,... | collective-permute-start | bytes 491528 | tf_op jit(solution)/shard_map/ppermute | solution.py:185
  76.2 20.2 %copy-start.4 = (f32[1,5,64,256]{3,2,1,0:T(8,128)S(1)}, f32[1,5,64,256]{3,2,1,0:T(8,128)}, u32[]{:S(2)}) copy-start(f32[1,5,64,256]{3,2,1,0:T(8,128)} %omega_ref.3) | copy-start | bytes 983044
  76.5 8.2 %collective-permute-start.13 = (bf16[1,5,64,256]{3,2,1,0:T(8,128)(2,1)S(1)}, bf16[1,5,64,256]{3,2,1,0:T(8,128)(2,1)S(1)}, u32[]{:S(2)}, u32[]{:S(2)}) collective-permute-start(bf16[1,5,64,256]{3,2,1,0:T(8,128)(2,1)S(1)} %get-tuple-element.36), channel_id=1, source_target_pairs={{0,2},{1,3},{2,0},{3,1},{4,6},{5,7},{6,4},{7,5},{8,10},{9,11},{10,... | collective-permute-start | bytes 491528 | tf_op jit(solution)/shard_map/ppermute | solution.py:185
  80.0 9.0 %collective-permute-start.22 = (bf16[5,64,256]{2,1,0:T(8,128)(2,1)S(1)}, bf16[5,64,256]{2,1,0:T(8,128)(2,1)S(1)}, u32[]{:S(2)}, u32[]{:S(2)}) collective-permute-start(bf16[5,64,256]{2,1,0:T(8,128)(2,1)S(1)} %add.35), channel_id=1, source_target_pairs={{0,24},{1,25},{2,26},{3,27},{4,28},{5,29},{6,30},{7,31},{8,16},{9,... | collective-permute-start | bytes 491528 | tf_op jit(solution)/shard_map/ppermute | solution.py:185
  83.6 12.8 %collective-permute-start.19 = (bf16[5,64,256]{2,1,0:T(8,128)(2,1)S(1)}, bf16[5,64,256]{2,1,0:T(8,128)(2,1)S(1)}, u32[]{:S(2)}, u32[]{:S(2)}) collective-permute-start(bf16[5,64,256]{2,1,0:T(8,128)(2,1)S(1)} %add.33), channel_id=1, source_target_pairs={{0,16},{1,17},{2,18},{3,19},{4,20},{5,21},{6,22},{7,23},{8,24},{9,... | collective-permute-start | bytes 491528 | tf_op jit(solution)/shard_map/ppermute | solution.py:185
  83.7 12.6 %collective-permute-start.16 = (bf16[5,64,256]{2,1,0:T(8,128)(2,1)S(1)}, bf16[5,64,256]{2,1,0:T(8,128)(2,1)S(1)}, u32[]{:S(2)}, u32[]{:S(2)}) collective-permute-start(bf16[5,64,256]{2,1,0:T(8,128)(2,1)S(1)} %add.31), channel_id=1, source_target_pairs={{0,8},{1,9},{2,10},{3,11},{4,12},{5,13},{6,14},{7,15},{8,0},{9,1},... | collective-permute-start | bytes 491528 | tf_op jit(solution)/shard_map/ppermute | solution.py:185

commit v9 on v8

--- a/solution.py
+++ b/solution.py
@@ -226,6 +226,7 @@
     )(kept, across)
     own = lax.all_to_all(dealt, "line", 0, 0)
     weights += [swap(array, 0, 1) for array in weights]
+    own, weights = lax.optimization_barrier((own, weights))
     tiles = pl.pallas_call(
         functools.partial(gather_kernel, teams, chips, tile_rows),
         out_shape=jax.ShapeDtypeStruct((teams, 3, width, width), BF16),
@@ -235,7 +236,6 @@
         compiler_params=tiny,
         name="gather",
     )(place, *weights)
-    own, tiles = lax.optimization_barrier((own, tiles))
 
     def mix(data):
         return pl.pallas_call(
@@ -281,43 +281,51 @@
 
     chip_range = range(chips)
 
-    def plane_sums(group, x_first):
+    def first_parts(group, x_first):
         size = len(group)
         if x_first:
-            (far,) = products(
-                {(mz, 1, my): (0, (my, n)) for n, mz in enumerate(group) for my in chip_range},
-                [shape((chips, size), BF16)],
-            )
-            far = swap(far, 1, 0)
-            (near,) = products(
-                {(mz, 0, my): (0, (my, n)) for n, mz in enumerate(group) for my in chip_range},
-                [shape((chips, size), F32)],
-            )
+            far, near = [
+                products(
+                    {(mz, mx, my): (0, (my, n)) for n, mz in enumerate(group) for my in chip_range},
+                    [shape((chips, size), BF16 if mx else F32)],
+                )[0]
+                for mx in (1, 0)
+            ]
+            return [far], near
+        kept, *sent = products(
+            {(mz, mx, my): (my, (mx, n)) for n, mz in enumerate(group) for mx in range(LOW) for my in chip_range},
+            [shape((LOW, size), BF16 if my else F32) for my in chip_range],
+        )
+        return sent, kept
+
+    def first_hop(x_first, sent):
+        return [swap(sent[0], 1, 0)] if x_first else [swap(array, 0, 2 * my) for my, array in enumerate(sent, 1)]
+
+    def second_hop(group, x_first, received, kept):
+        size = len(group)
+        if x_first:
             groups = [[(0, my), (1, my)] for my in chip_range]
-            parts = add(groups, [shape((size,), BF16 if my else F32) for my in chip_range], near, far)
-            parts = [swap(array, 0, 2 * my) if my else array for my, array in enumerate(parts)]
-        else:
-            parts = products(
-                {
-                    (mz, mx, my): (my, (mx, n))
-                    for n, mz in enumerate(group)
-                    for mx in range(LOW)
-                    for my in chip_range
-                },
-                [shape((LOW, size), BF16 if my else F32) for my in chip_range],
-            )
-            parts = [swap(array, 0, 2 * my) if my else array for my, array in enumerate(parts)]
-            groups = [[(m, mx) for m in chip_range] for mx in range(LOW)]
-            parts = add(groups, [shape((size,), BF16 if mx else F32) for mx in range(LOW)], *parts)
-            parts = [swap(array, mx, 0) if mx else array for mx, array in enumerate(parts)]
-        groups = [[(m, n) for m in range(len(parts))] for n in range(size)]
+            parts = add(groups, [shape((size,), BF16 if my else F32) for my in chip_range], kept, *received)
+            return [swap(array, 0, 2 * my) if my else array for my, array in enumerate(parts)]
+        groups = [[(m, mx) for m in chip_range] for mx in range(LOW)]
+        parts = add(groups, [shape((size,), BF16 if mx else F32) for mx in range(LOW)], kept, *received)
+        return [swap(array, mx, 0) if mx else array for mx, array in enumerate(parts)]
+
+    def sums_of(group, parts):
+        groups = [[(m, n) for m in range(len(parts))] for n in range(len(group))]
         return add(groups, [shape((), BF16 if mz else F32) for mz in group], *parts)
 
     quarter = count // 4
     bounds = [range(n * quarter, (n + 1) * quarter) for n in range(4)]
-    far_sums = [*plane_sums(bounds[2], True), *plane_sums(bounds[3], False)]
-    near_sums = [*plane_sums(bounds[0], True), *plane_sums(bounds[1], False)]
-    sums = along_line(near_sums + far_sums)
+    x_first = [True, False, True, False]
+    firsts = [first_parts(*each) for each in zip(bounds, x_first)]
+    received = [first_hop(first, sent) for first, (sent, _) in zip(x_first, firsts)]
+    sums = [None] * 4
+    for n in (2, 3, 0, 1):
+        sums[n] = sums_of(bounds[n], second_hop(bounds[n], x_first[n], received[n], firsts[n][1]))
+        if n == 3:
+            received[:2], firsts[:2], sums[2:] = lax.optimization_barrier((received[:2], firsts[:2], sums[2:]))
+    sums = along_line([total for group in sums for total in group])
 
     scale = 1.0 / (2.0 * teams * times * replicas)
     return pl.pallas_call(

time: 98.1 us -> 103 us (1.050)
  local copies, waits for them, and re-layouts: 5.8 us -> 11 us
  starting transfers between devices: 28.4 us -> 25.2 us
  waiting for transfers between devices: 45.1 us -> 47.7 us
    unnamed x10 -> x26, local copies, waits for them, and re-layouts: 5.72 us -> 10.9 us
    ppermute x23, starting transfers between devices: 24.5 us -> 21.3 us  [swap(): return lax.ppermute(array, AXES, route)]
    all_to_all x1, waiting for transfers between devices: 0.01 us -> 1.55 us  [per_device(): own = lax.all_to_all(dealt, 'line', 0, 0)]
    ppermute x23, waiting for transfers between devices: 45.1 us -> 46.1 us  [swap(): return lax.ppermute(array, AXES, route)]
  transfers between devices with their start and end apart: 24 -> 24, of which waited for: 14 -> 13; matrix products, arithmetic and copies ran while one was open for 1% -> 1% of each run, Pallas kernels for 12% -> 11%
where the time goes in v9:
time: 103 us; the launch traced here: 102 us
  waiting for transfers between devices  47.7 us (46%)
  starting transfers between devices  25.2 us (24%)
  Pallas kernels  17.5 us (17%)
  local copies, waits for them, and re-layouts  11 us (11%)
    ppermute x23, waiting for transfers between devices, swap(): return lax.ppermute(array, AXES, route)  46.1 us
    ppermute x23, starting transfers between devices, swap(): return lax.ppermute(array, AXES, route)  21.3 us
    unnamed x26, local copies, waits for them, and re-layouts  10.9 us
    pallas_call x6, Pallas kernels, products(): pl.pallas_call(functools.partial(product_kernel, teams, chips, wanted), o...  7.04 us
    pallas_call x2, Pallas kernels, mix(): pl.pallas_call(functools.partial(mix_kernel, teams, replicas, tile_rows),...  4.6 us
    all_to_all x1, starting transfers between devices, per_device(): own = lax.all_to_all(dealt, 'line', 0, 0)  3.91 us
    pallas_call x1, Pallas kernels, per_device(): pl.pallas_call(functools.partial(gather_kernel, teams, chips, tile_rows),...  2.44 us
  transfers between devices with their start and end apart: 24, of which 13 were waited for; matrix products, arithmetic and copies ran while one was open for 1% of the time, Pallas kernels for 11%

profile of v9, /device:TPU:0, one launch (start us, length us, event | category | flops | bytes accessed | tf_op | source)
XLA Modules:
  0.0 102.4 jit_solution(9596467843594776792)
XLA Ops:
  0.0 1.2 %copy-done = bf16[2048,256]{1,0:T(8,128)(2,1)S(1)} copy-done((bf16[2048,256]{1,0:T(8,128)(2,1)S(1)}, bf16[2048,256]{1,0:T(8,128)(2,1)}, u32[]{:S(2)}) %copy-start) | copy-done | bytes 1048600
  1.3 3.0 %collective-permute-start.3 = (bf16[1024,256]{1,0:T(8,128)(2,1)S(1)}, bf16[1024,256]{1,0:T(8,128)(2,1)S(1)}, u32[]{:S(2)}, u32[]{:S(2)}) collective-permute-start(bf16[1024,256]{1,0:T(8,128)(2,1)S(1)} %constant_dynamic-slice_fusion.1), channel_id=1, source_target_pairs={{0,4},{1,5},{2,6},{3,7},{4,0},{5,1},{6,2},{7,3},{8,12},{9,13},{10,... | collective-permute-start | bytes 1572872 | tf_op jit(solution)/shard_map/ppermute | solution.py:185
  4.3 0.7 pad_add_fusion.place_ref
  5.0 1.0 copy-done.1
  6.6 1.6 %collective-permute-start = (bf16[3,64,256]{2,1,0:T(8,128)(2,1)S(1)}, bf16[3,64,256]{2,1,0:T(8,128)(2,1)S(1)}, u32[]{:S(2)}, u32[]{:S(2)}) collective-permute-start(bf16[3,64,256]{2,1,0:T(8,128)(2,1)S(1)} %prepare.1), channel_id=1, source_target_pairs={{0,8},{1,9},{2,10},{3,11},{4,12},{5,13},{6,14},{7,15},{8,0},{9,1},... | collective-permute-start | bytes 294920 | tf_op jit(solution)/shard_map/ppermute | solution.py:185
  8.2 2.6 %collective-permute-start.1 = (bf16[3,64,256]{2,1,0:T(8,128)(2,1)S(1)}, bf16[3,64,256]{2,1,0:T(8,128)(2,1)S(1)}, u32[]{:S(2)}, u32[]{:S(2)}) collective-permute-start(bf16[3,64,256]{2,1,0:T(8,128)(2,1)S(1)} %prepare.1), channel_id=1, source_target_pairs={{0,16},{1,17},{2,18},{3,19},{4,20},{5,21},{6,22},{7,23},{8,24},{9,... | collective-permute-start | bytes 294920 | tf_op jit(solution)/shard_map/ppermute | solution.py:185
  11.0 1.2 %collective-permute-done = bf16[3,64,256]{2,1,0:T(8,128)(2,1)S(1)} collective-permute-done((bf16[3,64,256]{2,1,0:T(8,128)(2,1)S(1)}, bf16[3,64,256]{2,1,0:T(8,128)(2,1)S(1)}, u32[]{:S(2)}, u32[]{:S(2)}) %collective-permute-start) | collective-permute-done | bytes 98336 | tf_op jit(solution)/shard_map/ppermute | solution.py:185
  12.2 6.1 %collective-permute-done.1 = bf16[3,64,256]{2,1,0:T(8,128)(2,1)S(1)} collective-permute-done((bf16[3,64,256]{2,1,0:T(8,128)(2,1)S(1)}, bf16[3,64,256]{2,1,0:T(8,128)(2,1)S(1)}, u32[]{:S(2)}, u32[]{:S(2)}) %collective-permute-start.1) | collective-permute-done | bytes 98336 | tf_op jit(solution)/shard_map/ppermute | solution.py:185
  18.5 1.0 deal.1
  19.5 3.9 %all-to-all-start = ((bf16[4,2,256,256]{3,2,1,0:T(8,128)(2,1)}), bf16[4,2,256,256]{3,2,1,0:T(8,128)(2,1)S(1)}, u32[]{:S(2)}, u32[]{:S(2)}) async-start(bf16[4,2,256,256]{3,2,1,0:T(8,128)(2,1)} %deal.1), calls=%async_computation | async-start | bytes 2097152 | tf_op jit(solution)/shard_map/all_to_all | solution.py:227
  23.4 1.5 %collective-permute-start.6 = (bf16[4,3,64,256]{3,2,1,0:T(8,128)(2,1)S(1)}, bf16[4,3,64,256]{3,2,1,0:T(8,128)(2,1)S(1)}, u32[]{:S(2)}, u32[]{:S(2)}) collective-permute-start(bf16[4,3,64,256]{3,2,1,0:T(8,128)(2,1)S(1)} %pad_maximum_fusion.rest_0_), channel_id=1, source_target_pairs={{0,6},{1,7},{2,4},{3,5},{4,2},{5,3},{6,0},{7,1},{8,14},{9,15},{10,... | collective-permute-start | bytes 1179656 | tf_op jit(solution)/shard_map/ppermute | solution.py:185
  25.4 1.5 %collective-permute-start.5 = (bf16[4,3,64,256]{3,2,1,0:T(8,128)(2,1)S(1)}, bf16[4,3,64,256]{3,2,1,0:T(8,128)(2,1)S(1)}, u32[]{:S(2)}, u32[]{:S(2)}) collective-permute-start(bf16[4,3,64,256]{3,2,1,0:T(8,128)(2,1)S(1)} %pad_maximum_fusion.rest_0_), channel_id=1, source_target_pairs={{0,4},{1,5},{2,6},{3,7},{4,0},{5,1},{6,2},{7,3},{8,12},{9,13},{10,... | collective-permute-start | bytes 1179656 | tf_op jit(solution)/shard_map/ppermute | solution.py:185
  26.9 9.5 %collective-permute-done.6.rest_3_ = bf16[4,3,64,256]{3,2,1,0:T(8,128)(2,1)S(1)} collective-permute-done((bf16[4,3,64,256]{3,2,1,0:T(8,128)(2,1)S(1)}, bf16[4,3,64,256]{3,2,1,0:T(8,128)(2,1)S(1)}, u32[]{:S(2)}, u32[]{:S(2)}) %collective-permute-start.6) | collective-permute-done | bytes 393248 | tf_op jit(solution)/shard_map/ppermute | solution.py:185
  36.4 5.7 %collective-permute-done.4.rest_1_ = bf16[4,3,64,256]{3,2,1,0:T(8,128)(2,1)S(1)} collective-permute-done((bf16[4,3,64,256]{3,2,1,0:T(8,128)(2,1)S(1)}, bf16[4,3,64,256]{3,2,1,0:T(8,128)(2,1)S(1)}, u32[]{:S(2)}, u32[]{:S(2)}) %collective-permute-start.4) | collective-permute-done | bytes 393248 | tf_op jit(solution)/shard_map/ppermute | solution.py:185
  42.5 0.7 copy-done.3
  43.3 0.7 copy-done.5
  44.0 0.8 copy-done.7
  44.8 0.7 copy-done.9
  45.5 0.8 copy-done.11
  46.3 1.5 %all-to-all-done.data_ref = bf16[4,2,256,256]{3,2,1,0:T(8,128)(2,1)S(1)} async-done(((bf16[4,2,256,256]{3,2,1,0:T(8,128)(2,1)}), bf16[4,2,256,256]{3,2,1,0:T(8,128)(2,1)S(1)}, u32[]{:S(2)}, u32[]{:S(2)}) %all-to-all-start) | async-done | bytes 1048608 | tf_op jit(solution)/shard_map/all_to_all | solution.py:227
  47.8 1.0 copy-done.4
  48.8 1.0 copy-done.6
  49.8 1.0 copy-done.8
  50.8 1.0 copy-done.10
  51.8 1.0 copy-done.12
  52.8 2.4 %gather.1.omega_ref = bf16[8,3,256,256]{3,2,1,0:T(8,128)(2,1)S(1)} custom-call(s32[7]{0:T(128)S(1)} %pad_add_fusion.place_ref, bf16[4,3,64,256]{3,2,1,0:T(8,128)(2,1)S(1)} %pad_maximum_fusion.rest_0_, bf16[4,3,64,256]{3,2,1,0:T(8,128)(2,1)S(1)} %collective-permute-done.4.rest_1_, bf16[4,3,64,256]{3,2,1,0:T(8,128)(2,1)S(1)} %copy-done.4, ...), custom_call_target="tpu_custom_call" | custom-call | tf_op jit(solution)/shard_map/gather/pallas_call | solution.py:230
  55.3 2.3 %mix.2 = (bf16[8,512,256]{2,1,0:T(8,128)(2,1)S(1)}, bf16[8,128,512]{2,1,0:T(8,128)(2,1)S(1)}) custom-call(s32[7]{0:T(128)S(1)} %pad_add_fusion.place_ref, bf16[4,2,256,256]{3,2,1,0:T(8,128)(2,1)S(1)} %all-to-all-done.data_ref, bf16[8,3,256,256]{3,2,1,0:T(8,128)(2,1)S(1)} %gather.1.omega_ref), custom_call_target="tpu_custom_call" | custom-call | tf_op jit(solution)/shard_map/mix/pallas_call | solution.py:241
  57.6 2.3 %mix.3 = (bf16[8,512,256]{2,1,0:T(8,128)(2,1)S(1)}, bf16[8,128,512]{2,1,0:T(8,128)(2,1)S(1)}) custom-call(s32[7]{0:T(128)S(1)} %pad_add_fusion.place_ref, bf16[4,2,256,256]{3,2,1,0:T(8,128)(2,1)S(1)} %collective-permute-done.11.data_ref, bf16[8,3,256,256]{3,2,1,0:T(8,128)(2,1)S(1)} %gather.1.omega_ref), custom_call_target="tpu_custom_call" | custom-call | tf_op jit(solution)/shard_map/mix/pallas_call | solution.py:241
  59.9 1.4 %products.11 = (f32[2,1,5,64,256]{4,3,2,1,0:T(8,128)S(1)}, bf16[2,1,5,64,256]{4,3,2,1,0:T(8,128)(2,1)S(1)}) custom-call(s32[7]{0:T(128)S(1)} %pad_add_fusion.place_ref, bf16[8,512,256]{2,1,0:T(8,128)(2,1)S(1)} %get-tuple-element.51.rest_0_, bf16[8,128,512]{2,1,0:T(8,128)(2,1)S(1)} %get-tuple-element.52.rest_1_, ...), custom_call_target="tpu_custom_call" | custom-call | tf_op jit(solution)/shard_map/products/pallas_call | solution.py:263
  61.3 1.6 %collective-permute-start.16 = (bf16[2,1,5,64,256]{4,3,2,1,0:T(8,128)(2,1)S(1)}, bf16[2,1,5,64,256]{4,3,2,1,0:T(8,128)(2,1)S(1)}, u32[]{:S(2)}, u32[]{:S(2)}) collective-permute-start(bf16[2,1,5,64,256]{4,3,2,1,0:T(8,128)(2,1)S(1)} %get-tuple-element.60), channel_id=1, source_target_pairs={{0,2},{1,3},{2,0},{3,1},{4,6},{5,7},{6,4},{7,5},{8,10},{9,11},{10,... | collective-permute-start | bytes 983048 | tf_op jit(solution)/shard_map/ppermute | solution.py:185
  62.9 1.1 %products.10 = bf16[2,1,5,64,256]{4,3,2,1,0:T(8,128)(2,1)S(1)} custom-call(s32[7]{0:T(128)S(1)} %pad_add_fusion.place_ref, bf16[8,512,256]{2,1,0:T(8,128)(2,1)S(1)} %get-tuple-element.51.rest_0_, bf16[8,128,512]{2,1,0:T(8,128)(2,1)S(1)} %get-tuple-element.52.rest_1_, bf16[8,512,256]{2,1,0:T(8,128)(2,1)S(1)} %get-tuple-element.53.rest_2_, ...), custom_call_target="tpu_custom_call" | custom-call | tf_op jit(solution)/shard_map/products/pallas_call | solution.py:263
  64.0 1.0 collective-permute-start.14
  64.9 1.4 %products.7 = (f32[2,1,5,64,256]{4,3,2,1,0:T(8,128)S(1)}, bf16[2,1,5,64,256]{4,3,2,1,0:T(8,128)(2,1)S(1)}) custom-call(s32[7]{0:T(128)S(1)} %pad_add_fusion.place_ref, bf16[8,512,256]{2,1,0:T(8,128)(2,1)S(1)} %get-tuple-element.51.rest_0_, bf16[8,128,512]{2,1,0:T(8,128)(2,1)S(1)} %get-tuple-element.52.rest_1_, ...), custom_call_target="tpu_custom_call" | custom-call | tf_op jit(solution)/shard_map/products/pallas_call | solution.py:263
  66.3 1.1 %products.6 = bf16[2,1,5,64,256]{4,3,2,1,0:T(8,128)(2,1)S(1)} custom-call(s32[7]{0:T(128)S(1)} %pad_add_fusion.place_ref, bf16[8,512,256]{2,1,0:T(8,128)(2,1)S(1)} %get-tuple-element.51.rest_0_, bf16[8,128,512]{2,1,0:T(8,128)(2,1)S(1)} %get-tuple-element.52.rest_1_, bf16[8,512,256]{2,1,0:T(8,128)(2,1)S(1)} %get-tuple-element.53.rest_2_, ...), custom_call_target="tpu_custom_call" | custom-call | tf_op jit(solution)/shard_map/products/pallas_call | solution.py:263
  68.0 1.1 %collective-permute-start.12 = (bf16[2,1,5,64,256]{4,3,2,1,0:T(8,128)(2,1)S(1)}, bf16[2,1,5,64,256]{4,3,2,1,0:T(8,128)(2,1)S(1)}, u32[]{:S(2)}, u32[]{:S(2)}) collective-permute-start(bf16[2,1,5,64,256]{4,3,2,1,0:T(8,128)(2,1)S(1)} %products.6), channel_id=1, source_target_pairs={{0,4},{1,5},{2,6},{3,7},{4,0},{5,1},{6,2},{7,3},{8,12},{9,13},{10,... | collective-permute-start | bytes 983048 | tf_op jit(solution)/shard_map/ppermute | solution.py:185
  69.1 1.1 %products.9.refs_0_ = f32[2,1,5,64,256]{4,3,2,1,0:T(8,128)S(1)} custom-call(s32[7]{0:T(128)S(1)} %pad_add_fusion.place_ref, bf16[8,512,256]{2,1,0:T(8,128)(2,1)S(1)} %get-tuple-element.51.rest_0_, bf16[8,128,512]{2,1,0:T(8,128)(2,1)S(1)} %get-tuple-element.52.rest_1_, bf16[8,512,256]{2,1,0:T(8,128)(2,1)S(1)} %get-tuple-element.53.rest_2_, ...), custom_call_target="tpu_custom_call" | custom-call | tf_op jit(solution)/shard_map/products/pallas_call | solution.py:263
  70.2 1.7 %collective-permute-done.16.refs_1_ = bf16[2,1,5,64,256]{4,3,2,1,0:T(8,128)(2,1)S(1)} collective-permute-done((bf16[2,1,5,64,256]{4,3,2,1,0:T(8,128)(2,1)S(1)}, bf16[2,1,5,64,256]{4,3,2,1,0:T(8,128)(2,1)S(1)}, u32[]{:S(2)}, u32[]{:S(2)}) %collective-permute-start.16) | collective-permute-done | bytes 327712 | tf_op jit(solution)/shard_map/ppermute | solution.py:185
  72.0 0.9 collective-permute-start.17
  72.9 1.7 %collective-permute-done.14.refs_1_ = bf16[2,1,5,64,256]{4,3,2,1,0:T(8,128)(2,1)S(1)} collective-permute-done((bf16[2,1,5,64,256]{4,3,2,1,0:T(8,128)(2,1)S(1)}, bf16[2,1,5,64,256]{4,3,2,1,0:T(8,128)(2,1)S(1)}, u32[]{:S(2)}, u32[]{:S(2)}) %collective-permute-start.14) | collective-permute-done | bytes 327712 | tf_op jit(solution)/shard_map/ppermute | solution.py:185
  75.2 1.1 %products.8.refs_0_ = f32[2,1,5,64,256]{4,3,2,1,0:T(8,128)S(1)} custom-call(s32[7]{0:T(128)S(1)} %pad_add_fusion.place_ref, bf16[8,512,256]{2,1,0:T(8,128)(2,1)S(1)} %get-tuple-element.51.rest_0_, bf16[8,128,512]{2,1,0:T(8,128)(2,1)S(1)} %get-tuple-element.52.rest_1_, bf16[8,512,256]{2,1,0:T(8,128)(2,1)S(1)} %get-tuple-element.53.rest_2_, ...), custom_call_target="tpu_custom_call" | custom-call | tf_op jit(solution)/shard_map/products/pallas_call | solution.py:263
  76.3 8.2 %collective-permute-done.17.refs_1_ = bf16[1,5,64,256]{3,2,1,0:T(8,128)(2,1)S(1)} collective-permute-done((bf16[1,5,64,256]{3,2,1,0:T(8,128)(2,1)S(1)}, bf16[1,5,64,256]{3,2,1,0:T(8,128)(2,1)S(1)}, u32[]{:S(2)}, u32[]{:S(2)}) %collective-permute-start.17) | collective-permute-done | bytes 163872 | tf_op jit(solution)/shard_map/ppermute | solution.py:185
  84.6 1.0 collective-permute-start.19
  86.2 1.1 %collective-permute-start.21 = (bf16[5,64,256]{2,1,0:T(8,128)(2,1)S(1)}, bf16[5,64,256]{2,1,0:T(8,128)(2,1)S(1)}, u32[]{:S(2)}, u32[]{:S(2)}) collective-permute-start(bf16[5,64,256]{2,1,0:T(8,128)(2,1)S(1)} %add.29), channel_id=1, source_target_pairs={{0,16},{1,17},{2,18},{3,19},{4,20},{5,21},{6,22},{7,23},{8,24},{9,... | collective-permute-start | bytes 491528 | tf_op jit(solution)/shard_map/ppermute | solution.py:185
  87.3 1.5 %collective-permute-start.22 = (bf16[5,64,256]{2,1,0:T(8,128)(2,1)S(1)}, bf16[5,64,256]{2,1,0:T(8,128)(2,1)S(1)}, u32[]{:S(2)}, u32[]{:S(2)}) collective-permute-start(bf16[5,64,256]{2,1,0:T(8,128)(2,1)S(1)} %add.31), channel_id=1, source_target_pairs={{0,24},{1,25},{2,26},{3,27},{4,28},{5,29},{6,30},{7,31},{8,16},{9,... | collective-permute-start | bytes 491528 | tf_op jit(solution)/shard_map/ppermute | solution.py:185
  88.8 1.4 %collective-permute-done.19.refs_1_ = bf16[1,5,64,256]{3,2,1,0:T(8,128)(2,1)S(1)} collective-permute-done((bf16[1,5,64,256]{3,2,1,0:T(8,128)(2,1)S(1)}, bf16[1,5,64,256]{3,2,1,0:T(8,128)(2,1)S(1)}, u32[]{:S(2)}, u32[]{:S(2)}) %collective-permute-start.19) | collective-permute-done | bytes 163872 | tf_op jit(solution)/shard_map/ppermute | solution.py:185
  91.1 8.0 %collective-permute-done.21.rest_2_ = bf16[5,64,256]{2,1,0:T(8,128)(2,1)S(1)} collective-permute-done((bf16[5,64,256]{2,1,0:T(8,128)(2,1)S(1)}, bf16[5,64,256]{2,1,0:T(8,128)(2,1)S(1)}, u32[]{:S(2)}, u32[]{:S(2)}) %collective-permute-start.21) | collective-permute-done | bytes 163872 | tf_op jit(solution)/shard_map/ppermute | solution.py:185
  99.0 1.9 %collective-permute-done.20.rest_1_ = bf16[5,64,256]{2,1,0:T(8,128)(2,1)S(1)} collective-permute-done((bf16[5,64,256]{2,1,0:T(8,128)(2,1)S(1)}, bf16[5,64,256]{2,1,0:T(8,128)(2,1)S(1)}, u32[]{:S(2)}, u32[]{:S(2)}) %collective-permute-start.20) | collective-permute-done | bytes 163872 | tf_op jit(solution)/shard_map/ppermute | solution.py:185
  101.0 1.5 %update.1 = f32[1,5,64,256]{3,2,1,0:T(8,128)} custom-call(s32[7]{0:T(128)S(1)} %pad_add_fusion.place_ref, f32[1,5,64,256]{3,2,1,0:T(8,128)S(1)} %copy-done.2, f32[5,64,256]{2,1,0:T(8,128)S(1)} %add.33.rest_0_, bf16[5,64,256]{2,1,0:T(8,128)(2,1)S(1)} %collective-permute-done.20.rest_1_, bf16[5,64,256]{2,1,0:T(8,128)(2,1)S(1)} %collective-permute-done.21.rest_2_, ...), custom_call_target="tpu_custom_call" | custom-call | tf_op jit(solution)/shard_map/update/pallas_call | solution.py:331
  (50 shorter events, 4.9 us)
Async XLA Ops:
  0.0 1.2 %copy-start = (bf16[2048,256]{1,0:T(8,128)(2,1)S(1)}, bf16[2048,256]{1,0:T(8,128)(2,1)}, u32[]{:S(2)}) copy-start(bf16[2048,256]{1,0:T(8,128)(2,1)} %param.3) | copy-start | bytes 3145732
  1.3 17.1 %collective-permute-start.3 = (bf16[1024,256]{1,0:T(8,128)(2,1)S(1)}, bf16[1024,256]{1,0:T(8,128)(2,1)S(1)}, u32[]{:S(2)}, u32[]{:S(2)}) collective-permute-start(bf16[1024,256]{1,0:T(8,128)(2,1)S(1)} %constant_dynamic-slice_fusion.1), channel_id=1, source_target_pairs={{0,4},{1,5},{2,6},{3,7},{4,0},{5,1},{6,2},{7,3},{8,12},{9,13},{10,... | collective-permute-start | bytes 1572872 | tf_op jit(solution)/shard_map/ppermute | solution.py:185
  5.0 1.0 copy-start.1
  6.6 5.7 %collective-permute-start = (bf16[3,64,256]{2,1,0:T(8,128)(2,1)S(1)}, bf16[3,64,256]{2,1,0:T(8,128)(2,1)S(1)}, u32[]{:S(2)}, u32[]{:S(2)}) collective-permute-start(bf16[3,64,256]{2,1,0:T(8,128)(2,1)S(1)} %prepare.1), channel_id=1, source_target_pairs={{0,8},{1,9},{2,10},{3,11},{4,12},{5,13},{6,14},{7,15},{8,0},{9,1},... | collective-permute-start | bytes 294920 | tf_op jit(solution)/shard_map/ppermute | solution.py:185
  8.2 10.1 %collective-permute-start.1 = (bf16[3,64,256]{2,1,0:T(8,128)(2,1)S(1)}, bf16[3,64,256]{2,1,0:T(8,128)(2,1)S(1)}, u32[]{:S(2)}, u32[]{:S(2)}) collective-permute-start(bf16[3,64,256]{2,1,0:T(8,128)(2,1)S(1)} %prepare.1), channel_id=1, source_target_pairs={{0,16},{1,17},{2,18},{3,19},{4,20},{5,21},{6,22},{7,23},{8,24},{9,... | collective-permute-start | bytes 294920 | tf_op jit(solution)/shard_map/ppermute | solution.py:185
  10.8 7.6 %collective-permute-start.2 = (bf16[3,64,256]{2,1,0:T(8,128)(2,1)S(1)}, bf16[3,64,256]{2,1,0:T(8,128)(2,1)S(1)}, u32[]{:S(2)}, u32[]{:S(2)}) collective-permute-start(bf16[3,64,256]{2,1,0:T(8,128)(2,1)S(1)} %prepare.1), channel_id=1, source_target_pairs={{0,24},{1,25},{2,26},{3,27},{4,28},{5,29},{6,30},{7,31},{8,16},{9,... | collective-permute-start | bytes 294920 | tf_op jit(solution)/shard_map/ppermute | solution.py:185
  19.5 28.3 %all-to-all-start = ((bf16[4,2,256,256]{3,2,1,0:T(8,128)(2,1)}), bf16[4,2,256,256]{3,2,1,0:T(8,128)(2,1)S(1)}, u32[]{:S(2)}, u32[]{:S(2)}) async-start(bf16[4,2,256,256]{3,2,1,0:T(8,128)(2,1)} %deal.1), calls=%async_computation | async-start | bytes 2097152 | tf_op jit(solution)/shard_map/all_to_all | solution.py:227
  23.4 13.0 %collective-permute-start.6 = (bf16[4,3,64,256]{3,2,1,0:T(8,128)(2,1)S(1)}, bf16[4,3,64,256]{3,2,1,0:T(8,128)(2,1)S(1)}, u32[]{:S(2)}, u32[]{:S(2)}) collective-permute-start(bf16[4,3,64,256]{3,2,1,0:T(8,128)(2,1)S(1)} %pad_maximum_fusion.rest_0_), channel_id=1, source_target_pairs={{0,6},{1,7},{2,4},{3,5},{4,2},{5,3},{6,0},{7,1},{8,14},{9,15},{10,... | collective-permute-start | bytes 1179656 | tf_op jit(solution)/shard_map/ppermute | solution.py:185
  24.9 17.1 %collective-permute-start.4 = (bf16[4,3,64,256]{3,2,1,0:T(8,128)(2,1)S(1)}, bf16[4,3,64,256]{3,2,1,0:T(8,128)(2,1)S(1)}, u32[]{:S(2)}, u32[]{:S(2)}) collective-permute-start(bf16[4,3,64,256]{3,2,1,0:T(8,128)(2,1)S(1)} %pad_maximum_fusion.rest_0_), channel_id=1, source_target_pairs={{0,2},{1,3},{2,0},{3,1},{4,6},{5,7},{6,4},{7,5},{8,10},{9,11},{10,... | collective-permute-start | bytes 1179656 | tf_op jit(solution)/shard_map/ppermute | solution.py:185
  25.4 16.7 %collective-permute-start.5 = (bf16[4,3,64,256]{3,2,1,0:T(8,128)(2,1)S(1)}, bf16[4,3,64,256]{3,2,1,0:T(8,128)(2,1)S(1)}, u32[]{:S(2)}, u32[]{:S(2)}) collective-permute-start(bf16[4,3,64,256]{3,2,1,0:T(8,128)(2,1)S(1)} %pad_maximum_fusion.rest_0_), channel_id=1, source_target_pairs={{0,4},{1,5},{2,6},{3,7},{4,0},{5,1},{6,2},{7,3},{8,12},{9,13},{10,... | collective-permute-start | bytes 1179656 | tf_op jit(solution)/shard_map/ppermute | solution.py:185
  26.9 16.4 %collective-permute-start.7 = (bf16[4,3,64,256]{3,2,1,0:T(8,128)(2,1)S(1)}, bf16[4,3,64,256]{3,2,1,0:T(8,128)(2,1)S(1)}, u32[]{:S(2)}, u32[]{:S(2)}) collective-permute-start(bf16[4,3,64,256]{3,2,1,0:T(8,128)(2,1)S(1)} %pad_maximum_fusion.rest_0_), channel_id=1, source_target_pairs={{0,1},{1,0},{2,3},{3,2},{4,5},{5,4},{6,7},{7,6},{8,9},{9,8},{10,11... | collective-permute-start | bytes 1179656 | tf_op jit(solution)/shard_map/ppermute | solution.py:185
  36.4 7.7 %collective-permute-start.10 = (bf16[4,3,64,256]{3,2,1,0:T(8,128)(2,1)S(1)}, bf16[4,3,64,256]{3,2,1,0:T(8,128)(2,1)S(1)}, u32[]{:S(2)}, u32[]{:S(2)}) collective-permute-start(bf16[4,3,64,256]{3,2,1,0:T(8,128)(2,1)S(1)} %collective-permute-done.6.rest_3_), channel_id=1, source_target_pairs={{0,1},{1,0},{2,3},{3,2},{4,5},{5,4},{6,7},{7,6},{8,9},{9,8},{10,11... | collective-permute-start | bytes 1179656 | tf_op jit(solution)/shard_map/ppermute | solution.py:185
  42.0 2.8 %collective-permute-start.8 = (bf16[4,3,64,256]{3,2,1,0:T(8,128)(2,1)S(1)}, bf16[4,3,64,256]{3,2,1,0:T(8,128)(2,1)S(1)}, u32[]{:S(2)}, u32[]{:S(2)}) collective-permute-start(bf16[4,3,64,256]{3,2,1,0:T(8,128)(2,1)S(1)} %collective-permute-done.4.rest_1_), channel_id=1, source_target_pairs={{0,1},{1,0},{2,3},{3,2},{4,5},{5,4},{6,7},{7,6},{8,9},{9,8},{10,11... | collective-permute-start | bytes 1179656 | tf_op jit(solution)/shard_map/ppermute | solution.py:185
  42.1 3.4 %collective-permute-start.9 = (bf16[4,3,64,256]{3,2,1,0:T(8,128)(2,1)S(1)}, bf16[4,3,64,256]{3,2,1,0:T(8,128)(2,1)S(1)}, u32[]{:S(2)}, u32[]{:S(2)}) collective-permute-start(bf16[4,3,64,256]{3,2,1,0:T(8,128)(2,1)S(1)} %collective-permute-done.5.rest_2_), channel_id=1, source_target_pairs={{0,1},{1,0},{2,3},{3,2},{4,5},{5,4},{6,7},{7,6},{8,9},{9,8},{10,11... | collective-permute-start | bytes 1179656 | tf_op jit(solution)/shard_map/ppermute | solution.py:185
  42.5 0.7 copy-start.3
  43.3 0.7 copy-start.5
  44.0 0.8 copy-start.7
  44.8 0.7 copy-start.9
  45.5 0.8 copy-start.11
  47.8 9.8 %collective-permute-start.11 = (bf16[4,2,256,256]{3,2,1,0:T(8,128)(2,1)S(1)}, bf16[4,2,256,256]{3,2,1,0:T(8,128)(2,1)S(1)}, u32[]{:S(2)}, u32[]{:S(2)}) collective-permute-start(bf16[4,2,256,256]{3,2,1,0:T(8,128)(2,1)S(1)} %all-to-all-done.data_ref), channel_id=1, source_target_pairs={{0,1},{1,0},{2,3},{3,2},{4,5},{5,4},{6,7},{7,6},{8,9},{9,8},{10,11... | collective-permute-start | bytes 3145736 | tf_op jit(solution)/shard_map/ppermute | solution.py:185
  47.8 1.0 copy-start.4
  48.8 1.0 copy-start.6
  49.8 1.0 copy-start.8
  50.8 1.0 copy-start.10
  51.8 1.0 copy-start.12
  61.3 10.6 %collective-permute-start.16 = (bf16[2,1,5,64,256]{4,3,2,1,0:T(8,128)(2,1)S(1)}, bf16[2,1,5,64,256]{4,3,2,1,0:T(8,128)(2,1)S(1)}, u32[]{:S(2)}, u32[]{:S(2)}) collective-permute-start(bf16[2,1,5,64,256]{4,3,2,1,0:T(8,128)(2,1)S(1)} %get-tuple-element.60), channel_id=1, source_target_pairs={{0,2},{1,3},{2,0},{3,1},{4,6},{5,7},{6,4},{7,5},{8,10},{9,11},{10,... | collective-permute-start | bytes 983048 | tf_op jit(solution)/shard_map/ppermute | solution.py:185
  64.0 10.6 %collective-permute-start.14 = (bf16[2,1,5,64,256]{4,3,2,1,0:T(8,128)(2,1)S(1)}, bf16[2,1,5,64,256]{4,3,2,1,0:T(8,128)(2,1)S(1)}, u32[]{:S(2)}, u32[]{:S(2)}) collective-permute-start(bf16[2,1,5,64,256]{4,3,2,1,0:T(8,128)(2,1)S(1)} %products.10), channel_id=1, source_target_pairs={{0,4},{1,5},{2,6},{3,7},{4,0},{5,1},{6,2},{7,3},{8,12},{9,13},{10,... | collective-permute-start | bytes 983048 | tf_op jit(solution)/shard_map/ppermute | solution.py:185
  67.4 17.1 %collective-permute-start.13 = (bf16[2,1,5,64,256]{4,3,2,1,0:T(8,128)(2,1)S(1)}, bf16[2,1,5,64,256]{4,3,2,1,0:T(8,128)(2,1)S(1)}, u32[]{:S(2)}, u32[]{:S(2)}) collective-permute-start(bf16[2,1,5,64,256]{4,3,2,1,0:T(8,128)(2,1)S(1)} %get-tuple-element.55), channel_id=1, source_target_pairs={{0,2},{1,3},{2,0},{3,1},{4,6},{5,7},{6,4},{7,5},{8,10},{9,11},{10,... | collective-permute-start | bytes 983048 | tf_op jit(solution)/shard_map/ppermute | solution.py:185
  68.0 16.6 %collective-permute-start.12 = (bf16[2,1,5,64,256]{4,3,2,1,0:T(8,128)(2,1)S(1)}, bf16[2,1,5,64,256]{4,3,2,1,0:T(8,128)(2,1)S(1)}, u32[]{:S(2)}, u32[]{:S(2)}) collective-permute-start(bf16[2,1,5,64,256]{4,3,2,1,0:T(8,128)(2,1)S(1)} %products.6), channel_id=1, source_target_pairs={{0,4},{1,5},{2,6},{3,7},{4,0},{5,1},{6,2},{7,3},{8,12},{9,13},{10,... | collective-permute-start | bytes 983048 | tf_op jit(solution)/shard_map/ppermute | solution.py:185
  72.0 12.5 %collective-permute-start.17 = (bf16[1,5,64,256]{3,2,1,0:T(8,128)(2,1)S(1)}, bf16[1,5,64,256]{3,2,1,0:T(8,128)(2,1)S(1)}, u32[]{:S(2)}, u32[]{:S(2)}) collective-permute-start(bf16[1,5,64,256]{3,2,1,0:T(8,128)(2,1)S(1)} %get-tuple-element.62), channel_id=1, source_target_pairs={{0,4},{1,5},{2,6},{3,7},{4,0},{5,1},{6,2},{7,3},{8,12},{9,13},{10,... | collective-permute-start | bytes 491528 | tf_op jit(solution)/shard_map/ppermute | solution.py:185
  74.6 9.9 %collective-permute-start.15 = (bf16[1,5,64,256]{3,2,1,0:T(8,128)(2,1)S(1)}, bf16[1,5,64,256]{3,2,1,0:T(8,128)(2,1)S(1)}, u32[]{:S(2)}, u32[]{:S(2)}) collective-permute-start(bf16[1,5,64,256]{3,2,1,0:T(8,128)(2,1)S(1)} %get-tuple-element.58), channel_id=1, source_target_pairs={{0,2},{1,3},{2,0},{3,1},{4,6},{5,7},{6,4},{7,5},{8,10},{9,11},{10,... | collective-permute-start | bytes 491528 | tf_op jit(solution)/shard_map/ppermute | solution.py:185
  84.5 16.5 %copy-start.2 = (f32[1,5,64,256]{3,2,1,0:T(8,128)S(1)}, f32[1,5,64,256]{3,2,1,0:T(8,128)}, u32[]{:S(2)}) copy-start(f32[1,5,64,256]{3,2,1,0:T(8,128)} %omega_ref.3) | copy-start | bytes 983044
  84.6 5.6 %collective-permute-start.19 = (bf16[1,5,64,256]{3,2,1,0:T(8,128)(2,1)S(1)}, bf16[1,5,64,256]{3,2,1,0:T(8,128)(2,1)S(1)}, u32[]{:S(2)}, u32[]{:S(2)}) collective-permute-start(bf16[1,5,64,256]{3,2,1,0:T(8,128)(2,1)S(1)} %get-tuple-element.70), channel_id=1, source_target_pairs={{0,4},{1,5},{2,6},{3,7},{4,0},{5,1},{6,2},{7,3},{8,12},{9,13},{10,... | collective-permute-start | bytes 491528 | tf_op jit(solution)/shard_map/ppermute | solution.py:185
  85.6 5.4 %collective-permute-start.18 = (bf16[1,5,64,256]{3,2,1,0:T(8,128)(2,1)S(1)}, bf16[1,5,64,256]{3,2,1,0:T(8,128)(2,1)S(1)}, u32[]{:S(2)}, u32[]{:S(2)}) collective-permute-start(bf16[1,5,64,256]{3,2,1,0:T(8,128)(2,1)S(1)} %get-tuple-element.66), channel_id=1, source_target_pairs={{0,2},{1,3},{2,0},{3,1},{4,6},{5,7},{6,4},{7,5},{8,10},{9,11},{10,... | collective-permute-start | bytes 491528 | tf_op jit(solution)/shard_map/ppermute | solution.py:185
  86.2 12.8 %collective-permute-start.21 = (bf16[5,64,256]{2,1,0:T(8,128)(2,1)S(1)}, bf16[5,64,256]{2,1,0:T(8,128)(2,1)S(1)}, u32[]{:S(2)}, u32[]{:S(2)}) collective-permute-start(bf16[5,64,256]{2,1,0:T(8,128)(2,1)S(1)} %add.29), channel_id=1, source_target_pairs={{0,16},{1,17},{2,18},{3,19},{4,20},{5,21},{6,22},{7,23},{8,24},{9,... | collective-permute-start | bytes 491528 | tf_op jit(solution)/shard_map/ppermute | solution.py:185
  87.3 11.7 %collective-permute-start.22 = (bf16[5,64,256]{2,1,0:T(8,128)(2,1)S(1)}, bf16[5,64,256]{2,1,0:T(8,128)(2,1)S(1)}, u32[]{:S(2)}, u32[]{:S(2)}) collective-permute-start(bf16[5,64,256]{2,1,0:T(8,128)(2,1)S(1)} %add.31), channel_id=1, source_target_pairs={{0,24},{1,25},{2,26},{3,27},{4,28},{5,29},{6,30},{7,31},{8,16},{9,... | collective-permute-start | bytes 491528 | tf_op jit(solution)/shard_map/ppermute | solution.py:185
  90.3 10.7 %collective-permute-start.20 = (bf16[5,64,256]{2,1,0:T(8,128)(2,1)S(1)}, bf16[5,64,256]{2,1,0:T(8,128)(2,1)S(1)}, u32[]{:S(2)}, u32[]{:S(2)}) collective-permute-start(bf16[5,64,256]{2,1,0:T(8,128)(2,1)S(1)} %add.35), channel_id=1, source_target_pairs={{0,8},{1,9},{2,10},{3,11},{4,12},{5,13},{6,14},{7,15},{8,0},{9,1},... | collective-permute-start | bytes 491528 | tf_op jit(solution)/shard_map/ppermute | solution.py:185

commit v10 on v9

--- a/solution.py
+++ b/solution.py
@@ -118,7 +118,7 @@
     lax.fori_loop(0, teams, mix, 0, unroll=teams <= 8)
 
 
-def product_kernel(teams, chips, wanted, place_ref, *rest):
+def product_kernel(teams, chips, wanted, place_ref, _, *rest):
     rights, lefts, outs = rest[0:4:2], rest[1:4:2], rest[4:]
     team = place_ref[0]
     high, low = lax.div(team, LOW), lax.rem(team, LOW)
@@ -226,7 +226,6 @@
     )(kept, across)
     own = lax.all_to_all(dealt, "line", 0, 0)
     weights += [swap(array, 0, 1) for array in weights]
-    own, weights = lax.optimization_barrier((own, weights))
     tiles = pl.pallas_call(
         functools.partial(gather_kernel, teams, chips, tile_rows),
         out_shape=jax.ShapeDtypeStruct((teams, 3, width, width), BF16),
@@ -236,6 +235,8 @@
         compiler_params=tiny,
         name="gather",
     )(place, *weights)
+
+    own, tiles = lax.optimization_barrier((own, tiles))
 
     def mix(data):
         return pl.pallas_call(
@@ -263,11 +264,11 @@
         return pl.pallas_call(
             functools.partial(product_kernel, teams, chips, wanted),
             out_shape=shapes,
-            in_specs=[SMEM] + [VMEM] * 4,
+            in_specs=[SMEM, ANY] + [VMEM] * 4,
             out_specs=[VMEM] * len(shapes),
             compiler_params=small,
             name="products",
-        )(place, *cores)
+        )(place, own, *cores)
 
     def add(groups, shapes, *arrays):
         return pl.pallas_call(

time: 103 us -> 98 us (0.951)
  local copies, waits for them, and re-layouts: 11 us -> 5.8 us
  waiting for transfers between devices: 47.7 us -> 43.7 us
  starting transfers between devices: 25.2 us -> 28.8 us
    unnamed x26 -> x10, local copies, waits for them, and re-layouts: 10.9 us -> 5.72 us
    ppermute x23, starting transfers between devices: 21.3 us -> 24.9 us  [swap(): return lax.ppermute(array, AXES, route)]
    ppermute x23, waiting for transfers between devices: 46.1 us -> 43.7 us  [swap(): return lax.ppermute(array, AXES, route)]
    all_to_all x1, waiting for transfers between devices: 1.55 us -> 0.01 us  [per_device(): own = lax.all_to_all(dealt, 'line', 0, 0)]
  transfers between devices with their start and end apart: 24 -> 24, of which waited for: 13 -> 12; matrix products, arithmetic and copies ran while one was open for 1% -> 1% of each run, Pallas kernels for 11% -> 12%
where the time goes in v10:
time: 98 us; the launch traced here: 96.8 us
  waiting for transfers between devices  43.7 us (45%)
  starting transfers between devices  28.8 us (29%)
  Pallas kernels  17.5 us (18%)
  local copies, waits for them, and re-layouts  5.8 us (6%)
    ppermute x23, waiting for transfers between devices, swap(): return lax.ppermute(array, AXES, route)  43.7 us
    ppermute x23, starting transfers between devices, swap(): return lax.ppermute(array, AXES, route)  24.9 us
    pallas_call x6, Pallas kernels, products(): pl.pallas_call(functools.partial(product_kernel, teams, chips, wanted), o...  7.04 us
    unnamed x10, local copies, waits for them, and re-layouts  5.72 us
    pallas_call x2, Pallas kernels, mix(): pl.pallas_call(functools.partial(mix_kernel, teams, replicas, tile_rows),...  4.6 us
    all_to_all x1, starting transfers between devices, per_device(): own = lax.all_to_all(dealt, 'line', 0, 0)  3.91 us
    pallas_call x1, Pallas kernels, per_device(): pl.pallas_call(functools.partial(gather_kernel, teams, chips, tile_rows),...  2.44 us
  transfers between devices with their start and end apart: 24, of which 12 were waited for; matrix products, arithmetic and copies ran while one was open for 1% of the time, Pallas kernels for 12%

profile of v10, /device:TPU:0, one launch (start us, length us, event | category | flops | bytes accessed | tf_op | source)
XLA Modules:
  0.0 96.8 jit_solution(16404989097117958071)
XLA Ops:
  0.0 1.2 %copy-done = bf16[2048,256]{1,0:T(8,128)(2,1)S(1)} copy-done((bf16[2048,256]{1,0:T(8,128)(2,1)S(1)}, bf16[2048,256]{1,0:T(8,128)(2,1)}, u32[]{:S(2)}) %copy-start) | copy-done | bytes 1048600
  1.3 3.0 %collective-permute-start.3 = (bf16[1024,256]{1,0:T(8,128)(2,1)S(1)}, bf16[1024,256]{1,0:T(8,128)(2,1)S(1)}, u32[]{:S(2)}, u32[]{:S(2)}) collective-permute-start(bf16[1024,256]{1,0:T(8,128)(2,1)S(1)} %constant_dynamic-slice_fusion.1), channel_id=1, source_target_pairs={{0,4},{1,5},{2,6},{3,7},{4,0},{5,1},{6,2},{7,3},{8,12},{9,13},{10,... | collective-permute-start | bytes 1572872 | tf_op jit(solution)/shard_map/ppermute | solution.py:185
  4.3 0.7 pad_add_fusion.place_ref
  5.0 1.0 %copy-done.3 = f32[1,5,64,256]{3,2,1,0:T(8,128)S(1)} copy-done((f32[1,5,64,256]{3,2,1,0:T(8,128)S(1)}, f32[1,5,64,256]{3,2,1,0:T(8,128)}, u32[]{:S(2)}) %copy-start.3) | copy-done | bytes 327704
  6.0 0.6 prepare.1
  6.6 1.6 %collective-permute-start = (bf16[3,64,256]{2,1,0:T(8,128)(2,1)S(1)}, bf16[3,64,256]{2,1,0:T(8,128)(2,1)S(1)}, u32[]{:S(2)}, u32[]{:S(2)}) collective-permute-start(bf16[3,64,256]{2,1,0:T(8,128)(2,1)S(1)} %prepare.1), channel_id=1, source_target_pairs={{0,8},{1,9},{2,10},{3,11},{4,12},{5,13},{6,14},{7,15},{8,0},{9,1},... | collective-permute-start | bytes 294920 | tf_op jit(solution)/shard_map/ppermute | solution.py:185
  8.2 2.6 %collective-permute-start.1 = (bf16[3,64,256]{2,1,0:T(8,128)(2,1)S(1)}, bf16[3,64,256]{2,1,0:T(8,128)(2,1)S(1)}, u32[]{:S(2)}, u32[]{:S(2)}) collective-permute-start(bf16[3,64,256]{2,1,0:T(8,128)(2,1)S(1)} %prepare.1), channel_id=1, source_target_pairs={{0,16},{1,17},{2,18},{3,19},{4,20},{5,21},{6,22},{7,23},{8,24},{9,... | collective-permute-start | bytes 294920 | tf_op jit(solution)/shard_map/ppermute | solution.py:185
  10.8 0.2 collective-permute-start.2
  11.0 1.2 %collective-permute-done = bf16[3,64,256]{2,1,0:T(8,128)(2,1)S(1)} collective-permute-done((bf16[3,64,256]{2,1,0:T(8,128)(2,1)S(1)}, bf16[3,64,256]{2,1,0:T(8,128)(2,1)S(1)}, u32[]{:S(2)}, u32[]{:S(2)}) %collective-permute-start) | collective-permute-done | bytes 98336 | tf_op jit(solution)/shard_map/ppermute | solution.py:185
  12.2 6.1 %collective-permute-done.1 = bf16[3,64,256]{2,1,0:T(8,128)(2,1)S(1)} collective-permute-done((bf16[3,64,256]{2,1,0:T(8,128)(2,1)S(1)}, bf16[3,64,256]{2,1,0:T(8,128)(2,1)S(1)}, u32[]{:S(2)}, u32[]{:S(2)}) %collective-permute-start.1) | collective-permute-done | bytes 98336 | tf_op jit(solution)/shard_map/ppermute | solution.py:185
  18.5 1.0 %deal.1 = bf16[4,2,256,256]{3,2,1,0:T(8,128)(2,1)} custom-call(bf16[1024,256]{1,0:T(8,128)(2,1)S(1)} %constant_dynamic-slice_fusion.kept_ref, bf16[1024,256]{1,0:T(8,128)(2,1)S(1)} %collective-permute-done.3.across_ref), custom_call_target="tpu_custom_call" | custom-call | tf_op jit(solution)/shard_map/deal/pallas_call | solution.py:218
  19.5 3.9 %all-to-all-start = ((bf16[4,2,256,256]{3,2,1,0:T(8,128)(2,1)}), bf16[4,2,256,256]{3,2,1,0:T(8,128)(2,1)S(1)}, u32[]{:S(2)}, u32[]{:S(2)}) async-start(bf16[4,2,256,256]{3,2,1,0:T(8,128)(2,1)} %deal.1), calls=%async_computation | async-start | bytes 2097152 | tf_op jit(solution)/shard_map/all_to_all | solution.py:227
  23.4 1.5 %collective-permute-start.6 = (bf16[4,3,64,256]{3,2,1,0:T(8,128)(2,1)S(1)}, bf16[4,3,64,256]{3,2,1,0:T(8,128)(2,1)S(1)}, u32[]{:S(2)}, u32[]{:S(2)}) collective-permute-start(bf16[4,3,64,256]{3,2,1,0:T(8,128)(2,1)S(1)} %pad_maximum_fusion.rest_0_), channel_id=1, source_target_pairs={{0,6},{1,7},{2,4},{3,5},{4,2},{5,3},{6,0},{7,1},{8,14},{9,15},{10,... | collective-permute-start | bytes 1179656 | tf_op jit(solution)/shard_map/ppermute | solution.py:185
  24.9 0.5 collective-permute-start.4
  25.4 1.5 %collective-permute-start.5 = (bf16[4,3,64,256]{3,2,1,0:T(8,128)(2,1)S(1)}, bf16[4,3,64,256]{3,2,1,0:T(8,128)(2,1)S(1)}, u32[]{:S(2)}, u32[]{:S(2)}) collective-permute-start(bf16[4,3,64,256]{3,2,1,0:T(8,128)(2,1)S(1)} %pad_maximum_fusion.rest_0_), channel_id=1, source_target_pairs={{0,4},{1,5},{2,6},{3,7},{4,0},{5,1},{6,2},{7,3},{8,12},{9,13},{10,... | collective-permute-start | bytes 1179656 | tf_op jit(solution)/shard_map/ppermute | solution.py:185
  26.9 9.5 %collective-permute-done.6.rest_3_ = bf16[4,3,64,256]{3,2,1,0:T(8,128)(2,1)S(1)} collective-permute-done((bf16[4,3,64,256]{3,2,1,0:T(8,128)(2,1)S(1)}, bf16[4,3,64,256]{3,2,1,0:T(8,128)(2,1)S(1)}, u32[]{:S(2)}, u32[]{:S(2)}) %collective-permute-start.6) | collective-permute-done | bytes 393248 | tf_op jit(solution)/shard_map/ppermute | solution.py:185
  36.3 5.7 %collective-permute-done.4.rest_1_ = bf16[4,3,64,256]{3,2,1,0:T(8,128)(2,1)S(1)} collective-permute-done((bf16[4,3,64,256]{3,2,1,0:T(8,128)(2,1)S(1)}, bf16[4,3,64,256]{3,2,1,0:T(8,128)(2,1)S(1)}, u32[]{:S(2)}, u32[]{:S(2)}) %collective-permute-start.4) | collective-permute-done | bytes 393248 | tf_op jit(solution)/shard_map/ppermute | solution.py:185
  42.1 0.4 collective-permute-start.9
  42.5 1.2 %collective-permute-done.8.rest_5_ = bf16[4,3,64,256]{3,2,1,0:T(8,128)(2,1)S(1)} collective-permute-done((bf16[4,3,64,256]{3,2,1,0:T(8,128)(2,1)S(1)}, bf16[4,3,64,256]{3,2,1,0:T(8,128)(2,1)S(1)}, u32[]{:S(2)}, u32[]{:S(2)}) %collective-permute-start.8) | collective-permute-done | bytes 393248 | tf_op jit(solution)/shard_map/ppermute | solution.py:185
  43.7 0.6 collective-permute-done.9.rest_6_
  44.3 2.4 %gather.1.omega_ref = bf16[8,3,256,256]{3,2,1,0:T(8,128)(2,1)S(1)} custom-call(s32[7]{0:T(128)S(1)} %pad_add_fusion.place_ref, bf16[4,3,64,256]{3,2,1,0:T(8,128)(2,1)S(1)} %pad_maximum_fusion.rest_0_, bf16[4,3,64,256]{3,2,1,0:T(8,128)(2,1)S(1)} %collective-permute-done.4.rest_1_, bf16[4,3,64,256]{3,2,1,0:T(8,128)(2,1)S(1)} %collective-permute-done.5.rest_2_, ...), custom_call_target="tpu_custom_call" | custom-call | tf_op jit(solution)/shard_map/gather/pallas_call | solution.py:229
  46.7 1.6 %copy-done.1 = bf16[8,3,256,256]{3,2,1,0:T(8,128)(2,1)} copy-done((bf16[8,3,256,256]{3,2,1,0:T(8,128)(2,1)}, bf16[8,3,256,256]{3,2,1,0:T(8,128)(2,1)S(1)}, u32[]{:S(2)}) %copy-start.1) | copy-done | bytes 3145752
  48.4 0.1 collective-permute-start.11
  48.5 1.9 %copy-done.2 = bf16[8,3,256,256]{3,2,1,0:T(8,128)(2,1)S(1)} copy-done((bf16[8,3,256,256]{3,2,1,0:T(8,128)(2,1)S(1)}, bf16[8,3,256,256]{3,2,1,0:T(8,128)(2,1)}, u32[]{:S(2)}) %copy-start.2) | copy-done | bytes 3145752
  50.4 2.3 %mix.2 = (bf16[8,512,256]{2,1,0:T(8,128)(2,1)S(1)}, bf16[8,128,512]{2,1,0:T(8,128)(2,1)S(1)}) custom-call(s32[7]{0:T(128)S(1)} %pad_add_fusion.place_ref, bf16[4,2,256,256]{3,2,1,0:T(8,128)(2,1)S(1)} %all-to-all-done.data_ref._, bf16[8,3,256,256]{3,2,1,0:T(8,128)(2,1)S(1)} %copy-done.2), custom_call_target="tpu_custom_call" | custom-call | tf_op jit(solution)/shard_map/mix/pallas_call | solution.py:242
  52.7 2.3 %mix.3 = (bf16[8,512,256]{2,1,0:T(8,128)(2,1)S(1)}, bf16[8,128,512]{2,1,0:T(8,128)(2,1)S(1)}) custom-call(s32[7]{0:T(128)S(1)} %pad_add_fusion.place_ref, bf16[4,2,256,256]{3,2,1,0:T(8,128)(2,1)S(1)} %collective-permute-done.11.data_ref, bf16[8,3,256,256]{3,2,1,0:T(8,128)(2,1)S(1)} %copy-done.2), custom_call_target="tpu_custom_call" | custom-call | tf_op jit(solution)/shard_map/mix/pallas_call | solution.py:242
  55.0 1.4 %products.11 = (f32[2,1,5,64,256]{4,3,2,1,0:T(8,128)S(1)}, bf16[2,1,5,64,256]{4,3,2,1,0:T(8,128)(2,1)S(1)}) custom-call(s32[7]{0:T(128)S(1)} %pad_add_fusion.place_ref, bf16[4,2,256,256]{3,2,1,0:T(8,128)(2,1)S(1)} %all-to-all-done.data_ref._, bf16[8,512,256]{2,1,0:T(8,128)(2,1)S(1)} %get-tuple-element.37.rest_0_, ...), custom_call_target="tpu_custom_call" | custom-call | tf_op jit(solution)/shard_map/products/pallas_call | solution.py:264
  56.4 1.2 %collective-permute-start.16 = (bf16[2,1,5,64,256]{4,3,2,1,0:T(8,128)(2,1)S(1)}, bf16[2,1,5,64,256]{4,3,2,1,0:T(8,128)(2,1)S(1)}, u32[]{:S(2)}, u32[]{:S(2)}) collective-permute-start(bf16[2,1,5,64,256]{4,3,2,1,0:T(8,128)(2,1)S(1)} %get-tuple-element.46), channel_id=1, source_target_pairs={{0,2},{1,3},{2,0},{3,1},{4,6},{5,7},{6,4},{7,5},{8,10},{9,11},{10,... | collective-permute-start | bytes 983048 | tf_op jit(solution)/shard_map/ppermute | solution.py:185
  57.7 1.1 %products.10 = bf16[2,1,5,64,256]{4,3,2,1,0:T(8,128)(2,1)S(1)} custom-call(s32[7]{0:T(128)S(1)} %pad_add_fusion.place_ref, bf16[4,2,256,256]{3,2,1,0:T(8,128)(2,1)S(1)} %all-to-all-done.data_ref._, bf16[8,512,256]{2,1,0:T(8,128)(2,1)S(1)} %get-tuple-element.37.rest_0_, bf16[8,128,512]{2,1,0:T(8,128)(2,1)S(1)} %get-tuple-element.38.rest_1_, ...), custom_call_target="tpu_custom_call" | custom-call | tf_op jit(solution)/shard_map/products/pallas_call | solution.py:264
  58.8 1.2 %collective-permute-start.14 = (bf16[2,1,5,64,256]{4,3,2,1,0:T(8,128)(2,1)S(1)}, bf16[2,1,5,64,256]{4,3,2,1,0:T(8,128)(2,1)S(1)}, u32[]{:S(2)}, u32[]{:S(2)}) collective-permute-start(bf16[2,1,5,64,256]{4,3,2,1,0:T(8,128)(2,1)S(1)} %products.10), channel_id=1, source_target_pairs={{0,4},{1,5},{2,6},{3,7},{4,0},{5,1},{6,2},{7,3},{8,12},{9,13},{10,... | collective-permute-start | bytes 983048 | tf_op jit(solution)/shard_map/ppermute | solution.py:185
  60.0 1.4 %products.7 = (f32[2,1,5,64,256]{4,3,2,1,0:T(8,128)S(1)}, bf16[2,1,5,64,256]{4,3,2,1,0:T(8,128)(2,1)S(1)}) custom-call(s32[7]{0:T(128)S(1)} %pad_add_fusion.place_ref, bf16[4,2,256,256]{3,2,1,0:T(8,128)(2,1)S(1)} %all-to-all-done.data_ref._, bf16[8,512,256]{2,1,0:T(8,128)(2,1)S(1)} %get-tuple-element.37.rest_0_, ...), custom_call_target="tpu_custom_call" | custom-call | tf_op jit(solution)/shard_map/products/pallas_call | solution.py:264
  61.4 1.1 %products.6 = bf16[2,1,5,64,256]{4,3,2,1,0:T(8,128)(2,1)S(1)} custom-call(s32[7]{0:T(128)S(1)} %pad_add_fusion.place_ref, bf16[4,2,256,256]{3,2,1,0:T(8,128)(2,1)S(1)} %all-to-all-done.data_ref._, bf16[8,512,256]{2,1,0:T(8,128)(2,1)S(1)} %get-tuple-element.37.rest_0_, bf16[8,128,512]{2,1,0:T(8,128)(2,1)S(1)} %get-tuple-element.38.rest_1_, ...), custom_call_target="tpu_custom_call" | custom-call | tf_op jit(solution)/shard_map/products/pallas_call | solution.py:264
  62.4 0.7 collective-permute-start.13
  63.1 1.1 %collective-permute-start.12 = (bf16[2,1,5,64,256]{4,3,2,1,0:T(8,128)(2,1)S(1)}, bf16[2,1,5,64,256]{4,3,2,1,0:T(8,128)(2,1)S(1)}, u32[]{:S(2)}, u32[]{:S(2)}) collective-permute-start(bf16[2,1,5,64,256]{4,3,2,1,0:T(8,128)(2,1)S(1)} %products.6), channel_id=1, source_target_pairs={{0,4},{1,5},{2,6},{3,7},{4,0},{5,1},{6,2},{7,3},{8,12},{9,13},{10,... | collective-permute-start | bytes 983048 | tf_op jit(solution)/shard_map/ppermute | solution.py:185
  64.3 1.1 %products.9.refs_0_ = f32[2,1,5,64,256]{4,3,2,1,0:T(8,128)S(1)} custom-call(s32[7]{0:T(128)S(1)} %pad_add_fusion.place_ref, bf16[4,2,256,256]{3,2,1,0:T(8,128)(2,1)S(1)} %all-to-all-done.data_ref._, bf16[8,512,256]{2,1,0:T(8,128)(2,1)S(1)} %get-tuple-element.37.rest_0_, bf16[8,128,512]{2,1,0:T(8,128)(2,1)S(1)} %get-tuple-element.38.rest_1_, ...), custom_call_target="tpu_custom_call" | custom-call | tf_op jit(solution)/shard_map/products/pallas_call | solution.py:264
  65.3 1.7 %collective-permute-done.16.refs_1_ = bf16[2,1,5,64,256]{4,3,2,1,0:T(8,128)(2,1)S(1)} collective-permute-done((bf16[2,1,5,64,256]{4,3,2,1,0:T(8,128)(2,1)S(1)}, bf16[2,1,5,64,256]{4,3,2,1,0:T(8,128)(2,1)S(1)}, u32[]{:S(2)}, u32[]{:S(2)}) %collective-permute-start.16) | collective-permute-done | bytes 327712 | tf_op jit(solution)/shard_map/ppermute | solution.py:185
  67.1 1.0 collective-permute-start.17
  68.1 1.3 %collective-permute-done.14.refs_1_ = bf16[2,1,5,64,256]{4,3,2,1,0:T(8,128)(2,1)S(1)} collective-permute-done((bf16[2,1,5,64,256]{4,3,2,1,0:T(8,128)(2,1)S(1)}, bf16[2,1,5,64,256]{4,3,2,1,0:T(8,128)(2,1)S(1)}, u32[]{:S(2)}, u32[]{:S(2)}) %collective-permute-start.14) | collective-permute-done | bytes 327712 | tf_op jit(solution)/shard_map/ppermute | solution.py:185
  69.4 0.9 collective-permute-start.15
  70.4 1.1 %products.8.refs_0_ = f32[2,1,5,64,256]{4,3,2,1,0:T(8,128)S(1)} custom-call(s32[7]{0:T(128)S(1)} %pad_add_fusion.place_ref, bf16[4,2,256,256]{3,2,1,0:T(8,128)(2,1)S(1)} %all-to-all-done.data_ref._, bf16[8,512,256]{2,1,0:T(8,128)(2,1)S(1)} %get-tuple-element.37.rest_0_, bf16[8,128,512]{2,1,0:T(8,128)(2,1)S(1)} %get-tuple-element.38.rest_1_, ...), custom_call_target="tpu_custom_call" | custom-call | tf_op jit(solution)/shard_map/products/pallas_call | solution.py:264
  71.5 7.7 %collective-permute-done.17.refs_1_ = bf16[1,5,64,256]{3,2,1,0:T(8,128)(2,1)S(1)} collective-permute-done((bf16[1,5,64,256]{3,2,1,0:T(8,128)(2,1)S(1)}, bf16[1,5,64,256]{3,2,1,0:T(8,128)(2,1)S(1)}, u32[]{:S(2)}, u32[]{:S(2)}) %collective-permute-start.17) | collective-permute-done | bytes 163872 | tf_op jit(solution)/shard_map/ppermute | solution.py:185
  79.3 1.2 %collective-permute-start.19 = (bf16[1,5,64,256]{3,2,1,0:T(8,128)(2,1)S(1)}, bf16[1,5,64,256]{3,2,1,0:T(8,128)(2,1)S(1)}, u32[]{:S(2)}, u32[]{:S(2)}) collective-permute-start(bf16[1,5,64,256]{3,2,1,0:T(8,128)(2,1)S(1)} %get-tuple-element.56), channel_id=1, source_target_pairs={{0,4},{1,5},{2,6},{3,7},{4,0},{5,1},{6,2},{7,3},{8,12},{9,13},{10,... | collective-permute-start | bytes 491528 | tf_op jit(solution)/shard_map/ppermute | solution.py:185
  80.6 0.6 collective-permute-start.18
  81.2 2.6 %collective-permute-start.21 = (bf16[5,64,256]{2,1,0:T(8,128)(2,1)S(1)}, bf16[5,64,256]{2,1,0:T(8,128)(2,1)S(1)}, u32[]{:S(2)}, u32[]{:S(2)}) collective-permute-start(bf16[5,64,256]{2,1,0:T(8,128)(2,1)S(1)} %add.29), channel_id=1, source_target_pairs={{0,16},{1,17},{2,18},{3,19},{4,20},{5,21},{6,22},{7,23},{8,24},{9,... | collective-permute-start | bytes 491528 | tf_op jit(solution)/shard_map/ppermute | solution.py:185
  83.9 1.5 %collective-permute-start.22 = (bf16[5,64,256]{2,1,0:T(8,128)(2,1)S(1)}, bf16[5,64,256]{2,1,0:T(8,128)(2,1)S(1)}, u32[]{:S(2)}, u32[]{:S(2)}) collective-permute-start(bf16[5,64,256]{2,1,0:T(8,128)(2,1)S(1)} %add.31), channel_id=1, source_target_pairs={{0,24},{1,25},{2,26},{3,27},{4,28},{5,29},{6,30},{7,31},{8,16},{9,... | collective-permute-start | bytes 491528 | tf_op jit(solution)/shard_map/ppermute | solution.py:185
  85.4 1.3 %collective-permute-start.20 = (bf16[5,64,256]{2,1,0:T(8,128)(2,1)S(1)}, bf16[5,64,256]{2,1,0:T(8,128)(2,1)S(1)}, u32[]{:S(2)}, u32[]{:S(2)}) collective-permute-start(bf16[5,64,256]{2,1,0:T(8,128)(2,1)S(1)} %add.35), channel_id=1, source_target_pairs={{0,8},{1,9},{2,10},{3,11},{4,12},{5,13},{6,14},{7,15},{8,0},{9,1},... | collective-permute-start | bytes 491528 | tf_op jit(solution)/shard_map/ppermute | solution.py:185
  86.7 8.6 %collective-permute-done.21.rest_2_ = bf16[5,64,256]{2,1,0:T(8,128)(2,1)S(1)} collective-permute-done((bf16[5,64,256]{2,1,0:T(8,128)(2,1)S(1)}, bf16[5,64,256]{2,1,0:T(8,128)(2,1)S(1)}, u32[]{:S(2)}, u32[]{:S(2)}) %collective-permute-start.21) | collective-permute-done | bytes 163872 | tf_op jit(solution)/shard_map/ppermute | solution.py:185
  95.4 1.5 %update.1 = f32[1,5,64,256]{3,2,1,0:T(8,128)} custom-call(s32[7]{0:T(128)S(1)} %pad_add_fusion.place_ref, f32[1,5,64,256]{3,2,1,0:T(8,128)S(1)} %copy-done.4, f32[5,64,256]{2,1,0:T(8,128)S(1)} %add.33.rest_0_, bf16[5,64,256]{2,1,0:T(8,128)(2,1)S(1)} %collective-permute-done.20.rest_1_, bf16[5,64,256]{2,1,0:T(8,128)(2,1)S(1)} %collective-permute-done.21.rest_2_, ...), custom_call_target="tpu_custom_call" | custom-call | tf_op jit(solution)/shard_map/update/pallas_call | solution.py:332
  (34 shorter events, 0.8 us)
Async XLA Ops:
  0.0 1.2 %copy-start = (bf16[2048,256]{1,0:T(8,128)(2,1)S(1)}, bf16[2048,256]{1,0:T(8,128)(2,1)}, u32[]{:S(2)}) copy-start(bf16[2048,256]{1,0:T(8,128)(2,1)} %param.3) | copy-start | bytes 3145732
  1.3 17.1 %collective-permute-start.3 = (bf16[1024,256]{1,0:T(8,128)(2,1)S(1)}, bf16[1024,256]{1,0:T(8,128)(2,1)S(1)}, u32[]{:S(2)}, u32[]{:S(2)}) collective-permute-start(bf16[1024,256]{1,0:T(8,128)(2,1)S(1)} %constant_dynamic-slice_fusion.1), channel_id=1, source_target_pairs={{0,4},{1,5},{2,6},{3,7},{4,0},{5,1},{6,2},{7,3},{8,12},{9,13},{10,... | collective-permute-start | bytes 1572872 | tf_op jit(solution)/shard_map/ppermute | solution.py:185
  5.0 1.0 %copy-start.3 = (f32[1,5,64,256]{3,2,1,0:T(8,128)S(1)}, f32[1,5,64,256]{3,2,1,0:T(8,128)}, u32[]{:S(2)}) copy-start(f32[1,5,64,256]{3,2,1,0:T(8,128)} %omega_ref.3) | copy-start | bytes 983044
  6.6 5.7 %collective-permute-start = (bf16[3,64,256]{2,1,0:T(8,128)(2,1)S(1)}, bf16[3,64,256]{2,1,0:T(8,128)(2,1)S(1)}, u32[]{:S(2)}, u32[]{:S(2)}) collective-permute-start(bf16[3,64,256]{2,1,0:T(8,128)(2,1)S(1)} %prepare.1), channel_id=1, source_target_pairs={{0,8},{1,9},{2,10},{3,11},{4,12},{5,13},{6,14},{7,15},{8,0},{9,1},... | collective-permute-start | bytes 294920 | tf_op jit(solution)/shard_map/ppermute | solution.py:185
  8.2 10.1 %collective-permute-start.1 = (bf16[3,64,256]{2,1,0:T(8,128)(2,1)S(1)}, bf16[3,64,256]{2,1,0:T(8,128)(2,1)S(1)}, u32[]{:S(2)}, u32[]{:S(2)}) collective-permute-start(bf16[3,64,256]{2,1,0:T(8,128)(2,1)S(1)} %prepare.1), channel_id=1, source_target_pairs={{0,16},{1,17},{2,18},{3,19},{4,20},{5,21},{6,22},{7,23},{8,24},{9,... | collective-permute-start | bytes 294920 | tf_op jit(solution)/shard_map/ppermute | solution.py:185
  10.8 7.6 %collective-permute-start.2 = (bf16[3,64,256]{2,1,0:T(8,128)(2,1)S(1)}, bf16[3,64,256]{2,1,0:T(8,128)(2,1)S(1)}, u32[]{:S(2)}, u32[]{:S(2)}) collective-permute-start(bf16[3,64,256]{2,1,0:T(8,128)(2,1)S(1)} %prepare.1), channel_id=1, source_target_pairs={{0,24},{1,25},{2,26},{3,27},{4,28},{5,29},{6,30},{7,31},{8,16},{9,... | collective-permute-start | bytes 294920 | tf_op jit(solution)/shard_map/ppermute | solution.py:185
  19.5 28.9 %all-to-all-start = ((bf16[4,2,256,256]{3,2,1,0:T(8,128)(2,1)}), bf16[4,2,256,256]{3,2,1,0:T(8,128)(2,1)S(1)}, u32[]{:S(2)}, u32[]{:S(2)}) async-start(bf16[4,2,256,256]{3,2,1,0:T(8,128)(2,1)} %deal.1), calls=%async_computation | async-start | bytes 2097152 | tf_op jit(solution)/shard_map/all_to_all | solution.py:227
  23.4 13.0 %collective-permute-start.6 = (bf16[4,3,64,256]{3,2,1,0:T(8,128)(2,1)S(1)}, bf16[4,3,64,256]{3,2,1,0:T(8,128)(2,1)S(1)}, u32[]{:S(2)}, u32[]{:S(2)}) collective-permute-start(bf16[4,3,64,256]{3,2,1,0:T(8,128)(2,1)S(1)} %pad_maximum_fusion.rest_0_), channel_id=1, source_target_pairs={{0,6},{1,7},{2,4},{3,5},{4,2},{5,3},{6,0},{7,1},{8,14},{9,15},{10,... | collective-permute-start | bytes 1179656 | tf_op jit(solution)/shard_map/ppermute | solution.py:185
  24.9 17.1 %collective-permute-start.4 = (bf16[4,3,64,256]{3,2,1,0:T(8,128)(2,1)S(1)}, bf16[4,3,64,256]{3,2,1,0:T(8,128)(2,1)S(1)}, u32[]{:S(2)}, u32[]{:S(2)}) collective-permute-start(bf16[4,3,64,256]{3,2,1,0:T(8,128)(2,1)S(1)} %pad_maximum_fusion.rest_0_), channel_id=1, source_target_pairs={{0,2},{1,3},{2,0},{3,1},{4,6},{5,7},{6,4},{7,5},{8,10},{9,11},{10,... | collective-permute-start | bytes 1179656 | tf_op jit(solution)/shard_map/ppermute | solution.py:185
  25.4 16.7 %collective-permute-start.5 = (bf16[4,3,64,256]{3,2,1,0:T(8,128)(2,1)S(1)}, bf16[4,3,64,256]{3,2,1,0:T(8,128)(2,1)S(1)}, u32[]{:S(2)}, u32[]{:S(2)}) collective-permute-start(bf16[4,3,64,256]{3,2,1,0:T(8,128)(2,1)S(1)} %pad_maximum_fusion.rest_0_), channel_id=1, source_target_pairs={{0,4},{1,5},{2,6},{3,7},{4,0},{5,1},{6,2},{7,3},{8,12},{9,13},{10,... | collective-permute-start | bytes 1179656 | tf_op jit(solution)/shard_map/ppermute | solution.py:185
  26.9 15.6 %collective-permute-start.7 = (bf16[4,3,64,256]{3,2,1,0:T(8,128)(2,1)S(1)}, bf16[4,3,64,256]{3,2,1,0:T(8,128)(2,1)S(1)}, u32[]{:S(2)}, u32[]{:S(2)}) collective-permute-start(bf16[4,3,64,256]{3,2,1,0:T(8,128)(2,1)S(1)} %pad_maximum_fusion.rest_0_), channel_id=1, source_target_pairs={{0,1},{1,0},{2,3},{3,2},{4,5},{5,4},{6,7},{7,6},{8,9},{9,8},{10,11... | collective-permute-start | bytes 1179656 | tf_op jit(solution)/shard_map/ppermute | solution.py:185
  36.3 6.2 %collective-permute-start.10 = (bf16[4,3,64,256]{3,2,1,0:T(8,128)(2,1)S(1)}, bf16[4,3,64,256]{3,2,1,0:T(8,128)(2,1)S(1)}, u32[]{:S(2)}, u32[]{:S(2)}) collective-permute-start(bf16[4,3,64,256]{3,2,1,0:T(8,128)(2,1)S(1)} %collective-permute-done.6.rest_3_), channel_id=1, source_target_pairs={{0,1},{1,0},{2,3},{3,2},{4,5},{5,4},{6,7},{7,6},{8,9},{9,8},{10,11... | collective-permute-start | bytes 1179656 | tf_op jit(solution)/shard_map/ppermute | solution.py:185
  42.0 1.7 %collective-permute-start.8 = (bf16[4,3,64,256]{3,2,1,0:T(8,128)(2,1)S(1)}, bf16[4,3,64,256]{3,2,1,0:T(8,128)(2,1)S(1)}, u32[]{:S(2)}, u32[]{:S(2)}) collective-permute-start(bf16[4,3,64,256]{3,2,1,0:T(8,128)(2,1)S(1)} %collective-permute-done.4.rest_1_), channel_id=1, source_target_pairs={{0,1},{1,0},{2,3},{3,2},{4,5},{5,4},{6,7},{7,6},{8,9},{9,8},{10,11... | collective-permute-start | bytes 1179656 | tf_op jit(solution)/shard_map/ppermute | solution.py:185
  42.1 2.2 %collective-permute-start.9 = (bf16[4,3,64,256]{3,2,1,0:T(8,128)(2,1)S(1)}, bf16[4,3,64,256]{3,2,1,0:T(8,128)(2,1)S(1)}, u32[]{:S(2)}, u32[]{:S(2)}) collective-permute-start(bf16[4,3,64,256]{3,2,1,0:T(8,128)(2,1)S(1)} %collective-permute-done.5.rest_2_), channel_id=1, source_target_pairs={{0,1},{1,0},{2,3},{3,2},{4,5},{5,4},{6,7},{7,6},{8,9},{9,8},{10,11... | collective-permute-start | bytes 1179656 | tf_op jit(solution)/shard_map/ppermute | solution.py:185
  46.7 1.6 %copy-start.1 = (bf16[8,3,256,256]{3,2,1,0:T(8,128)(2,1)}, bf16[8,3,256,256]{3,2,1,0:T(8,128)(2,1)S(1)}, u32[]{:S(2)}) copy-start(bf16[8,3,256,256]{3,2,1,0:T(8,128)(2,1)S(1)} %gather.1.omega_ref) | copy-start | bytes 9437188
  48.4 4.4 %collective-permute-start.11 = (bf16[4,2,256,256]{3,2,1,0:T(8,128)(2,1)S(1)}, bf16[4,2,256,256]{3,2,1,0:T(8,128)(2,1)S(1)}, u32[]{:S(2)}, u32[]{:S(2)}) collective-permute-start(bf16[4,2,256,256]{3,2,1,0:T(8,128)(2,1)S(1)} %all-to-all-done.data_ref._), channel_id=1, source_target_pairs={{0,1},{1,0},{2,3},{3,2},{4,5},{5,4},{6,7},{7,6},{8,9},{9,8},{10,11... | collective-permute-start | bytes 3145736 | tf_op jit(solution)/shard_map/ppermute | solution.py:185
  48.5 1.9 %copy-start.2 = (bf16[8,3,256,256]{3,2,1,0:T(8,128)(2,1)S(1)}, bf16[8,3,256,256]{3,2,1,0:T(8,128)(2,1)}, u32[]{:S(2)}) copy-start(bf16[8,3,256,256]{3,2,1,0:T(8,128)(2,1)} %copy-done.1) | copy-start | bytes 9437188
  56.4 10.6 %collective-permute-start.16 = (bf16[2,1,5,64,256]{4,3,2,1,0:T(8,128)(2,1)S(1)}, bf16[2,1,5,64,256]{4,3,2,1,0:T(8,128)(2,1)S(1)}, u32[]{:S(2)}, u32[]{:S(2)}) collective-permute-start(bf16[2,1,5,64,256]{4,3,2,1,0:T(8,128)(2,1)S(1)} %get-tuple-element.46), channel_id=1, source_target_pairs={{0,2},{1,3},{2,0},{3,1},{4,6},{5,7},{6,4},{7,5},{8,10},{9,11},{10,... | collective-permute-start | bytes 983048 | tf_op jit(solution)/shard_map/ppermute | solution.py:185
  58.8 10.6 %collective-permute-start.14 = (bf16[2,1,5,64,256]{4,3,2,1,0:T(8,128)(2,1)S(1)}, bf16[2,1,5,64,256]{4,3,2,1,0:T(8,128)(2,1)S(1)}, u32[]{:S(2)}, u32[]{:S(2)}) collective-permute-start(bf16[2,1,5,64,256]{4,3,2,1,0:T(8,128)(2,1)S(1)} %products.10), channel_id=1, source_target_pairs={{0,4},{1,5},{2,6},{3,7},{4,0},{5,1},{6,2},{7,3},{8,12},{9,13},{10,... | collective-permute-start | bytes 983048 | tf_op jit(solution)/shard_map/ppermute | solution.py:185
  62.4 16.8 %collective-permute-start.13 = (bf16[2,1,5,64,256]{4,3,2,1,0:T(8,128)(2,1)S(1)}, bf16[2,1,5,64,256]{4,3,2,1,0:T(8,128)(2,1)S(1)}, u32[]{:S(2)}, u32[]{:S(2)}) collective-permute-start(bf16[2,1,5,64,256]{4,3,2,1,0:T(8,128)(2,1)S(1)} %get-tuple-element.41), channel_id=1, source_target_pairs={{0,2},{1,3},{2,0},{3,1},{4,6},{5,7},{6,4},{7,5},{8,10},{9,11},{10,... | collective-permute-start | bytes 983048 | tf_op jit(solution)/shard_map/ppermute | solution.py:185
  63.1 16.1 %collective-permute-start.12 = (bf16[2,1,5,64,256]{4,3,2,1,0:T(8,128)(2,1)S(1)}, bf16[2,1,5,64,256]{4,3,2,1,0:T(8,128)(2,1)S(1)}, u32[]{:S(2)}, u32[]{:S(2)}) collective-permute-start(bf16[2,1,5,64,256]{4,3,2,1,0:T(8,128)(2,1)S(1)} %products.6), channel_id=1, source_target_pairs={{0,4},{1,5},{2,6},{3,7},{4,0},{5,1},{6,2},{7,3},{8,12},{9,13},{10,... | collective-permute-start | bytes 983048 | tf_op jit(solution)/shard_map/ppermute | solution.py:185
  67.1 12.0 %collective-permute-start.17 = (bf16[1,5,64,256]{3,2,1,0:T(8,128)(2,1)S(1)}, bf16[1,5,64,256]{3,2,1,0:T(8,128)(2,1)S(1)}, u32[]{:S(2)}, u32[]{:S(2)}) collective-permute-start(bf16[1,5,64,256]{3,2,1,0:T(8,128)(2,1)S(1)} %get-tuple-element.48), channel_id=1, source_target_pairs={{0,4},{1,5},{2,6},{3,7},{4,0},{5,1},{6,2},{7,3},{8,12},{9,13},{10,... | collective-permute-start | bytes 491528 | tf_op jit(solution)/shard_map/ppermute | solution.py:185
  69.4 9.7 %collective-permute-start.15 = (bf16[1,5,64,256]{3,2,1,0:T(8,128)(2,1)S(1)}, bf16[1,5,64,256]{3,2,1,0:T(8,128)(2,1)S(1)}, u32[]{:S(2)}, u32[]{:S(2)}) collective-permute-start(bf16[1,5,64,256]{3,2,1,0:T(8,128)(2,1)S(1)} %get-tuple-element.44), channel_id=1, source_target_pairs={{0,2},{1,3},{2,0},{3,1},{4,6},{5,7},{6,4},{7,5},{8,10},{9,11},{10,... | collective-permute-start | bytes 491528 | tf_op jit(solution)/shard_map/ppermute | solution.py:185
  79.2 16.2 %copy-start.4 = (f32[1,5,64,256]{3,2,1,0:T(8,128)S(1)}, f32[1,5,64,256]{3,2,1,0:T(8,128)}, u32[]{:S(2)}) copy-start(f32[1,5,64,256]{3,2,1,0:T(8,128)} %omega_ref.3) | copy-start | bytes 983044
  79.3 6.0 %collective-permute-start.19 = (bf16[1,5,64,256]{3,2,1,0:T(8,128)(2,1)S(1)}, bf16[1,5,64,256]{3,2,1,0:T(8,128)(2,1)S(1)}, u32[]{:S(2)}, u32[]{:S(2)}) collective-permute-start(bf16[1,5,64,256]{3,2,1,0:T(8,128)(2,1)S(1)} %get-tuple-element.56), channel_id=1, source_target_pairs={{0,4},{1,5},{2,6},{3,7},{4,0},{5,1},{6,2},{7,3},{8,12},{9,13},{10,... | collective-permute-start | bytes 491528 | tf_op jit(solution)/shard_map/ppermute | solution.py:185
  80.6 6.1 %collective-permute-start.18 = (bf16[1,5,64,256]{3,2,1,0:T(8,128)(2,1)S(1)}, bf16[1,5,64,256]{3,2,1,0:T(8,128)(2,1)S(1)}, u32[]{:S(2)}, u32[]{:S(2)}) collective-permute-start(bf16[1,5,64,256]{3,2,1,0:T(8,128)(2,1)S(1)} %get-tuple-element.52), channel_id=1, source_target_pairs={{0,2},{1,3},{2,0},{3,1},{4,6},{5,7},{6,4},{7,5},{8,10},{9,11},{10,... | collective-permute-start | bytes 491528 | tf_op jit(solution)/shard_map/ppermute | solution.py:185
  81.2 14.1 %collective-permute-start.21 = (bf16[5,64,256]{2,1,0:T(8,128)(2,1)S(1)}, bf16[5,64,256]{2,1,0:T(8,128)(2,1)S(1)}, u32[]{:S(2)}, u32[]{:S(2)}) collective-permute-start(bf16[5,64,256]{2,1,0:T(8,128)(2,1)S(1)} %add.29), channel_id=1, source_target_pairs={{0,16},{1,17},{2,18},{3,19},{4,20},{5,21},{6,22},{7,23},{8,24},{9,... | collective-permute-start | bytes 491528 | tf_op jit(solution)/shard_map/ppermute | solution.py:185
  83.9 11.4 %collective-permute-start.22 = (bf16[5,64,256]{2,1,0:T(8,128)(2,1)S(1)}, bf16[5,64,256]{2,1,0:T(8,128)(2,1)S(1)}, u32[]{:S(2)}, u32[]{:S(2)}) collective-permute-start(bf16[5,64,256]{2,1,0:T(8,128)(2,1)S(1)} %add.31), channel_id=1, source_target_pairs={{0,24},{1,25},{2,26},{3,27},{4,28},{5,29},{6,30},{7,31},{8,16},{9,... | collective-permute-start | bytes 491528 | tf_op jit(solution)/shard_map/ppermute | solution.py:185
  85.4 10.0 %collective-permute-start.20 = (bf16[5,64,256]{2,1,0:T(8,128)(2,1)S(1)}, bf16[5,64,256]{2,1,0:T(8,128)(2,1)S(1)}, u32[]{:S(2)}, u32[]{:S(2)}) collective-permute-start(bf16[5,64,256]{2,1,0:T(8,128)(2,1)S(1)} %add.35), channel_id=1, source_target_pairs={{0,8},{1,9},{2,10},{3,11},{4,12},{5,13},{6,14},{7,15},{8,0},{9,1},... | collective-permute-start | bytes 491528 | tf_op jit(solution)/shard_map/ppermute | solution.py:185

commit v11 on v10

--- a/solution.py
+++ b/solution.py
@@ -12,6 +12,7 @@
 LOW = 2
 AXES = ("line", "low", "chip", "core")
 BLK, REP = AXES[:2], AXES[2:]
+COST = 12
 F32 = jnp.float32
 BF16 = jnp.bfloat16
 
@@ -270,13 +271,14 @@
             name="products",
         )(place, own, *cores)
 
-    def add(groups, shapes, *arrays):
+    def add(groups, shapes, *arrays, cost=None):
         return pl.pallas_call(
             functools.partial(add_kernel, groups),
             out_shape=shapes,
             in_specs=[VMEM] * len(arrays),
             out_specs=[VMEM] * len(shapes),
             compiler_params=small,
+            cost_estimate=cost,
             name="add",
         )(*arrays)
 
@@ -302,15 +304,16 @@
     def first_hop(x_first, sent):
         return [swap(sent[0], 1, 0)] if x_first else [swap(array, 0, 2 * my) for my, array in enumerate(sent, 1)]
 
-    def second_hop(group, x_first, received, kept):
+    def plane_add(group, x_first, received, kept):
         size = len(group)
         if x_first:
             groups = [[(0, my), (1, my)] for my in chip_range]
-            parts = add(groups, [shape((size,), BF16 if my else F32) for my in chip_range], kept, *received)
-            return [swap(array, 0, 2 * my) if my else array for my, array in enumerate(parts)]
+            return add(groups, [shape((size,), BF16 if my else F32) for my in chip_range], kept, *received)
         groups = [[(m, mx) for m in chip_range] for mx in range(LOW)]
-        parts = add(groups, [shape((size,), BF16 if mx else F32) for mx in range(LOW)], kept, *received)
-        return [swap(array, mx, 0) if mx else array for mx, array in enumerate(parts)]
+        return add(groups, [shape((size,), BF16 if mx else F32) for mx in range(LOW)], kept, *received)
+
+    def second_hop(x_first, parts):
+        return [swap(array, 0 if x_first else n, 2 * n if x_first else 0) if n else array for n, array in enumerate(parts)]
 
     def sums_of(group, parts):
         groups = [[(m, n) for m in range(len(parts))] for n in range(len(group))]
@@ -320,19 +323,29 @@
     bounds = [range(n * quarter, (n + 1) * quarter) for n in range(4)]
     x_first = [True, False, True, False]
     firsts = [first_parts(*each) for each in zip(bounds, x_first)]
-    received = [first_hop(first, sent) for first, (sent, _) in zip(x_first, firsts)]
-    sums = [None] * 4
-    for n in (2, 3, 0, 1):
-        sums[n] = sums_of(bounds[n], second_hop(bounds[n], x_first[n], received[n], firsts[n][1]))
-        if n == 3:
-            received[:2], firsts[:2], sums[2:] = lax.optimization_barrier((received[:2], firsts[:2], sums[2:]))
-    sums = along_line([total for group in sums for total in group])
+    far = [plane_add(bounds[n], x_first[n], first_hop(x_first[n], firsts[n][0]), firsts[n][1]) for n in (2, 3)]
+    far, near = lax.optimization_barrier((far, firsts[:2]))
+    far_sums = [sums_of(bounds[n], second_hop(x_first[n], far[n - 2])) for n in (2, 3)]
+    received = [first_hop(x_first[n], near[n][0]) for n in range(2)]
+    near_sums = [
+        sums_of(bounds[n], second_hop(x_first[n], plane_add(bounds[n], x_first[n], received[n], near[n][1])))
+        for n in range(2)
+    ]
+    sums = along_line([total for group in near_sums + far_sums for total in group])
+    half = 2 * quarter
+    (far_total,) = add(
+        [[(n, None) for n in range(half)]],
+        [shape((), F32)],
+        *sums[half:],
+        cost=pl.CostEstimate(flops=COST * 10**9, bytes_accessed=COST * 3 * 10**6, transcendentals=0),
+    )
+    sums = sums[:half] + [far_total]
 
     scale = 1.0 / (2.0 * teams * times * replicas)
     return pl.pallas_call(
         functools.partial(update_kernel, teams, scale),
         out_shape=jax.ShapeDtypeStruct(omega.shape, F32),
-        in_specs=[SMEM, VMEM] + [VMEM] * count,
+        in_specs=[SMEM, VMEM] + [VMEM] * len(sums),
         out_specs=VMEM,
         compiler_params=small,
         name="update",

time: 98 us -> 96.8 us (0.988)
  transfers between devices with their start and end apart: 24 -> 24, of which waited for: 12 -> 14; matrix products, arithmetic and copies ran while one was open for 1% -> 1% of each run, Pallas kernels for 12% -> 12%
where the time goes in v11:
time: 96.8 us; the launch traced here: 96.5 us
  waiting for transfers between devices  42.9 us (44%)
  starting transfers between devices  29.2 us (30%)
  Pallas kernels  17.5 us (18%)
  local copies, waits for them, and re-layouts  5.8 us (6%)
    ppermute x23, waiting for transfers between devices, swap(): return lax.ppermute(array, AXES, route)  42.9 us
    ppermute x23, starting transfers between devices, swap(): return lax.ppermute(array, AXES, route)  25.3 us
    pallas_call x6, Pallas kernels, products(): pl.pallas_call(functools.partial(product_kernel, teams, chips, wanted), o...  7.05 us
    unnamed x10, local copies, waits for them, and re-layouts  5.72 us
    pallas_call x2, Pallas kernels, mix(): pl.pallas_call(functools.partial(mix_kernel, teams, replicas, tile_rows),...  4.6 us
    all_to_all x1, starting transfers between devices, per_device(): own = lax.all_to_all(dealt, 'line', 0, 0)  3.91 us
    pallas_call x1, Pallas kernels, per_device(): pl.pallas_call(functools.partial(gather_kernel, teams, chips, tile_rows),...  2.44 us
  transfers between devices with their start and end apart: 24, of which 14 were waited for; matrix products, arithmetic and copies ran while one was open for 1% of the time, Pallas kernels for 12%

profile of v11, /device:TPU:0, one launch (start us, length us, event | category | flops | bytes accessed | tf_op | source)
XLA Modules:
  0.0 96.5 jit_solution(4982267577035008538)
XLA Ops:
  0.0 1.2 %copy-done = bf16[2048,256]{1,0:T(8,128)(2,1)S(1)} copy-done((bf16[2048,256]{1,0:T(8,128)(2,1)S(1)}, bf16[2048,256]{1,0:T(8,128)(2,1)}, u32[]{:S(2)}) %copy-start) | copy-done | bytes 1048600
  1.3 3.0 %collective-permute-start.3 = (bf16[1024,256]{1,0:T(8,128)(2,1)S(1)}, bf16[1024,256]{1,0:T(8,128)(2,1)S(1)}, u32[]{:S(2)}, u32[]{:S(2)}) collective-permute-start(bf16[1024,256]{1,0:T(8,128)(2,1)S(1)} %constant_dynamic-slice_fusion.1), channel_id=1, source_target_pairs={{0,4},{1,5},{2,6},{3,7},{4,0},{5,1},{6,2},{7,3},{8,12},{9,13},{10,... | collective-permute-start | bytes 1572872 | tf_op jit(solution)/shard_map/ppermute | solution.py:186
  4.3 0.7 pad_add_fusion.place_ref
  5.0 1.0 %copy-done.3 = f32[1,5,64,256]{3,2,1,0:T(8,128)S(1)} copy-done((f32[1,5,64,256]{3,2,1,0:T(8,128)S(1)}, f32[1,5,64,256]{3,2,1,0:T(8,128)}, u32[]{:S(2)}) %copy-start.3) | copy-done | bytes 327704
  6.0 0.6 prepare.1
  6.6 1.6 %collective-permute-start = (bf16[3,64,256]{2,1,0:T(8,128)(2,1)S(1)}, bf16[3,64,256]{2,1,0:T(8,128)(2,1)S(1)}, u32[]{:S(2)}, u32[]{:S(2)}) collective-permute-start(bf16[3,64,256]{2,1,0:T(8,128)(2,1)S(1)} %prepare.1), channel_id=1, source_target_pairs={{0,8},{1,9},{2,10},{3,11},{4,12},{5,13},{6,14},{7,15},{8,0},{9,1},... | collective-permute-start | bytes 294920 | tf_op jit(solution)/shard_map/ppermute | solution.py:186
  8.2 2.6 %collective-permute-start.1 = (bf16[3,64,256]{2,1,0:T(8,128)(2,1)S(1)}, bf16[3,64,256]{2,1,0:T(8,128)(2,1)S(1)}, u32[]{:S(2)}, u32[]{:S(2)}) collective-permute-start(bf16[3,64,256]{2,1,0:T(8,128)(2,1)S(1)} %prepare.1), channel_id=1, source_target_pairs={{0,16},{1,17},{2,18},{3,19},{4,20},{5,21},{6,22},{7,23},{8,24},{9,... | collective-permute-start | bytes 294920 | tf_op jit(solution)/shard_map/ppermute | solution.py:186
  10.8 0.2 collective-permute-start.2
  11.0 1.2 %collective-permute-done = bf16[3,64,256]{2,1,0:T(8,128)(2,1)S(1)} collective-permute-done((bf16[3,64,256]{2,1,0:T(8,128)(2,1)S(1)}, bf16[3,64,256]{2,1,0:T(8,128)(2,1)S(1)}, u32[]{:S(2)}, u32[]{:S(2)}) %collective-permute-start) | collective-permute-done | bytes 98336 | tf_op jit(solution)/shard_map/ppermute | solution.py:186
  12.2 6.1 %collective-permute-done.1 = bf16[3,64,256]{2,1,0:T(8,128)(2,1)S(1)} collective-permute-done((bf16[3,64,256]{2,1,0:T(8,128)(2,1)S(1)}, bf16[3,64,256]{2,1,0:T(8,128)(2,1)S(1)}, u32[]{:S(2)}, u32[]{:S(2)}) %collective-permute-start.1) | collective-permute-done | bytes 98336 | tf_op jit(solution)/shard_map/ppermute | solution.py:186
  18.5 1.0 %deal.1 = bf16[4,2,256,256]{3,2,1,0:T(8,128)(2,1)} custom-call(bf16[1024,256]{1,0:T(8,128)(2,1)S(1)} %constant_dynamic-slice_fusion.kept_ref, bf16[1024,256]{1,0:T(8,128)(2,1)S(1)} %collective-permute-done.3.across_ref), custom_call_target="tpu_custom_call" | custom-call | tf_op jit(solution)/shard_map/deal/pallas_call | solution.py:219
  19.5 3.9 %all-to-all-start = ((bf16[4,2,256,256]{3,2,1,0:T(8,128)(2,1)}), bf16[4,2,256,256]{3,2,1,0:T(8,128)(2,1)S(1)}, u32[]{:S(2)}, u32[]{:S(2)}) async-start(bf16[4,2,256,256]{3,2,1,0:T(8,128)(2,1)} %deal.1), calls=%async_computation | async-start | bytes 2097152 | tf_op jit(solution)/shard_map/all_to_all | solution.py:228
  23.4 1.5 %collective-permute-start.6 = (bf16[4,3,64,256]{3,2,1,0:T(8,128)(2,1)S(1)}, bf16[4,3,64,256]{3,2,1,0:T(8,128)(2,1)S(1)}, u32[]{:S(2)}, u32[]{:S(2)}) collective-permute-start(bf16[4,3,64,256]{3,2,1,0:T(8,128)(2,1)S(1)} %pad_maximum_fusion.rest_0_), channel_id=1, source_target_pairs={{0,6},{1,7},{2,4},{3,5},{4,2},{5,3},{6,0},{7,1},{8,14},{9,15},{10,... | collective-permute-start | bytes 1179656 | tf_op jit(solution)/shard_map/ppermute | solution.py:186
  24.9 0.5 collective-permute-start.4
  25.4 1.5 %collective-permute-start.5 = (bf16[4,3,64,256]{3,2,1,0:T(8,128)(2,1)S(1)}, bf16[4,3,64,256]{3,2,1,0:T(8,128)(2,1)S(1)}, u32[]{:S(2)}, u32[]{:S(2)}) collective-permute-start(bf16[4,3,64,256]{3,2,1,0:T(8,128)(2,1)S(1)} %pad_maximum_fusion.rest_0_), channel_id=1, source_target_pairs={{0,4},{1,5},{2,6},{3,7},{4,0},{5,1},{6,2},{7,3},{8,12},{9,13},{10,... | collective-permute-start | bytes 1179656 | tf_op jit(solution)/shard_map/ppermute | solution.py:186
  26.9 9.5 %collective-permute-done.6.rest_3_ = bf16[4,3,64,256]{3,2,1,0:T(8,128)(2,1)S(1)} collective-permute-done((bf16[4,3,64,256]{3,2,1,0:T(8,128)(2,1)S(1)}, bf16[4,3,64,256]{3,2,1,0:T(8,128)(2,1)S(1)}, u32[]{:S(2)}, u32[]{:S(2)}) %collective-permute-start.6) | collective-permute-done | bytes 393248 | tf_op jit(solution)/shard_map/ppermute | solution.py:186
  36.3 5.7 %collective-permute-done.4.rest_1_ = bf16[4,3,64,256]{3,2,1,0:T(8,128)(2,1)S(1)} collective-permute-done((bf16[4,3,64,256]{3,2,1,0:T(8,128)(2,1)S(1)}, bf16[4,3,64,256]{3,2,1,0:T(8,128)(2,1)S(1)}, u32[]{:S(2)}, u32[]{:S(2)}) %collective-permute-start.4) | collective-permute-done | bytes 393248 | tf_op jit(solution)/shard_map/ppermute | solution.py:186
  42.1 0.4 collective-permute-start.9
  42.5 1.2 %collective-permute-done.8.rest_5_ = bf16[4,3,64,256]{3,2,1,0:T(8,128)(2,1)S(1)} collective-permute-done((bf16[4,3,64,256]{3,2,1,0:T(8,128)(2,1)S(1)}, bf16[4,3,64,256]{3,2,1,0:T(8,128)(2,1)S(1)}, u32[]{:S(2)}, u32[]{:S(2)}) %collective-permute-start.8) | collective-permute-done | bytes 393248 | tf_op jit(solution)/shard_map/ppermute | solution.py:186
  43.7 0.6 collective-permute-done.9.rest_6_
  44.3 2.4 %gather.1.omega_ref = bf16[8,3,256,256]{3,2,1,0:T(8,128)(2,1)S(1)} custom-call(s32[7]{0:T(128)S(1)} %pad_add_fusion.place_ref, bf16[4,3,64,256]{3,2,1,0:T(8,128)(2,1)S(1)} %pad_maximum_fusion.rest_0_, bf16[4,3,64,256]{3,2,1,0:T(8,128)(2,1)S(1)} %collective-permute-done.4.rest_1_, bf16[4,3,64,256]{3,2,1,0:T(8,128)(2,1)S(1)} %collective-permute-done.5.rest_2_, ...), custom_call_target="tpu_custom_call" | custom-call | tf_op jit(solution)/shard_map/gather/pallas_call | solution.py:230
  46.7 1.6 %copy-done.1 = bf16[8,3,256,256]{3,2,1,0:T(8,128)(2,1)} copy-done((bf16[8,3,256,256]{3,2,1,0:T(8,128)(2,1)}, bf16[8,3,256,256]{3,2,1,0:T(8,128)(2,1)S(1)}, u32[]{:S(2)}) %copy-start.1) | copy-done | bytes 3145752
  48.5 1.9 %copy-done.2 = bf16[8,3,256,256]{3,2,1,0:T(8,128)(2,1)S(1)} copy-done((bf16[8,3,256,256]{3,2,1,0:T(8,128)(2,1)S(1)}, bf16[8,3,256,256]{3,2,1,0:T(8,128)(2,1)}, u32[]{:S(2)}) %copy-start.2) | copy-done | bytes 3145752
  50.4 2.3 %mix.2 = (bf16[8,512,256]{2,1,0:T(8,128)(2,1)S(1)}, bf16[8,128,512]{2,1,0:T(8,128)(2,1)S(1)}) custom-call(s32[7]{0:T(128)S(1)} %pad_add_fusion.place_ref, bf16[4,2,256,256]{3,2,1,0:T(8,128)(2,1)S(1)} %all-to-all-done.data_ref._, bf16[8,3,256,256]{3,2,1,0:T(8,128)(2,1)S(1)} %copy-done.2), custom_call_target="tpu_custom_call" | custom-call | tf_op jit(solution)/shard_map/mix/pallas_call | solution.py:243
  52.7 2.3 %mix.3 = (bf16[8,512,256]{2,1,0:T(8,128)(2,1)S(1)}, bf16[8,128,512]{2,1,0:T(8,128)(2,1)S(1)}) custom-call(s32[7]{0:T(128)S(1)} %pad_add_fusion.place_ref, bf16[4,2,256,256]{3,2,1,0:T(8,128)(2,1)S(1)} %collective-permute-done.11.data_ref, bf16[8,3,256,256]{3,2,1,0:T(8,128)(2,1)S(1)} %copy-done.2), custom_call_target="tpu_custom_call" | custom-call | tf_op jit(solution)/shard_map/mix/pallas_call | solution.py:243
  55.0 1.4 %products.8 = (f32[2,1,5,64,256]{4,3,2,1,0:T(8,128)S(1)}, bf16[2,1,5,64,256]{4,3,2,1,0:T(8,128)(2,1)S(1)}) custom-call(s32[7]{0:T(128)S(1)} %pad_add_fusion.place_ref, bf16[4,2,256,256]{3,2,1,0:T(8,128)(2,1)S(1)} %all-to-all-done.data_ref._, bf16[8,512,256]{2,1,0:T(8,128)(2,1)S(1)} %get-tuple-element.39.rest_0_, ...), custom_call_target="tpu_custom_call" | custom-call | tf_op jit(solution)/shard_map/products/pallas_call | solution.py:265
  56.4 1.2 %collective-permute-start.13 = (bf16[2,1,5,64,256]{4,3,2,1,0:T(8,128)(2,1)S(1)}, bf16[2,1,5,64,256]{4,3,2,1,0:T(8,128)(2,1)S(1)}, u32[]{:S(2)}, u32[]{:S(2)}) collective-permute-start(bf16[2,1,5,64,256]{4,3,2,1,0:T(8,128)(2,1)S(1)} %get-tuple-element.46), channel_id=1, source_target_pairs={{0,2},{1,3},{2,0},{3,1},{4,6},{5,7},{6,4},{7,5},{8,10},{9,11},{10,... | collective-permute-start | bytes 983048 | tf_op jit(solution)/shard_map/ppermute | solution.py:186
  57.7 1.1 %products.7 = bf16[2,1,5,64,256]{4,3,2,1,0:T(8,128)(2,1)S(1)} custom-call(s32[7]{0:T(128)S(1)} %pad_add_fusion.place_ref, bf16[4,2,256,256]{3,2,1,0:T(8,128)(2,1)S(1)} %all-to-all-done.data_ref._, bf16[8,512,256]{2,1,0:T(8,128)(2,1)S(1)} %get-tuple-element.39.rest_0_, bf16[8,128,512]{2,1,0:T(8,128)(2,1)S(1)} %get-tuple-element.40.rest_1_, ...), custom_call_target="tpu_custom_call" | custom-call | tf_op jit(solution)/shard_map/products/pallas_call | solution.py:265
  58.8 1.2 %collective-permute-start.12 = (bf16[2,1,5,64,256]{4,3,2,1,0:T(8,128)(2,1)S(1)}, bf16[2,1,5,64,256]{4,3,2,1,0:T(8,128)(2,1)S(1)}, u32[]{:S(2)}, u32[]{:S(2)}) collective-permute-start(bf16[2,1,5,64,256]{4,3,2,1,0:T(8,128)(2,1)S(1)} %products.7), channel_id=1, source_target_pairs={{0,4},{1,5},{2,6},{3,7},{4,0},{5,1},{6,2},{7,3},{8,12},{9,13},{10,... | collective-permute-start | bytes 983048 | tf_op jit(solution)/shard_map/ppermute | solution.py:186
  60.0 1.4 %products.11 = (f32[2,1,5,64,256]{4,3,2,1,0:T(8,128)S(1)}, bf16[2,1,5,64,256]{4,3,2,1,0:T(8,128)(2,1)S(1)}) custom-call(s32[7]{0:T(128)S(1)} %pad_add_fusion.place_ref, bf16[4,2,256,256]{3,2,1,0:T(8,128)(2,1)S(1)} %all-to-all-done.data_ref._, bf16[8,512,256]{2,1,0:T(8,128)(2,1)S(1)} %get-tuple-element.39.rest_0_, ...), custom_call_target="tpu_custom_call" | custom-call | tf_op jit(solution)/shard_map/products/pallas_call | solution.py:265
  61.4 1.1 %products.10.refs_0_ = f32[2,1,5,64,256]{4,3,2,1,0:T(8,128)S(1)} custom-call(s32[7]{0:T(128)S(1)} %pad_add_fusion.place_ref, bf16[4,2,256,256]{3,2,1,0:T(8,128)(2,1)S(1)} %all-to-all-done.data_ref._, bf16[8,512,256]{2,1,0:T(8,128)(2,1)S(1)} %get-tuple-element.39.rest_0_, bf16[8,128,512]{2,1,0:T(8,128)(2,1)S(1)} %get-tuple-element.40.rest_1_, ...), custom_call_target="tpu_custom_call" | custom-call | tf_op jit(solution)/shard_map/products/pallas_call | solution.py:265
  62.4 1.1 %products.9 = bf16[2,1,5,64,256]{4,3,2,1,0:T(8,128)(2,1)S(1)} custom-call(s32[7]{0:T(128)S(1)} %pad_add_fusion.place_ref, bf16[4,2,256,256]{3,2,1,0:T(8,128)(2,1)S(1)} %all-to-all-done.data_ref._, bf16[8,512,256]{2,1,0:T(8,128)(2,1)S(1)} %get-tuple-element.39.rest_0_, bf16[8,128,512]{2,1,0:T(8,128)(2,1)S(1)} %get-tuple-element.40.rest_1_, ...), custom_call_target="tpu_custom_call" | custom-call | tf_op jit(solution)/shard_map/products/pallas_call | solution.py:265
  63.5 1.1 %products.6.refs_0_ = f32[2,1,5,64,256]{4,3,2,1,0:T(8,128)S(1)} custom-call(s32[7]{0:T(128)S(1)} %pad_add_fusion.place_ref, bf16[4,2,256,256]{3,2,1,0:T(8,128)(2,1)S(1)} %all-to-all-done.data_ref._, bf16[8,512,256]{2,1,0:T(8,128)(2,1)S(1)} %get-tuple-element.39.rest_0_, bf16[8,128,512]{2,1,0:T(8,128)(2,1)S(1)} %get-tuple-element.40.rest_1_, ...), custom_call_target="tpu_custom_call" | custom-call | tf_op jit(solution)/shard_map/products/pallas_call | solution.py:265
  64.6 1.9 %collective-permute-done.13.refs_1_ = bf16[2,1,5,64,256]{4,3,2,1,0:T(8,128)(2,1)S(1)} collective-permute-done((bf16[2,1,5,64,256]{4,3,2,1,0:T(8,128)(2,1)S(1)}, bf16[2,1,5,64,256]{4,3,2,1,0:T(8,128)(2,1)S(1)}, u32[]{:S(2)}, u32[]{:S(2)}) %collective-permute-start.13) | collective-permute-done | bytes 327712 | tf_op jit(solution)/shard_map/ppermute | solution.py:186
  66.6 2.0 %collective-permute-done.12.refs_1_ = bf16[2,1,5,64,256]{4,3,2,1,0:T(8,128)(2,1)S(1)} collective-permute-done((bf16[2,1,5,64,256]{4,3,2,1,0:T(8,128)(2,1)S(1)}, bf16[2,1,5,64,256]{4,3,2,1,0:T(8,128)(2,1)S(1)}, u32[]{:S(2)}, u32[]{:S(2)}) %collective-permute-start.12) | collective-permute-done | bytes 327712 | tf_op jit(solution)/shard_map/ppermute | solution.py:186
  68.7 0.9 collective-permute-start.16
  69.5 0.9 collective-permute-start.21
  70.4 1.1 %collective-permute-start.14 = (bf16[2,1,5,64,256]{4,3,2,1,0:T(8,128)(2,1)S(1)}, bf16[2,1,5,64,256]{4,3,2,1,0:T(8,128)(2,1)S(1)}, u32[]{:S(2)}, u32[]{:S(2)}) collective-permute-start(bf16[2,1,5,64,256]{4,3,2,1,0:T(8,128)(2,1)S(1)} %products.9), channel_id=1, source_target_pairs={{0,4},{1,5},{2,6},{3,7},{4,0},{5,1},{6,2},{7,3},{8,12},{9,13},{10,... | collective-permute-start | bytes 983048 | tf_op jit(solution)/shard_map/ppermute | solution.py:186
  71.6 1.2 %collective-permute-start.19 = (bf16[1,5,64,256]{3,2,1,0:T(8,128)(2,1)S(1)}, bf16[1,5,64,256]{3,2,1,0:T(8,128)(2,1)S(1)}, u32[]{:S(2)}, u32[]{:S(2)}) collective-permute-start(bf16[1,5,64,256]{3,2,1,0:T(8,128)(2,1)S(1)} %get-tuple-element.60), channel_id=1, source_target_pairs={{0,2},{1,3},{2,0},{3,1},{4,6},{5,7},{6,4},{7,5},{8,10},{9,11},{10,... | collective-permute-start | bytes 491528 | tf_op jit(solution)/shard_map/ppermute | solution.py:186
  72.8 3.9 %collective-permute-done.21.refs_1_ = bf16[1,5,64,256]{3,2,1,0:T(8,128)(2,1)S(1)} collective-permute-done((bf16[1,5,64,256]{3,2,1,0:T(8,128)(2,1)S(1)}, bf16[1,5,64,256]{3,2,1,0:T(8,128)(2,1)S(1)}, u32[]{:S(2)}, u32[]{:S(2)}) %collective-permute-start.21) | collective-permute-done | bytes 163872 | tf_op jit(solution)/shard_map/ppermute | solution.py:186
  76.7 2.7 %collective-permute-done.16.refs_1_ = bf16[2,1,5,64,256]{4,3,2,1,0:T(8,128)(2,1)S(1)} collective-permute-done((bf16[2,1,5,64,256]{4,3,2,1,0:T(8,128)(2,1)S(1)}, bf16[2,1,5,64,256]{4,3,2,1,0:T(8,128)(2,1)S(1)}, u32[]{:S(2)}, u32[]{:S(2)}) %collective-permute-start.16) | collective-permute-done | bytes 327712 | tf_op jit(solution)/shard_map/ppermute | solution.py:186
  79.5 1.2 %collective-permute-start.17 = (bf16[1,5,64,256]{3,2,1,0:T(8,128)(2,1)S(1)}, bf16[1,5,64,256]{3,2,1,0:T(8,128)(2,1)S(1)}, u32[]{:S(2)}, u32[]{:S(2)}) collective-permute-start(bf16[1,5,64,256]{3,2,1,0:T(8,128)(2,1)S(1)} %get-tuple-element.58), channel_id=1, source_target_pairs={{0,4},{1,5},{2,6},{3,7},{4,0},{5,1},{6,2},{7,3},{8,12},{9,13},{10,... | collective-permute-start | bytes 491528 | tf_op jit(solution)/shard_map/ppermute | solution.py:186
  80.7 3.5 %collective-permute-start.22 = (bf16[5,64,256]{2,1,0:T(8,128)(2,1)S(1)}, bf16[5,64,256]{2,1,0:T(8,128)(2,1)S(1)}, u32[]{:S(2)}, u32[]{:S(2)}) collective-permute-start(bf16[5,64,256]{2,1,0:T(8,128)(2,1)S(1)} %add.36), channel_id=1, source_target_pairs={{0,24},{1,25},{2,26},{3,27},{4,28},{5,29},{6,30},{7,31},{8,16},{9,... | collective-permute-start | bytes 491528 | tf_op jit(solution)/shard_map/ppermute | solution.py:186
  84.4 0.6 collective-permute-start.15
  85.2 1.8 %collective-permute-start.18 = (bf16[5,64,256]{2,1,0:T(8,128)(2,1)S(1)}, bf16[5,64,256]{2,1,0:T(8,128)(2,1)S(1)}, u32[]{:S(2)}, u32[]{:S(2)}) collective-permute-start(bf16[5,64,256]{2,1,0:T(8,128)(2,1)S(1)} %add.34), channel_id=1, source_target_pairs={{0,8},{1,9},{2,10},{3,11},{4,12},{5,13},{6,14},{7,15},{8,0},{9,1},... | collective-permute-start | bytes 491528 | tf_op jit(solution)/shard_map/ppermute | solution.py:186
  87.0 1.7 %collective-permute-done.22.refs_1_ = bf16[5,64,256]{2,1,0:T(8,128)(2,1)S(1)} collective-permute-done((bf16[5,64,256]{2,1,0:T(8,128)(2,1)S(1)}, bf16[5,64,256]{2,1,0:T(8,128)(2,1)S(1)}, u32[]{:S(2)}, u32[]{:S(2)}) %collective-permute-start.22) | collective-permute-done | bytes 163872 | tf_op jit(solution)/shard_map/ppermute | solution.py:186
  88.7 6.3 %collective-permute-done.20.refs_0_ = bf16[5,64,256]{2,1,0:T(8,128)(2,1)S(1)} collective-permute-done((bf16[5,64,256]{2,1,0:T(8,128)(2,1)S(1)}, bf16[5,64,256]{2,1,0:T(8,128)(2,1)S(1)}, u32[]{:S(2)}, u32[]{:S(2)}) %collective-permute-start.20) | collective-permute-done | bytes 163872 | tf_op jit(solution)/shard_map/ppermute | solution.py:186
  95.0 1.4 %update.1 = f32[1,5,64,256]{3,2,1,0:T(8,128)} custom-call(s32[7]{0:T(128)S(1)} %pad_add_fusion.place_ref, f32[1,5,64,256]{3,2,1,0:T(8,128)S(1)} %copy-done.4, f32[5,64,256]{2,1,0:T(8,128)S(1)} %add.32.rest_0_, bf16[5,64,256]{2,1,0:T(8,128)(2,1)S(1)} %collective-permute-done.18.rest_1_, f32[5,64,256]{2,1,0:T(8,128)S(1)} %add.37.rest_2_), custom_call_target="tpu_custom_call" | custom-call | tf_op jit(solution)/shard_map/update/pallas_call | solution.py:345
  (35 shorter events, 1.1 us)
Async XLA Ops:
  0.0 1.2 %copy-start = (bf16[2048,256]{1,0:T(8,128)(2,1)S(1)}, bf16[2048,256]{1,0:T(8,128)(2,1)}, u32[]{:S(2)}) copy-start(bf16[2048,256]{1,0:T(8,128)(2,1)} %param.3) | copy-start | bytes 3145732
  1.3 17.1 %collective-permute-start.3 = (bf16[1024,256]{1,0:T(8,128)(2,1)S(1)}, bf16[1024,256]{1,0:T(8,128)(2,1)S(1)}, u32[]{:S(2)}, u32[]{:S(2)}) collective-permute-start(bf16[1024,256]{1,0:T(8,128)(2,1)S(1)} %constant_dynamic-slice_fusion.1), channel_id=1, source_target_pairs={{0,4},{1,5},{2,6},{3,7},{4,0},{5,1},{6,2},{7,3},{8,12},{9,13},{10,... | collective-permute-start | bytes 1572872 | tf_op jit(solution)/shard_map/ppermute | solution.py:186
  5.0 1.0 %copy-start.3 = (f32[1,5,64,256]{3,2,1,0:T(8,128)S(1)}, f32[1,5,64,256]{3,2,1,0:T(8,128)}, u32[]{:S(2)}) copy-start(f32[1,5,64,256]{3,2,1,0:T(8,128)} %omega_ref.3) | copy-start | bytes 983044
  6.6 5.7 %collective-permute-start = (bf16[3,64,256]{2,1,0:T(8,128)(2,1)S(1)}, bf16[3,64,256]{2,1,0:T(8,128)(2,1)S(1)}, u32[]{:S(2)}, u32[]{:S(2)}) collective-permute-start(bf16[3,64,256]{2,1,0:T(8,128)(2,1)S(1)} %prepare.1), channel_id=1, source_target_pairs={{0,8},{1,9},{2,10},{3,11},{4,12},{5,13},{6,14},{7,15},{8,0},{9,1},... | collective-permute-start | bytes 294920 | tf_op jit(solution)/shard_map/ppermute | solution.py:186
  8.2 10.1 %collective-permute-start.1 = (bf16[3,64,256]{2,1,0:T(8,128)(2,1)S(1)}, bf16[3,64,256]{2,1,0:T(8,128)(2,1)S(1)}, u32[]{:S(2)}, u32[]{:S(2)}) collective-permute-start(bf16[3,64,256]{2,1,0:T(8,128)(2,1)S(1)} %prepare.1), channel_id=1, source_target_pairs={{0,16},{1,17},{2,18},{3,19},{4,20},{5,21},{6,22},{7,23},{8,24},{9,... | collective-permute-start | bytes 294920 | tf_op jit(solution)/shard_map/ppermute | solution.py:186
  10.8 7.6 %collective-permute-start.2 = (bf16[3,64,256]{2,1,0:T(8,128)(2,1)S(1)}, bf16[3,64,256]{2,1,0:T(8,128)(2,1)S(1)}, u32[]{:S(2)}, u32[]{:S(2)}) collective-permute-start(bf16[3,64,256]{2,1,0:T(8,128)(2,1)S(1)} %prepare.1), channel_id=1, source_target_pairs={{0,24},{1,25},{2,26},{3,27},{4,28},{5,29},{6,30},{7,31},{8,16},{9,... | collective-permute-start | bytes 294920 | tf_op jit(solution)/shard_map/ppermute | solution.py:186
  19.5 28.9 %all-to-all-start = ((bf16[4,2,256,256]{3,2,1,0:T(8,128)(2,1)}), bf16[4,2,256,256]{3,2,1,0:T(8,128)(2,1)S(1)}, u32[]{:S(2)}, u32[]{:S(2)}) async-start(bf16[4,2,256,256]{3,2,1,0:T(8,128)(2,1)} %deal.1), calls=%async_computation | async-start | bytes 2097152 | tf_op jit(solution)/shard_map/all_to_all | solution.py:228
  23.4 13.0 %collective-permute-start.6 = (bf16[4,3,64,256]{3,2,1,0:T(8,128)(2,1)S(1)}, bf16[4,3,64,256]{3,2,1,0:T(8,128)(2,1)S(1)}, u32[]{:S(2)}, u32[]{:S(2)}) collective-permute-start(bf16[4,3,64,256]{3,2,1,0:T(8,128)(2,1)S(1)} %pad_maximum_fusion.rest_0_), channel_id=1, source_target_pairs={{0,6},{1,7},{2,4},{3,5},{4,2},{5,3},{6,0},{7,1},{8,14},{9,15},{10,... | collective-permute-start | bytes 1179656 | tf_op jit(solution)/shard_map/ppermute | solution.py:186
  24.9 17.1 %collective-permute-start.4 = (bf16[4,3,64,256]{3,2,1,0:T(8,128)(2,1)S(1)}, bf16[4,3,64,256]{3,2,1,0:T(8,128)(2,1)S(1)}, u32[]{:S(2)}, u32[]{:S(2)}) collective-permute-start(bf16[4,3,64,256]{3,2,1,0:T(8,128)(2,1)S(1)} %pad_maximum_fusion.rest_0_), channel_id=1, source_target_pairs={{0,2},{1,3},{2,0},{3,1},{4,6},{5,7},{6,4},{7,5},{8,10},{9,11},{10,... | collective-permute-start | bytes 1179656 | tf_op jit(solution)/shard_map/ppermute | solution.py:186
  25.4 16.7 %collective-permute-start.5 = (bf16[4,3,64,256]{3,2,1,0:T(8,128)(2,1)S(1)}, bf16[4,3,64,256]{3,2,1,0:T(8,128)(2,1)S(1)}, u32[]{:S(2)}, u32[]{:S(2)}) collective-permute-start(bf16[4,3,64,256]{3,2,1,0:T(8,128)(2,1)S(1)} %pad_maximum_fusion.rest_0_), channel_id=1, source_target_pairs={{0,4},{1,5},{2,6},{3,7},{4,0},{5,1},{6,2},{7,3},{8,12},{9,13},{10,... | collective-permute-start | bytes 1179656 | tf_op jit(solution)/shard_map/ppermute | solution.py:186
  26.9 15.6 %collective-permute-start.7 = (bf16[4,3,64,256]{3,2,1,0:T(8,128)(2,1)S(1)}, bf16[4,3,64,256]{3,2,1,0:T(8,128)(2,1)S(1)}, u32[]{:S(2)}, u32[]{:S(2)}) collective-permute-start(bf16[4,3,64,256]{3,2,1,0:T(8,128)(2,1)S(1)} %pad_maximum_fusion.rest_0_), channel_id=1, source_target_pairs={{0,1},{1,0},{2,3},{3,2},{4,5},{5,4},{6,7},{7,6},{8,9},{9,8},{10,11... | collective-permute-start | bytes 1179656 | tf_op jit(solution)/shard_map/ppermute | solution.py:186
  36.3 6.2 %collective-permute-start.10 = (bf16[4,3,64,256]{3,2,1,0:T(8,128)(2,1)S(1)}, bf16[4,3,64,256]{3,2,1,0:T(8,128)(2,1)S(1)}, u32[]{:S(2)}, u32[]{:S(2)}) collective-permute-start(bf16[4,3,64,256]{3,2,1,0:T(8,128)(2,1)S(1)} %collective-permute-done.6.rest_3_), channel_id=1, source_target_pairs={{0,1},{1,0},{2,3},{3,2},{4,5},{5,4},{6,7},{7,6},{8,9},{9,8},{10,11... | collective-permute-start | bytes 1179656 | tf_op jit(solution)/shard_map/ppermute | solution.py:186
  42.0 1.7 %collective-permute-start.8 = (bf16[4,3,64,256]{3,2,1,0:T(8,128)(2,1)S(1)}, bf16[4,3,64,256]{3,2,1,0:T(8,128)(2,1)S(1)}, u32[]{:S(2)}, u32[]{:S(2)}) collective-permute-start(bf16[4,3,64,256]{3,2,1,0:T(8,128)(2,1)S(1)} %collective-permute-done.4.rest_1_), channel_id=1, source_target_pairs={{0,1},{1,0},{2,3},{3,2},{4,5},{5,4},{6,7},{7,6},{8,9},{9,8},{10,11... | collective-permute-start | bytes 1179656 | tf_op jit(solution)/shard_map/ppermute | solution.py:186
  42.1 2.2 %collective-permute-start.9 = (bf16[4,3,64,256]{3,2,1,0:T(8,128)(2,1)S(1)}, bf16[4,3,64,256]{3,2,1,0:T(8,128)(2,1)S(1)}, u32[]{:S(2)}, u32[]{:S(2)}) collective-permute-start(bf16[4,3,64,256]{3,2,1,0:T(8,128)(2,1)S(1)} %collective-permute-done.5.rest_2_), channel_id=1, source_target_pairs={{0,1},{1,0},{2,3},{3,2},{4,5},{5,4},{6,7},{7,6},{8,9},{9,8},{10,11... | collective-permute-start | bytes 1179656 | tf_op jit(solution)/shard_map/ppermute | solution.py:186
  46.7 1.6 %copy-start.1 = (bf16[8,3,256,256]{3,2,1,0:T(8,128)(2,1)}, bf16[8,3,256,256]{3,2,1,0:T(8,128)(2,1)S(1)}, u32[]{:S(2)}) copy-start(bf16[8,3,256,256]{3,2,1,0:T(8,128)(2,1)S(1)} %gather.1.omega_ref) | copy-start | bytes 9437188
  48.4 4.4 %collective-permute-start.11 = (bf16[4,2,256,256]{3,2,1,0:T(8,128)(2,1)S(1)}, bf16[4,2,256,256]{3,2,1,0:T(8,128)(2,1)S(1)}, u32[]{:S(2)}, u32[]{:S(2)}) collective-permute-start(bf16[4,2,256,256]{3,2,1,0:T(8,128)(2,1)S(1)} %all-to-all-done.data_ref._), channel_id=1, source_target_pairs={{0,1},{1,0},{2,3},{3,2},{4,5},{5,4},{6,7},{7,6},{8,9},{9,8},{10,11... | collective-permute-start | bytes 3145736 | tf_op jit(solution)/shard_map/ppermute | solution.py:186
  48.5 1.9 %copy-start.2 = (bf16[8,3,256,256]{3,2,1,0:T(8,128)(2,1)S(1)}, bf16[8,3,256,256]{3,2,1,0:T(8,128)(2,1)}, u32[]{:S(2)}) copy-start(bf16[8,3,256,256]{3,2,1,0:T(8,128)(2,1)} %copy-done.1) | copy-start | bytes 9437188
  56.4 10.1 %collective-permute-start.13 = (bf16[2,1,5,64,256]{4,3,2,1,0:T(8,128)(2,1)S(1)}, bf16[2,1,5,64,256]{4,3,2,1,0:T(8,128)(2,1)S(1)}, u32[]{:S(2)}, u32[]{:S(2)}) collective-permute-start(bf16[2,1,5,64,256]{4,3,2,1,0:T(8,128)(2,1)S(1)} %get-tuple-element.46), channel_id=1, source_target_pairs={{0,2},{1,3},{2,0},{3,1},{4,6},{5,7},{6,4},{7,5},{8,10},{9,11},{10,... | collective-permute-start | bytes 983048 | tf_op jit(solution)/shard_map/ppermute | solution.py:186
  58.8 9.8 %collective-permute-start.12 = (bf16[2,1,5,64,256]{4,3,2,1,0:T(8,128)(2,1)S(1)}, bf16[2,1,5,64,256]{4,3,2,1,0:T(8,128)(2,1)S(1)}, u32[]{:S(2)}, u32[]{:S(2)}) collective-permute-start(bf16[2,1,5,64,256]{4,3,2,1,0:T(8,128)(2,1)S(1)} %products.7), channel_id=1, source_target_pairs={{0,4},{1,5},{2,6},{3,7},{4,0},{5,1},{6,2},{7,3},{8,12},{9,13},{10,... | collective-permute-start | bytes 983048 | tf_op jit(solution)/shard_map/ppermute | solution.py:186
  68.7 10.7 %collective-permute-start.16 = (bf16[2,1,5,64,256]{4,3,2,1,0:T(8,128)(2,1)S(1)}, bf16[2,1,5,64,256]{4,3,2,1,0:T(8,128)(2,1)S(1)}, u32[]{:S(2)}, u32[]{:S(2)}) collective-permute-start(bf16[2,1,5,64,256]{4,3,2,1,0:T(8,128)(2,1)S(1)} %get-tuple-element.56), channel_id=1, source_target_pairs={{0,2},{1,3},{2,0},{3,1},{4,6},{5,7},{6,4},{7,5},{8,10},{9,11},{10,... | collective-permute-start | bytes 983048 | tf_op jit(solution)/shard_map/ppermute | solution.py:186
  69.5 7.1 %collective-permute-start.21 = (bf16[1,5,64,256]{3,2,1,0:T(8,128)(2,1)S(1)}, bf16[1,5,64,256]{3,2,1,0:T(8,128)(2,1)S(1)}, u32[]{:S(2)}, u32[]{:S(2)}) collective-permute-start(bf16[1,5,64,256]{3,2,1,0:T(8,128)(2,1)S(1)} %get-tuple-element.62), channel_id=1, source_target_pairs={{0,4},{1,5},{2,6},{3,7},{4,0},{5,1},{6,2},{7,3},{8,12},{9,13},{10,... | collective-permute-start | bytes 491528 | tf_op jit(solution)/shard_map/ppermute | solution.py:186
  70.4 13.9 %collective-permute-start.14 = (bf16[2,1,5,64,256]{4,3,2,1,0:T(8,128)(2,1)S(1)}, bf16[2,1,5,64,256]{4,3,2,1,0:T(8,128)(2,1)S(1)}, u32[]{:S(2)}, u32[]{:S(2)}) collective-permute-start(bf16[2,1,5,64,256]{4,3,2,1,0:T(8,128)(2,1)S(1)} %products.9), channel_id=1, source_target_pairs={{0,4},{1,5},{2,6},{3,7},{4,0},{5,1},{6,2},{7,3},{8,12},{9,13},{10,... | collective-permute-start | bytes 983048 | tf_op jit(solution)/shard_map/ppermute | solution.py:186
  71.6 12.6 %collective-permute-start.19 = (bf16[1,5,64,256]{3,2,1,0:T(8,128)(2,1)S(1)}, bf16[1,5,64,256]{3,2,1,0:T(8,128)(2,1)S(1)}, u32[]{:S(2)}, u32[]{:S(2)}) collective-permute-start(bf16[1,5,64,256]{3,2,1,0:T(8,128)(2,1)S(1)} %get-tuple-element.60), channel_id=1, source_target_pairs={{0,2},{1,3},{2,0},{3,1},{4,6},{5,7},{6,4},{7,5},{8,10},{9,11},{10,... | collective-permute-start | bytes 491528 | tf_op jit(solution)/shard_map/ppermute | solution.py:186
  79.5 5.7 %collective-permute-start.17 = (bf16[1,5,64,256]{3,2,1,0:T(8,128)(2,1)S(1)}, bf16[1,5,64,256]{3,2,1,0:T(8,128)(2,1)S(1)}, u32[]{:S(2)}, u32[]{:S(2)}) collective-permute-start(bf16[1,5,64,256]{3,2,1,0:T(8,128)(2,1)S(1)} %get-tuple-element.58), channel_id=1, source_target_pairs={{0,4},{1,5},{2,6},{3,7},{4,0},{5,1},{6,2},{7,3},{8,12},{9,13},{10,... | collective-permute-start | bytes 491528 | tf_op jit(solution)/shard_map/ppermute | solution.py:186
  80.7 8.0 %collective-permute-start.22 = (bf16[5,64,256]{2,1,0:T(8,128)(2,1)S(1)}, bf16[5,64,256]{2,1,0:T(8,128)(2,1)S(1)}, u32[]{:S(2)}, u32[]{:S(2)}) collective-permute-start(bf16[5,64,256]{2,1,0:T(8,128)(2,1)S(1)} %add.36), channel_id=1, source_target_pairs={{0,24},{1,25},{2,26},{3,27},{4,28},{5,29},{6,30},{7,31},{8,16},{9,... | collective-permute-start | bytes 491528 | tf_op jit(solution)/shard_map/ppermute | solution.py:186
  84.2 10.7 %collective-permute-start.20 = (bf16[5,64,256]{2,1,0:T(8,128)(2,1)S(1)}, bf16[5,64,256]{2,1,0:T(8,128)(2,1)S(1)}, u32[]{:S(2)}, u32[]{:S(2)}) collective-permute-start(bf16[5,64,256]{2,1,0:T(8,128)(2,1)S(1)} %add.35), channel_id=1, source_target_pairs={{0,16},{1,17},{2,18},{3,19},{4,20},{5,21},{6,22},{7,23},{8,24},{9,... | collective-permute-start | bytes 491528 | tf_op jit(solution)/shard_map/ppermute | solution.py:186
  84.4 10.6 %collective-permute-start.15 = (bf16[1,5,64,256]{3,2,1,0:T(8,128)(2,1)S(1)}, bf16[1,5,64,256]{3,2,1,0:T(8,128)(2,1)S(1)}, u32[]{:S(2)}, u32[]{:S(2)}) collective-permute-start(bf16[1,5,64,256]{3,2,1,0:T(8,128)(2,1)S(1)} %get-tuple-element.54), channel_id=1, source_target_pairs={{0,2},{1,3},{2,0},{3,1},{4,6},{5,7},{6,4},{7,5},{8,10},{9,11},{10,... | collective-permute-start | bytes 491528 | tf_op jit(solution)/shard_map/ppermute | solution.py:186
  85.2 9.8 %copy-start.4 = (f32[1,5,64,256]{3,2,1,0:T(8,128)S(1)}, f32[1,5,64,256]{3,2,1,0:T(8,128)}, u32[]{:S(2)}) copy-start(f32[1,5,64,256]{3,2,1,0:T(8,128)} %omega_ref.3) | copy-start | bytes 983044
  85.2 9.8 %collective-permute-start.18 = (bf16[5,64,256]{2,1,0:T(8,128)(2,1)S(1)}, bf16[5,64,256]{2,1,0:T(8,128)(2,1)S(1)}, u32[]{:S(2)}, u32[]{:S(2)}) collective-permute-start(bf16[5,64,256]{2,1,0:T(8,128)(2,1)S(1)} %add.34), channel_id=1, source_target_pairs={{0,8},{1,9},{2,10},{3,11},{4,12},{5,13},{6,14},{7,15},{8,0},{9,1},... | collective-permute-start | bytes 491528 | tf_op jit(solution)/shard_map/ppermute | solution.py:186

commit v12 on v11

--- a/solution.py
+++ b/solution.py
@@ -88,13 +88,13 @@
     return data_ref[lax.div(c, LOW), lax.rem(c, LOW) ^ low]
 
 
-def mix_kernel(teams, replicas, tile_rows, place_ref, data_ref, omega_ref, right_ref, left_ref, flip_ref):
+def mix_kernel(teams, replicas, tile_rows, place_ref, data_ref, omega_ref, kept_ref, mixed_ref, left_ref, flip_ref):
     chips = replicas // 2
     team, replica = place_ref[0], place_ref[1]
     core, chip = lax.rem(replica, 2), lax.div(replica, 2)
     low = lax.rem(team, LOW)
     offsets, _ = stored_offsets(place_ref, teams)
-    times = right_ref.shape[1] // 2
+    times = mixed_ref.shape[1]
 
     def mix(i, carry):
         total = None
@@ -105,8 +105,8 @@
             total = term if total is None else total + term
         mixed = total.astype(BF16)
         data = block(data_ref, low, i)
-        right_ref[i, :times] = data
-        right_ref[i, times:] = mixed
+        kept_ref[i] = data
+        mixed_ref[i] = mixed
         for n, array in enumerate([mixed, data]):
             flip_ref[n] = array.T
             for m in range(chips):
@@ -119,8 +119,8 @@
     lax.fori_loop(0, teams, mix, 0, unroll=teams <= 8)
 
 
-def product_kernel(teams, chips, wanted, place_ref, _, *rest):
-    rights, lefts, outs = rest[0:4:2], rest[1:4:2], rest[4:]
+def product_kernel(teams, chips, wanted, place_ref, *rest):
+    rights, lefts, outs = rest[0:2] + rest[3:5], rest[2:6:3], rest[6:]
     team = place_ref[0]
     high, low = lax.div(team, LOW), lax.rem(team, LOW)
     offsets, _ = stored_offsets(place_ref, teams)
@@ -243,13 +243,14 @@
         return pl.pallas_call(
             functools.partial(mix_kernel, teams, replicas, tile_rows),
             out_shape=[
-                jax.ShapeDtypeStruct((teams, 2 * times, width), BF16),
+                jax.ShapeDtypeStruct((teams, times, width), BF16),
+                jax.ShapeDtypeStruct((teams, times, width), BF16),
                 jax.ShapeDtypeStruct((teams, chips * tile_rows, 2 * times), BF16),
             ],
             in_specs=[SMEM, VMEM, VMEM],
-            out_specs=[VMEM, VMEM],
+            out_specs=[VMEM] * 3,
             scratch_shapes=[pltpu.VMEM((2, width, times), BF16)],
-            compiler_params=small,
+            compiler_params=tiny,
             name="mix",
         )(place, data, tiles)
 
@@ -265,11 +266,11 @@
         return pl.pallas_call(
             functools.partial(product_kernel, teams, chips, wanted),
             out_shape=shapes,
-            in_specs=[SMEM, ANY] + [VMEM] * 4,
+            in_specs=[SMEM] + [VMEM] * 6,
             out_specs=[VMEM] * len(shapes),
             compiler_params=small,
             name="products",
-        )(place, own, *cores)
+        )(place, *cores)
 
     def add(groups, shapes, *arrays, cost=None):
         return pl.pallas_call(

time: 96.8 us -> 96.6 us (level)
  no operation moved by 1% of the time
where the time goes in v12:
time: 96.6 us; the launch traced here: 96.3 us
  waiting for transfers between devices  42.7 us (44%)
  starting transfers between devices  29.2 us (30%)
  Pallas kernels  17.6 us (18%)
  local copies, waits for them, and re-layouts  5.8 us (6%)
    ppermute x23, waiting for transfers between devices, swap(): return lax.ppermute(array, AXES, route)  42.7 us
    ppermute x23, starting transfers between devices, swap(): return lax.ppermute(array, AXES, route)  25.3 us
    pallas_call x6, Pallas kernels, products(): pl.pallas_call(functools.partial(product_kernel, teams, chips, wanted), o...  7.05 us
    unnamed x10, local copies, waits for them, and re-layouts  5.72 us
    pallas_call x2, Pallas kernels, mix(): pl.pallas_call(functools.partial(mix_kernel, teams, replicas, tile_rows),...  4.6 us
    all_to_all x1, starting transfers between devices, per_device(): own = lax.all_to_all(dealt, 'line', 0, 0)  3.91 us
    pallas_call x1, Pallas kernels, per_device(): pl.pallas_call(functools.partial(gather_kernel, teams, chips, tile_rows),...  2.44 us
  transfers between devices with their start and end apart: 24, of which 14 were waited for; matrix products, arithmetic and copies ran while one was open for 1% of the time, Pallas kernels for 12%

profile of v12, /device:TPU:0, one launch (start us, length us, event | category | flops | bytes accessed | tf_op | source)
XLA Modules:
  0.0 96.3 jit_solution(11242833158989326868)
XLA Ops:
  0.0 1.2 %copy-done = bf16[2048,256]{1,0:T(8,128)(2,1)S(1)} copy-done((bf16[2048,256]{1,0:T(8,128)(2,1)S(1)}, bf16[2048,256]{1,0:T(8,128)(2,1)}, u32[]{:S(2)}) %copy-start) | copy-done | bytes 1048600
  1.3 3.0 %collective-permute-start.3 = (bf16[1024,256]{1,0:T(8,128)(2,1)S(1)}, bf16[1024,256]{1,0:T(8,128)(2,1)S(1)}, u32[]{:S(2)}, u32[]{:S(2)}) collective-permute-start(bf16[1024,256]{1,0:T(8,128)(2,1)S(1)} %constant_dynamic-slice_fusion.1), channel_id=1, source_target_pairs={{0,4},{1,5},{2,6},{3,7},{4,0},{5,1},{6,2},{7,3},{8,12},{9,13},{10,... | collective-permute-start | bytes 1572872 | tf_op jit(solution)/shard_map/ppermute | solution.py:186
  4.3 0.7 pad_add_fusion.place_ref
  5.0 1.0 %copy-done.3 = f32[1,5,64,256]{3,2,1,0:T(8,128)S(1)} copy-done((f32[1,5,64,256]{3,2,1,0:T(8,128)S(1)}, f32[1,5,64,256]{3,2,1,0:T(8,128)}, u32[]{:S(2)}) %copy-start.3) | copy-done | bytes 327704
  6.0 0.6 prepare.1
  6.6 1.6 %collective-permute-start = (bf16[3,64,256]{2,1,0:T(8,128)(2,1)S(1)}, bf16[3,64,256]{2,1,0:T(8,128)(2,1)S(1)}, u32[]{:S(2)}, u32[]{:S(2)}) collective-permute-start(bf16[3,64,256]{2,1,0:T(8,128)(2,1)S(1)} %prepare.1), channel_id=1, source_target_pairs={{0,8},{1,9},{2,10},{3,11},{4,12},{5,13},{6,14},{7,15},{8,0},{9,1},... | collective-permute-start | bytes 294920 | tf_op jit(solution)/shard_map/ppermute | solution.py:186
  8.2 2.6 %collective-permute-start.1 = (bf16[3,64,256]{2,1,0:T(8,128)(2,1)S(1)}, bf16[3,64,256]{2,1,0:T(8,128)(2,1)S(1)}, u32[]{:S(2)}, u32[]{:S(2)}) collective-permute-start(bf16[3,64,256]{2,1,0:T(8,128)(2,1)S(1)} %prepare.1), channel_id=1, source_target_pairs={{0,16},{1,17},{2,18},{3,19},{4,20},{5,21},{6,22},{7,23},{8,24},{9,... | collective-permute-start | bytes 294920 | tf_op jit(solution)/shard_map/ppermute | solution.py:186
  10.8 0.2 collective-permute-start.2
  11.0 1.2 %collective-permute-done = bf16[3,64,256]{2,1,0:T(8,128)(2,1)S(1)} collective-permute-done((bf16[3,64,256]{2,1,0:T(8,128)(2,1)S(1)}, bf16[3,64,256]{2,1,0:T(8,128)(2,1)S(1)}, u32[]{:S(2)}, u32[]{:S(2)}) %collective-permute-start) | collective-permute-done | bytes 98336 | tf_op jit(solution)/shard_map/ppermute | solution.py:186
  12.2 6.1 %collective-permute-done.1 = bf16[3,64,256]{2,1,0:T(8,128)(2,1)S(1)} collective-permute-done((bf16[3,64,256]{2,1,0:T(8,128)(2,1)S(1)}, bf16[3,64,256]{2,1,0:T(8,128)(2,1)S(1)}, u32[]{:S(2)}, u32[]{:S(2)}) %collective-permute-start.1) | collective-permute-done | bytes 98336 | tf_op jit(solution)/shard_map/ppermute | solution.py:186
  18.5 1.0 %deal.1 = bf16[4,2,256,256]{3,2,1,0:T(8,128)(2,1)} custom-call(bf16[1024,256]{1,0:T(8,128)(2,1)S(1)} %constant_dynamic-slice_fusion.kept_ref, bf16[1024,256]{1,0:T(8,128)(2,1)S(1)} %collective-permute-done.3.across_ref), custom_call_target="tpu_custom_call" | custom-call | tf_op jit(solution)/shard_map/deal/pallas_call | solution.py:219
  19.5 3.9 %all-to-all-start = ((bf16[4,2,256,256]{3,2,1,0:T(8,128)(2,1)}), bf16[4,2,256,256]{3,2,1,0:T(8,128)(2,1)S(1)}, u32[]{:S(2)}, u32[]{:S(2)}) async-start(bf16[4,2,256,256]{3,2,1,0:T(8,128)(2,1)} %deal.1), calls=%async_computation | async-start | bytes 2097152 | tf_op jit(solution)/shard_map/all_to_all | solution.py:228
  23.4 1.5 %collective-permute-start.6 = (bf16[4,3,64,256]{3,2,1,0:T(8,128)(2,1)S(1)}, bf16[4,3,64,256]{3,2,1,0:T(8,128)(2,1)S(1)}, u32[]{:S(2)}, u32[]{:S(2)}) collective-permute-start(bf16[4,3,64,256]{3,2,1,0:T(8,128)(2,1)S(1)} %pad_maximum_fusion.rest_0_), channel_id=1, source_target_pairs={{0,6},{1,7},{2,4},{3,5},{4,2},{5,3},{6,0},{7,1},{8,14},{9,15},{10,... | collective-permute-start | bytes 1179656 | tf_op jit(solution)/shard_map/ppermute | solution.py:186
  24.9 0.5 collective-permute-start.4
  25.4 1.5 %collective-permute-start.5 = (bf16[4,3,64,256]{3,2,1,0:T(8,128)(2,1)S(1)}, bf16[4,3,64,256]{3,2,1,0:T(8,128)(2,1)S(1)}, u32[]{:S(2)}, u32[]{:S(2)}) collective-permute-start(bf16[4,3,64,256]{3,2,1,0:T(8,128)(2,1)S(1)} %pad_maximum_fusion.rest_0_), channel_id=1, source_target_pairs={{0,4},{1,5},{2,6},{3,7},{4,0},{5,1},{6,2},{7,3},{8,12},{9,13},{10,... | collective-permute-start | bytes 1179656 | tf_op jit(solution)/shard_map/ppermute | solution.py:186
  26.9 9.5 %collective-permute-done.6.rest_3_ = bf16[4,3,64,256]{3,2,1,0:T(8,128)(2,1)S(1)} collective-permute-done((bf16[4,3,64,256]{3,2,1,0:T(8,128)(2,1)S(1)}, bf16[4,3,64,256]{3,2,1,0:T(8,128)(2,1)S(1)}, u32[]{:S(2)}, u32[]{:S(2)}) %collective-permute-start.6) | collective-permute-done | bytes 393248 | tf_op jit(solution)/shard_map/ppermute | solution.py:186
  36.3 5.7 %collective-permute-done.4.rest_1_ = bf16[4,3,64,256]{3,2,1,0:T(8,128)(2,1)S(1)} collective-permute-done((bf16[4,3,64,256]{3,2,1,0:T(8,128)(2,1)S(1)}, bf16[4,3,64,256]{3,2,1,0:T(8,128)(2,1)S(1)}, u32[]{:S(2)}, u32[]{:S(2)}) %collective-permute-start.4) | collective-permute-done | bytes 393248 | tf_op jit(solution)/shard_map/ppermute | solution.py:186
  42.1 0.4 collective-permute-start.9
  42.5 1.2 %collective-permute-done.8.rest_5_ = bf16[4,3,64,256]{3,2,1,0:T(8,128)(2,1)S(1)} collective-permute-done((bf16[4,3,64,256]{3,2,1,0:T(8,128)(2,1)S(1)}, bf16[4,3,64,256]{3,2,1,0:T(8,128)(2,1)S(1)}, u32[]{:S(2)}, u32[]{:S(2)}) %collective-permute-start.8) | collective-permute-done | bytes 393248 | tf_op jit(solution)/shard_map/ppermute | solution.py:186
  43.7 0.6 collective-permute-done.9.rest_6_
  44.3 2.4 %gather.1.omega_ref = bf16[8,3,256,256]{3,2,1,0:T(8,128)(2,1)S(1)} custom-call(s32[7]{0:T(128)S(1)} %pad_add_fusion.place_ref, bf16[4,3,64,256]{3,2,1,0:T(8,128)(2,1)S(1)} %pad_maximum_fusion.rest_0_, bf16[4,3,64,256]{3,2,1,0:T(8,128)(2,1)S(1)} %collective-permute-done.4.rest_1_, bf16[4,3,64,256]{3,2,1,0:T(8,128)(2,1)S(1)} %collective-permute-done.5.rest_2_, ...), custom_call_target="tpu_custom_call" | custom-call | tf_op jit(solution)/shard_map/gather/pallas_call | solution.py:230
  46.7 1.6 %copy-done.1 = bf16[8,3,256,256]{3,2,1,0:T(8,128)(2,1)} copy-done((bf16[8,3,256,256]{3,2,1,0:T(8,128)(2,1)}, bf16[8,3,256,256]{3,2,1,0:T(8,128)(2,1)S(1)}, u32[]{:S(2)}) %copy-start.1) | copy-done | bytes 3145752
  48.5 1.9 %copy-done.2 = bf16[8,3,256,256]{3,2,1,0:T(8,128)(2,1)S(1)} copy-done((bf16[8,3,256,256]{3,2,1,0:T(8,128)(2,1)S(1)}, bf16[8,3,256,256]{3,2,1,0:T(8,128)(2,1)}, u32[]{:S(2)}) %copy-start.2) | copy-done | bytes 3145752
  50.4 2.3 %mix.2 = (bf16[8,256,256]{2,1,0:T(8,128)(2,1)S(1)}, bf16[8,256,256]{2,1,0:T(8,128)(2,1)S(1)}, bf16[8,128,512]{2,1,0:T(8,128)(2,1)S(1)}) custom-call(s32[7]{0:T(128)S(1)} %pad_add_fusion.place_ref, bf16[4,2,256,256]{3,2,1,0:T(8,128)(2,1)S(1)} %all-to-all-done.data_ref, bf16[8,3,256,256]{3,2,1,0:T(8,128)(2,1)S(1)} %copy-done.2), custom_call_target="tpu_custom_call" | custom-call | tf_op jit(solution)/shard_map/mix/pallas_call | solution.py:243
  52.7 2.3 %mix.3 = (bf16[8,256,256]{2,1,0:T(8,128)(2,1)S(1)}, bf16[8,256,256]{2,1,0:T(8,128)(2,1)S(1)}, bf16[8,128,512]{2,1,0:T(8,128)(2,1)S(1)}) custom-call(s32[7]{0:T(128)S(1)} %pad_add_fusion.place_ref, bf16[4,2,256,256]{3,2,1,0:T(8,128)(2,1)S(1)} %collective-permute-done.11.data_ref, bf16[8,3,256,256]{3,2,1,0:T(8,128)(2,1)S(1)} %copy-done.2), custom_call_target="tpu_custom_call" | custom-call | tf_op jit(solution)/shard_map/mix/pallas_call | solution.py:243
  55.0 1.4 %products.8 = (f32[2,1,5,64,256]{4,3,2,1,0:T(8,128)S(1)}, bf16[2,1,5,64,256]{4,3,2,1,0:T(8,128)(2,1)S(1)}) custom-call(s32[7]{0:T(128)S(1)} %pad_add_fusion.place_ref, bf16[8,256,256]{2,1,0:T(8,128)(2,1)S(1)} %get-tuple-element.41.rest_0_, bf16[8,256,256]{2,1,0:T(8,128)(2,1)S(1)} %get-tuple-element.42.rest_1_, ...), custom_call_target="tpu_custom_call" | custom-call | tf_op jit(solution)/shard_map/products/pallas_call | solution.py:266
  56.4 1.3 %collective-permute-start.13 = (bf16[2,1,5,64,256]{4,3,2,1,0:T(8,128)(2,1)S(1)}, bf16[2,1,5,64,256]{4,3,2,1,0:T(8,128)(2,1)S(1)}, u32[]{:S(2)}, u32[]{:S(2)}) collective-permute-start(bf16[2,1,5,64,256]{4,3,2,1,0:T(8,128)(2,1)S(1)} %get-tuple-element.50), channel_id=1, source_target_pairs={{0,2},{1,3},{2,0},{3,1},{4,6},{5,7},{6,4},{7,5},{8,10},{9,11},{10,... | collective-permute-start | bytes 983048 | tf_op jit(solution)/shard_map/ppermute | solution.py:186
  57.7 1.1 %products.7 = bf16[2,1,5,64,256]{4,3,2,1,0:T(8,128)(2,1)S(1)} custom-call(s32[7]{0:T(128)S(1)} %pad_add_fusion.place_ref, bf16[8,256,256]{2,1,0:T(8,128)(2,1)S(1)} %get-tuple-element.41.rest_0_, bf16[8,256,256]{2,1,0:T(8,128)(2,1)S(1)} %get-tuple-element.42.rest_1_, bf16[8,128,512]{2,1,0:T(8,128)(2,1)S(1)} %get-tuple-element.43.rest_2_, ...), custom_call_target="tpu_custom_call" | custom-call | tf_op jit(solution)/shard_map/products/pallas_call | solution.py:266
  58.8 1.2 %collective-permute-start.12 = (bf16[2,1,5,64,256]{4,3,2,1,0:T(8,128)(2,1)S(1)}, bf16[2,1,5,64,256]{4,3,2,1,0:T(8,128)(2,1)S(1)}, u32[]{:S(2)}, u32[]{:S(2)}) collective-permute-start(bf16[2,1,5,64,256]{4,3,2,1,0:T(8,128)(2,1)S(1)} %products.7), channel_id=1, source_target_pairs={{0,4},{1,5},{2,6},{3,7},{4,0},{5,1},{6,2},{7,3},{8,12},{9,13},{10,... | collective-permute-start | bytes 983048 | tf_op jit(solution)/shard_map/ppermute | solution.py:186
  60.0 1.4 %products.11 = (f32[2,1,5,64,256]{4,3,2,1,0:T(8,128)S(1)}, bf16[2,1,5,64,256]{4,3,2,1,0:T(8,128)(2,1)S(1)}) custom-call(s32[7]{0:T(128)S(1)} %pad_add_fusion.place_ref, bf16[8,256,256]{2,1,0:T(8,128)(2,1)S(1)} %get-tuple-element.41.rest_0_, bf16[8,256,256]{2,1,0:T(8,128)(2,1)S(1)} %get-tuple-element.42.rest_1_, ...), custom_call_target="tpu_custom_call" | custom-call | tf_op jit(solution)/shard_map/products/pallas_call | solution.py:266
  61.4 1.1 %products.10.refs_0_ = f32[2,1,5,64,256]{4,3,2,1,0:T(8,128)S(1)} custom-call(s32[7]{0:T(128)S(1)} %pad_add_fusion.place_ref, bf16[8,256,256]{2,1,0:T(8,128)(2,1)S(1)} %get-tuple-element.41.rest_0_, bf16[8,256,256]{2,1,0:T(8,128)(2,1)S(1)} %get-tuple-element.42.rest_1_, bf16[8,128,512]{2,1,0:T(8,128)(2,1)S(1)} %get-tuple-element.43.rest_2_, ...), custom_call_target="tpu_custom_call" | custom-call | tf_op jit(solution)/shard_map/products/pallas_call | solution.py:266
  62.4 1.1 %products.9 = bf16[2,1,5,64,256]{4,3,2,1,0:T(8,128)(2,1)S(1)} custom-call(s32[7]{0:T(128)S(1)} %pad_add_fusion.place_ref, bf16[8,256,256]{2,1,0:T(8,128)(2,1)S(1)} %get-tuple-element.41.rest_0_, bf16[8,256,256]{2,1,0:T(8,128)(2,1)S(1)} %get-tuple-element.42.rest_1_, bf16[8,128,512]{2,1,0:T(8,128)(2,1)S(1)} %get-tuple-element.43.rest_2_, ...), custom_call_target="tpu_custom_call" | custom-call | tf_op jit(solution)/shard_map/products/pallas_call | solution.py:266
  63.5 1.1 %products.6.refs_0_ = f32[2,1,5,64,256]{4,3,2,1,0:T(8,128)S(1)} custom-call(s32[7]{0:T(128)S(1)} %pad_add_fusion.place_ref, bf16[8,256,256]{2,1,0:T(8,128)(2,1)S(1)} %get-tuple-element.41.rest_0_, bf16[8,256,256]{2,1,0:T(8,128)(2,1)S(1)} %get-tuple-element.42.rest_1_, bf16[8,128,512]{2,1,0:T(8,128)(2,1)S(1)} %get-tuple-element.43.rest_2_, ...), custom_call_target="tpu_custom_call" | custom-call | tf_op jit(solution)/shard_map/products/pallas_call | solution.py:266
  64.6 1.9 %collective-permute-done.13.refs_1_ = bf16[2,1,5,64,256]{4,3,2,1,0:T(8,128)(2,1)S(1)} collective-permute-done((bf16[2,1,5,64,256]{4,3,2,1,0:T(8,128)(2,1)S(1)}, bf16[2,1,5,64,256]{4,3,2,1,0:T(8,128)(2,1)S(1)}, u32[]{:S(2)}, u32[]{:S(2)}) %collective-permute-start.13) | collective-permute-done | bytes 327712 | tf_op jit(solution)/shard_map/ppermute | solution.py:186
  66.6 2.0 %collective-permute-done.12.refs_1_ = bf16[2,1,5,64,256]{4,3,2,1,0:T(8,128)(2,1)S(1)} collective-permute-done((bf16[2,1,5,64,256]{4,3,2,1,0:T(8,128)(2,1)S(1)}, bf16[2,1,5,64,256]{4,3,2,1,0:T(8,128)(2,1)S(1)}, u32[]{:S(2)}, u32[]{:S(2)}) %collective-permute-start.12) | collective-permute-done | bytes 327712 | tf_op jit(solution)/shard_map/ppermute | solution.py:186
  68.7 0.9 collective-permute-start.16
  69.5 0.9 collective-permute-start.21
  70.4 1.1 %collective-permute-start.14 = (bf16[2,1,5,64,256]{4,3,2,1,0:T(8,128)(2,1)S(1)}, bf16[2,1,5,64,256]{4,3,2,1,0:T(8,128)(2,1)S(1)}, u32[]{:S(2)}, u32[]{:S(2)}) collective-permute-start(bf16[2,1,5,64,256]{4,3,2,1,0:T(8,128)(2,1)S(1)} %products.9), channel_id=1, source_target_pairs={{0,4},{1,5},{2,6},{3,7},{4,0},{5,1},{6,2},{7,3},{8,12},{9,13},{10,... | collective-permute-start | bytes 983048 | tf_op jit(solution)/shard_map/ppermute | solution.py:186
  71.6 1.2 %collective-permute-start.19 = (bf16[1,5,64,256]{3,2,1,0:T(8,128)(2,1)S(1)}, bf16[1,5,64,256]{3,2,1,0:T(8,128)(2,1)S(1)}, u32[]{:S(2)}, u32[]{:S(2)}) collective-permute-start(bf16[1,5,64,256]{3,2,1,0:T(8,128)(2,1)S(1)} %get-tuple-element.64), channel_id=1, source_target_pairs={{0,2},{1,3},{2,0},{3,1},{4,6},{5,7},{6,4},{7,5},{8,10},{9,11},{10,... | collective-permute-start | bytes 491528 | tf_op jit(solution)/shard_map/ppermute | solution.py:186
  72.8 3.9 %collective-permute-done.21.refs_1_ = bf16[1,5,64,256]{3,2,1,0:T(8,128)(2,1)S(1)} collective-permute-done((bf16[1,5,64,256]{3,2,1,0:T(8,128)(2,1)S(1)}, bf16[1,5,64,256]{3,2,1,0:T(8,128)(2,1)S(1)}, u32[]{:S(2)}, u32[]{:S(2)}) %collective-permute-start.21) | collective-permute-done | bytes 163872 | tf_op jit(solution)/shard_map/ppermute | solution.py:186
  76.7 2.7 %collective-permute-done.16.refs_1_ = bf16[2,1,5,64,256]{4,3,2,1,0:T(8,128)(2,1)S(1)} collective-permute-done((bf16[2,1,5,64,256]{4,3,2,1,0:T(8,128)(2,1)S(1)}, bf16[2,1,5,64,256]{4,3,2,1,0:T(8,128)(2,1)S(1)}, u32[]{:S(2)}, u32[]{:S(2)}) %collective-permute-start.16) | collective-permute-done | bytes 327712 | tf_op jit(solution)/shard_map/ppermute | solution.py:186
  79.5 1.2 %collective-permute-start.17 = (bf16[1,5,64,256]{3,2,1,0:T(8,128)(2,1)S(1)}, bf16[1,5,64,256]{3,2,1,0:T(8,128)(2,1)S(1)}, u32[]{:S(2)}, u32[]{:S(2)}) collective-permute-start(bf16[1,5,64,256]{3,2,1,0:T(8,128)(2,1)S(1)} %get-tuple-element.62), channel_id=1, source_target_pairs={{0,4},{1,5},{2,6},{3,7},{4,0},{5,1},{6,2},{7,3},{8,12},{9,13},{10,... | collective-permute-start | bytes 491528 | tf_op jit(solution)/shard_map/ppermute | solution.py:186
  80.7 3.5 %collective-permute-start.22 = (bf16[5,64,256]{2,1,0:T(8,128)(2,1)S(1)}, bf16[5,64,256]{2,1,0:T(8,128)(2,1)S(1)}, u32[]{:S(2)}, u32[]{:S(2)}) collective-permute-start(bf16[5,64,256]{2,1,0:T(8,128)(2,1)S(1)} %add.36), channel_id=1, source_target_pairs={{0,24},{1,25},{2,26},{3,27},{4,28},{5,29},{6,30},{7,31},{8,16},{9,... | collective-permute-start | bytes 491528 | tf_op jit(solution)/shard_map/ppermute | solution.py:186
  84.4 0.6 collective-permute-start.15
  85.2 1.8 %collective-permute-start.18 = (bf16[5,64,256]{2,1,0:T(8,128)(2,1)S(1)}, bf16[5,64,256]{2,1,0:T(8,128)(2,1)S(1)}, u32[]{:S(2)}, u32[]{:S(2)}) collective-permute-start(bf16[5,64,256]{2,1,0:T(8,128)(2,1)S(1)} %add.34), channel_id=1, source_target_pairs={{0,8},{1,9},{2,10},{3,11},{4,12},{5,13},{6,14},{7,15},{8,0},{9,1},... | collective-permute-start | bytes 491528 | tf_op jit(solution)/shard_map/ppermute | solution.py:186
  87.0 1.7 %collective-permute-done.22.refs_1_ = bf16[5,64,256]{2,1,0:T(8,128)(2,1)S(1)} collective-permute-done((bf16[5,64,256]{2,1,0:T(8,128)(2,1)S(1)}, bf16[5,64,256]{2,1,0:T(8,128)(2,1)S(1)}, u32[]{:S(2)}, u32[]{:S(2)}) %collective-permute-start.22) | collective-permute-done | bytes 163872 | tf_op jit(solution)/shard_map/ppermute | solution.py:186
  88.7 6.1 %collective-permute-done.20.refs_0_ = bf16[5,64,256]{2,1,0:T(8,128)(2,1)S(1)} collective-permute-done((bf16[5,64,256]{2,1,0:T(8,128)(2,1)S(1)}, bf16[5,64,256]{2,1,0:T(8,128)(2,1)S(1)}, u32[]{:S(2)}, u32[]{:S(2)}) %collective-permute-start.20) | collective-permute-done | bytes 163872 | tf_op jit(solution)/shard_map/ppermute | solution.py:186
  94.8 1.4 %update.1 = f32[1,5,64,256]{3,2,1,0:T(8,128)} custom-call(s32[7]{0:T(128)S(1)} %pad_add_fusion.place_ref, f32[1,5,64,256]{3,2,1,0:T(8,128)S(1)} %copy-done.4, f32[5,64,256]{2,1,0:T(8,128)S(1)} %add.32.rest_0_, bf16[5,64,256]{2,1,0:T(8,128)(2,1)S(1)} %collective-permute-done.18.rest_1_, f32[5,64,256]{2,1,0:T(8,128)S(1)} %add.37.rest_2_), custom_call_target="tpu_custom_call" | custom-call | tf_op jit(solution)/shard_map/update/pallas_call | solution.py:346
  (35 shorter events, 1.1 us)
Async XLA Ops:
  0.0 1.2 %copy-start = (bf16[2048,256]{1,0:T(8,128)(2,1)S(1)}, bf16[2048,256]{1,0:T(8,128)(2,1)}, u32[]{:S(2)}) copy-start(bf16[2048,256]{1,0:T(8,128)(2,1)} %param.3) | copy-start | bytes 3145732
  1.3 17.1 %collective-permute-start.3 = (bf16[1024,256]{1,0:T(8,128)(2,1)S(1)}, bf16[1024,256]{1,0:T(8,128)(2,1)S(1)}, u32[]{:S(2)}, u32[]{:S(2)}) collective-permute-start(bf16[1024,256]{1,0:T(8,128)(2,1)S(1)} %constant_dynamic-slice_fusion.1), channel_id=1, source_target_pairs={{0,4},{1,5},{2,6},{3,7},{4,0},{5,1},{6,2},{7,3},{8,12},{9,13},{10,... | collective-permute-start | bytes 1572872 | tf_op jit(solution)/shard_map/ppermute | solution.py:186
  5.0 1.0 %copy-start.3 = (f32[1,5,64,256]{3,2,1,0:T(8,128)S(1)}, f32[1,5,64,256]{3,2,1,0:T(8,128)}, u32[]{:S(2)}) copy-start(f32[1,5,64,256]{3,2,1,0:T(8,128)} %omega_ref.3) | copy-start | bytes 983044
  6.6 5.7 %collective-permute-start = (bf16[3,64,256]{2,1,0:T(8,128)(2,1)S(1)}, bf16[3,64,256]{2,1,0:T(8,128)(2,1)S(1)}, u32[]{:S(2)}, u32[]{:S(2)}) collective-permute-start(bf16[3,64,256]{2,1,0:T(8,128)(2,1)S(1)} %prepare.1), channel_id=1, source_target_pairs={{0,8},{1,9},{2,10},{3,11},{4,12},{5,13},{6,14},{7,15},{8,0},{9,1},... | collective-permute-start | bytes 294920 | tf_op jit(solution)/shard_map/ppermute | solution.py:186
  8.2 10.1 %collective-permute-start.1 = (bf16[3,64,256]{2,1,0:T(8,128)(2,1)S(1)}, bf16[3,64,256]{2,1,0:T(8,128)(2,1)S(1)}, u32[]{:S(2)}, u32[]{:S(2)}) collective-permute-start(bf16[3,64,256]{2,1,0:T(8,128)(2,1)S(1)} %prepare.1), channel_id=1, source_target_pairs={{0,16},{1,17},{2,18},{3,19},{4,20},{5,21},{6,22},{7,23},{8,24},{9,... | collective-permute-start | bytes 294920 | tf_op jit(solution)/shard_map/ppermute | solution.py:186
  10.8 7.6 %collective-permute-start.2 = (bf16[3,64,256]{2,1,0:T(8,128)(2,1)S(1)}, bf16[3,64,256]{2,1,0:T(8,128)(2,1)S(1)}, u32[]{:S(2)}, u32[]{:S(2)}) collective-permute-start(bf16[3,64,256]{2,1,0:T(8,128)(2,1)S(1)} %prepare.1), channel_id=1, source_target_pairs={{0,24},{1,25},{2,26},{3,27},{4,28},{5,29},{6,30},{7,31},{8,16},{9,... | collective-permute-start | bytes 294920 | tf_op jit(solution)/shard_map/ppermute | solution.py:186
  19.5 28.9 %all-to-all-start = ((bf16[4,2,256,256]{3,2,1,0:T(8,128)(2,1)}), bf16[4,2,256,256]{3,2,1,0:T(8,128)(2,1)S(1)}, u32[]{:S(2)}, u32[]{:S(2)}) async-start(bf16[4,2,256,256]{3,2,1,0:T(8,128)(2,1)} %deal.1), calls=%async_computation | async-start | bytes 2097152 | tf_op jit(solution)/shard_map/all_to_all | solution.py:228
  23.4 13.0 %collective-permute-start.6 = (bf16[4,3,64,256]{3,2,1,0:T(8,128)(2,1)S(1)}, bf16[4,3,64,256]{3,2,1,0:T(8,128)(2,1)S(1)}, u32[]{:S(2)}, u32[]{:S(2)}) collective-permute-start(bf16[4,3,64,256]{3,2,1,0:T(8,128)(2,1)S(1)} %pad_maximum_fusion.rest_0_), channel_id=1, source_target_pairs={{0,6},{1,7},{2,4},{3,5},{4,2},{5,3},{6,0},{7,1},{8,14},{9,15},{10,... | collective-permute-start | bytes 1179656 | tf_op jit(solution)/shard_map/ppermute | solution.py:186
  24.9 17.1 %collective-permute-start.4 = (bf16[4,3,64,256]{3,2,1,0:T(8,128)(2,1)S(1)}, bf16[4,3,64,256]{3,2,1,0:T(8,128)(2,1)S(1)}, u32[]{:S(2)}, u32[]{:S(2)}) collective-permute-start(bf16[4,3,64,256]{3,2,1,0:T(8,128)(2,1)S(1)} %pad_maximum_fusion.rest_0_), channel_id=1, source_target_pairs={{0,2},{1,3},{2,0},{3,1},{4,6},{5,7},{6,4},{7,5},{8,10},{9,11},{10,... | collective-permute-start | bytes 1179656 | tf_op jit(solution)/shard_map/ppermute | solution.py:186
  25.4 16.7 %collective-permute-start.5 = (bf16[4,3,64,256]{3,2,1,0:T(8,128)(2,1)S(1)}, bf16[4,3,64,256]{3,2,1,0:T(8,128)(2,1)S(1)}, u32[]{:S(2)}, u32[]{:S(2)}) collective-permute-start(bf16[4,3,64,256]{3,2,1,0:T(8,128)(2,1)S(1)} %pad_maximum_fusion.rest_0_), channel_id=1, source_target_pairs={{0,4},{1,5},{2,6},{3,7},{4,0},{5,1},{6,2},{7,3},{8,12},{9,13},{10,... | collective-permute-start | bytes 1179656 | tf_op jit(solution)/shard_map/ppermute | solution.py:186
  26.9 15.6 %collective-permute-start.7 = (bf16[4,3,64,256]{3,2,1,0:T(8,128)(2,1)S(1)}, bf16[4,3,64,256]{3,2,1,0:T(8,128)(2,1)S(1)}, u32[]{:S(2)}, u32[]{:S(2)}) collective-permute-start(bf16[4,3,64,256]{3,2,1,0:T(8,128)(2,1)S(1)} %pad_maximum_fusion.rest_0_), channel_id=1, source_target_pairs={{0,1},{1,0},{2,3},{3,2},{4,5},{5,4},{6,7},{7,6},{8,9},{9,8},{10,11... | collective-permute-start | bytes 1179656 | tf_op jit(solution)/shard_map/ppermute | solution.py:186
  36.3 6.2 %collective-permute-start.10 = (bf16[4,3,64,256]{3,2,1,0:T(8,128)(2,1)S(1)}, bf16[4,3,64,256]{3,2,1,0:T(8,128)(2,1)S(1)}, u32[]{:S(2)}, u32[]{:S(2)}) collective-permute-start(bf16[4,3,64,256]{3,2,1,0:T(8,128)(2,1)S(1)} %collective-permute-done.6.rest_3_), channel_id=1, source_target_pairs={{0,1},{1,0},{2,3},{3,2},{4,5},{5,4},{6,7},{7,6},{8,9},{9,8},{10,11... | collective-permute-start | bytes 1179656 | tf_op jit(solution)/shard_map/ppermute | solution.py:186
  42.0 1.7 %collective-permute-start.8 = (bf16[4,3,64,256]{3,2,1,0:T(8,128)(2,1)S(1)}, bf16[4,3,64,256]{3,2,1,0:T(8,128)(2,1)S(1)}, u32[]{:S(2)}, u32[]{:S(2)}) collective-permute-start(bf16[4,3,64,256]{3,2,1,0:T(8,128)(2,1)S(1)} %collective-permute-done.4.rest_1_), channel_id=1, source_target_pairs={{0,1},{1,0},{2,3},{3,2},{4,5},{5,4},{6,7},{7,6},{8,9},{9,8},{10,11... | collective-permute-start | bytes 1179656 | tf_op jit(solution)/shard_map/ppermute | solution.py:186
  42.1 2.2 %collective-permute-start.9 = (bf16[4,3,64,256]{3,2,1,0:T(8,128)(2,1)S(1)}, bf16[4,3,64,256]{3,2,1,0:T(8,128)(2,1)S(1)}, u32[]{:S(2)}, u32[]{:S(2)}) collective-permute-start(bf16[4,3,64,256]{3,2,1,0:T(8,128)(2,1)S(1)} %collective-permute-done.5.rest_2_), channel_id=1, source_target_pairs={{0,1},{1,0},{2,3},{3,2},{4,5},{5,4},{6,7},{7,6},{8,9},{9,8},{10,11... | collective-permute-start | bytes 1179656 | tf_op jit(solution)/shard_map/ppermute | solution.py:186
  46.7 1.6 %copy-start.1 = (bf16[8,3,256,256]{3,2,1,0:T(8,128)(2,1)}, bf16[8,3,256,256]{3,2,1,0:T(8,128)(2,1)S(1)}, u32[]{:S(2)}) copy-start(bf16[8,3,256,256]{3,2,1,0:T(8,128)(2,1)S(1)} %gather.1.omega_ref) | copy-start | bytes 9437188
  48.4 4.4 %collective-permute-start.11 = (bf16[4,2,256,256]{3,2,1,0:T(8,128)(2,1)S(1)}, bf16[4,2,256,256]{3,2,1,0:T(8,128)(2,1)S(1)}, u32[]{:S(2)}, u32[]{:S(2)}) collective-permute-start(bf16[4,2,256,256]{3,2,1,0:T(8,128)(2,1)S(1)} %all-to-all-done.data_ref), channel_id=1, source_target_pairs={{0,1},{1,0},{2,3},{3,2},{4,5},{5,4},{6,7},{7,6},{8,9},{9,8},{10,11... | collective-permute-start | bytes 3145736 | tf_op jit(solution)/shard_map/ppermute | solution.py:186
  48.5 1.9 %copy-start.2 = (bf16[8,3,256,256]{3,2,1,0:T(8,128)(2,1)S(1)}, bf16[8,3,256,256]{3,2,1,0:T(8,128)(2,1)}, u32[]{:S(2)}) copy-start(bf16[8,3,256,256]{3,2,1,0:T(8,128)(2,1)} %copy-done.1) | copy-start | bytes 9437188
  56.4 10.1 %collective-permute-start.13 = (bf16[2,1,5,64,256]{4,3,2,1,0:T(8,128)(2,1)S(1)}, bf16[2,1,5,64,256]{4,3,2,1,0:T(8,128)(2,1)S(1)}, u32[]{:S(2)}, u32[]{:S(2)}) collective-permute-start(bf16[2,1,5,64,256]{4,3,2,1,0:T(8,128)(2,1)S(1)} %get-tuple-element.50), channel_id=1, source_target_pairs={{0,2},{1,3},{2,0},{3,1},{4,6},{5,7},{6,4},{7,5},{8,10},{9,11},{10,... | collective-permute-start | bytes 983048 | tf_op jit(solution)/shard_map/ppermute | solution.py:186
  58.8 9.8 %collective-permute-start.12 = (bf16[2,1,5,64,256]{4,3,2,1,0:T(8,128)(2,1)S(1)}, bf16[2,1,5,64,256]{4,3,2,1,0:T(8,128)(2,1)S(1)}, u32[]{:S(2)}, u32[]{:S(2)}) collective-permute-start(bf16[2,1,5,64,256]{4,3,2,1,0:T(8,128)(2,1)S(1)} %products.7), channel_id=1, source_target_pairs={{0,4},{1,5},{2,6},{3,7},{4,0},{5,1},{6,2},{7,3},{8,12},{9,13},{10,... | collective-permute-start | bytes 983048 | tf_op jit(solution)/shard_map/ppermute | solution.py:186
  68.7 10.7 %collective-permute-start.16 = (bf16[2,1,5,64,256]{4,3,2,1,0:T(8,128)(2,1)S(1)}, bf16[2,1,5,64,256]{4,3,2,1,0:T(8,128)(2,1)S(1)}, u32[]{:S(2)}, u32[]{:S(2)}) collective-permute-start(bf16[2,1,5,64,256]{4,3,2,1,0:T(8,128)(2,1)S(1)} %get-tuple-element.60), channel_id=1, source_target_pairs={{0,2},{1,3},{2,0},{3,1},{4,6},{5,7},{6,4},{7,5},{8,10},{9,11},{10,... | collective-permute-start | bytes 983048 | tf_op jit(solution)/shard_map/ppermute | solution.py:186
  69.5 7.1 %collective-permute-start.21 = (bf16[1,5,64,256]{3,2,1,0:T(8,128)(2,1)S(1)}, bf16[1,5,64,256]{3,2,1,0:T(8,128)(2,1)S(1)}, u32[]{:S(2)}, u32[]{:S(2)}) collective-permute-start(bf16[1,5,64,256]{3,2,1,0:T(8,128)(2,1)S(1)} %get-tuple-element.66), channel_id=1, source_target_pairs={{0,4},{1,5},{2,6},{3,7},{4,0},{5,1},{6,2},{7,3},{8,12},{9,13},{10,... | collective-permute-start | bytes 491528 | tf_op jit(solution)/shard_map/ppermute | solution.py:186
  70.4 13.9 %collective-permute-start.14 = (bf16[2,1,5,64,256]{4,3,2,1,0:T(8,128)(2,1)S(1)}, bf16[2,1,5,64,256]{4,3,2,1,0:T(8,128)(2,1)S(1)}, u32[]{:S(2)}, u32[]{:S(2)}) collective-permute-start(bf16[2,1,5,64,256]{4,3,2,1,0:T(8,128)(2,1)S(1)} %products.9), channel_id=1, source_target_pairs={{0,4},{1,5},{2,6},{3,7},{4,0},{5,1},{6,2},{7,3},{8,12},{9,13},{10,... | collective-permute-start | bytes 983048 | tf_op jit(solution)/shard_map/ppermute | solution.py:186
  71.6 12.6 %collective-permute-start.19 = (bf16[1,5,64,256]{3,2,1,0:T(8,128)(2,1)S(1)}, bf16[1,5,64,256]{3,2,1,0:T(8,128)(2,1)S(1)}, u32[]{:S(2)}, u32[]{:S(2)}) collective-permute-start(bf16[1,5,64,256]{3,2,1,0:T(8,128)(2,1)S(1)} %get-tuple-element.64), channel_id=1, source_target_pairs={{0,2},{1,3},{2,0},{3,1},{4,6},{5,7},{6,4},{7,5},{8,10},{9,11},{10,... | collective-permute-start | bytes 491528 | tf_op jit(solution)/shard_map/ppermute | solution.py:186
  79.5 5.7 %collective-permute-start.17 = (bf16[1,5,64,256]{3,2,1,0:T(8,128)(2,1)S(1)}, bf16[1,5,64,256]{3,2,1,0:T(8,128)(2,1)S(1)}, u32[]{:S(2)}, u32[]{:S(2)}) collective-permute-start(bf16[1,5,64,256]{3,2,1,0:T(8,128)(2,1)S(1)} %get-tuple-element.62), channel_id=1, source_target_pairs={{0,4},{1,5},{2,6},{3,7},{4,0},{5,1},{6,2},{7,3},{8,12},{9,13},{10,... | collective-permute-start | bytes 491528 | tf_op jit(solution)/shard_map/ppermute | solution.py:186
  80.7 8.0 %collective-permute-start.22 = (bf16[5,64,256]{2,1,0:T(8,128)(2,1)S(1)}, bf16[5,64,256]{2,1,0:T(8,128)(2,1)S(1)}, u32[]{:S(2)}, u32[]{:S(2)}) collective-permute-start(bf16[5,64,256]{2,1,0:T(8,128)(2,1)S(1)} %add.36), channel_id=1, source_target_pairs={{0,24},{1,25},{2,26},{3,27},{4,28},{5,29},{6,30},{7,31},{8,16},{9,... | collective-permute-start | bytes 491528 | tf_op jit(solution)/shard_map/ppermute | solution.py:186
  84.2 10.5 %collective-permute-start.20 = (bf16[5,64,256]{2,1,0:T(8,128)(2,1)S(1)}, bf16[5,64,256]{2,1,0:T(8,128)(2,1)S(1)}, u32[]{:S(2)}, u32[]{:S(2)}) collective-permute-start(bf16[5,64,256]{2,1,0:T(8,128)(2,1)S(1)} %add.35), channel_id=1, source_target_pairs={{0,16},{1,17},{2,18},{3,19},{4,20},{5,21},{6,22},{7,23},{8,24},{9,... | collective-permute-start | bytes 491528 | tf_op jit(solution)/shard_map/ppermute | solution.py:186
  84.4 10.4 %collective-permute-start.15 = (bf16[1,5,64,256]{3,2,1,0:T(8,128)(2,1)S(1)}, bf16[1,5,64,256]{3,2,1,0:T(8,128)(2,1)S(1)}, u32[]{:S(2)}, u32[]{:S(2)}) collective-permute-start(bf16[1,5,64,256]{3,2,1,0:T(8,128)(2,1)S(1)} %get-tuple-element.58), channel_id=1, source_target_pairs={{0,2},{1,3},{2,0},{3,1},{4,6},{5,7},{6,4},{7,5},{8,10},{9,11},{10,... | collective-permute-start | bytes 491528 | tf_op jit(solution)/shard_map/ppermute | solution.py:186
  85.2 9.7 %copy-start.4 = (f32[1,5,64,256]{3,2,1,0:T(8,128)S(1)}, f32[1,5,64,256]{3,2,1,0:T(8,128)}, u32[]{:S(2)}) copy-start(f32[1,5,64,256]{3,2,1,0:T(8,128)} %omega_ref.3) | copy-start | bytes 983044
  85.2 9.6 %collective-permute-start.18 = (bf16[5,64,256]{2,1,0:T(8,128)(2,1)S(1)}, bf16[5,64,256]{2,1,0:T(8,128)(2,1)S(1)}, u32[]{:S(2)}, u32[]{:S(2)}) collective-permute-start(bf16[5,64,256]{2,1,0:T(8,128)(2,1)S(1)} %add.34), channel_id=1, source_target_pairs={{0,8},{1,9},{2,10},{3,11},{4,12},{5,13},{6,14},{7,15},{8,0},{9,1},... | collective-permute-start | bytes 491528 | tf_op jit(solution)/shard_map/ppermute | solution.py:186

commit v13 on v12

--- a/solution.py
+++ b/solution.py
@@ -56,7 +56,7 @@
 
 
 def gather_kernel(teams, chips, tile_rows, place_ref, *rest):
-    weight_refs, omega_ref, sems = rest[:-2], rest[-2], rest[-1]
+    weight_refs, omega_refs, sems = rest[:-4], rest[-4:-1], rest[-1]
     planes = LOW * chips
     depth = teams // LOW
     team, replica = place_ref[0], place_ref[1]
@@ -70,14 +70,15 @@
                 row = (2 * (chip ^ my) + (core ^ half)) * tile_rows
                 for mz in range(depth):
                     i = (high ^ mz) * LOW + (low ^ mx)
-                    target = omega_ref.at[i, :, pl.ds(pl.multiple_of(row, tile_rows), tile_rows)]
-                    copies.append(
-                        pltpu.make_async_copy(
-                            weight_refs[half * planes + plane].at[mz],
-                            target,
-                            sems.at[(half * planes + plane) * depth + mz],
+                    rows = pl.ds(pl.multiple_of(row, tile_rows), tile_rows)
+                    for k, omega_ref in enumerate(omega_refs):
+                        copies.append(
+                            pltpu.make_async_copy(
+                                weight_refs[half * planes + plane].at[mz, k],
+                                omega_ref.at[i, rows],
+                                sems.at[k, (half * planes + plane) * depth + mz],
+                            )
                         )
-                    )
     for copy in copies:
         copy.start()
     for copy in copies:
@@ -88,19 +89,20 @@
     return data_ref[lax.div(c, LOW), lax.rem(c, LOW) ^ low]
 
 
-def mix_kernel(teams, replicas, tile_rows, place_ref, data_ref, omega_ref, kept_ref, mixed_ref, left_ref, flip_ref):
+def mix_kernel(teams, replicas, tile_rows, place_ref, data_ref, omega_0, omega_1, omega_2, kept_ref, mixed_ref, left_ref, flip_ref):
     chips = replicas // 2
     team, replica = place_ref[0], place_ref[1]
     core, chip = lax.rem(replica, 2), lax.div(replica, 2)
     low = lax.rem(team, LOW)
     offsets, _ = stored_offsets(place_ref, teams)
     times = mixed_ref.shape[1]
+    omega_refs = omega_0, omega_1, omega_2
 
     def mix(i, carry):
         total = None
         for k, offset in enumerate(offsets):
             c = lax.rem(i + offset, teams)
-            right, dims = (omega_ref[i, k], NT) if k < 3 else (omega_ref[c, 5 - k], NN)
+            right, dims = (omega_refs[k][i], NT) if k < 3 else (omega_refs[5 - k][c], NN)
             term = lax.dot_general(block(data_ref, low, c), right, dims, preferred_element_type=F32)
             total = term if total is None else total + term
         mixed = total.astype(BF16)
@@ -189,7 +191,7 @@
     count = teams // LOW
     planes = LOW * chips
     count = teams // LOW
-    small = pltpu.CompilerParams(vmem_limit_bytes=(4 if teams <= 8 else 16) * 2**20)
+    small = pltpu.CompilerParams(vmem_limit_bytes=(6 if teams <= 8 else 16) * 2**20)
     tiny = pltpu.CompilerParams(vmem_limit_bytes=2 * 2**20)
 
     def across_plane(arrays):
@@ -229,11 +231,11 @@
     weights += [swap(array, 0, 1) for array in weights]
     tiles = pl.pallas_call(
         functools.partial(gather_kernel, teams, chips, tile_rows),
-        out_shape=jax.ShapeDtypeStruct((teams, 3, width, width), BF16),
+        out_shape=[jax.ShapeDtypeStruct((teams, width, width), BF16)] * 3,
         in_specs=[SMEM] + [ANY] * (2 * planes),
-        out_specs=VMEM,
-        scratch_shapes=[pltpu.SemaphoreType.DMA((2 * planes * count,))],
-        compiler_params=tiny,
+        out_specs=[VMEM] * 3,
+        scratch_shapes=[pltpu.SemaphoreType.DMA((3, 2 * planes * count))],
+        compiler_params=small,
         name="gather",
     )(place, *weights)
 
@@ -247,12 +249,12 @@
                 jax.ShapeDtypeStruct((teams, times, width), BF16),
                 jax.ShapeDtypeStruct((teams, chips * tile_rows, 2 * times), BF16),
             ],
-            in_specs=[SMEM, VMEM, VMEM],
+            in_specs=[SMEM] + [VMEM] * 4,
             out_specs=[VMEM] * 3,
             scratch_shapes=[pltpu.VMEM((2, width, times), BF16)],
-            compiler_params=tiny,
+            compiler_params=small,
             name="mix",
-        )(place, data, tiles)
+        )(place, data, *tiles)
 
     other = swap(own, 0, 1)
     cores = [*mix(own), *mix(other)]

time: 96.6 us -> 101 us (1.046)
  Pallas kernels: 17.6 us -> 22.1 us
    pallas_call x1, Pallas kernels: 2.44 us -> 6.31 us  [per_device(): pl.pallas_call(functools.partial(gather_kernel, teams, chips, tile_rows),...]
    unnamed x10 -> x12, local copies, waits for them, and re-layouts: 5.72 us -> 5 us
  transfers between devices with their start and end apart: 24 -> 24, of which waited for: 14 -> 13; matrix products, arithmetic and copies ran while one was open for 1% -> 0% of each run, Pallas kernels for 12% -> 16%
where the time goes in v13:
time: 101 us; the launch traced here: 100 us
  waiting for transfers between devices  42.8 us (42%)
  starting transfers between devices  30.1 us (30%)
  Pallas kernels  22.1 us (22%)
  local copies, waits for them, and re-layouts  5.08 us (5%)
    ppermute x23, waiting for transfers between devices, swap(): return lax.ppermute(array, AXES, route)  42.8 us
    ppermute x23, starting transfers between devices, swap(): return lax.ppermute(array, AXES, route)  25.8 us
    pallas_call x6, Pallas kernels, products(): pl.pallas_call(functools.partial(product_kernel, teams, chips, wanted), o...  7.05 us
    pallas_call x1, Pallas kernels, per_device(): pl.pallas_call(functools.partial(gather_kernel, teams, chips, tile_rows),...  6.31 us
    pallas_call x2, Pallas kernels, mix(): pl.pallas_call(functools.partial(mix_kernel, teams, replicas, tile_rows),...  5.29 us
    unnamed x12, local copies, waits for them, and re-layouts  5 us
    all_to_all x1, starting transfers between devices, per_device(): own = lax.all_to_all(dealt, 'line', 0, 0)  4.25 us
  transfers between devices with their start and end apart: 24, of which 13 were waited for; matrix products, arithmetic and copies ran while one was open for 0% of the time, Pallas kernels for 16%

profile of v13, /device:TPU:0, one launch (start us, length us, event | category | flops | bytes accessed | tf_op | source)
XLA Modules:
  0.0 100.4 jit_solution(14982856356361845541)
XLA Ops:
  0.0 1.2 %copy-done = bf16[2048,256]{1,0:T(8,128)(2,1)S(1)} copy-done((bf16[2048,256]{1,0:T(8,128)(2,1)S(1)}, bf16[2048,256]{1,0:T(8,128)(2,1)}, u32[]{:S(2)}) %copy-start) | copy-done | bytes 1048600
  1.3 3.0 %collective-permute-start.3 = (bf16[1024,256]{1,0:T(8,128)(2,1)S(1)}, bf16[1024,256]{1,0:T(8,128)(2,1)S(1)}, u32[]{:S(2)}, u32[]{:S(2)}) collective-permute-start(bf16[1024,256]{1,0:T(8,128)(2,1)S(1)} %constant_dynamic-slice_fusion.1), channel_id=1, source_target_pairs={{0,4},{1,5},{2,6},{3,7},{4,0},{5,1},{6,2},{7,3},{8,12},{9,13},{10,... | collective-permute-start | bytes 1572872 | tf_op jit(solution)/shard_map/ppermute | solution.py:188
  4.3 0.7 copy-done.5
  5.0 0.6 prepare.1
  5.6 1.6 %collective-permute-start = (bf16[3,64,256]{2,1,0:T(8,128)(2,1)S(1)}, bf16[3,64,256]{2,1,0:T(8,128)(2,1)S(1)}, u32[]{:S(2)}, u32[]{:S(2)}) collective-permute-start(bf16[3,64,256]{2,1,0:T(8,128)(2,1)S(1)} %prepare.1), channel_id=1, source_target_pairs={{0,8},{1,9},{2,10},{3,11},{4,12},{5,13},{6,14},{7,15},{8,0},{9,1},... | collective-permute-start | bytes 294920 | tf_op jit(solution)/shard_map/ppermute | solution.py:188
  7.2 2.6 %collective-permute-start.1 = (bf16[3,64,256]{2,1,0:T(8,128)(2,1)S(1)}, bf16[3,64,256]{2,1,0:T(8,128)(2,1)S(1)}, u32[]{:S(2)}, u32[]{:S(2)}) collective-permute-start(bf16[3,64,256]{2,1,0:T(8,128)(2,1)S(1)} %prepare.1), channel_id=1, source_target_pairs={{0,16},{1,17},{2,18},{3,19},{4,20},{5,21},{6,22},{7,23},{8,24},{9,... | collective-permute-start | bytes 294920 | tf_op jit(solution)/shard_map/ppermute | solution.py:188
  10.0 1.2 %collective-permute-done = bf16[3,64,256]{2,1,0:T(8,128)(2,1)S(1)} collective-permute-done((bf16[3,64,256]{2,1,0:T(8,128)(2,1)S(1)}, bf16[3,64,256]{2,1,0:T(8,128)(2,1)S(1)}, u32[]{:S(2)}, u32[]{:S(2)}) %collective-permute-start) | collective-permute-done | bytes 98336 | tf_op jit(solution)/shard_map/ppermute | solution.py:188
  11.3 6.1 %collective-permute-done.1 = bf16[3,64,256]{2,1,0:T(8,128)(2,1)S(1)} collective-permute-done((bf16[3,64,256]{2,1,0:T(8,128)(2,1)S(1)}, bf16[3,64,256]{2,1,0:T(8,128)(2,1)S(1)}, u32[]{:S(2)}, u32[]{:S(2)}) %collective-permute-start.1) | collective-permute-done | bytes 98336 | tf_op jit(solution)/shard_map/ppermute | solution.py:188
  17.5 1.0 deal.1
  18.5 4.3 %all-to-all-start = ((bf16[4,2,256,256]{3,2,1,0:T(8,128)(2,1)}), bf16[4,2,256,256]{3,2,1,0:T(8,128)(2,1)}, u32[]{:S(2)}, u32[]{:S(2)}) async-start(bf16[4,2,256,256]{3,2,1,0:T(8,128)(2,1)} %deal.1), calls=%async_computation | async-start | bytes 2097152 | tf_op jit(solution)/shard_map/all_to_all | solution.py:230
  22.7 2.1 %collective-permute-start.6 = (bf16[4,3,64,256]{3,2,1,0:T(8,128)(2,1)S(1)}, bf16[4,3,64,256]{3,2,1,0:T(8,128)(2,1)S(1)}, u32[]{:S(2)}, u32[]{:S(2)}) collective-permute-start(bf16[4,3,64,256]{3,2,1,0:T(8,128)(2,1)S(1)} %pad_maximum_fusion.rest_0_), channel_id=1, source_target_pairs={{0,6},{1,7},{2,4},{3,5},{4,2},{5,3},{6,0},{7,1},{8,14},{9,15},{10,... | collective-permute-start | bytes 1179656 | tf_op jit(solution)/shard_map/ppermute | solution.py:188
  24.8 0.5 collective-permute-start.4
  25.3 1.0 collective-permute-start.5
  26.3 9.5 %collective-permute-done.6.rest_3_ = bf16[4,3,64,256]{3,2,1,0:T(8,128)(2,1)S(1)} collective-permute-done((bf16[4,3,64,256]{3,2,1,0:T(8,128)(2,1)S(1)}, bf16[4,3,64,256]{3,2,1,0:T(8,128)(2,1)S(1)}, u32[]{:S(2)}, u32[]{:S(2)}) %collective-permute-start.6) | collective-permute-done | bytes 393248 | tf_op jit(solution)/shard_map/ppermute | solution.py:188
  35.8 5.6 %collective-permute-done.4.rest_1_ = bf16[4,3,64,256]{3,2,1,0:T(8,128)(2,1)S(1)} collective-permute-done((bf16[4,3,64,256]{3,2,1,0:T(8,128)(2,1)S(1)}, bf16[4,3,64,256]{3,2,1,0:T(8,128)(2,1)S(1)}, u32[]{:S(2)}, u32[]{:S(2)}) %collective-permute-start.4) | collective-permute-done | bytes 393248 | tf_op jit(solution)/shard_map/ppermute | solution.py:188
  41.5 0.4 collective-permute-start.9
  41.9 1.2 %collective-permute-done.8.rest_5_ = bf16[4,3,64,256]{3,2,1,0:T(8,128)(2,1)S(1)} collective-permute-done((bf16[4,3,64,256]{3,2,1,0:T(8,128)(2,1)S(1)}, bf16[4,3,64,256]{3,2,1,0:T(8,128)(2,1)S(1)}, u32[]{:S(2)}, u32[]{:S(2)}) %collective-permute-start.8) | collective-permute-done | bytes 393248 | tf_op jit(solution)/shard_map/ppermute | solution.py:188
  43.1 0.6 collective-permute-done.9.rest_6_
  43.7 6.3 %gather.1 = (bf16[8,256,256]{2,1,0:T(8,128)(2,1)S(1)}, bf16[8,256,256]{2,1,0:T(8,128)(2,1)S(1)}, bf16[8,256,256]{2,1,0:T(8,128)(2,1)S(1)}) custom-call(s32[7]{0:T(128)S(1)} %pad_add_fusion.place_ref, bf16[4,3,64,256]{3,2,1,0:T(8,128)(2,1)S(1)} %pad_maximum_fusion.rest_0_, bf16[4,3,64,256]{3,2,1,0:T(8,128)(2,1)S(1)} %collective-permute-done.4.rest_1_, ...), custom_call_target="tpu_custom_call" | custom-call | tf_op jit(solution)/shard_map/gather/pallas_call | solution.py:232
  50.0 1.0 copy-done.1
  51.1 1.2 %copy-done.2 = bf16[8,256,256]{2,1,0:T(8,128)(2,1)S(1)} copy-done((bf16[8,256,256]{2,1,0:T(8,128)(2,1)S(1)}, bf16[8,256,256]{2,1,0:T(8,128)(2,1)}, u32[]{:S(2)}) %copy-start.2) | copy-done | bytes 1048600
  52.3 3.0 %mix.2 = (bf16[8,256,256]{2,1,0:T(8,128)(2,1)S(1)}, bf16[8,256,256]{2,1,0:T(8,128)(2,1)S(1)}, bf16[8,128,512]{2,1,0:T(8,128)(2,1)S(1)}) custom-call(s32[7]{0:T(128)S(1)} %pad_add_fusion.place_ref, bf16[4,2,256,256]{3,2,1,0:T(8,128)(2,1)} %all-to-all-done.data_ref, bf16[8,256,256]{2,1,0:T(8,128)(2,1)S(1)} %get-tuple-element.48.omega_0, ...), custom_call_target="tpu_custom_call" | custom-call | tf_op jit(solution)/shard_map/mix/pallas_call | solution.py:245
  55.3 2.3 %mix.3 = (bf16[8,256,256]{2,1,0:T(8,128)(2,1)S(1)}, bf16[8,256,256]{2,1,0:T(8,128)(2,1)S(1)}, bf16[8,128,512]{2,1,0:T(8,128)(2,1)S(1)}) custom-call(s32[7]{0:T(128)S(1)} %pad_add_fusion.place_ref, bf16[4,2,256,256]{3,2,1,0:T(8,128)(2,1)S(1)} %collective-permute-done.11.data_ref, bf16[8,256,256]{2,1,0:T(8,128)(2,1)S(1)} %get-tuple-element.48.omega_0, ...), custom_call_target="tpu_custom_call" | custom-call | tf_op jit(solution)/shard_map/mix/pallas_call | solution.py:245
  57.7 1.4 %products.8 = (f32[2,1,5,64,256]{4,3,2,1,0:T(8,128)S(1)}, bf16[2,1,5,64,256]{4,3,2,1,0:T(8,128)(2,1)S(1)}) custom-call(s32[7]{0:T(128)S(1)} %pad_add_fusion.place_ref, bf16[8,256,256]{2,1,0:T(8,128)(2,1)S(1)} %get-tuple-element.51.rest_0_, bf16[8,256,256]{2,1,0:T(8,128)(2,1)S(1)} %get-tuple-element.52.rest_1_, ...), custom_call_target="tpu_custom_call" | custom-call | tf_op jit(solution)/shard_map/products/pallas_call | solution.py:268
  59.1 1.6 %collective-permute-start.13 = (bf16[2,1,5,64,256]{4,3,2,1,0:T(8,128)(2,1)S(1)}, bf16[2,1,5,64,256]{4,3,2,1,0:T(8,128)(2,1)S(1)}, u32[]{:S(2)}, u32[]{:S(2)}) collective-permute-start(bf16[2,1,5,64,256]{4,3,2,1,0:T(8,128)(2,1)S(1)} %get-tuple-element.60), channel_id=1, source_target_pairs={{0,2},{1,3},{2,0},{3,1},{4,6},{5,7},{6,4},{7,5},{8,10},{9,11},{10,... | collective-permute-start | bytes 983048 | tf_op jit(solution)/shard_map/ppermute | solution.py:188
  60.7 1.1 %products.7 = bf16[2,1,5,64,256]{4,3,2,1,0:T(8,128)(2,1)S(1)} custom-call(s32[7]{0:T(128)S(1)} %pad_add_fusion.place_ref, bf16[8,256,256]{2,1,0:T(8,128)(2,1)S(1)} %get-tuple-element.51.rest_0_, bf16[8,256,256]{2,1,0:T(8,128)(2,1)S(1)} %get-tuple-element.52.rest_1_, bf16[8,128,512]{2,1,0:T(8,128)(2,1)S(1)} %get-tuple-element.53.rest_2_, ...), custom_call_target="tpu_custom_call" | custom-call | tf_op jit(solution)/shard_map/products/pallas_call | solution.py:268
  61.7 0.9 collective-permute-start.12
  62.6 1.4 %products.11 = (f32[2,1,5,64,256]{4,3,2,1,0:T(8,128)S(1)}, bf16[2,1,5,64,256]{4,3,2,1,0:T(8,128)(2,1)S(1)}) custom-call(s32[7]{0:T(128)S(1)} %pad_add_fusion.place_ref, bf16[8,256,256]{2,1,0:T(8,128)(2,1)S(1)} %get-tuple-element.51.rest_0_, bf16[8,256,256]{2,1,0:T(8,128)(2,1)S(1)} %get-tuple-element.52.rest_1_, ...), custom_call_target="tpu_custom_call" | custom-call | tf_op jit(solution)/shard_map/products/pallas_call | solution.py:268
  64.0 1.1 %products.10.refs_0_ = f32[2,1,5,64,256]{4,3,2,1,0:T(8,128)S(1)} custom-call(s32[7]{0:T(128)S(1)} %pad_add_fusion.place_ref, bf16[8,256,256]{2,1,0:T(8,128)(2,1)S(1)} %get-tuple-element.51.rest_0_, bf16[8,256,256]{2,1,0:T(8,128)(2,1)S(1)} %get-tuple-element.52.rest_1_, bf16[8,128,512]{2,1,0:T(8,128)(2,1)S(1)} %get-tuple-element.53.rest_2_, ...), custom_call_target="tpu_custom_call" | custom-call | tf_op jit(solution)/shard_map/products/pallas_call | solution.py:268
  65.1 1.1 %products.9 = bf16[2,1,5,64,256]{4,3,2,1,0:T(8,128)(2,1)S(1)} custom-call(s32[7]{0:T(128)S(1)} %pad_add_fusion.place_ref, bf16[8,256,256]{2,1,0:T(8,128)(2,1)S(1)} %get-tuple-element.51.rest_0_, bf16[8,256,256]{2,1,0:T(8,128)(2,1)S(1)} %get-tuple-element.52.rest_1_, bf16[8,128,512]{2,1,0:T(8,128)(2,1)S(1)} %get-tuple-element.53.rest_2_, ...), custom_call_target="tpu_custom_call" | custom-call | tf_op jit(solution)/shard_map/products/pallas_call | solution.py:268
  66.2 1.1 %products.6.refs_0_ = f32[2,1,5,64,256]{4,3,2,1,0:T(8,128)S(1)} custom-call(s32[7]{0:T(128)S(1)} %pad_add_fusion.place_ref, bf16[8,256,256]{2,1,0:T(8,128)(2,1)S(1)} %get-tuple-element.51.rest_0_, bf16[8,256,256]{2,1,0:T(8,128)(2,1)S(1)} %get-tuple-element.52.rest_1_, bf16[8,128,512]{2,1,0:T(8,128)(2,1)S(1)} %get-tuple-element.53.rest_2_, ...), custom_call_target="tpu_custom_call" | custom-call | tf_op jit(solution)/shard_map/products/pallas_call | solution.py:268
  67.2 1.9 %collective-permute-done.13.refs_1_ = bf16[2,1,5,64,256]{4,3,2,1,0:T(8,128)(2,1)S(1)} collective-permute-done((bf16[2,1,5,64,256]{4,3,2,1,0:T(8,128)(2,1)S(1)}, bf16[2,1,5,64,256]{4,3,2,1,0:T(8,128)(2,1)S(1)}, u32[]{:S(2)}, u32[]{:S(2)}) %collective-permute-start.13) | collective-permute-done | bytes 327712 | tf_op jit(solution)/shard_map/ppermute | solution.py:188
  69.2 2.4 %collective-permute-done.12.refs_1_ = bf16[2,1,5,64,256]{4,3,2,1,0:T(8,128)(2,1)S(1)} collective-permute-done((bf16[2,1,5,64,256]{4,3,2,1,0:T(8,128)(2,1)S(1)}, bf16[2,1,5,64,256]{4,3,2,1,0:T(8,128)(2,1)S(1)}, u32[]{:S(2)}, u32[]{:S(2)}) %collective-permute-start.12) | collective-permute-done | bytes 327712 | tf_op jit(solution)/shard_map/ppermute | solution.py:188
  71.6 0.5 collective-permute-start.16
  72.2 1.5 %collective-permute-start.21 = (bf16[1,5,64,256]{3,2,1,0:T(8,128)(2,1)S(1)}, bf16[1,5,64,256]{3,2,1,0:T(8,128)(2,1)S(1)}, u32[]{:S(2)}, u32[]{:S(2)}) collective-permute-start(bf16[1,5,64,256]{3,2,1,0:T(8,128)(2,1)S(1)} %get-tuple-element.76), channel_id=1, source_target_pairs={{0,4},{1,5},{2,6},{3,7},{4,0},{5,1},{6,2},{7,3},{8,12},{9,13},{10,... | collective-permute-start | bytes 491528 | tf_op jit(solution)/shard_map/ppermute | solution.py:188
  73.7 0.5 collective-permute-start.14
  74.2 1.6 %collective-permute-start.19 = (bf16[1,5,64,256]{3,2,1,0:T(8,128)(2,1)S(1)}, bf16[1,5,64,256]{3,2,1,0:T(8,128)(2,1)S(1)}, u32[]{:S(2)}, u32[]{:S(2)}) collective-permute-start(bf16[1,5,64,256]{3,2,1,0:T(8,128)(2,1)S(1)} %get-tuple-element.74), channel_id=1, source_target_pairs={{0,2},{1,3},{2,0},{3,1},{4,6},{5,7},{6,4},{7,5},{8,10},{9,11},{10,... | collective-permute-start | bytes 491528 | tf_op jit(solution)/shard_map/ppermute | solution.py:188
  75.8 3.5 %collective-permute-done.21.refs_1_ = bf16[1,5,64,256]{3,2,1,0:T(8,128)(2,1)S(1)} collective-permute-done((bf16[1,5,64,256]{3,2,1,0:T(8,128)(2,1)S(1)}, bf16[1,5,64,256]{3,2,1,0:T(8,128)(2,1)S(1)}, u32[]{:S(2)}, u32[]{:S(2)}) %collective-permute-start.21) | collective-permute-done | bytes 163872 | tf_op jit(solution)/shard_map/ppermute | solution.py:188
  79.3 3.0 %collective-permute-done.16.refs_1_ = bf16[2,1,5,64,256]{4,3,2,1,0:T(8,128)(2,1)S(1)} collective-permute-done((bf16[2,1,5,64,256]{4,3,2,1,0:T(8,128)(2,1)S(1)}, bf16[2,1,5,64,256]{4,3,2,1,0:T(8,128)(2,1)S(1)}, u32[]{:S(2)}, u32[]{:S(2)}) %collective-permute-start.16) | collective-permute-done | bytes 327712 | tf_op jit(solution)/shard_map/ppermute | solution.py:188
  82.4 0.8 collective-permute-start.17
  83.2 3.5 %collective-permute-start.22 = (bf16[5,64,256]{2,1,0:T(8,128)(2,1)S(1)}, bf16[5,64,256]{2,1,0:T(8,128)(2,1)S(1)}, u32[]{:S(2)}, u32[]{:S(2)}) collective-permute-start(bf16[5,64,256]{2,1,0:T(8,128)(2,1)S(1)} %add.36), channel_id=1, source_target_pairs={{0,24},{1,25},{2,26},{3,27},{4,28},{5,29},{6,30},{7,31},{8,16},{9,... | collective-permute-start | bytes 491528 | tf_op jit(solution)/shard_map/ppermute | solution.py:188
  86.8 0.4 collective-permute-start.20
  87.2 1.0 collective-permute-start.15
  88.2 2.0 %collective-permute-start.18 = (bf16[5,64,256]{2,1,0:T(8,128)(2,1)S(1)}, bf16[5,64,256]{2,1,0:T(8,128)(2,1)S(1)}, u32[]{:S(2)}, u32[]{:S(2)}) collective-permute-start(bf16[5,64,256]{2,1,0:T(8,128)(2,1)S(1)} %add.34), channel_id=1, source_target_pairs={{0,8},{1,9},{2,10},{3,11},{4,12},{5,13},{6,14},{7,15},{8,0},{9,1},... | collective-permute-start | bytes 491528 | tf_op jit(solution)/shard_map/ppermute | solution.py:188
  90.2 1.1 %collective-permute-done.22.refs_1_ = bf16[5,64,256]{2,1,0:T(8,128)(2,1)S(1)} collective-permute-done((bf16[5,64,256]{2,1,0:T(8,128)(2,1)S(1)}, bf16[5,64,256]{2,1,0:T(8,128)(2,1)S(1)}, u32[]{:S(2)}, u32[]{:S(2)}) %collective-permute-start.22) | collective-permute-done | bytes 163872 | tf_op jit(solution)/shard_map/ppermute | solution.py:188
  91.3 6.6 %collective-permute-done.20.refs_0_ = bf16[5,64,256]{2,1,0:T(8,128)(2,1)S(1)} collective-permute-done((bf16[5,64,256]{2,1,0:T(8,128)(2,1)S(1)}, bf16[5,64,256]{2,1,0:T(8,128)(2,1)S(1)}, u32[]{:S(2)}, u32[]{:S(2)}) %collective-permute-start.20) | collective-permute-done | bytes 163872 | tf_op jit(solution)/shard_map/ppermute | solution.py:188
  98.0 0.9 copy-done.4
  98.9 1.4 %update.1 = f32[1,5,64,256]{3,2,1,0:T(8,128)} custom-call(s32[7]{0:T(128)S(1)} %pad_add_fusion.place_ref, f32[1,5,64,256]{3,2,1,0:T(8,128)S(1)} %copy-done.4, f32[5,64,256]{2,1,0:T(8,128)S(1)} %add.32.rest_0_, bf16[5,64,256]{2,1,0:T(8,128)(2,1)S(1)} %collective-permute-done.18.rest_1_, f32[5,64,256]{2,1,0:T(8,128)S(1)} %add.37.rest_2_), custom_call_target="tpu_custom_call" | custom-call | tf_op jit(solution)/shard_map/update/pallas_call | solution.py:348
  (37 shorter events, 1.1 us)
Async XLA Ops:
  0.0 1.2 %copy-start = (bf16[2048,256]{1,0:T(8,128)(2,1)S(1)}, bf16[2048,256]{1,0:T(8,128)(2,1)}, u32[]{:S(2)}) copy-start(bf16[2048,256]{1,0:T(8,128)(2,1)} %param.3) | copy-start | bytes 3145732
  1.2 3.8 %copy-start.3 = (f32[1,5,64,256]{3,2,1,0:T(8,128)S(1)}, f32[1,5,64,256]{3,2,1,0:T(8,128)}, u32[]{:S(2)}) copy-start(f32[1,5,64,256]{3,2,1,0:T(8,128)} %omega_ref.3) | copy-start | bytes 983044
  1.3 16.2 %collective-permute-start.3 = (bf16[1024,256]{1,0:T(8,128)(2,1)S(1)}, bf16[1024,256]{1,0:T(8,128)(2,1)S(1)}, u32[]{:S(2)}, u32[]{:S(2)}) collective-permute-start(bf16[1024,256]{1,0:T(8,128)(2,1)S(1)} %constant_dynamic-slice_fusion.1), channel_id=1, source_target_pairs={{0,4},{1,5},{2,6},{3,7},{4,0},{5,1},{6,2},{7,3},{8,12},{9,13},{10,... | collective-permute-start | bytes 1572872 | tf_op jit(solution)/shard_map/ppermute | solution.py:188
  4.3 0.7 copy-start.5
  5.6 5.7 %collective-permute-start = (bf16[3,64,256]{2,1,0:T(8,128)(2,1)S(1)}, bf16[3,64,256]{2,1,0:T(8,128)(2,1)S(1)}, u32[]{:S(2)}, u32[]{:S(2)}) collective-permute-start(bf16[3,64,256]{2,1,0:T(8,128)(2,1)S(1)} %prepare.1), channel_id=1, source_target_pairs={{0,8},{1,9},{2,10},{3,11},{4,12},{5,13},{6,14},{7,15},{8,0},{9,1},... | collective-permute-start | bytes 294920 | tf_op jit(solution)/shard_map/ppermute | solution.py:188
  7.2 10.1 %collective-permute-start.1 = (bf16[3,64,256]{2,1,0:T(8,128)(2,1)S(1)}, bf16[3,64,256]{2,1,0:T(8,128)(2,1)S(1)}, u32[]{:S(2)}, u32[]{:S(2)}) collective-permute-start(bf16[3,64,256]{2,1,0:T(8,128)(2,1)S(1)} %prepare.1), channel_id=1, source_target_pairs={{0,16},{1,17},{2,18},{3,19},{4,20},{5,21},{6,22},{7,23},{8,24},{9,... | collective-permute-start | bytes 294920 | tf_op jit(solution)/shard_map/ppermute | solution.py:188
  9.8 7.6 %collective-permute-start.2 = (bf16[3,64,256]{2,1,0:T(8,128)(2,1)S(1)}, bf16[3,64,256]{2,1,0:T(8,128)(2,1)S(1)}, u32[]{:S(2)}, u32[]{:S(2)}) collective-permute-start(bf16[3,64,256]{2,1,0:T(8,128)(2,1)S(1)} %prepare.1), channel_id=1, source_target_pairs={{0,24},{1,25},{2,26},{3,27},{4,28},{5,29},{6,30},{7,31},{8,16},{9,... | collective-permute-start | bytes 294920 | tf_op jit(solution)/shard_map/ppermute | solution.py:188
  18.5 32.5 %all-to-all-start = ((bf16[4,2,256,256]{3,2,1,0:T(8,128)(2,1)}), bf16[4,2,256,256]{3,2,1,0:T(8,128)(2,1)}, u32[]{:S(2)}, u32[]{:S(2)}) async-start(bf16[4,2,256,256]{3,2,1,0:T(8,128)(2,1)} %deal.1), calls=%async_computation | async-start | bytes 2097152 | tf_op jit(solution)/shard_map/all_to_all | solution.py:230
  22.7 13.1 %collective-permute-start.6 = (bf16[4,3,64,256]{3,2,1,0:T(8,128)(2,1)S(1)}, bf16[4,3,64,256]{3,2,1,0:T(8,128)(2,1)S(1)}, u32[]{:S(2)}, u32[]{:S(2)}) collective-permute-start(bf16[4,3,64,256]{3,2,1,0:T(8,128)(2,1)S(1)} %pad_maximum_fusion.rest_0_), channel_id=1, source_target_pairs={{0,6},{1,7},{2,4},{3,5},{4,2},{5,3},{6,0},{7,1},{8,14},{9,15},{10,... | collective-permute-start | bytes 1179656 | tf_op jit(solution)/shard_map/ppermute | solution.py:188
  24.8 16.6 %collective-permute-start.4 = (bf16[4,3,64,256]{3,2,1,0:T(8,128)(2,1)S(1)}, bf16[4,3,64,256]{3,2,1,0:T(8,128)(2,1)S(1)}, u32[]{:S(2)}, u32[]{:S(2)}) collective-permute-start(bf16[4,3,64,256]{3,2,1,0:T(8,128)(2,1)S(1)} %pad_maximum_fusion.rest_0_), channel_id=1, source_target_pairs={{0,2},{1,3},{2,0},{3,1},{4,6},{5,7},{6,4},{7,5},{8,10},{9,11},{10,... | collective-permute-start | bytes 1179656 | tf_op jit(solution)/shard_map/ppermute | solution.py:188
  25.3 16.2 %collective-permute-start.5 = (bf16[4,3,64,256]{3,2,1,0:T(8,128)(2,1)S(1)}, bf16[4,3,64,256]{3,2,1,0:T(8,128)(2,1)S(1)}, u32[]{:S(2)}, u32[]{:S(2)}) collective-permute-start(bf16[4,3,64,256]{3,2,1,0:T(8,128)(2,1)S(1)} %pad_maximum_fusion.rest_0_), channel_id=1, source_target_pairs={{0,4},{1,5},{2,6},{3,7},{4,0},{5,1},{6,2},{7,3},{8,12},{9,13},{10,... | collective-permute-start | bytes 1179656 | tf_op jit(solution)/shard_map/ppermute | solution.py:188
  26.3 15.6 %collective-permute-start.7 = (bf16[4,3,64,256]{3,2,1,0:T(8,128)(2,1)S(1)}, bf16[4,3,64,256]{3,2,1,0:T(8,128)(2,1)S(1)}, u32[]{:S(2)}, u32[]{:S(2)}) collective-permute-start(bf16[4,3,64,256]{3,2,1,0:T(8,128)(2,1)S(1)} %pad_maximum_fusion.rest_0_), channel_id=1, source_target_pairs={{0,1},{1,0},{2,3},{3,2},{4,5},{5,4},{6,7},{7,6},{8,9},{9,8},{10,11... | collective-permute-start | bytes 1179656 | tf_op jit(solution)/shard_map/ppermute | solution.py:188
  35.8 6.1 %collective-permute-start.10 = (bf16[4,3,64,256]{3,2,1,0:T(8,128)(2,1)S(1)}, bf16[4,3,64,256]{3,2,1,0:T(8,128)(2,1)S(1)}, u32[]{:S(2)}, u32[]{:S(2)}) collective-permute-start(bf16[4,3,64,256]{3,2,1,0:T(8,128)(2,1)S(1)} %collective-permute-done.6.rest_3_), channel_id=1, source_target_pairs={{0,1},{1,0},{2,3},{3,2},{4,5},{5,4},{6,7},{7,6},{8,9},{9,8},{10,11... | collective-permute-start | bytes 1179656 | tf_op jit(solution)/shard_map/ppermute | solution.py:188
  41.4 1.7 %collective-permute-start.8 = (bf16[4,3,64,256]{3,2,1,0:T(8,128)(2,1)S(1)}, bf16[4,3,64,256]{3,2,1,0:T(8,128)(2,1)S(1)}, u32[]{:S(2)}, u32[]{:S(2)}) collective-permute-start(bf16[4,3,64,256]{3,2,1,0:T(8,128)(2,1)S(1)} %collective-permute-done.4.rest_1_), channel_id=1, source_target_pairs={{0,1},{1,0},{2,3},{3,2},{4,5},{5,4},{6,7},{7,6},{8,9},{9,8},{10,11... | collective-permute-start | bytes 1179656 | tf_op jit(solution)/shard_map/ppermute | solution.py:188
  41.5 2.2 %collective-permute-start.9 = (bf16[4,3,64,256]{3,2,1,0:T(8,128)(2,1)S(1)}, bf16[4,3,64,256]{3,2,1,0:T(8,128)(2,1)S(1)}, u32[]{:S(2)}, u32[]{:S(2)}) collective-permute-start(bf16[4,3,64,256]{3,2,1,0:T(8,128)(2,1)S(1)} %collective-permute-done.5.rest_2_), channel_id=1, source_target_pairs={{0,1},{1,0},{2,3},{3,2},{4,5},{5,4},{6,7},{7,6},{8,9},{9,8},{10,11... | collective-permute-start | bytes 1179656 | tf_op jit(solution)/shard_map/ppermute | solution.py:188
  50.0 1.0 copy-start.1
  51.0 4.4 %collective-permute-start.11 = (bf16[4,2,256,256]{3,2,1,0:T(8,128)(2,1)}, bf16[4,2,256,256]{3,2,1,0:T(8,128)(2,1)S(1)}, u32[]{:S(2)}, u32[]{:S(2)}) collective-permute-start(bf16[4,2,256,256]{3,2,1,0:T(8,128)(2,1)} %all-to-all-done.data_ref), channel_id=1, source_target_pairs={{0,1},{1,0},{2,3},{3,2},{4,5},{5,4},{6,7},{7,6},{8,9},{9,8},{10,11... | collective-permute-start | bytes 3145736 | tf_op jit(solution)/shard_map/ppermute | solution.py:188
  51.1 1.2 %copy-start.2 = (bf16[8,256,256]{2,1,0:T(8,128)(2,1)S(1)}, bf16[8,256,256]{2,1,0:T(8,128)(2,1)}, u32[]{:S(2)}) copy-start(bf16[8,256,256]{2,1,0:T(8,128)(2,1)} %copy-done.1) | copy-start | bytes 3145732
  59.1 10.1 %collective-permute-start.13 = (bf16[2,1,5,64,256]{4,3,2,1,0:T(8,128)(2,1)S(1)}, bf16[2,1,5,64,256]{4,3,2,1,0:T(8,128)(2,1)S(1)}, u32[]{:S(2)}, u32[]{:S(2)}) collective-permute-start(bf16[2,1,5,64,256]{4,3,2,1,0:T(8,128)(2,1)S(1)} %get-tuple-element.60), channel_id=1, source_target_pairs={{0,2},{1,3},{2,0},{3,1},{4,6},{5,7},{6,4},{7,5},{8,10},{9,11},{10,... | collective-permute-start | bytes 983048 | tf_op jit(solution)/shard_map/ppermute | solution.py:188
  61.7 9.8 %collective-permute-start.12 = (bf16[2,1,5,64,256]{4,3,2,1,0:T(8,128)(2,1)S(1)}, bf16[2,1,5,64,256]{4,3,2,1,0:T(8,128)(2,1)S(1)}, u32[]{:S(2)}, u32[]{:S(2)}) collective-permute-start(bf16[2,1,5,64,256]{4,3,2,1,0:T(8,128)(2,1)S(1)} %products.7), channel_id=1, source_target_pairs={{0,4},{1,5},{2,6},{3,7},{4,0},{5,1},{6,2},{7,3},{8,12},{9,13},{10,... | collective-permute-start | bytes 983048 | tf_op jit(solution)/shard_map/ppermute | solution.py:188
  71.6 10.7 %collective-permute-start.16 = (bf16[2,1,5,64,256]{4,3,2,1,0:T(8,128)(2,1)S(1)}, bf16[2,1,5,64,256]{4,3,2,1,0:T(8,128)(2,1)S(1)}, u32[]{:S(2)}, u32[]{:S(2)}) collective-permute-start(bf16[2,1,5,64,256]{4,3,2,1,0:T(8,128)(2,1)S(1)} %get-tuple-element.70), channel_id=1, source_target_pairs={{0,2},{1,3},{2,0},{3,1},{4,6},{5,7},{6,4},{7,5},{8,10},{9,11},{10,... | collective-permute-start | bytes 983048 | tf_op jit(solution)/shard_map/ppermute | solution.py:188
  72.2 7.1 %collective-permute-start.21 = (bf16[1,5,64,256]{3,2,1,0:T(8,128)(2,1)S(1)}, bf16[1,5,64,256]{3,2,1,0:T(8,128)(2,1)S(1)}, u32[]{:S(2)}, u32[]{:S(2)}) collective-permute-start(bf16[1,5,64,256]{3,2,1,0:T(8,128)(2,1)S(1)} %get-tuple-element.76), channel_id=1, source_target_pairs={{0,4},{1,5},{2,6},{3,7},{4,0},{5,1},{6,2},{7,3},{8,12},{9,13},{10,... | collective-permute-start | bytes 491528 | tf_op jit(solution)/shard_map/ppermute | solution.py:188
  73.7 13.5 %collective-permute-start.14 = (bf16[2,1,5,64,256]{4,3,2,1,0:T(8,128)(2,1)S(1)}, bf16[2,1,5,64,256]{4,3,2,1,0:T(8,128)(2,1)S(1)}, u32[]{:S(2)}, u32[]{:S(2)}) collective-permute-start(bf16[2,1,5,64,256]{4,3,2,1,0:T(8,128)(2,1)S(1)} %products.9), channel_id=1, source_target_pairs={{0,4},{1,5},{2,6},{3,7},{4,0},{5,1},{6,2},{7,3},{8,12},{9,13},{10,... | collective-permute-start | bytes 983048 | tf_op jit(solution)/shard_map/ppermute | solution.py:188
  74.2 12.5 %collective-permute-start.19 = (bf16[1,5,64,256]{3,2,1,0:T(8,128)(2,1)S(1)}, bf16[1,5,64,256]{3,2,1,0:T(8,128)(2,1)S(1)}, u32[]{:S(2)}, u32[]{:S(2)}) collective-permute-start(bf16[1,5,64,256]{3,2,1,0:T(8,128)(2,1)S(1)} %get-tuple-element.74), channel_id=1, source_target_pairs={{0,2},{1,3},{2,0},{3,1},{4,6},{5,7},{6,4},{7,5},{8,10},{9,11},{10,... | collective-permute-start | bytes 491528 | tf_op jit(solution)/shard_map/ppermute | solution.py:188
  82.4 5.8 %collective-permute-start.17 = (bf16[1,5,64,256]{3,2,1,0:T(8,128)(2,1)S(1)}, bf16[1,5,64,256]{3,2,1,0:T(8,128)(2,1)S(1)}, u32[]{:S(2)}, u32[]{:S(2)}) collective-permute-start(bf16[1,5,64,256]{3,2,1,0:T(8,128)(2,1)S(1)} %get-tuple-element.72), channel_id=1, source_target_pairs={{0,4},{1,5},{2,6},{3,7},{4,0},{5,1},{6,2},{7,3},{8,12},{9,13},{10,... | collective-permute-start | bytes 491528 | tf_op jit(solution)/shard_map/ppermute | solution.py:188
  83.2 8.1 %collective-permute-start.22 = (bf16[5,64,256]{2,1,0:T(8,128)(2,1)S(1)}, bf16[5,64,256]{2,1,0:T(8,128)(2,1)S(1)}, u32[]{:S(2)}, u32[]{:S(2)}) collective-permute-start(bf16[5,64,256]{2,1,0:T(8,128)(2,1)S(1)} %add.36), channel_id=1, source_target_pairs={{0,24},{1,25},{2,26},{3,27},{4,28},{5,29},{6,30},{7,31},{8,16},{9,... | collective-permute-start | bytes 491528 | tf_op jit(solution)/shard_map/ppermute | solution.py:188
  86.8 11.1 %collective-permute-start.20 = (bf16[5,64,256]{2,1,0:T(8,128)(2,1)S(1)}, bf16[5,64,256]{2,1,0:T(8,128)(2,1)S(1)}, u32[]{:S(2)}, u32[]{:S(2)}) collective-permute-start(bf16[5,64,256]{2,1,0:T(8,128)(2,1)S(1)} %add.35), channel_id=1, source_target_pairs={{0,16},{1,17},{2,18},{3,19},{4,20},{5,21},{6,22},{7,23},{8,24},{9,... | collective-permute-start | bytes 491528 | tf_op jit(solution)/shard_map/ppermute | solution.py:188
  87.2 10.7 %collective-permute-start.15 = (bf16[1,5,64,256]{3,2,1,0:T(8,128)(2,1)S(1)}, bf16[1,5,64,256]{3,2,1,0:T(8,128)(2,1)S(1)}, u32[]{:S(2)}, u32[]{:S(2)}) collective-permute-start(bf16[1,5,64,256]{3,2,1,0:T(8,128)(2,1)S(1)} %get-tuple-element.68), channel_id=1, source_target_pairs={{0,2},{1,3},{2,0},{3,1},{4,6},{5,7},{6,4},{7,5},{8,10},{9,11},{10,... | collective-permute-start | bytes 491528 | tf_op jit(solution)/shard_map/ppermute | solution.py:188
  88.2 9.8 %collective-permute-start.18 = (bf16[5,64,256]{2,1,0:T(8,128)(2,1)S(1)}, bf16[5,64,256]{2,1,0:T(8,128)(2,1)S(1)}, u32[]{:S(2)}, u32[]{:S(2)}) collective-permute-start(bf16[5,64,256]{2,1,0:T(8,128)(2,1)S(1)} %add.34), channel_id=1, source_target_pairs={{0,8},{1,9},{2,10},{3,11},{4,12},{5,13},{6,14},{7,15},{8,0},{9,1},... | collective-permute-start | bytes 491528 | tf_op jit(solution)/shard_map/ppermute | solution.py:188
  97.9 1.0 copy-start.4
